TPU v7x, 128 devices: a whole 4x4x4 slice. The times are simulated.
128 devices in a mesh: section: 2 (over core), space: 64 (over z, y, x).
Axes of the slice: x: 4, y: 4, z: 4, core: 2. Of those that a mesh axis runs over, the one named last changes fastest.
Arguments:
- volume: bfloat16 [4, 32, 256, 8, 512], P(None, None, 'space'), may hold values from -6 to 6
- labels: int32 [4, 64, 2, 128], P(None, 'space'), may hold values from 0 to 3
- down_weight_two: bfloat16 [64, 32, 2, 2, 2], replicated, may hold values from -0.5 to 0.5
- w_conv_two: bfloat16 [64, 64, 3, 3, 3], replicated, may hold values from -0.21875 to 0.21875
- down_weight_three: bfloat16 [128, 64, 2, 2, 2], replicated, may hold values from -0.375 to 0.375
- w_conv_three: bfloat16 [128, 128, 3, 3, 3], replicated, may hold values from -0.15625 to 0.15625
- w_head: bfloat16 [128, 4], replicated, may hold values from -1.5 to 1.5
Outputs:
- grad_down_two: float32 [16384], P(('section', 'space'))
- grad_conv_two: float32 [110592], P(('section', 'space'))
- grad_down_three: float32 [65536], P(('section', 'space'))
- grad_conv_three: float32 [442368], P(('section', 'space'))
- grad_head: float32 [512], P(('section', 'space'))
All inputs are finite; a program needn't handle non-finite values.
Results may differ from a plain program's by a relative error of at most 0.017.
Values may be sent and summed in bfloat16 or wider, within the bound.
No kernel may reach another device: no remote copies, remote signals or barrier semaphores. Data moves between devices by JAX's collectives and lax.ppermute only.
A program may use at most 320 MiB of HBM per device.

v0:
```python
import math

import jax
import jax.numpy as jnp
from jax import lax
from jax.sharding import PartitionSpec as P

SHIFT = math.log(2.0)
FORWARD_DIMS = ("NCDHW", "OIDHW", "NCDHW")
MIRROR_DIMS = ("NCDHW", "IODHW", "NCDHW")
KERNEL_DIMS = ("CNDHW", "IODHW", "CNDHW")


def extended(block, sides, width):
    for axis, dim in sides:
        count = lax.axis_size(axis)
        forward = [(i, i + 1) for i in range(count - 1)]
        backward = [(target, source) for source, target in forward]
        low = lax.ppermute(
            lax.slice_in_dim(block, block.shape[dim] - width, None, axis=dim), axis, forward
        )
        high = lax.ppermute(lax.slice_in_dim(block, 0, width, axis=dim), axis, backward)
        block = jnp.concatenate([low, block, high], axis=dim)
    return block


def as_sent(shard):
    return jax.tree.map(lambda a: a.astype(jnp.bfloat16) if a.dtype == jnp.float32 else a, shard)


def from_partner(shard, axis, distance):
    return lax.ppermute(shard, axis, [(i, i ^ 1 << distance) for i in range(lax.axis_size(axis))])


def leaky_rectifier(value):
    return jax.nn.softplus(value) - SHIFT


def slope_of(stored):
    return 1.0 - 0.5 * jnp.exp(-stored.astype(jnp.float32))


def strided_reduce(input_volumes, filter_weight):
    return lax.conv_general_dilated(
        input_volumes,
        filter_weight,
        (2, 2, 2),
        "VALID",
        dimension_numbers=FORWARD_DIMS,
        preferred_element_type=jnp.float32,
    )


def down_input_grad(grads, filter_weight):
    return lax.conv_general_dilated(
        grads,
        filter_weight[:, :, ::-1, ::-1, ::-1],
        (1, 1, 1),
        ((1, 1), (1, 1), (1, 1)),
        lhs_dilation=(2, 2, 2),
        dimension_numbers=MIRROR_DIMS,
        preferred_element_type=jnp.float32,
    )


def down_weight_grad(input_volumes, grads):
    return lax.conv_general_dilated(
        input_volumes,
        grads,
        (1, 1, 1),
        "VALID",
        rhs_dilation=(2, 2, 2),
        dimension_numbers=KERNEL_DIMS,
        preferred_element_type=jnp.float32,
    )


def convolve(padded, filter_weight):
    return lax.conv_general_dilated(
        padded,
        filter_weight,
        (1, 1, 1),
        ((0, 0), (1, 1), (1, 1)),
        dimension_numbers=FORWARD_DIMS,
        preferred_element_type=jnp.float32,
    )


def mirrored(grads, filter_weight, depth_pad):
    return lax.conv_general_dilated(
        grads,
        filter_weight[:, :, ::-1, ::-1, ::-1],
        (1, 1, 1),
        (depth_pad, (1, 1), (1, 1)),
        dimension_numbers=MIRROR_DIMS,
        preferred_element_type=jnp.float32,
    )


def input_grad_parts(grads, filter_weight):
    inner = mirrored(grads, filter_weight, (1, 1))
    lower_rim = mirrored(grads[:, :, :1], filter_weight, (2, 2))[:, :, :1]
    upper_rim = mirrored(grads[:, :, -1:], filter_weight, (2, 2))[:, :, -1:]
    return (inner, jnp.concatenate([lower_rim, upper_rim], axis=2))


def conv_weight_grad(padded, grads):
    return lax.conv_general_dilated(
        padded,
        grads,
        (1, 1, 1),
        ((0, 0), (1, 1), (1, 1)),
        dimension_numbers=KERNEL_DIMS,
        preferred_element_type=jnp.float32,
    )


def with_faces(block):
    return extended(block, (("space", 2),), 1)


def fold_rims(inner, rims):
    outer = extended(as_sent(rims), (("space", 2),), 1).astype(rims.dtype)
    inner = inner.at[:, :, :1].add(outer[:, :, :1])
    return inner.at[:, :, -1:].add(outer[:, :, -1:])


def trade(block):
    return jax.tree.map(
        lambda part, own: part.astype(own.dtype), from_partner(as_sent(block), "section", 0), block
    )


def on_core(which, work, *operands):

    def blank(*values):
        return jax.tree.map(jnp.zeros_like, work(*values))

    return lax.cond(lax.axis_index("section") == which, work, blank, *operands)


def per_device(
    volume, labels, down_weight_two, w_conv_two, down_weight_three, w_conv_three, w_head
):
    classes = w_head.shape[1]
    voxels = (
        labels.shape[0]
        * labels.shape[1]
        * lax.axis_size("space")
        * labels.shape[2]
        * labels.shape[3]
    )
    scale = 1.0 / math.sqrt(voxels)
    levels = jnp.arange(classes, dtype=jnp.int32).reshape(1, classes, 1, 1, 1)

    def first_down(input_volumes):
        return leaky_rectifier(strided_reduce(input_volumes, down_weight_two)).astype(jnp.bfloat16)

    def first_conv(padded):
        hidden_features = leaky_rectifier(convolve(padded, w_conv_two)).astype(jnp.bfloat16)
        return (hidden_features, hidden_features)

    def second_down(incoming_faces):
        return leaky_rectifier(strided_reduce(incoming_faces, down_weight_three)).astype(
            jnp.bfloat16
        )

    def second_conv(padded, marks):
        top = leaky_rectifier(convolve(padded, w_conv_three)).astype(jnp.bfloat16)
        logits = jnp.einsum("ncdhw,ck->nkdhw", top, w_head, preferred_element_type=jnp.float32)
        powers = jnp.exp(logits)
        chosen = (marks[:, None] == levels).astype(jnp.float32)
        grad_logits = ((powers / jnp.sum(powers, axis=1, keepdims=True) - chosen) * scale).astype(
            jnp.bfloat16
        )
        grad_head = jnp.einsum(
            "ncdhw,nkdhw->ck", top, grad_logits, preferred_element_type=jnp.float32
        )
        grad_top = jnp.einsum(
            "nkdhw,ck->ncdhw", grad_logits, w_head, preferred_element_type=jnp.float32
        )
        grad_pre = (grad_top * slope_of(top)).astype(jnp.bfloat16)
        inner, rims = input_grad_parts(grad_pre, w_conv_three)
        return (grad_head, conv_weight_grad(padded, grad_pre), inner, rims)

    def second_tail(grad_mid, middle_features, incoming_faces):
        grad_low = (grad_mid * slope_of(middle_features)).astype(jnp.bfloat16)
        grad_back = (
            down_input_grad(grad_low, down_weight_three) * slope_of(incoming_faces)
        ).astype(jnp.bfloat16)
        return (down_weight_grad(incoming_faces, grad_low), grad_back)

    def first_back(grad_in, hidden_features, padded):
        grad_down = jnp.zeros(down_weight_three.shape, jnp.float32)
        inner, rims = input_grad_parts(grad_in, w_conv_two)
        return (grad_down, conv_weight_grad(padded, grad_in), inner, rims)

    def first_tail(grad_mid, leading_volume, input_volumes):
        grad_low = (grad_mid * slope_of(leading_volume)).astype(jnp.bfloat16)
        return down_weight_grad(input_volumes, grad_low)

    leading_volume = on_core(0, first_down, volume)
    padded = with_faces(leading_volume)
    hidden_features, sent = on_core(0, first_conv, padded)
    saved, sent = ((padded, hidden_features, leading_volume), sent)
    incoming_faces = trade(sent)
    middle_features = on_core(1, second_down, incoming_faces)
    padded = with_faces(middle_features)
    grad_head, grad_conv, inner, rims = on_core(1, second_conv, padded, labels)
    grad_down, grad_back = on_core(
        1, second_tail, fold_rims(inner, rims), middle_features, incoming_faces
    )
    grad_back, upper = (grad_back, (grad_head, grad_conv, grad_down))
    padded, hidden_features, leading_volume = saved
    grad_down, grad_conv, inner, rims = on_core(
        0, first_back, trade(grad_back), hidden_features, padded
    )
    grad_first = on_core(0, first_tail, fold_rims(inner, rims), leading_volume, volume)
    totals = (grad_first, grad_conv, grad_down + upper[2], upper[1], upper[0])
    flat = tuple((total.reshape(-1) for total in totals))
    return (
        lax.psum_scatter(flat[0], ("section", "space"), scatter_dimension=0, tiled=True),
        lax.psum_scatter(flat[1], ("section", "space"), scatter_dimension=0, tiled=True),
        lax.psum_scatter(flat[2], ("section", "space"), scatter_dimension=0, tiled=True),
        lax.psum_scatter(flat[3], ("section", "space"), scatter_dimension=0, tiled=True),
        lax.psum_scatter(flat[4], ("section", "space"), scatter_dimension=0, tiled=True),
    )


def solution(mesh):
    return jax.shard_map(
        per_device,
        mesh=mesh,
        in_specs=(
            P(None, None, "space", None, None),
            P(None, "space", None, None),
            P(),
            P(),
            P(),
            P(),
            P(),
        ),
        out_specs=(
            P(("section", "space")),
            P(("section", "space")),
            P(("section", "space")),
            P(("section", "space")),
            P(("section", "space")),
        ),
        check_vma=False,
    )
```

profile of v0, /device:TPU:1, one launch (start us, length us, event | category | flops | bytes accessed | tf_op | source)
XLA Modules:
  0.0 765.5 jit_solution(17420610322088265184)
XLA Ops:
  7.2 6.0 conditional.7
  14.6 2.3 copy.179
  17.0 4.7 collective-permute-start
  24.1 3.0 copy.148
  27.3 1.7 copy.147
  29.0 4.0 collective-permute-done.1
  33.1 2.3 copy.149
  35.3 6.0 pad_maximum_fusion.2
  41.4 4.7 conditional.8
  47.1 105.3 %collective-permute-start.2 = (bf16[4,64,2,4,256]{4,1,3,2,0:T(8,128)(2,1)S(1)}, bf16[4,64,2,4,256]{4,1,3,2,0:T(8,128)(2,1)S(1)}, u32[]{:S(2)}, u32[]{:S(2)}) collective-permute-start(bf16[4,64,2,4,256]{4,1,3,2,0:T(8,128)(2,1)S(1)} %copy.150), channel_id=1, source_target_pairs={{0,64},{64,0},{1,65},{65,1},{2,66},{66,2},{3,67},{67,3},{4,68},{68... | collective-permute-start | bytes 3145736 | tf_op jit(solution)/shard_map/ppermute | solution.py:32
  152.4 2.3 collective-permute-done.2
  154.7 3.2 conditional.9
  158.1 2.3 collective-permute-start.3
  161.8 2.5 collective-permute-done.3
  164.3 4.1 collective-permute-done.4
  169.1 20.0 %conditional.10 = (f32[128,4]{0,1:T(4,128)}, f32[128,128,3,3,3]{0,1,4,3,2:T(8,128)}, f32[4,128,1,2,128]{1,3,4,0,2:T(2,128)}, bf16[4,128,2,2,128]{1,3,4,0,2:T(2,128)(2,1)S(1)}) conditional(s32[]{:T(128)} %convert_element_type.78, () %tuple.97, (bf16[4,128,3,2,128]{1,0,4,3,2:T(4,128)(2,1)S(1)}, bf16[128,128,3,3,3]{1,0,4,3,2:T(8,128)(2,1)}, ...), branch_computations={%region_6.7_spmd, %region_7.9_spmd} | conditional | flops 2108042240 | bytes 30224220 | solution.py:139
  169.8 4.4 multiply_subtract_fusion
  177.4 1.5 convolution_select_fusion
  179.9 2.1 convolution_select_fusion.1
  183.3 4.8 fusion.51
  189.4 4.8 collective-permute-start.5
  195.6 1.6 collective-permute-done.5
  197.1 4.5 collective-permute-done.6
  203.1 21.4 %conditional.11 = (f32[128,64,2,2,2]{0,1,4,3,2:T(8,128)}, bf16[4,64,2,4,256]{1,3,4,0,2:T(4,128)(2,1)S(1)}) conditional(s32[]{:T(128)} %convert_element_type.78, () %tuple.96, (f32[4,128,4,2,128]{1,3,4,0,2:T(2,128)S(1)}, f32[4,128,1,2,128]{1,3,4,0,2:T(2,128)}, bf16[4,128,1,2,128]{1,4,0,3,2:T(8,128)(2,1)S(1)}, ...), branch_computations={%region_9.10_spmd, %region_10.11_spmd} | conditional | flops 281575424 | bytes 21791882 | solution.py:139
  203.1 1.8 multiply_convert_fusion.1
  207.0 4.9 copy.133
  211.9 2.4 copy.158
  214.4 3.9 fusion.61
  218.2 2.5 copy.130
  220.7 3.8 fusion.63
  225.7 2.6 collective-permute-done.7
  228.3 13.7 %conditional.12 = (f32[64,64,3,3,3]{0,1,4,3,2:T(8,128)}, f32[4,64,2,4,256]{1,3,4,0,2:T(4,128)}, f32[4,64,2,4,256]{1,3,4,0,2:T(4,128)}, f32[]{:T(128)}, f32[4,64,1,4,256]{1,3,4,0,2:T(4,128)}) conditional(s32[]{:T(128)} %convert_element_type.77, () %tuple.93, (bf16[4,64,4,4,256]{1,0,4,3,2:T(4,128)(2,1)}, bf16[4,64,2,4,256]{4,1,3,2,0:T(8,128)(2,1)S(1)}, ...), branch_computations={%region_11.12_spmd, %region_12.13_spmd} | conditional | flops 3071655936 | bytes 72826272 | solution.py:139
  228.3 2.7 broadcast.247
  231.0 2.7 broadcast.247.clone
  233.7 1.6 broadcast.248
  242.0 3.2 copy.162
  246.3 4.5 collective-permute-start.8
  252.1 75.5 %copy.171 = f32[128,128,3,3,3]{4,3,2,1,0:T(4,128)} copy(f32[128,128,3,3,3]{0,1,4,3,2:T(8,128)} %get-tuple-element.247) | data formatting | bytes 3538944 | tf_op jit(solution)/shard_map/cond | solution.py:139
  327.6 73.9 %reshape.224 = f32[442368]{0:T(1024)} reshape(f32[128,128,3,3,3]{4,3,2,1,0:T(4,128)} %copy.171) | data formatting | bytes 3538944 | tf_op jit(solution)/shard_map/reshape | solution.py:220
  402.5 12.1 %copy.170 = f32[128,64,2,2,2]{4,3,2,1,0:T(2,128)} copy(f32[128,64,2,2,2]{0,1,4,3,2:T(8,128)S(1)} %broadcast_add_fusion) | data formatting | bytes 524288 | tf_op jit(solution)/shard_map/add | solution.py:219
  414.6 22.7 %reshape.223 = f32[65536]{0:T(1024)} reshape(f32[128,64,2,2,2]{4,3,2,1,0:T(2,128)} %copy.170) | data formatting | bytes 524288 | tf_op jit(solution)/shard_map/reshape | solution.py:220
  437.3 24.0 %copy.169 = f32[64,64,3,3,3]{4,3,2,1,0:T(4,128)} copy(f32[64,64,3,3,3]{0,1,4,3,2:T(8,128)} %get-tuple-element.244) | data formatting | bytes 884736 | tf_op jit(solution)/shard_map/cond | solution.py:139
  461.3 20.0 %reshape.222 = f32[110592]{0:T(1024)} reshape(f32[64,64,3,3,3]{4,3,2,1,0:T(4,128)} %copy.169) | data formatting | bytes 884736 | tf_op jit(solution)/shard_map/reshape | solution.py:220
  481.3 3.6 maximum_convert_fusion
  485.2 4.8 copy.168
  490.0 7.3 reshape.221
  498.2 168.0 %all-reduce.4 = f32[512]{0:T(512)S(1)} all-reduce(f32[512]{0:T(512)S(1)} %reshape.225), channel_id=6, replica_groups=mesh['section'=2,'space'=64] {'section','space'}, use_global_device_ids=true, to_apply=%region_19.20.clone | all-reduce | flops 512 | bytes 4096
  666.8 86.0 %all-reduce.8.cloned.1.call-done = (f32[16384]{0:T(1024)}, f32[110592]{0:T(1024)}, f32[65536]{0:T(1024)}, f32[442368]{0:T(1024)}) async-done(((f32[16384]{0:T(1024)}, f32[110592]{0:T(1024)}, f32[65536]{0:T(1024)}, f32[442368]{0:T(1024)}), (f32[16384]{0:T(1024)}, f32[110592]{0:T(1024)}, f32[65536]{0:T(1024)}, f32[442368]{0:T(1024)})) %all-reduce.8.cloned.1.call-update) | async-done | bytes 2539536
  (88 shorter events, 35.8 us)
Async XLA Ops:
  7.2 745.7 %all-reduce.8.cloned.1.call-start = ((), (), s32[]{:S(2)}) async-start(), calls=%async_computation | async-start | bytes 5079040
  13.3 13.8 %copy-start.1 = (bf16[4,64,2,4,256]{1,4,0,3,2:T(8,128)(2,1)}, bf16[4,64,2,4,256]{1,4,0,3,2:T(8,128)(2,1)S(1)}, u32[]{:S(2)}) copy-start(bf16[4,64,2,4,256]{1,4,0,3,2:T(8,128)(2,1)S(1)} %get-tuple-element.365) | copy-start | bytes 3145732
  17.0 10.4 %collective-permute-start = (bf16[4,64,1,4,256]{4,1,3,2,0:T(8,128)(2,1)}, bf16[4,64,1,4,256]{4,1,3,2,0:T(8,128)(2,1)}, u32[]{:S(2)}, u32[]{:S(2)}) collective-permute-start(bf16[4,64,1,4,256]{4,1,3,2,0:T(8,128)(2,1)} %copy.179), channel_id=1, source_target_pairs={{0,1},{1,2},{2,3},{3,4},{4,5},{5,6},{6,7},{7,8},{8,9},{9,10},{10,1... | collective-permute-start | bytes 1572872 | tf_op jit(solution)/shard_map/ppermute | solution.py:19
  22.8 10.2 %collective-permute-start.1 = (bf16[4,64,1,4,256]{4,1,3,2,0:T(8,128)(2,1)}, bf16[4,64,1,4,256]{4,1,3,2,0:T(8,128)(2,1)}, u32[]{:S(2)}, u32[]{:S(2)}) collective-permute-start(bf16[4,64,1,4,256]{4,1,3,2,0:T(8,128)(2,1)} %copy.180), channel_id=1, source_target_pairs={{1,0},{2,1},{3,2},{4,3},{5,4},{6,5},{7,6},{8,7},{9,8},{10,9},{11,1... | collective-permute-start | bytes 1572872 | tf_op jit(solution)/shard_map/ppermute | solution.py:22
  27.1 8.2 %copy-start.6 = (bf16[4,64,2,4,256]{1,0,4,3,2:T(4,128)(2,1)S(1)}, bf16[4,64,2,4,256]{1,0,4,3,2:T(4,128)(2,1)}, u32[]{:S(2)}) copy-start(bf16[4,64,2,4,256]{1,0,4,3,2:T(4,128)(2,1)} %copy.148) | copy-start | bytes 3145732
  41.4 113.4 %copy-start.12 = (bf16[128,64,2,2,2]{0,4,3,2,1:T(2,128)(2,1)S(1)}, bf16[128,64,2,2,2]{0,4,3,2,1:T(2,128)(2,1)}, u32[]{:S(2)}) copy-start(bf16[128,64,2,2,2]{0,4,3,2,1:T(2,128)(2,1)} %param.37) | copy-start | bytes 393220
  47.1 107.6 %collective-permute-start.2 = (bf16[4,64,2,4,256]{4,1,3,2,0:T(8,128)(2,1)S(1)}, bf16[4,64,2,4,256]{4,1,3,2,0:T(8,128)(2,1)S(1)}, u32[]{:S(2)}, u32[]{:S(2)}) collective-permute-start(bf16[4,64,2,4,256]{4,1,3,2,0:T(8,128)(2,1)S(1)} %copy.150), channel_id=1, source_target_pairs={{0,64},{64,0},{1,65},{65,1},{2,66},{66,2},{3,67},{67,3},{4,68},{68... | collective-permute-start | bytes 3145736 | tf_op jit(solution)/shard_map/ppermute | solution.py:32
  154.7 14.3 %copy-start.15 = (s32[4,1,2,128]{3,2,1,0:T(2,128)S(1)}, s32[4,1,2,128]{3,2,1,0:T(2,128)}, u32[]{:S(2)}) copy-start(s32[4,1,2,128]{3,2,1,0:T(2,128)} %param.34) | copy-start | bytes 12292
  154.7 14.3 %copy-start.16 = (bf16[128,4]{0,1:T(4,128)(2,1)S(1)}, bf16[128,4]{0,1:T(4,128)(2,1)}, u32[]{:S(2)}) copy-start(bf16[128,4]{0,1:T(4,128)(2,1)} %param.39) | copy-start | bytes 3076
  157.9 11.2 %copy-start.8 = (bf16[4,128,1,2,128]{1,4,0,3,2:T(8,128)(2,1)}, bf16[4,128,1,2,128]{1,4,0,3,2:T(8,128)(2,1)S(1)}, u32[]{:S(2)}) copy-start(bf16[4,128,1,2,128]{1,4,0,3,2:T(8,128)(2,1)S(1)} %get-tuple-element.367) | copy-start | bytes 786436
  158.1 6.1 collective-permute-start.3
  160.5 7.9 %collective-permute-start.4 = (bf16[4,128,1,2,128]{1,0,4,3,2:T(4,128)(2,1)S(1)}, bf16[4,128,1,2,128]{1,0,4,3,2:T(4,128)(2,1)S(1)}, u32[]{:S(2)}, u32[]{:S(2)}) collective-permute-start(bf16[4,128,1,2,128]{1,0,4,3,2:T(4,128)(2,1)S(1)} %copy.153), channel_id=1, source_target_pairs={{1,0},{2,1},{3,2},{4,3},{5,4},{6,5},{7,6},{8,7},{9,8},{10,9},{11,1... | collective-permute-start | bytes 786440 | tf_op jit(solution)/shard_map/ppermute | solution.py:22
  174.3 3.2 copy-start.7
  174.3 3.2 copy-start.14
  189.1 14.0 %copy-start.9 = (bf16[4,128,1,2,128]{1,4,0,3,2:T(8,128)(2,1)S(1)}, bf16[4,128,1,2,128]{1,4,0,3,2:T(8,128)(2,1)}, u32[]{:S(2)}) copy-start(bf16[4,128,1,2,128]{1,4,0,3,2:T(8,128)(2,1)} %copy-done.8) | copy-start | bytes 786436
  189.1 14.0 %copy-start.13 = (bf16[128,64,2,2,2]{0,4,3,2,1:T(2,128)(2,1)S(1)}, bf16[128,64,2,2,2]{0,4,3,2,1:T(2,128)(2,1)}, u32[]{:S(2)}) copy-start(bf16[128,64,2,2,2]{0,4,3,2,1:T(2,128)(2,1)} %param.37) | copy-start | bytes 393220
  189.4 7.7 %collective-permute-start.5 = (bf16[4,128,1,2,128]{1,3,4,0,2:T(2,128)(2,1)S(1)}, bf16[4,128,1,2,128]{1,3,4,0,2:T(2,128)(2,1)S(1)}, u32[]{:S(2)}, u32[]{:S(2)}) collective-permute-start(bf16[4,128,1,2,128]{1,3,4,0,2:T(2,128)(2,1)S(1)} %get-tuple-element.337), channel_id=1, source_target_pairs={{0,1},{1,2},{2,3},{3,4},{4,5},{5,6},{6,7},{7,8},{8,9},{9,10},{10,1... | collective-permute-start | bytes 786440 | tf_op jit(solution)/shard_map/ppermute | solution.py:19
  194.3 7.4 collective-permute-start.6
  204.9 0.7 copy-start.10
  214.4 6.3 copy-start.11
  225.6 2.7 collective-permute-start.7
  246.3 235.0 %collective-permute-start.8 = (bf16[4,64,1,4,256]{4,1,3,2,0:T(8,128)(2,1)}, bf16[4,64,1,4,256]{4,1,3,2,0:T(8,128)(2,1)}, u32[]{:S(2)}, u32[]{:S(2)}) collective-permute-start(bf16[4,64,1,4,256]{4,1,3,2,0:T(8,128)(2,1)} %get-tuple-element.335), channel_id=1, source_target_pairs={{0,1},{1,2},{2,3},{3,4},{4,5},{5,6},{6,7},{7,8},{8,9},{9,10},{10,1... | collective-permute-start | bytes 1572872 | tf_op jit(solution)/shard_map/ppermute | solution.py:19
  250.9 230.4 %collective-permute-start.9 = (bf16[4,64,1,4,256]{4,1,3,2,0:T(8,128)(2,1)}, bf16[4,64,1,4,256]{4,1,3,2,0:T(8,128)(2,1)}, u32[]{:S(2)}, u32[]{:S(2)}) collective-permute-start(bf16[4,64,1,4,256]{4,1,3,2,0:T(8,128)(2,1)} %get-tuple-element.336), channel_id=1, source_target_pairs={{1,0},{2,1},{3,2},{4,3},{5,4},{6,5},{7,6},{8,7},{9,8},{10,9},{11,1... | collective-permute-start | bytes 1572872 | tf_op jit(solution)/shard_map/ppermute | solution.py:22
  481.3 3.6 copy-start.2
Sparse Core Ops, SparseCore 0:
  497.5 255.3 all-reduce.7
where the time goes:
time: 776 us; the launch traced here: 765 us
  local copies, waits for them, and re-layouts  292 us (38%)
  blocking collectives  168 us (22%)
  starting transfers between devices  127 us (16%)
  waiting for transfers between devices  108 us (14%)
  matrix products  20.5 us (3%)
  other arithmetic  19.3 us (2%)
  loops' own time  16.1 us (2%)
  between operations  14.7 us (2%)
    unnamed x1, blocking collectives  168 us
    reshape x5, local copies, waits for them, and re-layouts, per_device(): flat = tuple((total.reshape(-1) for total in totals))  124 us
    cond x9, local copies, waits for them, and re-layouts, on_core(): return lax.cond(lax.axis_index('section') == which, work, blank, *operands)  114 us
    ppermute x2, starting transfers between devices, from_partner(): lax.ppermute(shard, axis, [(i, i ^ 1 << distance) for i in range(lax.axis...  105 us
    unnamed x2, waiting for transfers between devices  86 us
    ppermute x4, starting transfers between devices, extended(): lax.ppermute(lax.slice_in_dim(block, block.shape[dim] - width, None, axis...  16.4 us
    another operation x7, loops' own time, on_core(): return lax.cond(lax.axis_index('section') == which, work, blank, *operands)  16.1 us
  transfers between devices with their start and end apart: 11, of which 9 were waited for; matrix products, arithmetic and copies ran while one was open for 31% of the time, Pallas kernels for 0%

commit v1 on v0

v1 whole, which is shorter than its diff:
```python
import functools
import math

import jax
import jax.numpy as jnp
from jax import lax
from jax.experimental import pallas as pl
from jax.experimental.pallas import tpu as pltpu
from jax.sharding import PartitionSpec as P


F32 = jnp.float32
BF16 = jnp.bfloat16
SHIFT = math.log(2.0)
CROPS = 2
T = 256
ROWS = 40
DOWN3, CONV2, DOWN2, HEAD = 27, 31, 38, 39


def params(megabytes=48):
    return pltpu.CompilerParams(vmem_limit_bytes=megabytes << 20)


def rectified(v):
    return jnp.maximum(v, 0.0) + jnp.log1p(jnp.exp(-jnp.abs(v))) - SHIFT


def slope(stored):
    return 1.0 - 0.5 * jnp.exp(-stored.astype(F32))


def dot(a, b):
    return jnp.dot(a, b, preferred_element_type=F32)


def dot_tn(a, b):
    return lax.dot_general(a, b, (((0,), (0,)), ((), ())), preferred_element_type=F32)


def dot_nt(a, b):
    return lax.dot_general(a, b, (((1,), (1,)), ((), ())), preferred_element_type=F32)


def moved(x, by):
    x = x.astype(F32)
    lane = lax.broadcasted_iota(jnp.int32, x.shape, 1)
    edge = 0 if by == 1 else 127
    return jnp.where(lane == edge, 0.0, pltpu.roll(x, by % 128, 1)).astype(BF16)


def three_two(x):
    even, odd = x[:, :128], x[:, 128:]
    return ((moved(odd, 1), even), (even, odd), (odd, moved(even, -1)))


def three_three(x):
    first, second = x[:, :128], x[:, 128:]
    return ((moved(first, 1), moved(second, 1)), (first, second), (moved(first, -1), moved(second, -1)))


def put_three(ref, row, shifted):
    for j, (left, right) in enumerate(shifted):
        ref[pl.ds(row + j * T, T), 0:128] = left
        ref[pl.ds(row + j * T, T), 128:256] = right


def call(kernel, outs, *args, scratch=(), **more):
    return pl.pallas_call(
        kernel,
        out_shape=[jax.ShapeDtypeStruct(s, d) for s, d in outs],
        scratch_shapes=list(scratch),
        compiler_params=params(),
        **more,
    )(*args)


def first_kernel(sec_ref, vol_ref, w_ref, vp_ref, a_ref, sort_ref, wt_ref):
    @pl.when(pl.program_id(0) == 0)
    def _():
        w = lax.broadcasted_iota(jnp.int32, (512, 512), 0)
        to = lax.broadcasted_iota(jnp.int32, (512, 512), 1)
        source = (to % 128) * 4 + (to // 128) % 2 * 2 + to // 256
        sort_ref[...] = jnp.where(w == source, 1.0, 0.0).astype(BF16)
        for d in range(2):
            wt_ref[:, pl.ds(d * 512, 512)] = w_ref[d].astype(F32).T.astype(BF16)

    for d in range(2):
        v = vol_ref[0, :, d].astype(F32).reshape(256, 512).astype(BF16)
        s = dot(v, sort_ref[...]).astype(BF16)
        vp_ref[0, 0, pl.ds(d * 512, 256), :] = s[:, :256]
        vp_ref[0, 0, pl.ds(d * 512 + 256, 256), :] = s[:, 256:]
    a_ref[0, 0] = rectified(dot(wt_ref[...], vp_ref[0, 0])).astype(BF16)


def first(sec, volume, w1):
    return pl.pallas_call(
        first_kernel,
        grid_spec=pltpu.PrefetchScalarGridSpec(
            num_scalar_prefetch=1,
            grid=(4,),
            in_specs=[
                pl.BlockSpec((1, 32, 2, 8, 512), lambda i, s: (2 * s[0] + i // 2, 0, i % 2, 0, 0)),
                pl.BlockSpec((2, 512, 256), lambda i, s: (0, 0, 0)),
            ],
            out_specs=[
                pl.BlockSpec((1, 1, 1024, 256), lambda i, s: (i // 2, i % 2, 0, 0)),
                pl.BlockSpec((1, 1, 256, 256), lambda i, s: (i // 2, i % 2, 0, 0)),
            ],
            scratch_shapes=[pltpu.VMEM((512, 512), BF16), pltpu.VMEM((256, 1024), BF16)],
        ),
        out_shape=[
            jax.ShapeDtypeStruct((CROPS, 2, 1024, 256), BF16),
            jax.ShapeDtypeStruct((CROPS, 2, 256, 256), BF16),
        ],
        compiler_params=params(),
    )(sec, volume, w1)


def prepare_kernel(w2_ref, w3_ref, f2_ref, b2_ref, f3_ref, b3_ref, perm_ref):
    low = lax.broadcasted_iota(jnp.int32, (64, 128), 1) < 64
    zero = jnp.zeros((64, 128), F32)
    for d in range(3):
        for j in range(3):
            at = (d * 3 + j) * T
            back = (8 - d * 3 - j) * T
            w = [w2_ref[d * 9 + h * 3 + j].astype(F32) for h in range(3)]
            pairs = {
                (0, 0): jnp.where(low, w[1], w[2]),
                (0, 1): zero,
                (1, 0): jnp.where(low, w[0], w[1]),
                (1, 1): jnp.where(low, w[2], 0.0),
                (2, 0): jnp.where(low, 0.0, w[0]),
                (2, 1): jnp.where(low, w[1], w[2]),
                (3, 0): zero,
                (3, 1): jnp.where(low, w[0], w[1]),
            }
            for (row, col), block in pairs.items():
                f2_ref[pl.ds(row * 64, 64), pl.ds(at + col * 128, 128)] = block.astype(BF16)
            b2_ref[:, pl.ds(back, T)] = f2_ref[:, pl.ds(at, T)].astype(F32).T.astype(BF16)
            for row in range(2):
                for col in range(2):
                    block = w3_ref[d * 9 + (col - row + 1) * 3 + j]
                    f3_ref[pl.ds(row * 128, 128), pl.ds(at + col * 128, 128)] = block
                    b3_ref[pl.ds(col * 128, 128), pl.ds(back + row * 128, 128)] = block.astype(F32).T.astype(BF16)
    r = lax.broadcasted_iota(jnp.int32, (1024, 256), 0)
    to = lax.broadcasted_iota(jnp.int32, (1024, 256), 1)
    c, h = r // 8 % 32, r % 8
    target = c // 16 * 128 + c % 16 * 8 + r // 512 * 4 + h * 2 + r // 256 % 2
    perm_ref[...] = jnp.where((target == to) & (h < 2), 1.0, 0.0).astype(BF16)


def prepare(w2, w3):
    wide = ((T, 9 * T), BF16)
    return call(prepare_kernel, [wide] * 4 + [((1024, 256), BF16)], w2, w3)


def second_kernel(lo_ref, a_ref, hi_ref, f2_ref, wd_ref, h_ref, a3_ref, b_ref):
    for n in range(CROPS):
        planes = (lo_ref[n, 0], a_ref[n, 0], a_ref[n, 1], hi_ref[n, 0])
        for k, plane in enumerate(planes):
            put_three(b_ref, k * 3 * T, three_two(plane))
        for d in range(2):
            h = rectified(dot(f2_ref[...], b_ref[pl.ds(d * 3 * T, 9 * T), :])).astype(BF16)
            for p in range(2):
                h_ref[2 * d + p, :, pl.ds(n * 128, 128)] = h[:, p * 128 : (p + 1) * 128]
    total = dot_tn(wd_ref[0], h_ref[0])
    for k in range(1, 4):
        total += dot_tn(wd_ref[k], h_ref[k])
    a3_ref[...] = rectified(total).astype(BF16)


def second(lo, a, hi, f2, wd):
    return call(
        second_kernel,
        [((4, T, T), BF16), ((T, T), BF16)],
        lo, a, hi, f2, wd,
        scratch=[pltpu.VMEM((12 * T, T), BF16)],
    )


def head_kernel(scale, lo_ref, a_ref, hi_ref, f3_ref, wh_ref, wht_ref, marks_ref, gz_ref, gh_ref, b_ref):
    for k, ref in enumerate((lo_ref, a_ref, hi_ref)):
        put_three(b_ref, k * 3 * T, three_three(ref[...]))
    top = rectified(dot(f3_ref[...], b_ref[...])).astype(BF16)
    row = lax.broadcasted_iota(jnp.int32, (128, T), 0)
    total = jnp.zeros((128, 128), F32)
    for h in range(2):
        mine = top[h * 128 : (h + 1) * 128]
        logits = dot(wht_ref[...], mine)
        powers = jnp.where(row < 4, jnp.exp(logits), 0.0)
        share = powers / jnp.sum(powers, axis=0, keepdims=True)
        chosen = jnp.where(row == marks_ref[pl.ds(h, 1), :], 1.0, 0.0)
        g = jnp.where(row < 4, (share - chosen) * scale, 0.0).astype(BF16)
        total += dot_nt(mine, g)
        gz_ref[pl.ds(h * 128, 128), :] = (dot(wh_ref[...], g) * slope(mine)).astype(BF16)
    gh_ref[...] = total


def head(lo, a, hi, f3, wh, wht, marks, scale):
    return call(
        functools.partial(head_kernel, scale),
        [((T, T), BF16), ((128, 128), F32)],
        lo, a, hi, f3, wh, wht, marks,
        scratch=[pltpu.VMEM((9 * T, T), BF16)],
    )


def weight_three_kernel(g_ref, lo_ref, a_ref, hi_ref, out_ref, s_ref):
    put_three(s_ref, 0, three_three(g_ref[...]))
    for d, ref in enumerate((lo_ref, a_ref, hi_ref)):
        a = ref[...]
        for j in range(3):
            t = dot_nt(s_ref[pl.ds((2 - j) * T, T), :], a)
            out_ref[d * 9 + j] = t[128:, :128]
            out_ref[d * 9 + 3 + j] = t[:128, :128] + t[128:, 128:]
            out_ref[d * 9 + 6 + j] = t[:128, 128:]


def weight_three(g, lo, a, hi):
    return call(
        weight_three_kernel,
        [((27, 128, 128), F32)],
        g, lo, a, hi,
        scratch=[pltpu.VMEM((3 * T, T), BF16)],
    )[0]


def middle_kernel(lo_ref, g_ref, hi_ref, b3_ref, a3_ref, h_ref, wd_ref, gz2_ref, gd_ref, b_ref):
    for k, ref in enumerate((lo_ref, g_ref, hi_ref)):
        put_three(b_ref, k * 3 * T, three_three(ref[...]))
    gy = (dot(b3_ref[...], b_ref[...]) * slope(a3_ref[...])).astype(BF16)
    for d in range(2):
        for p in range(2):
            k = 2 * d + p
            q = (dot(wd_ref[k], gy) * slope(h_ref[k])).astype(BF16)
            for n in range(CROPS):
                gz2_ref[n, d, :, pl.ds(p * 128, 128)] = q[:, n * 128 : (n + 1) * 128]
    for k in range(4):
        gd_ref[k] = dot_nt(gy[:128], h_ref[k, :128]) + dot_nt(gy[128:], h_ref[k, 128:])


def middle(lo, g, hi, b3, a3, h, wd):
    return call(
        middle_kernel,
        [((CROPS, 2, T, T), BF16), ((4, 128, 128), F32)],
        lo, g, hi, b3, a3, h, wd,
        scratch=[pltpu.VMEM((9 * T, T), BF16)],
    )


def weight_two_kernel(g_ref, lo_ref, a_ref, hi_ref, out_ref, gs_ref, as_ref):
    for n in range(CROPS):
        planes = (lo_ref[n, 0], a_ref[n, 0], a_ref[n, 1], hi_ref[n, 0])
        for d in range(2):
            at = (2 * n + d) * T
            for j, (left, right) in enumerate(three_two(g_ref[n, d])):
                gs_ref[2 - j, :, pl.ds(at, 128)] = left
                gs_ref[2 - j, :, pl.ds(at + 128, 128)] = right
            for k in range(3):
                as_ref[k, :, pl.ds(at, T)] = planes[d + k]
    low = lax.broadcasted_iota(jnp.int32, (64, 128), 1) < 64
    block = (lax.broadcasted_iota(jnp.int32, (64, 128), 1) // 32) % 2 == 0
    sums = {}
    for d in range(3):
        for j in range(3):
            t = dot_nt(gs_ref[j], as_ref[d])
            q = lambda r, c: t[r * 64 : (r + 1) * 64, c * 128 : (c + 1) * 128]
            sums[d, 0, j] = jnp.where(low, q(1, 0) + q(3, 1), q(2, 0))
            sums[d, 1, j] = jnp.where(low, q(0, 0) + q(2, 1), q(1, 0) + q(3, 1))
            sums[d, 2, j] = jnp.where(low, q(1, 1), q(0, 0) + q(2, 1))
        for h in range(3):
            for j in range(3):
                s = sums[d, h, j]
                sums[d, h, j] = s + pltpu.roll(s, 64, 1)
    taps = [sums[t // 9, t // 3 % 3, t % 3] for t in range(27)] + [jnp.zeros((64, 128), F32)]
    for g in range(7):
        four = taps[4 * g : 4 * g + 4]
        turned = [pltpu.roll(x, 32, 1) for x in four]
        out_ref[g, 0] = jnp.where(low, jnp.where(block, four[0], turned[1]), jnp.where(block, four[2], turned[3]))
        out_ref[g, 1] = jnp.where(low, jnp.where(block, turned[0], four[1]), jnp.where(block, turned[2], four[3]))


def weight_two(g, lo, a, hi):
    return call(
        weight_two_kernel,
        [((7, 2, 64, 128), F32)],
        g, lo, a, hi,
        scratch=[pltpu.VMEM((3, T, 4 * T), BF16), pltpu.VMEM((3, T, 4 * T), BF16)],
    )[0]


def last_kernel(
    lo_ref, g_ref, hi_ref, b2_ref, a_ref, vp_ref, perm_ref, w3_ref, d3_ref, w2_ref, gh_ref, out_ref, b_ref, t_ref, pack_ref
):
    for n in range(CROPS):
        planes = (lo_ref[n, 0], g_ref[n, 0], g_ref[n, 1], hi_ref[n, 0])
        for k, plane in enumerate(planes):
            put_three(b_ref, k * 3 * T, three_two(plane))
        for d in range(2):
            gy = (dot(b2_ref[...], b_ref[pl.ds(d * 3 * T, 9 * T), :]) * slope(a_ref[n, d])).astype(BF16)
            t = dot_nt(gy, vp_ref[n, d])
            if n + d == 0:
                t_ref[...] = t
            else:
                t_ref[...] += t
    pairs = []
    lane = lax.broadcasted_iota(jnp.int32, (64, 128), 1)
    for tile in range(8):
        at = pl.ds(tile * 128, 128)
        x = jnp.zeros((64, 128), F32)
        for h in range(4):
            x = jnp.where(lane % 8 // 2 == h, t_ref[pl.ds(h * 64, 64), at], x)
        x = x + pltpu.roll(x, 126, 1)
        x = x + pltpu.roll(x, 124, 1)
        pairs.append(x.astype(BF16))
    down = dot(jnp.concatenate(pairs, axis=1), perm_ref[...])
    for t in range(27):
        pack_ref[pl.ds(t, 128, stride=ROWS), :] = w3_ref[t]
    for k in range(4):
        pack_ref[pl.ds(DOWN3 + k, 128, stride=ROWS), :] = d3_ref[k]
    for half in range(2):
        for g in range(7):
            pack_ref[pl.ds(half * ROWS + CONV2 + g, 64, stride=2 * ROWS), :] = w2_ref[g, half]
        pack_ref[pl.ds(half * ROWS + DOWN2, 64, stride=2 * ROWS), :] = down[:, half * 128 : (half + 1) * 128]
    pack_ref[pl.ds(HEAD, 128, stride=ROWS), :] = gh_ref[...]
    out_ref[...] = pack_ref[...].astype(BF16)


def last(*args):
    return call(
        last_kernel,
        [((128 * ROWS, 128), BF16)],
        *args,
        scratch=[pltpu.VMEM((12 * T, T), BF16), pltpu.VMEM((T, 1024), F32), pltpu.VMEM((128 * ROWS, 128), F32)],
    )[0]


def neighbours(to_upper, to_lower):
    count = lax.axis_size("space")
    up = [(i, i + 1) for i in range(count - 1)]
    down = [(i + 1, i) for i in range(count - 1)]
    return lax.ppermute(to_upper, "space", up), lax.ppermute(to_lower, "space", down)


def unpack(sums):
    return (
        sums[DOWN2],
        sums[CONV2:DOWN2].reshape(28, 32)[:27].T.reshape(-1),
        sums[DOWN3:CONV2].reshape(2, 2, 2, 64).transpose(3, 0, 2, 1).reshape(-1),
        sums[:27].T.reshape(-1),
        sums[HEAD, :4],
    )


def finish(pack):
    terms = lax.all_to_all(pack, ("section", "space"), 0, 0, tiled=True)
    return unpack(jnp.sum(terms.astype(F32), axis=0))


def per_device(volume, labels, down_weight_two, w_conv_two, down_weight_three, w_conv_three, w_head):
    count = lax.axis_size("space")
    voxels = labels.shape[0] * labels.shape[1] * count * labels.shape[2] * labels.shape[3]
    scale = 1.0 / math.sqrt(voxels)
    sec = lax.axis_index("section").astype(jnp.int32)

    eye4 = jnp.eye(4, dtype=BF16)
    w1 = down_weight_two.transpose(2, 4, 1, 3, 0)[:, :, :, None, :, None, :] * eye4[:, None, :, None]
    w1 = w1.reshape(2, 512, 256)
    eye2 = jnp.eye(2, dtype=BF16)
    wd = down_weight_three.transpose(2, 4, 3, 1, 0)[:, :, None, :, :, None, :] * eye2[:, None, None, :, None]
    wd = wd.reshape(4, 256, 256)
    w2 = w_conv_two.transpose(2, 3, 4, 0, 1).reshape(27, 64, 64)
    w2 = jnp.concatenate([w2, w2], axis=2)
    w3 = w_conv_three.transpose(2, 3, 4, 0, 1).reshape(27, 128, 128)
    wh = jnp.pad(w_head, ((0, 0), (0, 124)))
    wht = jnp.pad(w_head.T, ((0, 124), (0, 0)))
    marks = lax.dynamic_slice_in_dim(labels[:, 0], CROPS * sec, CROPS, axis=0)
    marks = marks.transpose(1, 0, 2).reshape(2, 256)

    vp, a2 = first(sec[None], volume, w1)
    a2_lo, a2_hi = neighbours(a2[:, 1:], a2[:, :1])
    f2, b2, f3, b3, perm = prepare(w2, w3)
    h2, a3 = second(a2_lo, a2, a2_hi, f2, wd)
    a3_lo, a3_hi = neighbours(a3, a3)
    gz4, gh = head(a3_lo, a3, a3_hi, f3, wh, wht, marks, scale)
    gz4_lo, gz4_hi = neighbours(gz4, gz4)
    gw3 = weight_three(gz4, a3_lo, a3, a3_hi)
    gz2, gd3 = middle(gz4_lo, gz4, gz4_hi, b3, a3, h2, wd)
    gz2_lo, gz2_hi = neighbours(gz2[:, 1:], gz2[:, :1])
    gw2 = weight_two(gz2, a2_lo, a2, a2_hi)
    pack = last(gz2_lo, gz2, gz2_hi, b2, a2, vp, perm, gw3, gd3, gw2, gh)

    return finish(pack.reshape(128, ROWS, 128))


def solution(mesh):
    whole = P(("section", "space"))
    return jax.shard_map(
        per_device,
        mesh=mesh,
        in_specs=(P(None, None, "space", None, None), P(None, "space", None, None), P(), P(), P(), P(), P()),
        out_specs=(whole,) * 5,
        check_vma=False,
    )
```

time: 776 us -> 121 us (0.16); the launches traced: 765 us -> 121 us
  local copies, waits for them, and re-layouts: 292 us -> 18.6 us
  blocking collectives: 168 us -> 45.5 us
  starting transfers between devices: 127 us -> 21.6 us
  waiting for transfers between devices: 108 us -> 8.03 us
  Pallas kernels: 0 us -> 25.3 us
  matrix products: 20.5 us -> 0 us
  other arithmetic: 19.3 us -> 0.59 us
  loops' own time: 16.1 us -> 0 us
  between operations: 14.7 us -> 0.97 us
    unnamed x1 -> x0, blocking collectives: 168 us -> none
    reshape x5 -> x7, local copies, waits for them, and re-layouts: 124 us -> 2.58 us  [the longest x3 1 us: unpack(): sums[DOWN3:CONV2].reshape(2, 2, 2, 64).transpose(3, 0, 2, 1).reshape(-1)]
    cond x19 -> x0, local copies, waits for them, and re-layouts: 114 us -> none  [the longest x9 114 us: on_core(): return lax.cond(lax.axis_index('section') == which, work, blank, *operands)]
    ppermute x10 -> x8, starting transfers between devices: 127 us -> 21.6 us  [the longest x4 16.3 us: neighbours(): lax.ppermute(to_upper, 'space', up)]
    unnamed x2 -> x0, waiting for transfers between devices: 86 us -> none
    all_to_all x0 -> x1, blocking collectives: none -> 45.5 us  [finish(): terms = lax.all_to_all(pack, ('section', 'space'), 0, 0, tiled=True)]
    pallas_call x0 -> x8, Pallas kernels: none -> 25.3 us  [the longest x7 20.1 us: call(): pl.pallas_call(kernel, out_shape=[jax.ShapeDtypeStruct(s, d) for s, d in...]
    conv_general_dilated x7 -> x0, matrix products: 19.2 us -> none  [the longest x1 4.77 us: conv_weight_grad(): lax.conv_general_dilated(padded, grads, (1, 1, 1), ((0, 0), (1, 1), (1, 1...]
  transfers between devices with their start and end apart: 11 -> 8, of which waited for: 9 -> 5; matrix products, arithmetic and copies ran while one was open for 31% -> 4% of each run, Pallas kernels for 0% -> 6%
where the time goes in v1:
time: 121 us
  blocking collectives  45.5 us (38%)
  Pallas kernels  25.3 us (21%)
  starting transfers between devices  21.6 us (18%)
  local copies, waits for them, and re-layouts  18.6 us (15%)
  waiting for transfers between devices  8.03 us (7%)
    all_to_all x1, blocking collectives, finish(): terms = lax.all_to_all(pack, ('section', 'space'), 0, 0, tiled=True)  45.5 us
    pallas_call x7, Pallas kernels, call(): pl.pallas_call(kernel, out_shape=[jax.ShapeDtypeStruct(s, d) for s, d in...  20.1 us
    ppermute x4, starting transfers between devices, neighbours(): lax.ppermute(to_upper, 'space', up)  16.3 us
    unnamed x33, local copies, waits for them, and re-layouts  7.94 us
    ppermute x4, waiting for transfers between devices, neighbours(): lax.ppermute(to_lower, 'space', down)  7.4 us
    ppermute x4, starting transfers between devices, neighbours(): lax.ppermute(to_lower, 'space', down)  5.32 us
    pallas_call x1, Pallas kernels, first(): pl.pallas_call(first_kernel, grid_spec=pltpu.PrefetchScalarGridSpec(num_s...  5.21 us
  transfers between devices with their start and end apart: 8, of which 5 were waited for; matrix products, arithmetic and copies ran while one was open for 4% of the time, Pallas kernels for 6%

profile of v1, /device:TPU:1, one launch (start us, length us, event | category | flops | bytes accessed | tf_op | source)
XLA Modules:
  0.0 120.7 jit_solution(174771494199169421)
XLA Ops:
  0.7 0.9 copy.15
  1.5 0.3 mul.40
  1.8 0.7 mul.41
  2.5 0.2 mul.42
  2.7 0.3 mul.43
  3.1 5.2 %shard_map.110 = (bf16[2,2,1024,256]{3,2,1,0:T(8,128)(2,1)S(1)}, bf16[2,2,256,256]{3,2,1,0:T(8,128)(2,1)S(1)}) custom-call(s32[1]{0:T(128)} %bitcast.sec_ref, bf16[4,32,4,8,512]{4,3,2,1,0:T(8,128)(2,1)} %vol_ref.1, bf16[2,512,256]{2,1,0:T(8,128)(2,1)S(1)} %broadcast_multiply_fusion.1.w_ref), custom_call_target="tpu_custom_call" | custom-call | tf_op jit(solution)/shard_map/pallas_call | solution.py:97
  8.3 1.3 %copy-done.2 = bf16[2,2,1024,256]{3,2,1,0:T(8,128)(2,1)} copy-done((bf16[2,2,1024,256]{3,2,1,0:T(8,128)(2,1)}, bf16[2,2,1024,256]{3,2,1,0:T(8,128)(2,1)S(1)}, u32[]{:S(2)}) %copy-start.2) | copy-done | bytes 2097176
  9.7 0.9 fusion.2
  10.5 4.6 %collective-permute-start = (bf16[2,1,256,256]{3,2,1,0:T(8,128)(2,1)}, bf16[2,1,256,256]{3,2,1,0:T(8,128)(2,1)}, u32[]{:S(2)}, u32[]{:S(2)}) collective-permute-start(bf16[2,1,256,256]{3,2,1,0:T(8,128)(2,1)} %get-tuple-element.34), channel_id=1, source_target_pairs={{0,1},{1,2},{2,3},{3,4},{4,5},{5,6},{6,7},{7,8},{8,9},{9,10},{10,1... | collective-permute-start | bytes 786440 | tf_op jit(solution)/shard_map/ppermute | solution.py:343
  15.2 1.3 %collective-permute-start.1 = (bf16[2,1,256,256]{3,2,1,0:T(8,128)(2,1)}, bf16[2,1,256,256]{3,2,1,0:T(8,128)(2,1)}, u32[]{:S(2)}, u32[]{:S(2)}) collective-permute-start(bf16[2,1,256,256]{3,2,1,0:T(8,128)(2,1)} %get-tuple-element.33), channel_id=1, source_target_pairs={{1,0},{2,1},{3,2},{4,3},{5,4},{6,5},{7,6},{8,7},{9,8},{10,9},{11,1... | collective-permute-start | bytes 786440 | tf_op jit(solution)/shard_map/ppermute | solution.py:343
  16.5 0.2 pad_maximum_fusion.w2_ref
  16.8 0.4 mul.46
  17.2 1.2 mul.47
  18.3 0.1 mul.48
  18.5 1.2 copy-done.4
  19.7 2.8 %shard_map.111 = (bf16[256,2304]{1,0:T(8,128)(2,1)S(1)}, bf16[256,2304]{1,0:T(8,128)(2,1)S(1)}, bf16[256,2304]{1,0:T(8,128)(2,1)S(1)}, bf16[256,2304]{1,0:T(8,128)(2,1)}, bf16[1024,256]{1,0:T(8,128)(2,1)S(1)}) custom-call(bf16[27,64,128]{2,1,0:T(8,128)(2,1)S(1)} %pad_maximum_fusion.w2_ref, bf16[27,128,128]{2,1,0:T(8,128)(2,1)S(1)} %bitcast.32), custom_call_target="tpu_custom_call" | custom-call | tf_op jit(solution)/shard_map/pallas_call | solution.py:69
  22.5 1.7 %collective-permute-done.1.hi_ref = bf16[2,1,256,256]{3,2,1,0:T(8,128)(2,1)} collective-permute-done((bf16[2,1,256,256]{3,2,1,0:T(8,128)(2,1)}, bf16[2,1,256,256]{3,2,1,0:T(8,128)(2,1)}, u32[]{:S(2)}, u32[]{:S(2)}) %collective-permute-start.1) | collective-permute-done | bytes 262176 | tf_op jit(solution)/shard_map/ppermute | solution.py:343
  24.2 3.6 %shard_map.112 = (bf16[4,256,256]{2,1,0:T(8,128)(2,1)S(1)}, bf16[256,256]{1,0:T(8,128)(2,1)S(1)}) custom-call(bf16[2,1,256,256]{3,2,1,0:T(8,128)(2,1)} %collective-permute-done.lo_ref, bf16[2,2,256,256]{3,2,1,0:T(8,128)(2,1)S(1)} %get-tuple-element.18.a_ref, bf16[2,1,256,256]{3,2,1,0:T(8,128)(2,1)} %collective-permute-done.1.hi_ref, ...), custom_call_target="tpu_custom_call" | custom-call | tf_op jit(solution)/shard_map/pallas_call | solution.py:69
  27.8 0.8 copy-done.7
  28.7 3.1 %collective-permute-start.2 = (bf16[256,256]{1,0:T(8,128)(2,1)S(1)}, bf16[256,256]{1,0:T(8,128)(2,1)}, u32[]{:S(2)}, u32[]{:S(2)}) collective-permute-start(bf16[256,256]{1,0:T(8,128)(2,1)S(1)} %get-tuple-element.20.a_ref.a3_ref), channel_id=1, source_target_pairs={{0,1},{1,2},{2,3},{3,4},{4,5},{5,6},{6,7},{7,8},{8,9},{9,10},{10,1... | collective-permute-start | bytes 393224 | tf_op jit(solution)/shard_map/ppermute | solution.py:343
  31.7 1.3 %collective-permute-start.3 = (bf16[256,256]{1,0:T(8,128)(2,1)S(1)}, bf16[256,256]{1,0:T(8,128)(2,1)}, u32[]{:S(2)}, u32[]{:S(2)}) collective-permute-start(bf16[256,256]{1,0:T(8,128)(2,1)S(1)} %get-tuple-element.20.a_ref.a3_ref), channel_id=1, source_target_pairs={{1,0},{2,1},{3,2},{4,3},{5,4},{6,5},{7,6},{8,7},{9,8},{10,9},{11,1... | collective-permute-start | bytes 393224 | tf_op jit(solution)/shard_map/ppermute | solution.py:343
  33.0 0.7 copy.17
  33.8 1.4 %pad.8.wh_ref = bf16[128,128]{1,0:T(8,128)(2,1)} pad(bf16[128,4]{1,0:T(8,128)(2,1)} %copy.17, bf16[]{:T(256)} %constant.12.clone.1), padding=0_0x0_124 | pad | bytes 33794 | tf_op jit(solution)/shard_map/jit(_pad)/pad | solution.py:376
  35.1 0.6 pad.9.wht_ref
  35.7 1.8 %collective-permute-done.3.hi_ref = bf16[256,256]{1,0:T(8,128)(2,1)} collective-permute-done((bf16[256,256]{1,0:T(8,128)(2,1)S(1)}, bf16[256,256]{1,0:T(8,128)(2,1)}, u32[]{:S(2)}, u32[]{:S(2)}) %collective-permute-start.3) | collective-permute-done | bytes 131104 | tf_op jit(solution)/shard_map/ppermute | solution.py:343
  37.5 0.8 copy-done.9
  38.3 0.8 copy-done.10
  39.1 2.2 %shard_map.113 = (bf16[256,256]{1,0:T(8,128)(2,1)S(1)}, f32[128,128]{1,0:T(8,128)S(1)}) custom-call(bf16[256,256]{1,0:T(8,128)(2,1)} %collective-permute-done.2.lo_ref, bf16[256,256]{1,0:T(8,128)(2,1)S(1)} %get-tuple-element.20.a_ref.a3_ref, bf16[256,256]{1,0:T(8,128)(2,1)} %collective-permute-done.3.hi_ref, bf16[256,2304]{1,0:T(8,128)(2,1)S(1)} %get-tuple-element.21.f3_ref, ...), custom_call_target="tpu_custom_call" | custom-call | tf_op jit(solution)/shard_map/pallas_call | solution.py:69
  41.3 4.1 %collective-permute-start.4 = (bf16[256,256]{1,0:T(8,128)(2,1)S(1)}, bf16[256,256]{1,0:T(8,128)(2,1)S(1)}, u32[]{:S(2)}, u32[]{:S(2)}) collective-permute-start(bf16[256,256]{1,0:T(8,128)(2,1)S(1)} %get-tuple-element.22.g_ref), channel_id=1, source_target_pairs={{0,1},{1,2},{2,3},{3,4},{4,5},{5,6},{6,7},{7,8},{8,9},{9,10},{10,1... | collective-permute-start | bytes 393224 | tf_op jit(solution)/shard_map/ppermute | solution.py:343
  45.4 1.3 %collective-permute-start.5 = (bf16[256,256]{1,0:T(8,128)(2,1)S(1)}, bf16[256,256]{1,0:T(8,128)(2,1)S(1)}, u32[]{:S(2)}, u32[]{:S(2)}) collective-permute-start(bf16[256,256]{1,0:T(8,128)(2,1)S(1)} %get-tuple-element.22.g_ref), channel_id=1, source_target_pairs={{1,0},{2,1},{3,2},{4,3},{5,4},{6,5},{7,6},{8,7},{9,8},{10,9},{11,1... | collective-permute-start | bytes 393224 | tf_op jit(solution)/shard_map/ppermute | solution.py:343
  46.7 0.6 collective-permute-done.4.lo_ref
  47.3 3.8 %collective-permute-done.5.hi_ref = bf16[256,256]{1,0:T(8,128)(2,1)S(1)} collective-permute-done((bf16[256,256]{1,0:T(8,128)(2,1)S(1)}, bf16[256,256]{1,0:T(8,128)(2,1)S(1)}, u32[]{:S(2)}, u32[]{:S(2)}) %collective-permute-start.5) | collective-permute-done | bytes 131104 | tf_op jit(solution)/shard_map/ppermute | solution.py:343
  51.1 1.0 copy-done.8
  52.1 1.5 %shard_map.114 = (bf16[2,2,256,256]{3,2,1,0:T(8,128)(2,1)S(1)}, f32[4,128,128]{2,1,0:T(8,128)S(1)}) custom-call(bf16[256,256]{1,0:T(8,128)(2,1)S(1)} %collective-permute-done.4.lo_ref, bf16[256,256]{1,0:T(8,128)(2,1)S(1)} %get-tuple-element.22.g_ref, bf16[256,256]{1,0:T(8,128)(2,1)S(1)} %collective-permute-done.5.hi_ref, bf16[256,2304]{1,0:T(8,128)(2,1)S(1)} %copy-done.3, ...), custom_call_target="tpu_custom_call" | custom-call | tf_op jit(solution)/shard_map/pallas_call | solution.py:69
  53.7 4.5 %collective-permute-start.6 = (bf16[2,1,256,256]{3,2,1,0:T(8,128)(2,1)S(1)}, bf16[2,1,256,256]{3,2,1,0:T(8,128)(2,1)S(1)}, u32[]{:S(2)}, u32[]{:S(2)}) collective-permute-start(bf16[2,1,256,256]{3,2,1,0:T(8,128)(2,1)S(1)} %get-tuple-element.32), channel_id=1, source_target_pairs={{0,1},{1,2},{2,3},{3,4},{4,5},{5,6},{6,7},{7,8},{8,9},{9,10},{10,1... | collective-permute-start | bytes 786440 | tf_op jit(solution)/shard_map/ppermute | solution.py:343
  58.2 1.5 %collective-permute-start.7 = (bf16[2,1,256,256]{3,2,1,0:T(8,128)(2,1)S(1)}, bf16[2,1,256,256]{3,2,1,0:T(8,128)(2,1)S(1)}, u32[]{:S(2)}, u32[]{:S(2)}) collective-permute-start(bf16[2,1,256,256]{3,2,1,0:T(8,128)(2,1)S(1)} %get-tuple-element.31), channel_id=1, source_target_pairs={{1,0},{2,1},{3,2},{4,3},{5,4},{6,5},{7,6},{8,7},{9,8},{10,9},{11,1... | collective-permute-start | bytes 786440 | tf_op jit(solution)/shard_map/ppermute | solution.py:343
  59.7 1.5 %shard_map.115.w3_ref = f32[27,128,128]{2,1,0:T(8,128)S(1)} custom-call(bf16[256,256]{1,0:T(8,128)(2,1)S(1)} %get-tuple-element.22.g_ref, bf16[256,256]{1,0:T(8,128)(2,1)} %collective-permute-done.2.lo_ref, bf16[256,256]{1,0:T(8,128)(2,1)S(1)} %get-tuple-element.20.a_ref.a3_ref, bf16[256,256]{1,0:T(8,128)(2,1)} %collective-permute-done.3.hi_ref), custom_call_target="tpu_custom_call" | custom-call | tf_op jit(solution)/shard_map/pallas_call | solution.py:69
  61.2 1.2 %copy-done.1 = f32[27,128,128]{2,1,0:T(8,128)} copy-done((f32[27,128,128]{2,1,0:T(8,128)}, f32[27,128,128]{2,1,0:T(8,128)S(1)}, u32[]{:S(2)}) %copy-start.1) | copy-done | bytes 1769496
  62.4 2.8 %shard_map.116.w2_ref = f32[7,2,64,128]{3,2,1,0:T(8,128)S(1)} custom-call(bf16[2,2,256,256]{3,2,1,0:T(8,128)(2,1)S(1)} %get-tuple-element.25.g_ref, bf16[2,1,256,256]{3,2,1,0:T(8,128)(2,1)} %collective-permute-done.lo_ref, bf16[2,2,256,256]{3,2,1,0:T(8,128)(2,1)S(1)} %get-tuple-element.18.a_ref, bf16[2,1,256,256]{3,2,1,0:T(8,128)(2,1)} %collective-permute-done.1.hi_ref), custom_call_target="tpu_custom_call" | custom-call | tf_op jit(solution)/shard_map/pallas_call | solution.py:69
  65.3 5.8 %shard_map.117 = bf16[5120,128]{1,0:T(8,128)(2,1)S(1)} custom-call(bf16[2,1,256,256]{3,2,1,0:T(8,128)(2,1)S(1)} %collective-permute-done.6.lo_ref, bf16[2,2,256,256]{3,2,1,0:T(8,128)(2,1)S(1)} %get-tuple-element.25.g_ref, bf16[2,1,256,256]{3,2,1,0:T(8,128)(2,1)S(1)} %collective-permute-done.7.hi_ref, bf16[256,2304]{1,0:T(8,128)(2,1)S(1)} %get-tuple-element.26.b2_ref, ...), custom_call_target="tpu_custom_call" | custom-call | tf_op jit(solution)/shard_map/pallas_call | solution.py:69
  71.1 45.5 %all_to_all.5 = bf16[128,40,128]{2,1,0:T(8,128)(2,1)S(1)} all-to-all(bf16[128,40,128]{2,1,0:T(8,128)(2,1)S(1)} %bitcast.31), channel_id=1, replica_groups=mesh['section'=2,'space'=64] {'section','space'}, dimensions={0} | all-to-all | bytes 2621440 | tf_op jit(solution)/shard_map/all_to_all | solution.py:357
  116.6 0.2 convert_reduce_fusion
  116.9 0.5 slice_bitcast_fusion.1
  117.4 0.5 slice_bitcast_fusion.2
  118.0 0.2 copy.19
  118.1 0.8 reshape.69
  119.0 0.8 reshape.70
  120.0 0.7 reshape.67
  (42 shorter events, 0.7 us)
Async XLA Ops:
  0.6 35.1 %copy-start = (s32[4,1,2,128]{3,2,1,0:T(2,128)S(1)}, s32[4,1,2,128]{3,2,1,0:T(2,128)}, u32[]{:S(2)}) copy-start(s32[4,1,2,128]{3,2,1,0:T(2,128)} %param.8) | copy-start | bytes 12292
  8.3 1.3 %copy-start.2 = (bf16[2,2,1024,256]{3,2,1,0:T(8,128)(2,1)}, bf16[2,2,1024,256]{3,2,1,0:T(8,128)(2,1)S(1)}, u32[]{:S(2)}) copy-start(bf16[2,2,1024,256]{3,2,1,0:T(8,128)(2,1)S(1)} %get-tuple-element.27.vp_ref) | copy-start | bytes 6291460
  9.7 6.8 %copy-start.12 = (bf16[64,64,3,3,3]{1,0,4,3,2:T(8,128)(2,1)S(1)}, bf16[64,64,3,3,3]{1,0,4,3,2:T(8,128)(2,1)}, u32[]{:S(2)}) copy-start(bf16[64,64,3,3,3]{1,0,4,3,2:T(8,128)(2,1)} %param.10) | copy-start | bytes 663556
  9.7 7.1 %copy-start.13 = (bf16[128,64,2,2,2]{0,4,3,2,1:T(2,128)(2,1)S(1)}, bf16[128,64,2,2,2]{0,4,3,2,1:T(2,128)(2,1)}, u32[]{:S(2)}) copy-start(bf16[128,64,2,2,2]{0,4,3,2,1:T(2,128)(2,1)} %param.11) | copy-start | bytes 393220
  10.5 12.0 %collective-permute-start = (bf16[2,1,256,256]{3,2,1,0:T(8,128)(2,1)}, bf16[2,1,256,256]{3,2,1,0:T(8,128)(2,1)}, u32[]{:S(2)}, u32[]{:S(2)}) collective-permute-start(bf16[2,1,256,256]{3,2,1,0:T(8,128)(2,1)} %get-tuple-element.34), channel_id=1, source_target_pairs={{0,1},{1,2},{2,3},{3,4},{4,5},{5,6},{6,7},{7,8},{8,9},{9,10},{10,1... | collective-permute-start | bytes 786440 | tf_op jit(solution)/shard_map/ppermute | solution.py:343
  15.2 9.1 %collective-permute-start.1 = (bf16[2,1,256,256]{3,2,1,0:T(8,128)(2,1)}, bf16[2,1,256,256]{3,2,1,0:T(8,128)(2,1)}, u32[]{:S(2)}, u32[]{:S(2)}) collective-permute-start(bf16[2,1,256,256]{3,2,1,0:T(8,128)(2,1)} %get-tuple-element.33), channel_id=1, source_target_pairs={{1,0},{2,1},{3,2},{4,3},{5,4},{6,5},{7,6},{8,7},{9,8},{10,9},{11,1... | collective-permute-start | bytes 786440 | tf_op jit(solution)/shard_map/ppermute | solution.py:343
  18.5 1.2 copy-start.4
  19.7 2.8 %copy-start.11 = (bf16[4,256,256]{2,1,0:T(8,128)(2,1)S(1)}, bf16[4,256,256]{2,1,0:T(8,128)(2,1)}, u32[]{:S(2)}) copy-start(bf16[4,256,256]{2,1,0:T(8,128)(2,1)} %mul.47) | copy-start | bytes 1572868
  22.4 5.4 %copy-start.5 = (bf16[1024,256]{1,0:T(8,128)(2,1)}, bf16[1024,256]{1,0:T(8,128)(2,1)S(1)}, u32[]{:S(2)}) copy-start(bf16[1024,256]{1,0:T(8,128)(2,1)S(1)} %get-tuple-element.28.perm_ref) | copy-start | bytes 1572868
  24.2 8.8 %copy-start.14 = (bf16[128,4]{0,1:T(4,128)(2,1)S(1)}, bf16[128,4]{0,1:T(4,128)(2,1)}, u32[]{:S(2)}) copy-start(bf16[128,4]{0,1:T(4,128)(2,1)} %param.13) | copy-start | bytes 3076
  27.8 0.8 copy-start.7
  28.7 7.1 %collective-permute-start.2 = (bf16[256,256]{1,0:T(8,128)(2,1)S(1)}, bf16[256,256]{1,0:T(8,128)(2,1)}, u32[]{:S(2)}, u32[]{:S(2)}) collective-permute-start(bf16[256,256]{1,0:T(8,128)(2,1)S(1)} %get-tuple-element.20.a_ref.a3_ref), channel_id=1, source_target_pairs={{0,1},{1,2},{2,3},{3,4},{4,5},{5,6},{6,7},{7,8},{8,9},{9,10},{10,1... | collective-permute-start | bytes 393224 | tf_op jit(solution)/shard_map/ppermute | solution.py:343
  31.7 5.8 %collective-permute-start.3 = (bf16[256,256]{1,0:T(8,128)(2,1)S(1)}, bf16[256,256]{1,0:T(8,128)(2,1)}, u32[]{:S(2)}, u32[]{:S(2)}) collective-permute-start(bf16[256,256]{1,0:T(8,128)(2,1)S(1)} %get-tuple-element.20.a_ref.a3_ref), channel_id=1, source_target_pairs={{1,0},{2,1},{3,2},{4,3},{5,4},{6,5},{7,6},{8,7},{9,8},{10,9},{11,1... | collective-permute-start | bytes 393224 | tf_op jit(solution)/shard_map/ppermute | solution.py:343
  35.7 15.3 %copy-start.3 = (bf16[256,2304]{1,0:T(8,128)(2,1)S(1)}, bf16[256,2304]{1,0:T(8,128)(2,1)}, u32[]{:S(2)}) copy-start(bf16[256,2304]{1,0:T(8,128)(2,1)} %get-tuple-element.23.b3_ref) | copy-start | bytes 3538948
  37.5 0.8 copy-start.9
  38.3 0.8 copy-start.10
  41.3 6.0 %collective-permute-start.4 = (bf16[256,256]{1,0:T(8,128)(2,1)S(1)}, bf16[256,256]{1,0:T(8,128)(2,1)S(1)}, u32[]{:S(2)}, u32[]{:S(2)}) collective-permute-start(bf16[256,256]{1,0:T(8,128)(2,1)S(1)} %get-tuple-element.22.g_ref), channel_id=1, source_target_pairs={{0,1},{1,2},{2,3},{3,4},{4,5},{5,6},{6,7},{7,8},{8,9},{9,10},{10,1... | collective-permute-start | bytes 393224 | tf_op jit(solution)/shard_map/ppermute | solution.py:343
  45.4 5.7 %collective-permute-start.5 = (bf16[256,256]{1,0:T(8,128)(2,1)S(1)}, bf16[256,256]{1,0:T(8,128)(2,1)S(1)}, u32[]{:S(2)}, u32[]{:S(2)}) collective-permute-start(bf16[256,256]{1,0:T(8,128)(2,1)S(1)} %get-tuple-element.22.g_ref), channel_id=1, source_target_pairs={{1,0},{2,1},{3,2},{4,3},{5,4},{6,5},{7,6},{8,7},{9,8},{10,9},{11,1... | collective-permute-start | bytes 393224 | tf_op jit(solution)/shard_map/ppermute | solution.py:343
  51.1 1.0 copy-start.8
  53.7 11.6 %collective-permute-start.6 = (bf16[2,1,256,256]{3,2,1,0:T(8,128)(2,1)S(1)}, bf16[2,1,256,256]{3,2,1,0:T(8,128)(2,1)S(1)}, u32[]{:S(2)}, u32[]{:S(2)}) collective-permute-start(bf16[2,1,256,256]{3,2,1,0:T(8,128)(2,1)S(1)} %get-tuple-element.32), channel_id=1, source_target_pairs={{0,1},{1,2},{2,3},{3,4},{4,5},{5,6},{6,7},{7,8},{8,9},{9,10},{10,1... | collective-permute-start | bytes 786440 | tf_op jit(solution)/shard_map/ppermute | solution.py:343
  58.2 7.1 %collective-permute-start.7 = (bf16[2,1,256,256]{3,2,1,0:T(8,128)(2,1)S(1)}, bf16[2,1,256,256]{3,2,1,0:T(8,128)(2,1)S(1)}, u32[]{:S(2)}, u32[]{:S(2)}) collective-permute-start(bf16[2,1,256,256]{3,2,1,0:T(8,128)(2,1)S(1)} %get-tuple-element.31), channel_id=1, source_target_pairs={{1,0},{2,1},{3,2},{4,3},{5,4},{6,5},{7,6},{8,7},{9,8},{10,9},{11,1... | collective-permute-start | bytes 786440 | tf_op jit(solution)/shard_map/ppermute | solution.py:343
  61.2 1.2 %copy-start.1 = (f32[27,128,128]{2,1,0:T(8,128)}, f32[27,128,128]{2,1,0:T(8,128)S(1)}, u32[]{:S(2)}) copy-start(f32[27,128,128]{2,1,0:T(8,128)S(1)} %shard_map.115.w3_ref) | copy-start | bytes 5308420
  62.4 2.9 %copy-start.6 = (bf16[1024,256]{1,0:T(8,128)(2,1)S(1)}, bf16[1024,256]{1,0:T(8,128)(2,1)}, u32[]{:S(2)}) copy-start(bf16[1024,256]{1,0:T(8,128)(2,1)} %copy-done.5) | copy-start | bytes 1572868

commit v2 on v1

--- a/solution.py
+++ b/solution.py
@@ -18,7 +18,7 @@
 DOWN3, CONV2, DOWN2, HEAD = 27, 31, 38, 39
 
 
-def params(megabytes=48):
+def params(megabytes=24):
     return pltpu.CompilerParams(vmem_limit_bytes=megabytes << 20)
 
 
@@ -65,35 +65,58 @@
         ref[pl.ds(row + j * T, T), 128:256] = right
 
 
-def call(kernel, outs, *args, scratch=(), **more):
+def call(kernel, outs, *args, scratch=()):
+    spec = pl.BlockSpec(memory_space=pltpu.VMEM)
+    scalar = pl.BlockSpec(memory_space=pltpu.SMEM)
     return pl.pallas_call(
         kernel,
+        in_specs=[scalar if a.dtype == jnp.int32 and a.ndim == 1 else spec for a in args],
+        out_specs=[spec] * len(outs),
         out_shape=[jax.ShapeDtypeStruct(s, d) for s, d in outs],
         scratch_shapes=list(scratch),
         compiler_params=params(),
-        **more,
     )(*args)
 
 
-def first_kernel(sec_ref, vol_ref, w_ref, vp_ref, a_ref, sort_ref, wt_ref):
+def sorted_out(where_ref, one, two):
+    even = where_ref[1] == 0
+    return jnp.where(even, two, one), jnp.where(even, one, two)
+
+
+def first_kernel(where_ref, vol_ref, w_ref, vp_ref, a_ref, one_ref, two_ref, sort_ref, wt_ref):
     @pl.when(pl.program_id(0) == 0)
     def _():
-        w = lax.broadcasted_iota(jnp.int32, (512, 512), 0)
-        to = lax.broadcasted_iota(jnp.int32, (512, 512), 1)
+        to = lax.broadcasted_iota(jnp.int32, (1, 512), 1)
         source = (to % 128) * 4 + (to // 128) % 2 * 2 + to // 256
-        sort_ref[...] = jnp.where(w == source, 1.0, 0.0).astype(BF16)
-        for d in range(2):
-            wt_ref[:, pl.ds(d * 512, 512)] = w_ref[d].astype(F32).T.astype(BF16)
+        sort_ref[...] = jnp.where(lax.broadcasted_iota(jnp.int32, (512, 512), 0) == source, 1.0, 0.0).astype(BF16)
+        to = lax.broadcasted_iota(jnp.int32, (1, 1024), 1)
+        height = to % 8
+        source = to // 8 % 32 * 8 + to // 512 * 4 + height % 2 * 2 + to // 256 % 2
+        pick = jnp.where(lax.broadcasted_iota(jnp.int32, (256, 1024), 0) == source, 1.0, 0.0).astype(BF16)
+        w = dot_tn(w_ref[...], pick)
+        for h in range(4):
+            wt_ref[pl.ds(h * 64, 64), :] = jnp.where(height // 2 == h, w, 0.0).astype(BF16)
 
     for d in range(2):
         v = vol_ref[0, :, d].astype(F32).reshape(256, 512).astype(BF16)
         s = dot(v, sort_ref[...]).astype(BF16)
         vp_ref[0, 0, pl.ds(d * 512, 256), :] = s[:, :256]
         vp_ref[0, 0, pl.ds(d * 512 + 256, 256), :] = s[:, 256:]
-    a_ref[0, 0] = rectified(dot(wt_ref[...], vp_ref[0, 0])).astype(BF16)
-
-
-def first(sec, volume, w1):
+    a = rectified(dot(wt_ref[...], vp_ref[0, 0])).astype(BF16)
+    a_ref[0, 0] = a
+    upper = pl.program_id(0) % 2
+
+    @pl.when(upper == where_ref[1])
+    def _():
+        two_ref[0] = a
+
+    @pl.when(upper != where_ref[1])
+    def _():
+        one_ref[0] = a
+
+
+def first(where, volume, w1):
+    half = pl.BlockSpec((1, T, T), lambda i, s: (i // 2, 0, 0))
     return pl.pallas_call(
         first_kernel,
         grid_spec=pltpu.PrefetchScalarGridSpec(
@@ -101,23 +124,29 @@
             grid=(4,),
             in_specs=[
                 pl.BlockSpec((1, 32, 2, 8, 512), lambda i, s: (2 * s[0] + i // 2, 0, i % 2, 0, 0)),
-                pl.BlockSpec((2, 512, 256), lambda i, s: (0, 0, 0)),
+                pl.BlockSpec((256, 64), lambda i, s: (0, 0)),
             ],
             out_specs=[
                 pl.BlockSpec((1, 1, 1024, 256), lambda i, s: (i // 2, i % 2, 0, 0)),
                 pl.BlockSpec((1, 1, 256, 256), lambda i, s: (i // 2, i % 2, 0, 0)),
+                half,
+                half,
             ],
             scratch_shapes=[pltpu.VMEM((512, 512), BF16), pltpu.VMEM((256, 1024), BF16)],
         ),
         out_shape=[
             jax.ShapeDtypeStruct((CROPS, 2, 1024, 256), BF16),
             jax.ShapeDtypeStruct((CROPS, 2, 256, 256), BF16),
+            jax.ShapeDtypeStruct((CROPS, 256, 256), BF16),
+            jax.ShapeDtypeStruct((CROPS, 256, 256), BF16),
         ],
         compiler_params=params(),
-    )(sec, volume, w1)
-
-
-def prepare_kernel(w2_ref, w3_ref, f2_ref, b2_ref, f3_ref, b3_ref, perm_ref):
+    )(where, volume, w1)
+
+
+def prepare_kernel(
+    w2_ref, w3_ref, wd_ref, head_ref, f2_ref, b2_ref, f3_ref, b3_ref, perm_ref, d_ref, wh_ref, wht_ref, rows_ref
+):
     low = lax.broadcasted_iota(jnp.int32, (64, 128), 1) < 64
     zero = jnp.zeros((64, 128), F32)
     for d in range(3):
@@ -143,21 +172,38 @@
                     block = w3_ref[d * 9 + (col - row + 1) * 3 + j]
                     f3_ref[pl.ds(row * 128, 128), pl.ds(at + col * 128, 128)] = block
                     b3_ref[pl.ds(col * 128, 128), pl.ds(back + row * 128, 128)] = block.astype(F32).T.astype(BF16)
-    r = lax.broadcasted_iota(jnp.int32, (1024, 256), 0)
-    to = lax.broadcasted_iota(jnp.int32, (1024, 256), 1)
-    c, h = r // 8 % 32, r % 8
-    target = c // 16 * 128 + c % 16 * 8 + r // 512 * 4 + h * 2 + r // 256 % 2
-    perm_ref[...] = jnp.where((target == to) & (h < 2), 1.0, 0.0).astype(BF16)
-
-
-def prepare(w2, w3):
+    rows_ref[...] = wd_ref[...].astype(F32)
+    for d in range(2):
+        for p in range(2):
+            for h in range(4):
+                block = rows_ref[pl.ds(d * 4 + h % 2 * 2 + p, 64, stride=8), :].astype(BF16)
+                d_ref[2 * d + p, pl.ds(h * 64, 64), pl.ds(h // 2 * 128, 128)] = block
+                d_ref[2 * d + p, pl.ds(h * 64, 64), pl.ds(128 - h // 2 * 128, 128)] = jnp.zeros_like(block)
+    rows_ref[pl.ds(0, 128), :] = jnp.zeros((128, 128), F32)
+    rows_ref[pl.ds(0, 4), :] = head_ref[...].astype(F32)
+    wht = rows_ref[pl.ds(0, 128), :]
+    wht_ref[...] = wht.astype(BF16)
+    wh_ref[...] = wht.T.astype(BF16)
+    to = lax.broadcasted_iota(jnp.int32, (1, 256), 1)
+    source = to // 4 % 2 * 512 + to % 2 * 256 + (to // 128 * 16 + to // 8 % 16) * 8 + to // 2 % 2
+    perm_ref[...] = jnp.where(lax.broadcasted_iota(jnp.int32, (1024, 256), 0) == source, 1.0, 0.0).astype(BF16)
+
+
+def prepare(w2, w3, wd, wh):
     wide = ((T, 9 * T), BF16)
-    return call(prepare_kernel, [wide] * 4 + [((1024, 256), BF16)], w2, w3)
-
-
-def second_kernel(lo_ref, a_ref, hi_ref, f2_ref, wd_ref, h_ref, a3_ref, b_ref):
+    square = ((128, 128), BF16)
+    return call(
+        prepare_kernel,
+        [wide] * 4 + [((1024, 256), BF16), ((4, T, T), BF16), square, square],
+        w2, w3, wd, wh,
+        scratch=[pltpu.VMEM((512, 128), F32)],
+    )
+
+
+def second_kernel(where_ref, one_ref, a_ref, two_ref, f2_ref, wd_ref, h_ref, a3_ref, b_ref):
     for n in range(CROPS):
-        planes = (lo_ref[n, 0], a_ref[n, 0], a_ref[n, 1], hi_ref[n, 0])
+        lo, hi = sorted_out(where_ref, one_ref[n], two_ref[n])
+        planes = (lo, a_ref[n, 0], a_ref[n, 1], hi)
         for k, plane in enumerate(planes):
             put_three(b_ref, k * 3 * T, three_two(plane))
         for d in range(2):
@@ -170,18 +216,19 @@
     a3_ref[...] = rectified(total).astype(BF16)
 
 
-def second(lo, a, hi, f2, wd):
+def second(where, one, a, two, f2, wd):
     return call(
         second_kernel,
         [((4, T, T), BF16), ((T, T), BF16)],
-        lo, a, hi, f2, wd,
+        where, one, a, two, f2, wd,
         scratch=[pltpu.VMEM((12 * T, T), BF16)],
     )
 
 
-def head_kernel(scale, lo_ref, a_ref, hi_ref, f3_ref, wh_ref, wht_ref, marks_ref, gz_ref, gh_ref, b_ref):
-    for k, ref in enumerate((lo_ref, a_ref, hi_ref)):
-        put_three(b_ref, k * 3 * T, three_three(ref[...]))
+def head_kernel(scale, where_ref, one_ref, a_ref, two_ref, f3_ref, wh_ref, wht_ref, marks_ref, gz_ref, gh_ref, b_ref):
+    lo, hi = sorted_out(where_ref, one_ref[...], two_ref[...])
+    for k, plane in enumerate((lo, a_ref[...], hi)):
+        put_three(b_ref, k * 3 * T, three_three(plane))
     top = rectified(dot(f3_ref[...], b_ref[...])).astype(BF16)
     row = lax.broadcasted_iota(jnp.int32, (128, T), 0)
     total = jnp.zeros((128, 128), F32)
@@ -197,19 +244,19 @@
     gh_ref[...] = total
 
 
-def head(lo, a, hi, f3, wh, wht, marks, scale):
+def head(where, one, a, two, f3, wh, wht, marks, scale):
     return call(
         functools.partial(head_kernel, scale),
         [((T, T), BF16), ((128, 128), F32)],
-        lo, a, hi, f3, wh, wht, marks,
+        where, one, a, two, f3, wh, wht, marks,
         scratch=[pltpu.VMEM((9 * T, T), BF16)],
     )
 
 
-def weight_three_kernel(g_ref, lo_ref, a_ref, hi_ref, out_ref, s_ref):
+def weight_three_kernel(where_ref, g_ref, one_ref, a_ref, two_ref, out_ref, s_ref):
     put_three(s_ref, 0, three_three(g_ref[...]))
-    for d, ref in enumerate((lo_ref, a_ref, hi_ref)):
-        a = ref[...]
+    lo, hi = sorted_out(where_ref, one_ref[...], two_ref[...])
+    for d, a in enumerate((lo, a_ref[...], hi)):
         for j in range(3):
             t = dot_nt(s_ref[pl.ds((2 - j) * T, T), :], a)
             out_ref[d * 9 + j] = t[128:, :128]
@@ -217,18 +264,21 @@
             out_ref[d * 9 + 6 + j] = t[:128, 128:]
 
 
-def weight_three(g, lo, a, hi):
+def weight_three(where, g, one, a, two):
     return call(
         weight_three_kernel,
         [((27, 128, 128), F32)],
-        g, lo, a, hi,
+        where, g, one, a, two,
         scratch=[pltpu.VMEM((3 * T, T), BF16)],
     )[0]
 
 
-def middle_kernel(lo_ref, g_ref, hi_ref, b3_ref, a3_ref, h_ref, wd_ref, gz2_ref, gd_ref, b_ref):
-    for k, ref in enumerate((lo_ref, g_ref, hi_ref)):
-        put_three(b_ref, k * 3 * T, three_three(ref[...]))
+def middle_kernel(
+    where_ref, one_ref, g_ref, two_ref, b3_ref, a3_ref, h_ref, wd_ref, gz2_ref, gone_ref, gtwo_ref, gd_ref, b_ref
+):
+    lo, hi = sorted_out(where_ref, one_ref[...], two_ref[...])
+    for k, plane in enumerate((lo, g_ref[...], hi)):
+        put_three(b_ref, k * 3 * T, three_three(plane))
     gy = (dot(b3_ref[...], b_ref[...]) * slope(a3_ref[...])).astype(BF16)
     for d in range(2):
         for p in range(2):
@@ -236,22 +286,27 @@
             q = (dot(wd_ref[k], gy) * slope(h_ref[k])).astype(BF16)
             for n in range(CROPS):
                 gz2_ref[n, d, :, pl.ds(p * 128, 128)] = q[:, n * 128 : (n + 1) * 128]
+    even = where_ref[1] == 0
+    for n in range(CROPS):
+        gone_ref[n] = jnp.where(even, gz2_ref[n, 1], gz2_ref[n, 0])
+        gtwo_ref[n] = jnp.where(even, gz2_ref[n, 0], gz2_ref[n, 1])
     for k in range(4):
         gd_ref[k] = dot_nt(gy[:128], h_ref[k, :128]) + dot_nt(gy[128:], h_ref[k, 128:])
 
 
-def middle(lo, g, hi, b3, a3, h, wd):
+def middle(where, one, g, two, b3, a3, h, wd):
     return call(
         middle_kernel,
-        [((CROPS, 2, T, T), BF16), ((4, 128, 128), F32)],
-        lo, g, hi, b3, a3, h, wd,
+        [((CROPS, 2, T, T), BF16), ((CROPS, T, T), BF16), ((CROPS, T, T), BF16), ((4, 128, 128), F32)],
+        where, one, g, two, b3, a3, h, wd,
         scratch=[pltpu.VMEM((9 * T, T), BF16)],
     )
 
 
-def weight_two_kernel(g_ref, lo_ref, a_ref, hi_ref, out_ref, gs_ref, as_ref):
+def weight_two_kernel(where_ref, g_ref, one_ref, a_ref, two_ref, out_ref, gs_ref, as_ref):
     for n in range(CROPS):
-        planes = (lo_ref[n, 0], a_ref[n, 0], a_ref[n, 1], hi_ref[n, 0])
+        lo, hi = sorted_out(where_ref, one_ref[n], two_ref[n])
+        planes = (lo, a_ref[n, 0], a_ref[n, 1], hi)
         for d in range(2):
             at = (2 * n + d) * T
             for j, (left, right) in enumerate(three_two(g_ref[n, d])):
@@ -281,20 +336,37 @@
         out_ref[g, 1] = jnp.where(low, jnp.where(block, turned[0], four[1]), jnp.where(block, turned[2], four[3]))
 
 
-def weight_two(g, lo, a, hi):
+def weight_two(where, g, one, a, two):
     return call(
         weight_two_kernel,
         [((7, 2, 64, 128), F32)],
-        g, lo, a, hi,
+        where, g, one, a, two,
         scratch=[pltpu.VMEM((3, T, 4 * T), BF16), pltpu.VMEM((3, T, 4 * T), BF16)],
     )[0]
 
 
+def pack_kernel(w3_ref, d3_ref, w2_ref, gh_ref, out_ref):
+    for t in range(27):
+        out_ref[pl.ds(t, 128, stride=ROWS), :] = w3_ref[t]
+    for k in range(4):
+        out_ref[pl.ds(DOWN3 + k, 128, stride=ROWS), :] = d3_ref[k]
+    for half in range(2):
+        for g in range(7):
+            out_ref[pl.ds(half * ROWS + CONV2 + g, 64, stride=2 * ROWS), :] = w2_ref[g, half]
+    out_ref[pl.ds(DOWN2, 128, stride=ROWS), :] = jnp.zeros((128, 128), F32)
+    out_ref[pl.ds(HEAD, 128, stride=ROWS), :] = gh_ref[...]
+
+
+def packed(*args):
+    return call(pack_kernel, [((128 * ROWS, 128), F32)], *args)[0]
+
+
 def last_kernel(
-    lo_ref, g_ref, hi_ref, b2_ref, a_ref, vp_ref, perm_ref, w3_ref, d3_ref, w2_ref, gh_ref, out_ref, b_ref, t_ref, pack_ref
+    where_ref, one_ref, g_ref, two_ref, b2_ref, a_ref, vp_ref, perm_ref, pack_ref, out_ref, b_ref, t_ref, d_ref
 ):
     for n in range(CROPS):
-        planes = (lo_ref[n, 0], g_ref[n, 0], g_ref[n, 1], hi_ref[n, 0])
+        lo, hi = sorted_out(where_ref, one_ref[n], two_ref[n])
+        planes = (lo, g_ref[n, 0], g_ref[n, 1], hi)
         for k, plane in enumerate(planes):
             put_three(b_ref, k * 3 * T, three_two(plane))
         for d in range(2):
@@ -315,16 +387,12 @@
         x = x + pltpu.roll(x, 124, 1)
         pairs.append(x.astype(BF16))
     down = dot(jnp.concatenate(pairs, axis=1), perm_ref[...])
-    for t in range(27):
-        pack_ref[pl.ds(t, 128, stride=ROWS), :] = w3_ref[t]
-    for k in range(4):
-        pack_ref[pl.ds(DOWN3 + k, 128, stride=ROWS), :] = d3_ref[k]
     for half in range(2):
-        for g in range(7):
-            pack_ref[pl.ds(half * ROWS + CONV2 + g, 64, stride=2 * ROWS), :] = w2_ref[g, half]
-        pack_ref[pl.ds(half * ROWS + DOWN2, 64, stride=2 * ROWS), :] = down[:, half * 128 : (half + 1) * 128]
-    pack_ref[pl.ds(HEAD, 128, stride=ROWS), :] = gh_ref[...]
-    out_ref[...] = pack_ref[...].astype(BF16)
+        d_ref[pl.ds(half * ROWS + DOWN2, 64, stride=2 * ROWS), :] = down[:, half * 128 : (half + 1) * 128]
+    row = lax.broadcasted_iota(jnp.int32, (ROWS, 128), 0)
+    for j in range(128):
+        at = pl.ds(j * ROWS, ROWS)
+        out_ref[at, :] = jnp.where(row == DOWN2, d_ref[at, :], pack_ref[at, :]).astype(BF16)
 
 
 def last(*args):
@@ -336,11 +404,12 @@
     )[0]
 
 
-def neighbours(to_upper, to_lower):
+def swapped(one, two):
     count = lax.axis_size("space")
-    up = [(i, i + 1) for i in range(count - 1)]
-    down = [(i + 1, i) for i in range(count - 1)]
-    return lax.ppermute(to_upper, "space", up), lax.ppermute(to_lower, "space", down)
+    near = [(i, i ^ 1) for i in range(count)]
+    far = [(i, ((i + 1) ^ 1) - 1) for i in range(1, count - 1)]
+    two = lax.ppermute(two, "space", far)
+    return lax.ppermute(one, "space", near), two
 
 
 def unpack(sums):
@@ -363,34 +432,30 @@
     voxels = labels.shape[0] * labels.shape[1] * count * labels.shape[2] * labels.shape[3]
     scale = 1.0 / math.sqrt(voxels)
     sec = lax.axis_index("section").astype(jnp.int32)
-
-    eye4 = jnp.eye(4, dtype=BF16)
-    w1 = down_weight_two.transpose(2, 4, 1, 3, 0)[:, :, :, None, :, None, :] * eye4[:, None, :, None]
-    w1 = w1.reshape(2, 512, 256)
-    eye2 = jnp.eye(2, dtype=BF16)
-    wd = down_weight_three.transpose(2, 4, 3, 1, 0)[:, :, None, :, :, None, :] * eye2[:, None, None, :, None]
-    wd = wd.reshape(4, 256, 256)
+    where = jnp.stack([sec, lax.axis_index("space").astype(jnp.int32) % 2])
+
+    w1 = down_weight_two.transpose(1, 2, 3, 4, 0).reshape(256, 64)
+    wd = down_weight_three.transpose(1, 2, 3, 4, 0).reshape(512, 128)
     w2 = w_conv_two.transpose(2, 3, 4, 0, 1).reshape(27, 64, 64)
     w2 = jnp.concatenate([w2, w2], axis=2)
     w3 = w_conv_three.transpose(2, 3, 4, 0, 1).reshape(27, 128, 128)
-    wh = jnp.pad(w_head, ((0, 0), (0, 124)))
-    wht = jnp.pad(w_head.T, ((0, 124), (0, 0)))
     marks = lax.dynamic_slice_in_dim(labels[:, 0], CROPS * sec, CROPS, axis=0)
     marks = marks.transpose(1, 0, 2).reshape(2, 256)
 
-    vp, a2 = first(sec[None], volume, w1)
-    a2_lo, a2_hi = neighbours(a2[:, 1:], a2[:, :1])
-    f2, b2, f3, b3, perm = prepare(w2, w3)
-    h2, a3 = second(a2_lo, a2, a2_hi, f2, wd)
-    a3_lo, a3_hi = neighbours(a3, a3)
-    gz4, gh = head(a3_lo, a3, a3_hi, f3, wh, wht, marks, scale)
-    gz4_lo, gz4_hi = neighbours(gz4, gz4)
-    gw3 = weight_three(gz4, a3_lo, a3, a3_hi)
-    gz2, gd3 = middle(gz4_lo, gz4, gz4_hi, b3, a3, h2, wd)
-    gz2_lo, gz2_hi = neighbours(gz2[:, 1:], gz2[:, :1])
-    gw2 = weight_two(gz2, a2_lo, a2, a2_hi)
-    pack = last(gz2_lo, gz2, gz2_hi, b2, a2, vp, perm, gw3, gd3, gw2, gh)
-
+    vp, a2, one, two = first(where, volume, w1)
+    a2_one, a2_two = swapped(one, two)
+    f2, b2, f3, b3, perm, wd, wh, wht = prepare(w2, w3, wd, w_head.T)
+    h2, a3 = second(where, a2_one, a2, a2_two, f2, wd)
+    a3_one, a3_two = swapped(a3, a3)
+    gz4, gh = head(where, a3_one, a3, a3_two, f3, wh, wht, marks, scale)
+    gz4_one, gz4_two = swapped(gz4, gz4)
+    gw3 = weight_three(where, gz4, a3_one, a3, a3_two)
+    gz4_one, gz4_two, gw3 = lax.optimization_barrier((gz4_one, gz4_two, gw3))
+    gz2, one, two, gd3 = middle(where, gz4_one, gz4, gz4_two, b3, a3, h2, wd)
+    gz2_one, gz2_two = swapped(one, two)
+    gw2 = weight_two(where, gz2, a2_one, a2, a2_two)
+    pack = packed(gw3, gd3, gw2, gh)
+    pack = last(where, gz2_one, gz2, gz2_two, b2, a2, vp, perm, pack)
     return finish(pack.reshape(128, ROWS, 128))
 
 

time: 121 us -> 109 us (0.901)
  local copies, waits for them, and re-layouts: 18.6 us -> 12.8 us
  Pallas kernels: 25.3 us -> 21.9 us
  waiting for transfers between devices: 8.03 us -> 4.72 us
  blocking collectives: 45.5 us -> 48.7 us
  starting transfers between devices: 21.6 us -> 19.2 us
    ppermute x8, waiting for transfers between devices: 8.03 us -> 4.72 us  [the longest x4 4.71 us: swapped(): return (lax.ppermute(one, 'space', near), two)]
    all_to_all x1, blocking collectives: 45.5 us -> 48.7 us  [finish(): terms = lax.all_to_all(pack, ('section', 'space'), 0, 0, tiled=True)]
    mul x7 -> x0, local copies, waits for them, and re-layouts: 3.18 us -> none  [the longest x3 1.69 us: per_device(): down_weight_three.transpose(2, 4, 3, 1, 0)[:, :, None, :, :, None, :]]
    pallas_call x7 -> x8, Pallas kernels: 20.1 us -> 17.2 us  [call(): pl.pallas_call(kernel, in_specs=[scalar if a.dtype == jnp.int32 and a.ndi...]
    ppermute x8, starting transfers between devices: 21.6 us -> 19.2 us  [the longest x4 15.5 us: swapped(): return (lax.ppermute(one, 'space', near), two)]
    pad x2 -> x0, local copies, waits for them, and re-layouts: 1.98 us -> none  [the longest x1 1.37 us: per_device(): wh = jnp.pad(w_head, ((0, 0), (0, 124)))]
    unnamed x33 -> x47, local copies, waits for them, and re-layouts: 7.94 us -> 9.11 us
  transfers between devices with their start and end apart: 8 -> 8, of which waited for: 5 -> 3; matrix products, arithmetic and copies ran while one was open for 4% -> 0% of each run, Pallas kernels for 6% -> 5%
where the time goes in v2:
time: 109 us
  blocking collectives  48.7 us (45%)
  Pallas kernels  21.9 us (20%)
  starting transfers between devices  19.2 us (18%)
  local copies, waits for them, and re-layouts  12.8 us (12%)
  waiting for transfers between devices  4.72 us (4%)
    all_to_all x1, blocking collectives, finish(): terms = lax.all_to_all(pack, ('section', 'space'), 0, 0, tiled=True)  48.7 us
    pallas_call x8, Pallas kernels, call(): pl.pallas_call(kernel, in_specs=[scalar if a.dtype == jnp.int32 and a.ndi...  17.2 us
    ppermute x4, starting transfers between devices, swapped(): return (lax.ppermute(one, 'space', near), two)  15.5 us
    unnamed x47, local copies, waits for them, and re-layouts  9.11 us
    pallas_call x1, Pallas kernels, first(): pl.pallas_call(first_kernel, grid_spec=pltpu.PrefetchScalarGridSpec(num_s...  4.72 us
    ppermute x4, waiting for transfers between devices, swapped(): return (lax.ppermute(one, 'space', near), two)  4.71 us
    ppermute x4, starting transfers between devices, swapped(): two = lax.ppermute(two, 'space', far)  3.64 us
  transfers between devices with their start and end apart: 8, of which 3 were waited for; matrix products, arithmetic and copies ran while one was open for 0% of the time, Pallas kernels for 5%

profile of v2, /device:TPU:1, one launch (start us, length us, event | category | flops | bytes accessed | tf_op | source)
XLA Modules:
  0.0 108.9 jit_solution(17868344751609395667)
XLA Ops:
  0.6 0.0 copy-start
  0.7 0.1 pad_add_fusion.where_ref
  0.7 2.2 %copy-done.1 = bf16[4,32,4,8,512]{4,3,2,1,0:T(8,128)(2,1)S(1)} copy-done((bf16[4,32,4,8,512]{4,3,2,1,0:T(8,128)(2,1)S(1)}, bf16[4,32,4,8,512]{4,3,2,1,0:T(8,128)(2,1)}, u32[]{:S(2)}) %copy-start.1) | copy-done | bytes 4194328
  2.9 0.8 copy-done.16
  3.8 4.7 %shard_map.110 = (bf16[2,2,1024,256]{3,2,1,0:T(8,128)(2,1)S(1)}, bf16[2,2,256,256]{3,2,1,0:T(8,128)(2,1)S(1)}, bf16[2,256,256]{2,1,0:T(8,128)(2,1)S(1)}, bf16[2,256,256]{2,1,0:T(8,128)(2,1)S(1)}) custom-call(s32[2]{0:T(128)S(1)} %pad_add_fusion.where_ref, bf16[4,32,4,8,512]{4,3,2,1,0:T(8,128)(2,1)S(1)} %copy-done.1, bf16[256,64]{1,0:T(8,128)(2,1)S(1)} %bitcast.34), custom_call_target="tpu_custom_call" | custom-call | tf_op jit(solution)/shard_map/pallas_call | solution.py:120
  8.5 0.0 copy-start.10
  8.5 2.1 %collective-permute-start = (bf16[2,256,256]{2,1,0:T(8,128)(2,1)S(1)}, bf16[2,256,256]{2,1,0:T(8,128)(2,1)S(1)}, u32[]{:S(2)}, u32[]{:S(2)}) collective-permute-start(bf16[2,256,256]{2,1,0:T(8,128)(2,1)S(1)} %get-tuple-element.28), channel_id=1, source_target_pairs={{0,1},{1,0},{2,3},{3,2},{4,5},{5,4},{6,7},{7,6},{8,9},{9,8},{10,11... | collective-permute-start | bytes 786440 | tf_op jit(solution)/shard_map/ppermute | solution.py:412
  10.6 0.7 collective-permute-start.1
  11.3 0.2 pad_maximum_fusion.w2_ref
  11.6 1.3 %shard_map.111 = (bf16[256,2304]{1,0:T(8,128)(2,1)S(1)}, bf16[256,2304]{1,0:T(8,128)(2,1)S(1)}, bf16[256,2304]{1,0:T(8,128)(2,1)S(1)}, bf16[256,2304]{1,0:T(8,12...) custom-call(bf16[27,64,128]{2,1,0:T(8,128)(2,1)S(1)} %pad_maximum_fu, ...), custom_call_target="tpu_custom_call" | custom-call | tf_op jit(solution)/shard_map/pallas_call | solution.py:71
  12.9 1.0 copy-done.2
  13.9 0.8 copy-done.11
  14.7 1.4 %collective-permute-done.one_ref = bf16[2,256,256]{2,1,0:T(8,128)(2,1)S(1)} collective-permute-done((bf16[2,256,256]{2,1,0:T(8,128)(2,1)S(1)}, bf16[2,256,256]{2,1,0:T(8,128)(2,1)S(1)}, u32[]{:S(2)}, u32[]{:S(2)}) %collective-permute-start) | collective-permute-done | bytes 262176 | tf_op jit(solution)/shard_map/ppermute | solution.py:412
  16.1 0.0 collective-permute-done.1.two_ref
  16.2 3.1 %shard_map.112 = (bf16[4,256,256]{2,1,0:T(8,128)(2,1)S(1)}, bf16[256,256]{1,0:T(8,128)(2,1)S(1)}) custom-call(s32[2]{0:T(128)S(1)} %pad_add_fusion.where_ref, bf16[2,256,256]{2,1,0:T(8,128)(2,1)S(1)} %collective-permute-done.one_ref, bf16[2,2,256,256]{3,2,1,0:T(8,128)(2,1)S(1)} %get-tuple-element.29.a_ref, ...), custom_call_target="tpu_custom_call" | custom-call | tf_op jit(solution)/shard_map/pallas_call | solution.py:71
  19.4 0.8 copy-done.13
  20.1 1.3 %collective-permute-start.3 = (bf16[256,256]{1,0:T(8,128)(2,1)S(1)}, bf16[256,256]{1,0:T(8,128)(2,1)}, u32[]{:S(2)}, u32[]{:S(2)}) collective-permute-start(bf16[256,256]{1,0:T(8,128)(2,1)S(1)} %get-tuple-element.33.a_ref.a3_ref), channel_id=1, source_target_pairs={{1,2},{2,1},{3,4},{4,3},{5,6},{6,5},{7,8},{8,7},{9,10},{10,9},{11,... | collective-permute-start | bytes 393224 | tf_op jit(solution)/shard_map/ppermute | solution.py:411
  21.5 6.0 %collective-permute-start.2 = (bf16[256,256]{1,0:T(8,128)(2,1)S(1)}, bf16[256,256]{1,0:T(8,128)(2,1)}, u32[]{:S(2)}, u32[]{:S(2)}) collective-permute-start(bf16[256,256]{1,0:T(8,128)(2,1)S(1)} %get-tuple-element.33.a_ref.a3_ref), channel_id=1, source_target_pairs={{0,1},{1,0},{2,3},{3,2},{4,5},{5,4},{6,7},{7,6},{8,9},{9,8},{10,11... | collective-permute-start | bytes 393224 | tf_op jit(solution)/shard_map/ppermute | solution.py:412
  27.5 2.5 %collective-permute-done.2.one_ref = bf16[256,256]{1,0:T(8,128)(2,1)} collective-permute-done((bf16[256,256]{1,0:T(8,128)(2,1)S(1)}, bf16[256,256]{1,0:T(8,128)(2,1)}, u32[]{:S(2)}, u32[]{:S(2)}) %collective-permute-start.2) | collective-permute-done | bytes 131104 | tf_op jit(solution)/shard_map/ppermute | solution.py:412
  29.9 1.3 %copy-done.7 = bf16[256,2304]{1,0:T(8,128)(2,1)S(1)} copy-done((bf16[256,2304]{1,0:T(8,128)(2,1)S(1)}, bf16[256,2304]{1,0:T(8,128)(2,1)}, u32[]{:S(2)}) %copy-start.7) | copy-done | bytes 1179672
  31.2 0.8 copy-done.18
  32.0 0.8 copy-done.20
  32.7 2.2 %shard_map.113 = (bf16[256,256]{1,0:T(8,128)(2,1)S(1)}, f32[128,128]{1,0:T(8,128)S(1)}) custom-call(s32[2]{0:T(128)S(1)} %pad_add_fusion.where_ref, bf16[256,256]{1,0:T(8,128)(2,1)} %collective-permute-done.2.one_ref, bf16[256,256]{1,0:T(8,128)(2,1)S(1)} %get-tuple-element.33.a_ref.a3_ref, bf16[256,256]{1,0:T(8,128)(2,1)} %collective-permute-done.3.two_ref, ...), custom_call_target="tpu_custom_call" | custom-call | tf_op jit(solution)/shard_map/pallas_call | solution.py:71
  35.0 0.8 collective-permute-start.5
  35.8 5.9 %collective-permute-start.4 = (bf16[256,256]{1,0:T(8,128)(2,1)S(1)}, bf16[256,256]{1,0:T(8,128)(2,1)S(1)}, u32[]{:S(2)}, u32[]{:S(2)}) collective-permute-start(bf16[256,256]{1,0:T(8,128)(2,1)S(1)} %get-tuple-element.37.g_ref), channel_id=1, source_target_pairs={{0,1},{1,0},{2,3},{3,2},{4,5},{5,4},{6,7},{7,6},{8,9},{9,8},{10,11... | collective-permute-start | bytes 393224 | tf_op jit(solution)/shard_map/ppermute | solution.py:412
  41.7 1.5 %shard_map.114.w3_ref = f32[27,128,128]{2,1,0:T(8,128)S(1)} custom-call(s32[2]{0:T(128)S(1)} %pad_add_fusion.where_ref, bf16[256,256]{1,0:T(8,128)(2,1)S(1)} %get-tuple-element.37.g_ref, bf16[256,256]{1,0:T(8,128)(2,1)} %collective-permute-done.2.one_ref, bf16[256,256]{1,0:T(8,128)(2,1)S(1)} %get-tuple-element.33.a_ref.a3_ref, ...), custom_call_target="tpu_custom_call" | custom-call | tf_op jit(solution)/shard_map/pallas_call | solution.py:71
  43.2 0.8 collective-permute-done.4.one_ref
  44.0 2.1 %shard_map.115 = (bf16[2,2,256,256]{3,2,1,0:T(8,128)(2,1)S(1)}, bf16[2,256,256]{2,1,0:T(8,128)(2,1)S(1)}, bf16[2,256,256]{2,1,0:T(8,128)(2,1)S(1)}, f32[4,128,128]{2,1,0:T(8,128)S(1)}) custom-call(s32[2]{0:T(128)S(1)} %pad_add_fusion.where_ref, bf16[256,256]{1,0:T(8,128)(2,1)S(1)} %collective-permute-done.4.one_ref, ...), custom_call_target="tpu_custom_call" | custom-call | tf_op jit(solution)/shard_map/pallas_call | solution.py:71
  46.1 1.5 %collective-permute-start.6 = (bf16[2,256,256]{2,1,0:T(8,128)(2,1)S(1)}, bf16[2,256,256]{2,1,0:T(8,128)(2,1)S(1)}, u32[]{:S(2)}, u32[]{:S(2)}) collective-permute-start(bf16[2,256,256]{2,1,0:T(8,128)(2,1)S(1)} %get-tuple-element.42), channel_id=1, source_target_pairs={{0,1},{1,0},{2,3},{3,2},{4,5},{5,4},{6,7},{7,6},{8,9},{9,8},{10,11... | collective-permute-start | bytes 786440 | tf_op jit(solution)/shard_map/ppermute | solution.py:412
  47.6 0.8 collective-permute-start.7
  48.5 2.3 %shard_map.116.w2_ref = f32[7,2,64,128]{3,2,1,0:T(8,128)S(1)} custom-call(s32[2]{0:T(128)S(1)} %pad_add_fusion.where_ref, bf16[2,2,256,256]{3,2,1,0:T(8,128)(2,1)S(1)} %get-tuple-element.43.g_ref, bf16[2,256,256]{2,1,0:T(8,128)(2,1)S(1)} %collective-permute-done.one_ref, bf16[2,2,256,256]{3,2,1,0:T(8,128)(2,1)S(1)} %get-tuple-element.29.a_ref, ...), custom_call_target="tpu_custom_call" | custom-call | tf_op jit(solution)/shard_map/pallas_call | solution.py:71
  50.8 0.8 shard_map.117.pack_ref
  51.6 0.0 collective-permute-done.7.two_ref
  51.6 0.4 copy-done.3
  52.1 0.1 copy-done.12
  52.2 3.9 %shard_map.118 = bf16[5120,128]{1,0:T(8,128)(2,1)S(1)} custom-call(s32[2]{0:T(128)S(1)} %pad_add_fusion.where_ref, bf16[2,256,256]{2,1,0:T(8,128)(2,1)S(1)} %collective-permute-done.6.one_ref, bf16[2,2,256,256]{3,2,1,0:T(8,128)(2,1)S(1)} %get-tuple-element.43.g_ref, bf16[2,256,256]{2,1,0:T(8,128)(2,1)S(1)} %collective-permute-done.7.two_ref, ...), custom_call_target="tpu_custom_call" | custom-call | tf_op jit(solution)/shard_map/pallas_call | solution.py:71
  56.1 48.7 %all_to_all.5 = bf16[128,40,128]{2,1,0:T(8,128)(2,1)S(1)} all-to-all(bf16[128,40,128]{2,1,0:T(8,128)(2,1)S(1)} %bitcast.31), channel_id=1, replica_groups=mesh['section'=2,'space'=64] {'section','space'}, dimensions={0} | all-to-all | bytes 2621440 | tf_op jit(solution)/shard_map/all_to_all | solution.py:426
  104.8 0.2 convert_reduce_fusion
  105.0 0.5 slice_bitcast_fusion.1
  105.6 0.5 slice_bitcast_fusion.2
  106.1 0.1 reshape.52
  106.2 0.1 reshape.50
  106.2 0.1 copy.15
  106.3 0.7 reshape.51
  107.0 0.1 copy.14
  107.1 0.8 reshape.54
  107.9 0.2 copy.13
  108.1 0.8 reshape.53
  (41 shorter events, 0.1 us)
Async XLA Ops:
  0.6 26.8 %copy-start = (s32[4,1,2,128]{3,2,1,0:T(2,128)S(1)}, s32[4,1,2,128]{3,2,1,0:T(2,128)}, u32[]{:S(2)}) copy-start(s32[4,1,2,128]{3,2,1,0:T(2,128)} %param.8) | copy-start | bytes 12292
  0.7 2.2 %copy-start.1 = (bf16[4,32,4,8,512]{4,3,2,1,0:T(8,128)(2,1)S(1)}, bf16[4,32,4,8,512]{4,3,2,1,0:T(8,128)(2,1)}, u32[]{:S(2)}) copy-start(bf16[4,32,4,8,512]{4,3,2,1,0:T(8,128)(2,1)} %vol_ref.1) | copy-start | bytes 12582916
  2.9 0.8 copy-start.16
  3.8 7.5 %copy-start.22 = (bf16[64,64,3,3,3]{1,0,4,3,2:T(8,128)(2,1)S(1)}, bf16[64,64,3,3,3]{1,0,4,3,2:T(8,128)(2,1)}, u32[]{:S(2)}) copy-start(bf16[64,64,3,3,3]{1,0,4,3,2:T(8,128)(2,1)} %param.10) | copy-start | bytes 663556
  3.8 7.8 %copy-start.15 = (bf16[128,64,2,2,2]{0,4,3,2,1:T(2,128)(2,1)S(1)}, bf16[128,64,2,2,2]{0,4,3,2,1:T(2,128)(2,1)}, u32[]{:S(2)}) copy-start(bf16[128,64,2,2,2]{0,4,3,2,1:T(2,128)(2,1)} %param.11) | copy-start | bytes 393220
  3.8 7.8 %copy-start.21 = (bf16[128,4]{0,1:T(4,128)(2,1)S(1)}, bf16[128,4]{0,1:T(4,128)(2,1)}, u32[]{:S(2)}) copy-start(bf16[128,4]{0,1:T(4,128)(2,1)} %param.13) | copy-start | bytes 3076
  8.5 3.1 %copy-start.10 = (bf16[128,128,3,3,3]{1,0,4,3,2:T(8,128)(2,1)S(1)}, bf16[128,128,3,3,3]{1,0,4,3,2:T(8,128)(2,1)}, u32[]{:S(2)}) copy-start(bf16[128,128,3,3,3]{1,0,4,3,2:T(8,128)(2,1)} %param.12) | copy-start | bytes 2654212
  8.5 7.6 %collective-permute-start = (bf16[2,256,256]{2,1,0:T(8,128)(2,1)S(1)}, bf16[2,256,256]{2,1,0:T(8,128)(2,1)S(1)}, u32[]{:S(2)}, u32[]{:S(2)}) collective-permute-start(bf16[2,256,256]{2,1,0:T(8,128)(2,1)S(1)} %get-tuple-element.28), channel_id=1, source_target_pairs={{0,1},{1,0},{2,3},{3,2},{4,5},{5,4},{6,7},{7,6},{8,9},{9,8},{10,11... | collective-permute-start | bytes 786440 | tf_op jit(solution)/shard_map/ppermute | solution.py:412
  10.6 5.5 %collective-permute-start.1 = (bf16[2,256,256]{2,1,0:T(8,128)(2,1)S(1)}, bf16[2,256,256]{2,1,0:T(8,128)(2,1)S(1)}, u32[]{:S(2)}, u32[]{:S(2)}) collective-permute-start(bf16[2,256,256]{2,1,0:T(8,128)(2,1)S(1)} %get-tuple-element.30), channel_id=1, source_target_pairs={{1,2},{2,1},{3,4},{4,3},{5,6},{6,5},{7,8},{8,7},{9,10},{10,9},{11,... | collective-permute-start | bytes 786440 | tf_op jit(solution)/shard_map/ppermute | solution.py:411
  12.9 1.0 copy-start.2
  13.9 0.8 copy-start.11
  14.7 4.6 %copy-start.4 = (bf16[256,2304]{1,0:T(8,128)(2,1)}, bf16[256,2304]{1,0:T(8,128)(2,1)S(1)}, u32[]{:S(2)}) copy-start(bf16[256,2304]{1,0:T(8,128)(2,1)S(1)} %get-tuple-element.40.b3_ref) | copy-start | bytes 3538948
  14.7 4.6 %copy-start.6 = (bf16[256,2304]{1,0:T(8,128)(2,1)}, bf16[256,2304]{1,0:T(8,128)(2,1)S(1)}, u32[]{:S(2)}) copy-start(bf16[256,2304]{1,0:T(8,128)(2,1)S(1)} %get-tuple-element.34.f3_ref) | copy-start | bytes 3538948
  14.7 4.6 %copy-start.17 = (bf16[128,128]{1,0:T(8,128)(2,1)}, bf16[128,128]{1,0:T(8,128)(2,1)S(1)}, u32[]{:S(2)}) copy-start(bf16[128,128]{1,0:T(8,128)(2,1)S(1)} %get-tuple-element.35.wh_ref) | copy-start | bytes 98308
  14.7 4.6 %copy-start.19 = (bf16[128,128]{1,0:T(8,128)(2,1)}, bf16[128,128]{1,0:T(8,128)(2,1)S(1)}, u32[]{:S(2)}) copy-start(bf16[128,128]{1,0:T(8,128)(2,1)S(1)} %get-tuple-element.36.wht_ref) | copy-start | bytes 98308
  16.2 3.2 %copy-start.8 = (bf16[2,256,256]{2,1,0:T(8,128)(2,1)}, bf16[2,256,256]{2,1,0:T(8,128)(2,1)S(1)}, u32[]{:S(2)}) copy-start(bf16[2,256,256]{2,1,0:T(8,128)(2,1)S(1)} %collective-permute-done.1.two_ref) | copy-start | bytes 786436
  19.3 0.8 copy-start.13
  20.1 7.3 %collective-permute-start.3 = (bf16[256,256]{1,0:T(8,128)(2,1)S(1)}, bf16[256,256]{1,0:T(8,128)(2,1)}, u32[]{:S(2)}, u32[]{:S(2)}) collective-permute-start(bf16[256,256]{1,0:T(8,128)(2,1)S(1)} %get-tuple-element.33.a_ref.a3_ref), channel_id=1, source_target_pairs={{1,2},{2,1},{3,4},{4,3},{5,6},{6,5},{7,8},{8,7},{9,10},{10,9},{11,... | collective-permute-start | bytes 393224 | tf_op jit(solution)/shard_map/ppermute | solution.py:411
  21.5 8.5 %collective-permute-start.2 = (bf16[256,256]{1,0:T(8,128)(2,1)S(1)}, bf16[256,256]{1,0:T(8,128)(2,1)}, u32[]{:S(2)}, u32[]{:S(2)}) collective-permute-start(bf16[256,256]{1,0:T(8,128)(2,1)S(1)} %get-tuple-element.33.a_ref.a3_ref), channel_id=1, source_target_pairs={{0,1},{1,0},{2,3},{3,2},{4,5},{5,4},{6,7},{7,6},{8,9},{9,8},{10,11... | collective-permute-start | bytes 393224 | tf_op jit(solution)/shard_map/ppermute | solution.py:412
  29.9 1.3 %copy-start.7 = (bf16[256,2304]{1,0:T(8,128)(2,1)S(1)}, bf16[256,2304]{1,0:T(8,128)(2,1)}, u32[]{:S(2)}) copy-start(bf16[256,2304]{1,0:T(8,128)(2,1)} %copy-done.6) | copy-start | bytes 3538948
  31.2 0.8 copy-start.18
  32.0 0.8 copy-start.20
  35.0 9.0 %copy-start.5 = (bf16[256,2304]{1,0:T(8,128)(2,1)S(1)}, bf16[256,2304]{1,0:T(8,128)(2,1)}, u32[]{:S(2)}) copy-start(bf16[256,2304]{1,0:T(8,128)(2,1)} %copy-done.4) | copy-start | bytes 3538948
  35.0 9.0 %copy-start.14 = (bf16[4,256,256]{2,1,0:T(8,128)(2,1)S(1)}, bf16[4,256,256]{2,1,0:T(8,128)(2,1)}, u32[]{:S(2)}) copy-start(bf16[4,256,256]{2,1,0:T(8,128)(2,1)} %copy-done.13) | copy-start | bytes 1572868
  35.0 8.2 %collective-permute-start.5 = (bf16[256,256]{1,0:T(8,128)(2,1)S(1)}, bf16[256,256]{1,0:T(8,128)(2,1)S(1)}, u32[]{:S(2)}, u32[]{:S(2)}) collective-permute-start(bf16[256,256]{1,0:T(8,128)(2,1)S(1)} %get-tuple-element.37.g_ref), channel_id=1, source_target_pairs={{1,2},{2,1},{3,4},{4,3},{5,6},{6,5},{7,8},{8,7},{9,10},{10,9},{11,... | collective-permute-start | bytes 393224 | tf_op jit(solution)/shard_map/ppermute | solution.py:411
  35.8 8.2 %collective-permute-start.4 = (bf16[256,256]{1,0:T(8,128)(2,1)S(1)}, bf16[256,256]{1,0:T(8,128)(2,1)S(1)}, u32[]{:S(2)}, u32[]{:S(2)}) collective-permute-start(bf16[256,256]{1,0:T(8,128)(2,1)S(1)} %get-tuple-element.37.g_ref), channel_id=1, source_target_pairs={{0,1},{1,0},{2,3},{3,2},{4,5},{5,4},{6,7},{7,6},{8,9},{9,8},{10,11... | collective-permute-start | bytes 393224 | tf_op jit(solution)/shard_map/ppermute | solution.py:412
  44.0 4.5 %copy-start.9 = (bf16[2,256,256]{2,1,0:T(8,128)(2,1)S(1)}, bf16[2,256,256]{2,1,0:T(8,128)(2,1)}, u32[]{:S(2)}) copy-start(bf16[2,256,256]{2,1,0:T(8,128)(2,1)} %copy-done.8) | copy-start | bytes 786436
  46.1 5.5 %collective-permute-start.6 = (bf16[2,256,256]{2,1,0:T(8,128)(2,1)S(1)}, bf16[2,256,256]{2,1,0:T(8,128)(2,1)S(1)}, u32[]{:S(2)}, u32[]{:S(2)}) collective-permute-start(bf16[2,256,256]{2,1,0:T(8,128)(2,1)S(1)} %get-tuple-element.42), channel_id=1, source_target_pairs={{0,1},{1,0},{2,3},{3,2},{4,5},{5,4},{6,7},{7,6},{8,9},{9,8},{10,11... | collective-permute-start | bytes 786440 | tf_op jit(solution)/shard_map/ppermute | solution.py:412
  47.6 4.0 %collective-permute-start.7 = (bf16[2,256,256]{2,1,0:T(8,128)(2,1)S(1)}, bf16[2,256,256]{2,1,0:T(8,128)(2,1)S(1)}, u32[]{:S(2)}, u32[]{:S(2)}) collective-permute-start(bf16[2,256,256]{2,1,0:T(8,128)(2,1)S(1)} %get-tuple-element.44), channel_id=1, source_target_pairs={{1,2},{2,1},{3,4},{4,3},{5,6},{6,5},{7,8},{8,7},{9,10},{10,9},{11,... | collective-permute-start | bytes 786440 | tf_op jit(solution)/shard_map/ppermute | solution.py:411
  50.8 1.3 %copy-start.3 = (bf16[256,2304]{1,0:T(8,128)(2,1)S(1)}, bf16[256,2304]{1,0:T(8,128)(2,1)}, u32[]{:S(2)}) copy-start(bf16[256,2304]{1,0:T(8,128)(2,1)} %copy-done.2) | copy-start | bytes 3538948
  50.8 1.4 %copy-start.12 = (bf16[1024,256]{1,0:T(8,128)(2,1)S(1)}, bf16[1024,256]{1,0:T(8,128)(2,1)}, u32[]{:S(2)}) copy-start(bf16[1024,256]{1,0:T(8,128)(2,1)} %copy-done.11) | copy-start | bytes 1572868

commit v3 on v2

--- a/solution.py
+++ b/solution.py
@@ -72,7 +72,7 @@
         kernel,
         in_specs=[scalar if a.dtype == jnp.int32 and a.ndim == 1 else spec for a in args],
         out_specs=[spec] * len(outs),
-        out_shape=[jax.ShapeDtypeStruct(s, d) for s, d in outs],
+        out_shape=[pltpu.VMEM(s, d) for s, d in outs],
         scratch_shapes=list(scratch),
         compiler_params=params(),
     )(*args)
@@ -135,13 +135,13 @@
             scratch_shapes=[pltpu.VMEM((512, 512), BF16), pltpu.VMEM((256, 1024), BF16)],
         ),
         out_shape=[
-            jax.ShapeDtypeStruct((CROPS, 2, 1024, 256), BF16),
-            jax.ShapeDtypeStruct((CROPS, 2, 256, 256), BF16),
-            jax.ShapeDtypeStruct((CROPS, 256, 256), BF16),
-            jax.ShapeDtypeStruct((CROPS, 256, 256), BF16),
+            pltpu.VMEM((CROPS, 2, 1024, 256), BF16),
+            pltpu.VMEM((CROPS, 2, 256, 256), BF16),
+            pltpu.VMEM((CROPS, 256, 256), BF16),
+            pltpu.VMEM((CROPS, 256, 256), BF16),
         ],
         compiler_params=params(),
-    )(where, volume, w1)
+    )(where, pltpu.with_memory_space_constraint(volume, pltpu.HBM), pltpu.with_memory_space_constraint(w1, pltpu.HBM))
 
 
 def prepare_kernel(

time: 109 us -> 107 us (0.982)
  local copies, waits for them, and re-layouts: 12.8 us -> 11 us
  waiting for transfers between devices: 4.72 us -> 3.51 us
  Pallas kernels: 21.9 us -> 23 us
    unnamed x47 -> x43, local copies, waits for them, and re-layouts: 9.11 us -> 7.29 us
    ppermute x4, waiting for transfers between devices: 4.71 us -> 3.5 us  [swapped(): return (lax.ppermute(one, 'space', near), two)]
  transfers between devices with their start and end apart: 8 -> 8, of which waited for: 3 -> 3; matrix products, arithmetic and copies ran while one was open for 0% -> 0% of each run, Pallas kernels for 5% -> 6%
where the time goes in v3:
time: 107 us
  blocking collectives  48.7 us (46%)
  Pallas kernels  23 us (21%)
  starting transfers between devices  19.2 us (18%)
  local copies, waits for them, and re-layouts  11 us (10%)
  waiting for transfers between devices  3.51 us (3%)
    all_to_all x1, blocking collectives, finish(): terms = lax.all_to_all(pack, ('section', 'space'), 0, 0, tiled=True)  48.7 us
    pallas_call x8, Pallas kernels, call(): pl.pallas_call(kernel, in_specs=[scalar if a.dtype == jnp.int32 and a.ndi...  17.2 us
    ppermute x4, starting transfers between devices, swapped(): return (lax.ppermute(one, 'space', near), two)  15.5 us
    unnamed x43, local copies, waits for them, and re-layouts  7.29 us
    pallas_call x1, Pallas kernels, first(): pl.pallas_call(first_kernel, grid_spec=pltpu.PrefetchScalarGridSpec(num_s...  5.78 us
    ppermute x4, starting transfers between devices, swapped(): two = lax.ppermute(two, 'space', far)  3.63 us
    ppermute x4, waiting for transfers between devices, swapped(): return (lax.ppermute(one, 'space', near), two)  3.5 us
  transfers between devices with their start and end apart: 8, of which 3 were waited for; matrix products, arithmetic and copies ran while one was open for 0% of the time, Pallas kernels for 6%

profile of v3, /device:TPU:1, one launch (start us, length us, event | category | flops | bytes accessed | tf_op | source)
XLA Modules:
  0.0 106.9 jit_solution(9057712633686239360)
XLA Ops:
  0.6 0.0 copy-start
  0.7 0.1 pad_add_fusion.where_ref
  0.7 5.8 %shard_map.110 = (bf16[2,2,1024,256]{3,2,1,0:T(8,128)(2,1)S(1)}, bf16[2,2,256,256]{3,2,1,0:T(8,128)(2,1)S(1)}, bf16[2,256,256]{2,1,0:T(8,128)(2,1)S(1)}, bf16[2,256,256]{2,1,0:T(8,128)(2,1)S(1)}) custom-call(s32[2]{0:T(128)S(1)} %pad_add_fusion.where_ref, bf16[4,32,4,8,512]{4,3,2,1,0:T(8,128)(2,1)} %vol_ref.1, bf16[256,64]{1,0:T(8,128)(2,1)} %bitcast.37), custom_call_target="tpu_custom_call" | custom-call | tf_op jit(solution)/shard_map/pallas_call | solution.py:120
  6.5 0.0 copy-start.9
  6.5 2.1 %collective-permute-start = (bf16[2,256,256]{2,1,0:T(8,128)(2,1)S(1)}, bf16[2,256,256]{2,1,0:T(8,128)(2,1)S(1)}, u32[]{:S(2)}, u32[]{:S(2)}) collective-permute-start(bf16[2,256,256]{2,1,0:T(8,128)(2,1)S(1)} %get-tuple-element.28), channel_id=1, source_target_pairs={{0,1},{1,0},{2,3},{3,2},{4,5},{5,4},{6,7},{7,6},{8,9},{9,8},{10,11... | collective-permute-start | bytes 786440 | tf_op jit(solution)/shard_map/ppermute | solution.py:412
  8.7 0.7 collective-permute-start.1
  9.3 0.2 pad_maximum_fusion.w2_ref
  9.6 1.3 %shard_map.111 = (bf16[256,2304]{1,0:T(8,128)(2,1)S(1)}, bf16[256,2304]{1,0:T(8,128)(2,1)S(1)}, bf16[256,2304]{1,0:T(8,128)(2,1)S(1)}, bf16[256,2304]{1,0:T(8,12...) custom-call(bf16[27,64,128]{2,1,0:T(8,128)(2,1)S(1)} %pad_maximum_fu, ...), custom_call_target="tpu_custom_call" | custom-call | tf_op jit(solution)/shard_map/pallas_call | solution.py:71
  10.9 1.0 copy-done.1
  12.0 0.8 copy-done.10
  12.8 0.6 copy-done.15
  13.4 0.6 copy-done.17
  14.0 0.2 collective-permute-done.one_ref
  14.2 3.1 %shard_map.112 = (bf16[4,256,256]{2,1,0:T(8,128)(2,1)S(1)}, bf16[256,256]{1,0:T(8,128)(2,1)S(1)}) custom-call(s32[2]{0:T(128)S(1)} %pad_add_fusion.where_ref, bf16[2,256,256]{2,1,0:T(8,128)(2,1)S(1)} %collective-permute-done.one_ref, bf16[2,2,256,256]{3,2,1,0:T(8,128)(2,1)S(1)} %get-tuple-element.29.a_ref, ...), custom_call_target="tpu_custom_call" | custom-call | tf_op jit(solution)/shard_map/pallas_call | solution.py:71
  17.4 0.8 copy-done.12
  18.1 1.3 %collective-permute-start.3 = (bf16[256,256]{1,0:T(8,128)(2,1)S(1)}, bf16[256,256]{1,0:T(8,128)(2,1)}, u32[]{:S(2)}, u32[]{:S(2)}) collective-permute-start(bf16[256,256]{1,0:T(8,128)(2,1)S(1)} %get-tuple-element.33.a_ref.a3_ref), channel_id=1, source_target_pairs={{1,2},{2,1},{3,4},{4,3},{5,6},{6,5},{7,8},{8,7},{9,10},{10,9},{11,... | collective-permute-start | bytes 393224 | tf_op jit(solution)/shard_map/ppermute | solution.py:411
  19.5 6.0 %collective-permute-start.2 = (bf16[256,256]{1,0:T(8,128)(2,1)S(1)}, bf16[256,256]{1,0:T(8,128)(2,1)}, u32[]{:S(2)}, u32[]{:S(2)}) collective-permute-start(bf16[256,256]{1,0:T(8,128)(2,1)S(1)} %get-tuple-element.33.a_ref.a3_ref), channel_id=1, source_target_pairs={{0,1},{1,0},{2,3},{3,2},{4,5},{5,4},{6,7},{7,6},{8,9},{9,8},{10,11... | collective-permute-start | bytes 393224 | tf_op jit(solution)/shard_map/ppermute | solution.py:412
  25.5 2.5 %collective-permute-done.2.one_ref = bf16[256,256]{1,0:T(8,128)(2,1)} collective-permute-done((bf16[256,256]{1,0:T(8,128)(2,1)S(1)}, bf16[256,256]{1,0:T(8,128)(2,1)}, u32[]{:S(2)}, u32[]{:S(2)}) %collective-permute-start.2) | collective-permute-done | bytes 131104 | tf_op jit(solution)/shard_map/ppermute | solution.py:412
  27.9 1.3 %copy-done.6 = bf16[256,2304]{1,0:T(8,128)(2,1)S(1)} copy-done((bf16[256,2304]{1,0:T(8,128)(2,1)S(1)}, bf16[256,2304]{1,0:T(8,128)(2,1)}, u32[]{:S(2)}) %copy-start.6) | copy-done | bytes 1179672
  29.2 0.8 copy-done.16
  30.0 0.8 copy-done.18
  30.7 2.2 %shard_map.113 = (bf16[256,256]{1,0:T(8,128)(2,1)S(1)}, f32[128,128]{1,0:T(8,128)S(1)}) custom-call(s32[2]{0:T(128)S(1)} %pad_add_fusion.where_ref, bf16[256,256]{1,0:T(8,128)(2,1)} %collective-permute-done.2.one_ref, bf16[256,256]{1,0:T(8,128)(2,1)S(1)} %get-tuple-element.33.a_ref.a3_ref, bf16[256,256]{1,0:T(8,128)(2,1)} %collective-permute-done.3.two_ref, ...), custom_call_target="tpu_custom_call" | custom-call | tf_op jit(solution)/shard_map/pallas_call | solution.py:71
  33.0 0.8 collective-permute-start.5
  33.8 5.9 %collective-permute-start.4 = (bf16[256,256]{1,0:T(8,128)(2,1)S(1)}, bf16[256,256]{1,0:T(8,128)(2,1)S(1)}, u32[]{:S(2)}, u32[]{:S(2)}) collective-permute-start(bf16[256,256]{1,0:T(8,128)(2,1)S(1)} %get-tuple-element.37.g_ref), channel_id=1, source_target_pairs={{0,1},{1,0},{2,3},{3,2},{4,5},{5,4},{6,7},{7,6},{8,9},{9,8},{10,11... | collective-permute-start | bytes 393224 | tf_op jit(solution)/shard_map/ppermute | solution.py:412
  39.7 1.5 %shard_map.114.w3_ref = f32[27,128,128]{2,1,0:T(8,128)S(1)} custom-call(s32[2]{0:T(128)S(1)} %pad_add_fusion.where_ref, bf16[256,256]{1,0:T(8,128)(2,1)S(1)} %get-tuple-element.37.g_ref, bf16[256,256]{1,0:T(8,128)(2,1)} %collective-permute-done.2.one_ref, bf16[256,256]{1,0:T(8,128)(2,1)S(1)} %get-tuple-element.33.a_ref.a3_ref, ...), custom_call_target="tpu_custom_call" | custom-call | tf_op jit(solution)/shard_map/pallas_call | solution.py:71
  41.2 0.0 collective-permute-done.5.two_ref
  41.2 0.8 collective-permute-done.4.one_ref
  42.0 2.1 %shard_map.115 = (bf16[2,2,256,256]{3,2,1,0:T(8,128)(2,1)S(1)}, bf16[2,256,256]{2,1,0:T(8,128)(2,1)S(1)}, bf16[2,256,256]{2,1,0:T(8,128)(2,1)S(1)}, f32[4,128,128]{2,1,0:T(8,128)S(1)}) custom-call(s32[2]{0:T(128)S(1)} %pad_add_fusion.where_ref, bf16[256,256]{1,0:T(8,128)(2,1)S(1)} %collective-permute-done.4.one_ref, ...), custom_call_target="tpu_custom_call" | custom-call | tf_op jit(solution)/shard_map/pallas_call | solution.py:71
  44.1 1.5 %collective-permute-start.6 = (bf16[2,256,256]{2,1,0:T(8,128)(2,1)S(1)}, bf16[2,256,256]{2,1,0:T(8,128)(2,1)S(1)}, u32[]{:S(2)}, u32[]{:S(2)}) collective-permute-start(bf16[2,256,256]{2,1,0:T(8,128)(2,1)S(1)} %get-tuple-element.42), channel_id=1, source_target_pairs={{0,1},{1,0},{2,3},{3,2},{4,5},{5,4},{6,7},{7,6},{8,9},{9,8},{10,11... | collective-permute-start | bytes 786440 | tf_op jit(solution)/shard_map/ppermute | solution.py:412
  45.6 0.8 collective-permute-start.7
  46.5 2.3 %shard_map.116.w2_ref = f32[7,2,64,128]{3,2,1,0:T(8,128)S(1)} custom-call(s32[2]{0:T(128)S(1)} %pad_add_fusion.where_ref, bf16[2,2,256,256]{3,2,1,0:T(8,128)(2,1)S(1)} %get-tuple-element.43.g_ref, bf16[2,256,256]{2,1,0:T(8,128)(2,1)S(1)} %collective-permute-done.one_ref, bf16[2,2,256,256]{3,2,1,0:T(8,128)(2,1)S(1)} %get-tuple-element.29.a_ref, ...), custom_call_target="tpu_custom_call" | custom-call | tf_op jit(solution)/shard_map/pallas_call | solution.py:71
  48.8 0.8 shard_map.117.pack_ref
  49.6 0.0 collective-permute-done.7.two_ref
  49.6 0.4 copy-done.2
  50.1 0.1 copy-done.11
  50.2 3.9 %shard_map.118 = bf16[5120,128]{1,0:T(8,128)(2,1)S(1)} custom-call(s32[2]{0:T(128)S(1)} %pad_add_fusion.where_ref, bf16[2,256,256]{2,1,0:T(8,128)(2,1)S(1)} %collective-permute-done.6.one_ref, bf16[2,2,256,256]{3,2,1,0:T(8,128)(2,1)S(1)} %get-tuple-element.43.g_ref, bf16[2,256,256]{2,1,0:T(8,128)(2,1)S(1)} %collective-permute-done.7.two_ref, ...), custom_call_target="tpu_custom_call" | custom-call | tf_op jit(solution)/shard_map/pallas_call | solution.py:71
  54.1 48.7 %all_to_all.5 = bf16[128,40,128]{2,1,0:T(8,128)(2,1)S(1)} all-to-all(bf16[128,40,128]{2,1,0:T(8,128)(2,1)S(1)} %bitcast.31), channel_id=1, replica_groups=mesh['section'=2,'space'=64] {'section','space'}, dimensions={0} | all-to-all | bytes 2621440 | tf_op jit(solution)/shard_map/all_to_all | solution.py:426
  102.8 0.2 convert_reduce_fusion
  103.0 0.5 slice_bitcast_fusion.1
  103.6 0.5 slice_bitcast_fusion.2
  104.1 0.1 reshape.52
  104.2 0.1 reshape.50
  104.2 0.1 copy.15
  104.3 0.7 reshape.51
  105.0 0.1 copy.14
  105.1 0.8 reshape.54
  105.9 0.2 copy.13
  106.1 0.8 reshape.53
  (37 shorter events, 0.1 us)
Async XLA Ops:
  0.6 24.8 %copy-start = (s32[4,1,2,128]{3,2,1,0:T(2,128)S(1)}, s32[4,1,2,128]{3,2,1,0:T(2,128)}, u32[]{:S(2)}) copy-start(s32[4,1,2,128]{3,2,1,0:T(2,128)} %param.8) | copy-start | bytes 12292
  0.7 8.6 %copy-start.20 = (bf16[64,64,3,3,3]{1,0,4,3,2:T(8,128)(2,1)S(1)}, bf16[64,64,3,3,3]{1,0,4,3,2:T(8,128)(2,1)}, u32[]{:S(2)}) copy-start(bf16[64,64,3,3,3]{1,0,4,3,2:T(8,128)(2,1)} %param.10) | copy-start | bytes 663556
  0.7 8.9 %copy-start.14 = (bf16[128,64,2,2,2]{0,4,3,2,1:T(2,128)(2,1)S(1)}, bf16[128,64,2,2,2]{0,4,3,2,1:T(2,128)(2,1)}, u32[]{:S(2)}) copy-start(bf16[128,64,2,2,2]{0,4,3,2,1:T(2,128)(2,1)} %param.11) | copy-start | bytes 393220
  0.7 8.9 %copy-start.19 = (bf16[128,4]{0,1:T(4,128)(2,1)S(1)}, bf16[128,4]{0,1:T(4,128)(2,1)}, u32[]{:S(2)}) copy-start(bf16[128,4]{0,1:T(4,128)(2,1)} %param.13) | copy-start | bytes 3076
  6.5 3.1 %copy-start.9 = (bf16[128,128,3,3,3]{1,0,4,3,2:T(8,128)(2,1)S(1)}, bf16[128,128,3,3,3]{1,0,4,3,2:T(8,128)(2,1)}, u32[]{:S(2)}) copy-start(bf16[128,128,3,3,3]{1,0,4,3,2:T(8,128)(2,1)} %param.12) | copy-start | bytes 2654212
  6.5 7.6 %collective-permute-start = (bf16[2,256,256]{2,1,0:T(8,128)(2,1)S(1)}, bf16[2,256,256]{2,1,0:T(8,128)(2,1)S(1)}, u32[]{:S(2)}, u32[]{:S(2)}) collective-permute-start(bf16[2,256,256]{2,1,0:T(8,128)(2,1)S(1)} %get-tuple-element.28), channel_id=1, source_target_pairs={{0,1},{1,0},{2,3},{3,2},{4,5},{5,4},{6,7},{7,6},{8,9},{9,8},{10,11... | collective-permute-start | bytes 786440 | tf_op jit(solution)/shard_map/ppermute | solution.py:412
  8.7 5.5 %collective-permute-start.1 = (bf16[2,256,256]{2,1,0:T(8,128)(2,1)S(1)}, bf16[2,256,256]{2,1,0:T(8,128)(2,1)S(1)}, u32[]{:S(2)}, u32[]{:S(2)}) collective-permute-start(bf16[2,256,256]{2,1,0:T(8,128)(2,1)S(1)} %get-tuple-element.30), channel_id=1, source_target_pairs={{1,2},{2,1},{3,4},{4,3},{5,6},{6,5},{7,8},{8,7},{9,10},{10,9},{11,... | collective-permute-start | bytes 786440 | tf_op jit(solution)/shard_map/ppermute | solution.py:411
  10.9 1.0 copy-start.1
  12.0 0.8 copy-start.10
  12.7 0.6 copy-start.15
  13.4 0.6 copy-start.17
  14.0 3.4 %copy-start.3 = (bf16[256,2304]{1,0:T(8,128)(2,1)}, bf16[256,2304]{1,0:T(8,128)(2,1)S(1)}, u32[]{:S(2)}) copy-start(bf16[256,2304]{1,0:T(8,128)(2,1)S(1)} %get-tuple-element.40.b3_ref) | copy-start | bytes 3538948
  14.0 3.4 %copy-start.5 = (bf16[256,2304]{1,0:T(8,128)(2,1)}, bf16[256,2304]{1,0:T(8,128)(2,1)S(1)}, u32[]{:S(2)}) copy-start(bf16[256,2304]{1,0:T(8,128)(2,1)S(1)} %get-tuple-element.34.f3_ref) | copy-start | bytes 3538948
  14.2 3.2 %copy-start.7 = (bf16[2,256,256]{2,1,0:T(8,128)(2,1)}, bf16[2,256,256]{2,1,0:T(8,128)(2,1)S(1)}, u32[]{:S(2)}) copy-start(bf16[2,256,256]{2,1,0:T(8,128)(2,1)S(1)} %collective-permute-done.1.two_ref) | copy-start | bytes 786436
  17.3 0.8 copy-start.12
  18.1 7.3 %collective-permute-start.3 = (bf16[256,256]{1,0:T(8,128)(2,1)S(1)}, bf16[256,256]{1,0:T(8,128)(2,1)}, u32[]{:S(2)}, u32[]{:S(2)}) collective-permute-start(bf16[256,256]{1,0:T(8,128)(2,1)S(1)} %get-tuple-element.33.a_ref.a3_ref), channel_id=1, source_target_pairs={{1,2},{2,1},{3,4},{4,3},{5,6},{6,5},{7,8},{8,7},{9,10},{10,9},{11,... | collective-permute-start | bytes 393224 | tf_op jit(solution)/shard_map/ppermute | solution.py:411
  19.5 8.5 %collective-permute-start.2 = (bf16[256,256]{1,0:T(8,128)(2,1)S(1)}, bf16[256,256]{1,0:T(8,128)(2,1)}, u32[]{:S(2)}, u32[]{:S(2)}) collective-permute-start(bf16[256,256]{1,0:T(8,128)(2,1)S(1)} %get-tuple-element.33.a_ref.a3_ref), channel_id=1, source_target_pairs={{0,1},{1,0},{2,3},{3,2},{4,5},{5,4},{6,7},{7,6},{8,9},{9,8},{10,11... | collective-permute-start | bytes 393224 | tf_op jit(solution)/shard_map/ppermute | solution.py:412
  27.9 1.3 %copy-start.6 = (bf16[256,2304]{1,0:T(8,128)(2,1)S(1)}, bf16[256,2304]{1,0:T(8,128)(2,1)}, u32[]{:S(2)}) copy-start(bf16[256,2304]{1,0:T(8,128)(2,1)} %copy-done.5) | copy-start | bytes 3538948
  29.2 0.8 copy-start.16
  30.0 0.8 copy-start.18
  33.0 9.0 %copy-start.4 = (bf16[256,2304]{1,0:T(8,128)(2,1)S(1)}, bf16[256,2304]{1,0:T(8,128)(2,1)}, u32[]{:S(2)}) copy-start(bf16[256,2304]{1,0:T(8,128)(2,1)} %copy-done.3) | copy-start | bytes 3538948
  33.0 9.0 %copy-start.13 = (bf16[4,256,256]{2,1,0:T(8,128)(2,1)S(1)}, bf16[4,256,256]{2,1,0:T(8,128)(2,1)}, u32[]{:S(2)}) copy-start(bf16[4,256,256]{2,1,0:T(8,128)(2,1)} %copy-done.12) | copy-start | bytes 1572868
  33.0 8.2 %collective-permute-start.5 = (bf16[256,256]{1,0:T(8,128)(2,1)S(1)}, bf16[256,256]{1,0:T(8,128)(2,1)S(1)}, u32[]{:S(2)}, u32[]{:S(2)}) collective-permute-start(bf16[256,256]{1,0:T(8,128)(2,1)S(1)} %get-tuple-element.37.g_ref), channel_id=1, source_target_pairs={{1,2},{2,1},{3,4},{4,3},{5,6},{6,5},{7,8},{8,7},{9,10},{10,9},{11,... | collective-permute-start | bytes 393224 | tf_op jit(solution)/shard_map/ppermute | solution.py:411
  33.8 8.2 %collective-permute-start.4 = (bf16[256,256]{1,0:T(8,128)(2,1)S(1)}, bf16[256,256]{1,0:T(8,128)(2,1)S(1)}, u32[]{:S(2)}, u32[]{:S(2)}) collective-permute-start(bf16[256,256]{1,0:T(8,128)(2,1)S(1)} %get-tuple-element.37.g_ref), channel_id=1, source_target_pairs={{0,1},{1,0},{2,3},{3,2},{4,5},{5,4},{6,7},{7,6},{8,9},{9,8},{10,11... | collective-permute-start | bytes 393224 | tf_op jit(solution)/shard_map/ppermute | solution.py:412
  42.0 4.5 %copy-start.8 = (bf16[2,256,256]{2,1,0:T(8,128)(2,1)S(1)}, bf16[2,256,256]{2,1,0:T(8,128)(2,1)}, u32[]{:S(2)}) copy-start(bf16[2,256,256]{2,1,0:T(8,128)(2,1)} %copy-done.7) | copy-start | bytes 786436
  44.1 5.5 %collective-permute-start.6 = (bf16[2,256,256]{2,1,0:T(8,128)(2,1)S(1)}, bf16[2,256,256]{2,1,0:T(8,128)(2,1)S(1)}, u32[]{:S(2)}, u32[]{:S(2)}) collective-permute-start(bf16[2,256,256]{2,1,0:T(8,128)(2,1)S(1)} %get-tuple-element.42), channel_id=1, source_target_pairs={{0,1},{1,0},{2,3},{3,2},{4,5},{5,4},{6,7},{7,6},{8,9},{9,8},{10,11... | collective-permute-start | bytes 786440 | tf_op jit(solution)/shard_map/ppermute | solution.py:412
  45.6 4.0 %collective-permute-start.7 = (bf16[2,256,256]{2,1,0:T(8,128)(2,1)S(1)}, bf16[2,256,256]{2,1,0:T(8,128)(2,1)S(1)}, u32[]{:S(2)}, u32[]{:S(2)}) collective-permute-start(bf16[2,256,256]{2,1,0:T(8,128)(2,1)S(1)} %get-tuple-element.44), channel_id=1, source_target_pairs={{1,2},{2,1},{3,4},{4,3},{5,6},{6,5},{7,8},{8,7},{9,10},{10,9},{11,... | collective-permute-start | bytes 786440 | tf_op jit(solution)/shard_map/ppermute | solution.py:411
  48.8 1.3 %copy-start.2 = (bf16[256,2304]{1,0:T(8,128)(2,1)S(1)}, bf16[256,2304]{1,0:T(8,128)(2,1)}, u32[]{:S(2)}) copy-start(bf16[256,2304]{1,0:T(8,128)(2,1)} %copy-done.1) | copy-start | bytes 3538948
  48.8 1.4 %copy-start.11 = (bf16[1024,256]{1,0:T(8,128)(2,1)S(1)}, bf16[1024,256]{1,0:T(8,128)(2,1)}, u32[]{:S(2)}) copy-start(bf16[1024,256]{1,0:T(8,128)(2,1)} %copy-done.10) | copy-start | bytes 1572868

commit v4 on v3

--- a/solution.py
+++ b/solution.py
@@ -15,7 +15,7 @@
 CROPS = 2
 T = 256
 ROWS = 40
-DOWN3, CONV2, DOWN2, HEAD = 27, 31, 38, 39
+DOWN3, CONV2, DOWN2 = 27, 31, 38
 
 
 def params(megabytes=24):
@@ -65,17 +65,18 @@
         ref[pl.ds(row + j * T, T), 128:256] = right
 
 
-def call(kernel, outs, *args, scratch=()):
+def call(kernel, outs, *args, scratch=(), far=()):
     spec = pl.BlockSpec(memory_space=pltpu.VMEM)
     scalar = pl.BlockSpec(memory_space=pltpu.SMEM)
+    remote = pl.BlockSpec(memory_space=pl.ANY)
     return pl.pallas_call(
         kernel,
-        in_specs=[scalar if a.dtype == jnp.int32 and a.ndim == 1 else spec for a in args],
+        in_specs=[remote if i in far else scalar if a.dtype == jnp.int32 and a.ndim == 1 else spec for i, a in enumerate(args)],
         out_specs=[spec] * len(outs),
-        out_shape=[pltpu.VMEM(s, d) for s, d in outs],
+        out_shape=[space(s, d) for s, d, space in outs],
         scratch_shapes=list(scratch),
         compiler_params=params(),
-    )(*args)
+    )(*[pltpu.with_memory_space_constraint(a, pltpu.HBM) if i in far else a for i, a in enumerate(args)])
 
 
 def sorted_out(where_ref, one, two):
@@ -135,7 +136,7 @@
             scratch_shapes=[pltpu.VMEM((512, 512), BF16), pltpu.VMEM((256, 1024), BF16)],
         ),
         out_shape=[
-            pltpu.VMEM((CROPS, 2, 1024, 256), BF16),
+            pltpu.HBM((CROPS, 2, 1024, 256), BF16),
             pltpu.VMEM((CROPS, 2, 256, 256), BF16),
             pltpu.VMEM((CROPS, 256, 256), BF16),
             pltpu.VMEM((CROPS, 256, 256), BF16),
@@ -145,7 +146,7 @@
 
 
 def prepare_kernel(
-    w2_ref, w3_ref, wd_ref, head_ref, f2_ref, b2_ref, f3_ref, b3_ref, perm_ref, d_ref, wh_ref, wht_ref, rows_ref
+    w2_ref, w3_ref, wd_ref, head_ref, f2_ref, b2_ref, f3_ref, b3_ref, perm_ref, d_ref, wh_ref, rows_ref
 ):
     low = lax.broadcasted_iota(jnp.int32, (64, 128), 1) < 64
     zero = jnp.zeros((64, 128), F32)
@@ -182,19 +183,21 @@
     rows_ref[pl.ds(0, 128), :] = jnp.zeros((128, 128), F32)
     rows_ref[pl.ds(0, 4), :] = head_ref[...].astype(F32)
     wht = rows_ref[pl.ds(0, 128), :]
-    wht_ref[...] = wht.astype(BF16)
-    wh_ref[...] = wht.T.astype(BF16)
+    wh_ref[pl.ds(0, 128), :] = wht.T.astype(BF16)
+    wh_ref[pl.ds(128, 128), :] = wht.astype(BF16)
     to = lax.broadcasted_iota(jnp.int32, (1, 256), 1)
     source = to // 4 % 2 * 512 + to % 2 * 256 + (to // 128 * 16 + to // 8 % 16) * 8 + to // 2 % 2
     perm_ref[...] = jnp.where(lax.broadcasted_iota(jnp.int32, (1024, 256), 0) == source, 1.0, 0.0).astype(BF16)
 
 
 def prepare(w2, w3, wd, wh):
-    wide = ((T, 9 * T), BF16)
-    square = ((128, 128), BF16)
+    def wide(space):
+        return ((T, 9 * T), BF16, space)
+
     return call(
         prepare_kernel,
-        [wide] * 4 + [((1024, 256), BF16), ((4, T, T), BF16), square, square],
+        [wide(pltpu.VMEM), wide(pltpu.HBM), wide(pltpu.HBM), wide(pltpu.HBM)]
+        + [((1024, 256), BF16, pltpu.HBM), ((4, T, T), BF16, pltpu.VMEM), ((256, 128), BF16, pltpu.HBM)],
         w2, w3, wd, wh,
         scratch=[pltpu.VMEM((512, 128), F32)],
     )
@@ -219,37 +222,53 @@
 def second(where, one, a, two, f2, wd):
     return call(
         second_kernel,
-        [((4, T, T), BF16), ((T, T), BF16)],
+        [((4, T, T), BF16, pltpu.HBM), ((T, T), BF16, pltpu.VMEM)],
         where, one, a, two, f2, wd,
         scratch=[pltpu.VMEM((12 * T, T), BF16)],
     )
 
 
-def head_kernel(scale, where_ref, one_ref, a_ref, two_ref, f3_ref, wh_ref, wht_ref, marks_ref, gz_ref, gh_ref, b_ref):
+def head_kernel(
+    scale, where_ref, one_ref, a_ref, two_ref, f3_far, wh_far, marks_ref, gz_ref, gh_ref, b_ref, f3_ref, wh_ref, sems
+):
+    fetches = [
+        pltpu.make_async_copy(f3_far, f3_ref, sems.at[0]),
+        pltpu.make_async_copy(wh_far, wh_ref, sems.at[1]),
+    ]
+    for fetch in fetches:
+        fetch.start()
     lo, hi = sorted_out(where_ref, one_ref[...], two_ref[...])
     for k, plane in enumerate((lo, a_ref[...], hi)):
         put_three(b_ref, k * 3 * T, three_three(plane))
+    for fetch in fetches:
+        fetch.wait()
     top = rectified(dot(f3_ref[...], b_ref[...])).astype(BF16)
     row = lax.broadcasted_iota(jnp.int32, (128, T), 0)
     total = jnp.zeros((128, 128), F32)
     for h in range(2):
         mine = top[h * 128 : (h + 1) * 128]
-        logits = dot(wht_ref[...], mine)
+        logits = dot(wh_ref[pl.ds(128, 128), :], mine)
         powers = jnp.where(row < 4, jnp.exp(logits), 0.0)
         share = powers / jnp.sum(powers, axis=0, keepdims=True)
         chosen = jnp.where(row == marks_ref[pl.ds(h, 1), :], 1.0, 0.0)
         g = jnp.where(row < 4, (share - chosen) * scale, 0.0).astype(BF16)
         total += dot_nt(mine, g)
-        gz_ref[pl.ds(h * 128, 128), :] = (dot(wh_ref[...], g) * slope(mine)).astype(BF16)
+        gz_ref[pl.ds(h * 128, 128), :] = (dot(wh_ref[pl.ds(0, 128), :], g) * slope(mine)).astype(BF16)
     gh_ref[...] = total
 
 
-def head(where, one, a, two, f3, wh, wht, marks, scale):
+def head(where, one, a, two, f3, wh, marks, scale):
     return call(
         functools.partial(head_kernel, scale),
-        [((T, T), BF16), ((128, 128), F32)],
-        where, one, a, two, f3, wh, wht, marks,
-        scratch=[pltpu.VMEM((9 * T, T), BF16)],
+        [((T, T), BF16, pltpu.VMEM), ((128, 128), F32, pltpu.VMEM)],
+        where, one, a, two, f3, wh, marks,
+        scratch=[
+            pltpu.VMEM((9 * T, T), BF16),
+            pltpu.VMEM((T, 9 * T), BF16),
+            pltpu.VMEM((256, 128), BF16),
+            pltpu.SemaphoreType.DMA((2,)),
+        ],
+        far=(4, 5),
     )
 
 
@@ -267,7 +286,7 @@
 def weight_three(where, g, one, a, two):
     return call(
         weight_three_kernel,
-        [((27, 128, 128), F32)],
+        [((27, 128, 128), F32, pltpu.VMEM)],
         where, g, one, a, two,
         scratch=[pltpu.VMEM((3 * T, T), BF16)],
     )[0]
@@ -297,7 +316,12 @@
 def middle(where, one, g, two, b3, a3, h, wd):
     return call(
         middle_kernel,
-        [((CROPS, 2, T, T), BF16), ((CROPS, T, T), BF16), ((CROPS, T, T), BF16), ((4, 128, 128), F32)],
+        [
+            ((CROPS, 2, T, T), BF16, pltpu.VMEM),
+            ((CROPS, T, T), BF16, pltpu.VMEM),
+            ((CROPS, T, T), BF16, pltpu.VMEM),
+            ((4, 128, 128), F32, pltpu.VMEM),
+        ],
         where, one, g, two, b3, a3, h, wd,
         scratch=[pltpu.VMEM((9 * T, T), BF16)],
     )
@@ -339,38 +363,61 @@
 def weight_two(where, g, one, a, two):
     return call(
         weight_two_kernel,
-        [((7, 2, 64, 128), F32)],
+        [((7, 2, 64, 128), F32, pltpu.VMEM)],
         where, g, one, a, two,
         scratch=[pltpu.VMEM((3, T, 4 * T), BF16), pltpu.VMEM((3, T, 4 * T), BF16)],
     )[0]
 
 
-def pack_kernel(w3_ref, d3_ref, w2_ref, gh_ref, out_ref):
+def pack_kernel(where_ref, w3_ref, d3_ref, w2_ref, gh_ref, keep_ref, send_ref, pack_ref):
     for t in range(27):
-        out_ref[pl.ds(t, 128, stride=ROWS), :] = w3_ref[t]
+        pack_ref[pl.ds(t, 128, stride=ROWS), :] = w3_ref[t]
     for k in range(4):
-        out_ref[pl.ds(DOWN3 + k, 128, stride=ROWS), :] = d3_ref[k]
+        pack_ref[pl.ds(DOWN3 + k, 128, stride=ROWS), :] = d3_ref[k]
+    lane = lax.broadcasted_iota(jnp.int32, (64, 128), 1)
     for half in range(2):
-        for g in range(7):
-            out_ref[pl.ds(half * ROWS + CONV2 + g, 64, stride=2 * ROWS), :] = w2_ref[g, half]
-    out_ref[pl.ds(DOWN2, 128, stride=ROWS), :] = jnp.zeros((128, 128), F32)
-    out_ref[pl.ds(HEAD, 128, stride=ROWS), :] = gh_ref[...]
+        for g in range(6):
+            pack_ref[pl.ds(half * ROWS + CONV2 + g, 64, stride=2 * ROWS), :] = w2_ref[g, half]
+        heads = pltpu.roll(gh_ref[pl.ds(half, 64, stride=2), :], 96, 1)
+        pack_ref[pl.ds(half * ROWS + CONV2 + 6, 64, stride=2 * ROWS), :] = jnp.where(lane < 96, w2_ref[6, half], heads)
+    zero = jnp.zeros((128, 128), F32)
+    pack_ref[pl.ds(DOWN2, 128, stride=ROWS), :] = zero
+    pack_ref[pl.ds(DOWN2 + 1, 128, stride=ROWS), :] = zero
+    keep_ref[...] = pack_ref[pl.ds(pl.multiple_of(where_ref[0] * 64 * ROWS, 64 * ROWS), 64 * ROWS), :]
+    send_ref[...] = pack_ref[pl.ds(pl.multiple_of((1 - where_ref[0]) * 64 * ROWS, 64 * ROWS), 64 * ROWS), :].astype(BF16)
 
 
 def packed(*args):
-    return call(pack_kernel, [((128 * ROWS, 128), F32)], *args)[0]
+    half = (64 * ROWS, 128)
+    return call(
+        pack_kernel,
+        [(half, F32, pltpu.VMEM), (half, BF16, pltpu.VMEM)],
+        *args,
+        scratch=[pltpu.VMEM((128 * ROWS, 128), F32)],
+    )
 
 
 def last_kernel(
-    where_ref, one_ref, g_ref, two_ref, b2_ref, a_ref, vp_ref, perm_ref, pack_ref, out_ref, b_ref, t_ref, d_ref
+    where_ref, one_ref, g_ref, two_ref, b2_far, a_ref, vp_far, perm_far, keep_ref, came_ref, out_ref, b_ref, t_ref, d_ref,
+    down_ref, b2_ref, vp_ref, perm_ref, sems
 ):
+    fetches = [
+        pltpu.make_async_copy(far, ref, sems.at[i])
+        for i, (far, ref) in enumerate(((b2_far, b2_ref), (vp_far, vp_ref), (perm_far, perm_ref)))
+    ]
+    for fetch in fetches:
+        fetch.start()
     for n in range(CROPS):
         lo, hi = sorted_out(where_ref, one_ref[n], two_ref[n])
         planes = (lo, g_ref[n, 0], g_ref[n, 1], hi)
         for k, plane in enumerate(planes):
             put_three(b_ref, k * 3 * T, three_two(plane))
         for d in range(2):
+            if n + d == 0:
+                fetches[0].wait()
             gy = (dot(b2_ref[...], b_ref[pl.ds(d * 3 * T, 9 * T), :]) * slope(a_ref[n, d])).astype(BF16)
+            if n + d == 0:
+                fetches[1].wait()
             t = dot_nt(gy, vp_ref[n, d])
             if n + d == 0:
                 t_ref[...] = t
@@ -386,21 +433,36 @@
         x = x + pltpu.roll(x, 126, 1)
         x = x + pltpu.roll(x, 124, 1)
         pairs.append(x.astype(BF16))
-    down = dot(jnp.concatenate(pairs, axis=1), perm_ref[...])
-    for half in range(2):
-        d_ref[pl.ds(half * ROWS + DOWN2, 64, stride=2 * ROWS), :] = down[:, half * 128 : (half + 1) * 128]
+    fetches[2].wait()
+    down_ref[...] = dot(jnp.concatenate(pairs, axis=1), perm_ref[...])
+    for k, sec in enumerate((where_ref[0], 1 - where_ref[0])):
+        mine = pl.ds(pl.multiple_of(sec * 32, 32), 32)
+        for half in range(2):
+            to = pl.ds(half * ROWS + DOWN2 + k, 32, stride=2 * ROWS)
+            d_ref[to, :] = down_ref[mine, half * 128 : (half + 1) * 128]
     row = lax.broadcasted_iota(jnp.int32, (ROWS, 128), 0)
-    for j in range(128):
+    for j in range(64):
         at = pl.ds(j * ROWS, ROWS)
-        out_ref[at, :] = jnp.where(row == DOWN2, d_ref[at, :], pack_ref[at, :]).astype(BF16)
+        both = keep_ref[at, :] + came_ref[at, :].astype(F32)
+        out_ref[at, :] = jnp.where(row >= DOWN2, d_ref[at, :], both).astype(BF16)
 
 
 def last(*args):
     return call(
         last_kernel,
-        [((128 * ROWS, 128), BF16)],
+        [((64 * ROWS, 128), BF16, pltpu.VMEM)],
         *args,
-        scratch=[pltpu.VMEM((12 * T, T), BF16), pltpu.VMEM((T, 1024), F32), pltpu.VMEM((128 * ROWS, 128), F32)],
+        scratch=[
+            pltpu.VMEM((12 * T, T), BF16),
+            pltpu.VMEM((T, 1024), F32),
+            pltpu.VMEM((64 * ROWS, 128), F32),
+            pltpu.VMEM((64, 256), F32),
+            pltpu.VMEM((T, 9 * T), BF16),
+            pltpu.VMEM((CROPS, 2, 1024, T), BF16),
+            pltpu.VMEM((1024, 256), BF16),
+            pltpu.SemaphoreType.DMA((3,)),
+        ],
+        far=(4, 6, 7),
     )[0]
 
 
@@ -412,19 +474,24 @@
     return lax.ppermute(one, "space", near), two
 
 
-def unpack(sums):
+def partner(x):
+    return lax.ppermute(x, "section", [(0, 1), (1, 0)])
+
+
+def unpack(sums, down):
     return (
-        sums[DOWN2],
+        down,
         sums[CONV2:DOWN2].reshape(28, 32)[:27].T.reshape(-1),
         sums[DOWN3:CONV2].reshape(2, 2, 2, 64).transpose(3, 0, 2, 1).reshape(-1),
         sums[:27].T.reshape(-1),
-        sums[HEAD, :4],
+        sums[DOWN2 - 1, 96:100],
     )
 
 
 def finish(pack):
-    terms = lax.all_to_all(pack, ("section", "space"), 0, 0, tiled=True)
-    return unpack(jnp.sum(terms.astype(F32), axis=0))
+    terms = lax.all_to_all(pack, "space", 0, 0, tiled=True)
+    sums = jnp.sum(terms.astype(F32), axis=0)
+    return unpack(sums, sums[DOWN2] + partner(sums[DOWN2 + 1]))
 
 
 def per_device(volume, labels, down_weight_two, w_conv_two, down_weight_three, w_conv_three, w_head):
@@ -444,19 +511,20 @@
 
     vp, a2, one, two = first(where, volume, w1)
     a2_one, a2_two = swapped(one, two)
-    f2, b2, f3, b3, perm, wd, wh, wht = prepare(w2, w3, wd, w_head.T)
+    f2, b2, f3, b3, perm, wd, wh = prepare(w2, w3, wd, w_head.T)
     h2, a3 = second(where, a2_one, a2, a2_two, f2, wd)
     a3_one, a3_two = swapped(a3, a3)
-    gz4, gh = head(where, a3_one, a3, a3_two, f3, wh, wht, marks, scale)
+    gz4, gh = head(where, a3_one, a3, a3_two, f3, wh, marks, scale)
     gz4_one, gz4_two = swapped(gz4, gz4)
     gw3 = weight_three(where, gz4, a3_one, a3, a3_two)
     gz4_one, gz4_two, gw3 = lax.optimization_barrier((gz4_one, gz4_two, gw3))
     gz2, one, two, gd3 = middle(where, gz4_one, gz4, gz4_two, b3, a3, h2, wd)
     gz2_one, gz2_two = swapped(one, two)
     gw2 = weight_two(where, gz2, a2_one, a2, a2_two)
-    pack = packed(gw3, gd3, gw2, gh)
-    pack = last(where, gz2_one, gz2, gz2_two, b2, a2, vp, perm, pack)
-    return finish(pack.reshape(128, ROWS, 128))
+    keep, send = packed(where, gw3, gd3, gw2, gh)
+    came = partner(send)
+    pack = last(where, gz2_one, gz2, gz2_two, b2, a2, vp, perm, keep, came)
+    return finish(pack.reshape(64, ROWS, 128))
 
 
 def solution(mesh):

time: 107 us -> 108 us (level)
  blocking collectives: 48.7 us -> 37.2 us
  local copies, waits for them, and re-layouts: 11 us -> 3.4 us
  waiting for transfers between devices: 3.51 us -> 11 us
  starting transfers between devices: 19.2 us -> 26 us
  Pallas kernels: 23 us -> 28.4 us
    all_to_all x1, blocking collectives: 48.7 us -> 37.2 us  [finish(): terms = lax.all_to_all(pack, 'space', 0, 0, tiled=True)]
    ppermute x4, waiting for transfers between devices: 3.5 us -> 11 us  [swapped(): return (lax.ppermute(one, 'space', near), two)]
    unnamed x43 -> x15, local copies, waits for them, and re-layouts: 7.29 us -> 0.12 us
    ppermute x0 -> x2, starting transfers between devices: none -> 6.75 us  [partner(): return lax.ppermute(x, 'section', [(0, 1), (1, 0)])]
    pallas_call x8, Pallas kernels: 17.2 us -> 21.7 us  [call(): pl.pallas_call(kernel, in_specs=[remote if i in far else scalar if a.dtyp...]
  transfers between devices with their start and end apart: 8 -> 10, of which waited for: 3 -> 4; matrix products, arithmetic and copies ran while one was open for 0% -> 3% of each run, Pallas kernels for 6% -> 4%
where the time goes in v4:
time: 108 us
  blocking collectives  37.2 us (34%)
  Pallas kernels  28.4 us (26%)
  starting transfers between devices  26 us (24%)
  waiting for transfers between devices  11 us (10%)
  local copies, waits for them, and re-layouts  3.4 us (3%)
    all_to_all x1, blocking collectives, finish(): terms = lax.all_to_all(pack, 'space', 0, 0, tiled=True)  37.2 us
    pallas_call x8, Pallas kernels, call(): pl.pallas_call(kernel, in_specs=[remote if i in far else scalar if a.dtyp...  21.7 us
    ppermute x4, starting transfers between devices, swapped(): return (lax.ppermute(one, 'space', near), two)  16.3 us
    ppermute x4, waiting for transfers between devices, swapped(): return (lax.ppermute(one, 'space', near), two)  11 us
    pallas_call x1, Pallas kernels, first(): pl.pallas_call(first_kernel, grid_spec=pltpu.PrefetchScalarGridSpec(num_s...  6.77 us
    ppermute x2, starting transfers between devices, partner(): return lax.ppermute(x, 'section', [(0, 1), (1, 0)])  6.75 us
    ppermute x4, starting transfers between devices, swapped(): two = lax.ppermute(two, 'space', far)  2.97 us
  transfers between devices with their start and end apart: 10, of which 4 were waited for; matrix products, arithmetic and copies ran while one was open for 3% of the time, Pallas kernels for 4%

profile of v4, /device:TPU:1, one launch (start us, length us, event | category | flops | bytes accessed | tf_op | source)
XLA Modules:
  0.0 107.8 jit_solution(8370890325970407199)
XLA Ops:
  0.6 0.0 copy-start
  0.7 0.1 pad_add_fusion.where_ref
  0.7 6.8 %shard_map.110 = (bf16[2,2,1024,256]{3,2,1,0:T(8,128)(2,1)}, bf16[2,2,256,256]{3,2,1,0:T(8,128)(2,1)S(1)}, bf16[2,256,256]{2,1,0:T(8,128)(2,1)S(1)}, bf16[2,256,256]{2,1,0:T(8,128)(2,1)S(1)}) custom-call(s32[2]{0:T(128)S(1)} %pad_add_fusion.where_ref, bf16[4,32,4,8,512]{4,3,2,1,0:T(8,128)(2,1)} %vol_ref.1, bf16[256,64]{1,0:T(8,128)(2,1)} %bitcast.41), custom_call_target="tpu_custom_call" | custom-call | tf_op jit(solution)/shard_map/pallas_call | solution.py:121
  7.5 2.0 %collective-permute-start = (bf16[2,256,256]{2,1,0:T(8,128)(2,1)S(1)}, bf16[2,256,256]{2,1,0:T(8,128)(2,1)S(1)}, u32[]{:S(2)}, u32[]{:S(2)}) collective-permute-start(bf16[2,256,256]{2,1,0:T(8,128)(2,1)S(1)} %get-tuple-element.29), channel_id=1, source_target_pairs={{0,1},{1,0},{2,3},{3,2},{4,5},{5,4},{6,7},{7,6},{8,9},{9,8},{10,11... | collective-permute-start | bytes 786440 | tf_op jit(solution)/shard_map/ppermute | solution.py:474
  9.5 0.7 collective-permute-start.1
  10.2 0.2 pad_maximum_fusion.w2_ref
  10.5 0.0 copy-done.4
  10.5 0.0 copy-done.5
  10.5 0.0 copy-done.2
  10.5 2.9 %shard_map.111 = (bf16[256,2304]{1,0:T(8,128)(2,1)S(1)}, bf16[256,2304]{1,0:T(8,128)(2,1)}, bf16[256,2304]{1,0:T(8,128)(2,1)}, bf16[256,2304]{1,0:T(8,128)(2,1)}...) custom-call(bf16[27,64,128]{2,1,0:T(8,128)(2,1)S(1)} %pad_maximum_fusion.w2_ref, ...), custom_call_target="tpu_custom_call" | custom-call | tf_op jit(solution)/shard_map/pallas_call | solution.py:72
  13.4 1.6 %collective-permute-done.one_ref = bf16[2,256,256]{2,1,0:T(8,128)(2,1)S(1)} collective-permute-done((bf16[2,256,256]{2,1,0:T(8,128)(2,1)S(1)}, bf16[2,256,256]{2,1,0:T(8,128)(2,1)S(1)}, u32[]{:S(2)}, u32[]{:S(2)}) %collective-permute-start) | collective-permute-done | bytes 262176 | tf_op jit(solution)/shard_map/ppermute | solution.py:474
  15.0 0.0 collective-permute-done.1.two_ref
  15.0 3.6 %shard_map.112 = (bf16[4,256,256]{2,1,0:T(8,128)(2,1)}, bf16[256,256]{1,0:T(8,128)(2,1)S(1)}) custom-call(s32[2]{0:T(128)S(1)} %pad_add_fusion.where_ref, bf16[2,256,256]{2,1,0:T(8,128)(2,1)S(1)} %collective-permute-done.one_ref, bf16[2,2,256,256]{3,2,1,0:T(8,128)(2,1)S(1)} %get-tuple-element.30.a_ref, ...), custom_call_target="tpu_custom_call" | custom-call | tf_op jit(solution)/shard_map/pallas_call | solution.py:72
  18.6 0.7 collective-permute-start.3
  19.3 6.7 %collective-permute-start.2 = (bf16[256,256]{1,0:T(8,128)(2,1)S(1)}, bf16[256,256]{1,0:T(8,128)(2,1)S(1)}, u32[]{:S(2)}, u32[]{:S(2)}) collective-permute-start(bf16[256,256]{1,0:T(8,128)(2,1)S(1)} %get-tuple-element.34.a_ref.a3_ref), channel_id=1, source_target_pairs={{0,1},{1,0},{2,3},{3,2},{4,5},{5,4},{6,7},{7,6},{8,9},{9,8},{10,11... | collective-permute-start | bytes 393224 | tf_op jit(solution)/shard_map/ppermute | solution.py:474
  26.0 0.0 collective-permute-done.3.two_ref
  26.0 2.4 %collective-permute-done.2.one_ref = bf16[256,256]{1,0:T(8,128)(2,1)S(1)} collective-permute-done((bf16[256,256]{1,0:T(8,128)(2,1)S(1)}, bf16[256,256]{1,0:T(8,128)(2,1)S(1)}, u32[]{:S(2)}, u32[]{:S(2)}) %collective-permute-start.2) | collective-permute-done | bytes 131104 | tf_op jit(solution)/shard_map/ppermute | solution.py:474
  28.4 3.1 %shard_map.113 = (bf16[256,256]{1,0:T(8,128)(2,1)S(1)}, f32[128,128]{1,0:T(8,128)S(1)}) custom-call(s32[2]{0:T(128)S(1)} %pad_add_fusion.where_ref, bf16[256,256]{1,0:T(8,128)(2,1)S(1)} %collective-permute-done.2.one_ref, bf16[256,256]{1,0:T(8,128)(2,1)S(1)} %get-tuple-element.34.a_ref.a3_ref, bf16[256,256]{1,0:T(8,128)(2,1)S(1)} %collective-permute-done.3.two_ref, ...), custom_call_target="tpu_custom_call" | custom-call | tf_op jit(solution)/shard_map/pallas_call | solution.py:72
  31.5 0.8 collective-permute-start.5
  32.3 5.8 %collective-permute-start.4 = (bf16[256,256]{1,0:T(8,128)(2,1)S(1)}, bf16[256,256]{1,0:T(8,128)(2,1)S(1)}, u32[]{:S(2)}, u32[]{:S(2)}) collective-permute-start(bf16[256,256]{1,0:T(8,128)(2,1)S(1)} %get-tuple-element.37.g_ref), channel_id=1, source_target_pairs={{0,1},{1,0},{2,3},{3,2},{4,5},{5,4},{6,7},{7,6},{8,9},{9,8},{10,11... | collective-permute-start | bytes 393224 | tf_op jit(solution)/shard_map/ppermute | solution.py:474
  38.1 1.1 shard_map.114.w3_ref
  39.2 0.0 collective-permute-done.5.two_ref
  39.2 1.3 %collective-permute-done.4.one_ref = bf16[256,256]{1,0:T(8,128)(2,1)S(1)} collective-permute-done((bf16[256,256]{1,0:T(8,128)(2,1)S(1)}, bf16[256,256]{1,0:T(8,128)(2,1)S(1)}, u32[]{:S(2)}, u32[]{:S(2)}) %collective-permute-start.4) | collective-permute-done | bytes 131104 | tf_op jit(solution)/shard_map/ppermute | solution.py:474
  40.5 0.0 copy-done.3
  40.5 2.1 %shard_map.115 = (bf16[2,2,256,256]{3,2,1,0:T(8,128)(2,1)S(1)}, bf16[2,256,256]{2,1,0:T(8,128)(2,1)S(1)}, bf16[2,256,256]{2,1,0:T(8,128)(2,1)S(1)}, f32[4,128,128]{2,1,0:T(8,128)S(1)}) custom-call(s32[2]{0:T(128)S(1)} %pad_add_fusion.where_ref, bf16[256,256]{1,0:T(8,128)(2,1)S(1)} %collective-permute-done.4.one_ref, ...), custom_call_target="tpu_custom_call" | custom-call | tf_op jit(solution)/shard_map/pallas_call | solution.py:72
  42.6 2.3 %shard_map.116.w2_ref = f32[7,2,64,128]{3,2,1,0:T(8,128)S(1)} custom-call(s32[2]{0:T(128)S(1)} %pad_add_fusion.where_ref, bf16[2,2,256,256]{3,2,1,0:T(8,128)(2,1)S(1)} %get-tuple-element.43.g_ref, bf16[2,256,256]{2,1,0:T(8,128)(2,1)S(1)} %collective-permute-done.one_ref, bf16[2,2,256,256]{3,2,1,0:T(8,128)(2,1)S(1)} %get-tuple-element.30.a_ref, ...), custom_call_target="tpu_custom_call" | custom-call | tf_op jit(solution)/shard_map/pallas_call | solution.py:72
  44.9 1.5 %shard_map.117 = (f32[2560,128]{1,0:T(8,128)S(1)}, bf16[2560,128]{1,0:T(8,128)(2,1)S(1)}) custom-call(s32[2]{0:T(128)S(1)} %pad_add_fusion.where_ref, f32[27,128,128]{2,1,0:T(8,128)S(1)} %shard_map.114.w3_ref, f32[4,128,128]{2,1,0:T(8,128)S(1)} %get-tuple-element.49.d3_ref, f32[7,2,64,128]{3,2,1,0:T(8,128)S(1)} %shard_map.116.w2_ref, ...), custom_call_target="tpu_custom_call" | custom-call | tf_op jit(solution)/shard_map/pallas_call | solution.py:72
  46.4 4.3 %collective-permute-start.8 = (bf16[2560,128]{1,0:T(8,128)(2,1)S(1)}, bf16[2560,128]{1,0:T(8,128)(2,1)S(1)}, u32[]{:S(2)}, u32[]{:S(2)}) collective-permute-start(bf16[2560,128]{1,0:T(8,128)(2,1)S(1)} %get-tuple-element.52), channel_id=1, source_target_pairs={{0,64},{64,0},{1,65},{65,1},{2,66},{66,2},{3,67},{67,3},{4,68},{68... | collective-permute-start | bytes 1966088 | tf_op jit(solution)/shard_map/ppermute | solution.py:478
  50.6 1.8 %collective-permute-start.6 = (bf16[2,256,256]{2,1,0:T(8,128)(2,1)S(1)}, bf16[2,256,256]{2,1,0:T(8,128)(2,1)S(1)}, u32[]{:S(2)}, u32[]{:S(2)}) collective-permute-start(bf16[2,256,256]{2,1,0:T(8,128)(2,1)S(1)} %get-tuple-element.42), channel_id=1, source_target_pairs={{0,1},{1,0},{2,3},{3,2},{4,5},{5,4},{6,7},{7,6},{8,9},{9,8},{10,11... | collective-permute-start | bytes 786440 | tf_op jit(solution)/shard_map/ppermute | solution.py:474
  52.4 0.8 collective-permute-start.7
  53.2 5.7 %collective-permute-done.6.one_ref = bf16[2,256,256]{2,1,0:T(8,128)(2,1)S(1)} collective-permute-done((bf16[2,256,256]{2,1,0:T(8,128)(2,1)S(1)}, bf16[2,256,256]{2,1,0:T(8,128)(2,1)S(1)}, u32[]{:S(2)}, u32[]{:S(2)}) %collective-permute-start.6) | collective-permute-done | bytes 262176 | tf_op jit(solution)/shard_map/ppermute | solution.py:474
  59.0 0.0 collective-permute-done.7.two_ref
  59.0 0.0 collective-permute-done.8.came_ref
  59.0 5.1 %shard_map.118 = bf16[2560,128]{1,0:T(8,128)(2,1)S(1)} custom-call(s32[2]{0:T(128)S(1)} %pad_add_fusion.where_ref, bf16[2,256,256]{2,1,0:T(8,128)(2,1)S(1)} %collective-permute-done.6.one_ref, bf16[2,2,256,256]{3,2,1,0:T(8,128)(2,1)S(1)} %get-tuple-element.43.g_ref, bf16[2,256,256]{2,1,0:T(8,128)(2,1)S(1)} %collective-permute-done.7.two_ref, ...), custom_call_target="tpu_custom_call" | custom-call | tf_op jit(solution)/shard_map/pallas_call | solution.py:72
  64.1 37.2 %all_to_all.5 = bf16[64,40,128]{2,1,0:T(8,128)(2,1)S(1)} all-to-all(bf16[64,40,128]{2,1,0:T(8,128)(2,1)S(1)} %bitcast.35), channel_id=1, replica_groups=mesh['section'=2,'space'=64] {'space'}, dimensions={0} | all-to-all | bytes 1310720 | tf_op jit(solution)/shard_map/all_to_all | solution.py:492
  101.3 0.1 convert_reduce_fusion
  101.4 0.6 slice_bitcast_fusion.1
  102.0 0.1 reshape.52
  102.1 2.5 %collective-permute-start.9 = (f32[128]{0:T(128)S(1)}, f32[128]{0:T(128)S(1)}, u32[]{:S(2)}, u32[]{:S(2)}) collective-permute-start(f32[128]{0:T(128)S(1)} %slice_bitcast_fusion.2), channel_id=1, source_target_pairs={{0,64},{64,0},{1,65},{65,1},{2,66},{66,2},{3,67},{67,3},{4,68},{68... | collective-permute-start | bytes 1544 | tf_op jit(solution)/shard_map/ppermute | solution.py:478
  104.6 0.1 reshape.50
  104.6 0.1 copy.15
  104.7 0.7 reshape.51
  105.4 0.1 copy.14
  105.5 0.8 reshape.54
  106.3 0.2 copy.13
  106.5 0.8 reshape.53
  107.3 0.0 collective-permute-done.9
  107.3 0.5 fusion
  (14 shorter events, 0.0 us)
Async XLA Ops:
  0.6 25.4 %copy-start = (s32[4,1,2,128]{3,2,1,0:T(2,128)S(1)}, s32[4,1,2,128]{3,2,1,0:T(2,128)}, u32[]{:S(2)}) copy-start(s32[4,1,2,128]{3,2,1,0:T(2,128)} %param.8) | copy-start | bytes 12292
  0.7 9.5 %copy-start.6 = (bf16[64,64,3,3,3]{1,0,4,3,2:T(8,128)(2,1)S(1)}, bf16[64,64,3,3,3]{1,0,4,3,2:T(8,128)(2,1)}, u32[]{:S(2)}) copy-start(bf16[64,64,3,3,3]{1,0,4,3,2:T(8,128)(2,1)} %param.10) | copy-start | bytes 663556
  0.7 9.7 %copy-start.4 = (bf16[128,64,2,2,2]{0,4,3,2,1:T(2,128)(2,1)S(1)}, bf16[128,64,2,2,2]{0,4,3,2,1:T(2,128)(2,1)}, u32[]{:S(2)}) copy-start(bf16[128,64,2,2,2]{0,4,3,2,1:T(2,128)(2,1)} %param.11) | copy-start | bytes 393220
  0.7 9.8 %copy-start.5 = (bf16[128,4]{0,1:T(4,128)(2,1)S(1)}, bf16[128,4]{0,1:T(4,128)(2,1)}, u32[]{:S(2)}) copy-start(bf16[128,4]{0,1:T(4,128)(2,1)} %param.13) | copy-start | bytes 3076
  7.5 3.0 %copy-start.2 = (bf16[128,128,3,3,3]{1,0,4,3,2:T(8,128)(2,1)S(1)}, bf16[128,128,3,3,3]{1,0,4,3,2:T(8,128)(2,1)}, u32[]{:S(2)}) copy-start(bf16[128,128,3,3,3]{1,0,4,3,2:T(8,128)(2,1)} %param.12) | copy-start | bytes 2654212
  7.5 7.5 %collective-permute-start = (bf16[2,256,256]{2,1,0:T(8,128)(2,1)S(1)}, bf16[2,256,256]{2,1,0:T(8,128)(2,1)S(1)}, u32[]{:S(2)}, u32[]{:S(2)}) collective-permute-start(bf16[2,256,256]{2,1,0:T(8,128)(2,1)S(1)} %get-tuple-element.29), channel_id=1, source_target_pairs={{0,1},{1,0},{2,3},{3,2},{4,5},{5,4},{6,7},{7,6},{8,9},{9,8},{10,11... | collective-permute-start | bytes 786440 | tf_op jit(solution)/shard_map/ppermute | solution.py:474
  9.5 5.5 %collective-permute-start.1 = (bf16[2,256,256]{2,1,0:T(8,128)(2,1)S(1)}, bf16[2,256,256]{2,1,0:T(8,128)(2,1)S(1)}, u32[]{:S(2)}, u32[]{:S(2)}) collective-permute-start(bf16[2,256,256]{2,1,0:T(8,128)(2,1)S(1)} %get-tuple-element.31), channel_id=1, source_target_pairs={{1,2},{2,1},{3,4},{4,3},{5,6},{6,5},{7,8},{8,7},{9,10},{10,9},{11,... | collective-permute-start | bytes 786440 | tf_op jit(solution)/shard_map/ppermute | solution.py:473
  18.6 7.4 %collective-permute-start.3 = (bf16[256,256]{1,0:T(8,128)(2,1)S(1)}, bf16[256,256]{1,0:T(8,128)(2,1)S(1)}, u32[]{:S(2)}, u32[]{:S(2)}) collective-permute-start(bf16[256,256]{1,0:T(8,128)(2,1)S(1)} %get-tuple-element.34.a_ref.a3_ref), channel_id=1, source_target_pairs={{1,2},{2,1},{3,4},{4,3},{5,6},{6,5},{7,8},{8,7},{9,10},{10,9},{11,... | collective-permute-start | bytes 393224 | tf_op jit(solution)/shard_map/ppermute | solution.py:473
  19.3 9.1 %collective-permute-start.2 = (bf16[256,256]{1,0:T(8,128)(2,1)S(1)}, bf16[256,256]{1,0:T(8,128)(2,1)S(1)}, u32[]{:S(2)}, u32[]{:S(2)}) collective-permute-start(bf16[256,256]{1,0:T(8,128)(2,1)S(1)} %get-tuple-element.34.a_ref.a3_ref), channel_id=1, source_target_pairs={{0,1},{1,0},{2,3},{3,2},{4,5},{5,4},{6,7},{7,6},{8,9},{9,8},{10,11... | collective-permute-start | bytes 393224 | tf_op jit(solution)/shard_map/ppermute | solution.py:474
  31.5 9.0 %copy-start.1 = (bf16[256,2304]{1,0:T(8,128)(2,1)S(1)}, bf16[256,2304]{1,0:T(8,128)(2,1)}, u32[]{:S(2)}) copy-start(bf16[256,2304]{1,0:T(8,128)(2,1)} %get-tuple-element.40.b3_ref) | copy-start | bytes 3538948
  31.5 9.0 %copy-start.3 = (bf16[4,256,256]{2,1,0:T(8,128)(2,1)S(1)}, bf16[4,256,256]{2,1,0:T(8,128)(2,1)}, u32[]{:S(2)}) copy-start(bf16[4,256,256]{2,1,0:T(8,128)(2,1)} %get-tuple-element.41.h_ref) | copy-start | bytes 1572868
  31.5 7.7 %collective-permute-start.5 = (bf16[256,256]{1,0:T(8,128)(2,1)S(1)}, bf16[256,256]{1,0:T(8,128)(2,1)S(1)}, u32[]{:S(2)}, u32[]{:S(2)}) collective-permute-start(bf16[256,256]{1,0:T(8,128)(2,1)S(1)} %get-tuple-element.37.g_ref), channel_id=1, source_target_pairs={{1,2},{2,1},{3,4},{4,3},{5,6},{6,5},{7,8},{8,7},{9,10},{10,9},{11,... | collective-permute-start | bytes 393224 | tf_op jit(solution)/shard_map/ppermute | solution.py:473
  32.3 8.2 %collective-permute-start.4 = (bf16[256,256]{1,0:T(8,128)(2,1)S(1)}, bf16[256,256]{1,0:T(8,128)(2,1)S(1)}, u32[]{:S(2)}, u32[]{:S(2)}) collective-permute-start(bf16[256,256]{1,0:T(8,128)(2,1)S(1)} %get-tuple-element.37.g_ref), channel_id=1, source_target_pairs={{0,1},{1,0},{2,3},{3,2},{4,5},{5,4},{6,7},{7,6},{8,9},{9,8},{10,11... | collective-permute-start | bytes 393224 | tf_op jit(solution)/shard_map/ppermute | solution.py:474
  46.4 12.6 %collective-permute-start.8 = (bf16[2560,128]{1,0:T(8,128)(2,1)S(1)}, bf16[2560,128]{1,0:T(8,128)(2,1)S(1)}, u32[]{:S(2)}, u32[]{:S(2)}) collective-permute-start(bf16[2560,128]{1,0:T(8,128)(2,1)S(1)} %get-tuple-element.52), channel_id=1, source_target_pairs={{0,64},{64,0},{1,65},{65,1},{2,66},{66,2},{3,67},{67,3},{4,68},{68... | collective-permute-start | bytes 1966088 | tf_op jit(solution)/shard_map/ppermute | solution.py:478
  50.6 8.3 %collective-permute-start.6 = (bf16[2,256,256]{2,1,0:T(8,128)(2,1)S(1)}, bf16[2,256,256]{2,1,0:T(8,128)(2,1)S(1)}, u32[]{:S(2)}, u32[]{:S(2)}) collective-permute-start(bf16[2,256,256]{2,1,0:T(8,128)(2,1)S(1)} %get-tuple-element.42), channel_id=1, source_target_pairs={{0,1},{1,0},{2,3},{3,2},{4,5},{5,4},{6,7},{7,6},{8,9},{9,8},{10,11... | collective-permute-start | bytes 786440 | tf_op jit(solution)/shard_map/ppermute | solution.py:474
  52.4 6.6 %collective-permute-start.7 = (bf16[2,256,256]{2,1,0:T(8,128)(2,1)S(1)}, bf16[2,256,256]{2,1,0:T(8,128)(2,1)S(1)}, u32[]{:S(2)}, u32[]{:S(2)}) collective-permute-start(bf16[2,256,256]{2,1,0:T(8,128)(2,1)S(1)} %get-tuple-element.44), channel_id=1, source_target_pairs={{1,2},{2,1},{3,4},{4,3},{5,6},{6,5},{7,8},{8,7},{9,10},{10,9},{11,... | collective-permute-start | bytes 786440 | tf_op jit(solution)/shard_map/ppermute | solution.py:473
  102.1 5.2 %collective-permute-start.9 = (f32[128]{0:T(128)S(1)}, f32[128]{0:T(128)S(1)}, u32[]{:S(2)}, u32[]{:S(2)}) collective-permute-start(f32[128]{0:T(128)S(1)} %slice_bitcast_fusion.2), channel_id=1, source_target_pairs={{0,64},{64,0},{1,65},{65,1},{2,66},{66,2},{3,67},{67,3},{4,68},{68... | collective-permute-start | bytes 1544 | tf_op jit(solution)/shard_map/ppermute | solution.py:478

commit v5 on v4

--- a/solution.py
+++ b/solution.py
@@ -136,7 +136,7 @@
             scratch_shapes=[pltpu.VMEM((512, 512), BF16), pltpu.VMEM((256, 1024), BF16)],
         ),
         out_shape=[
-            pltpu.HBM((CROPS, 2, 1024, 256), BF16),
+            pltpu.VMEM((CROPS, 2, 1024, 256), BF16),
             pltpu.VMEM((CROPS, 2, 256, 256), BF16),
             pltpu.VMEM((CROPS, 256, 256), BF16),
             pltpu.VMEM((CROPS, 256, 256), BF16),
@@ -196,8 +196,8 @@
 
     return call(
         prepare_kernel,
-        [wide(pltpu.VMEM), wide(pltpu.HBM), wide(pltpu.HBM), wide(pltpu.HBM)]
-        + [((1024, 256), BF16, pltpu.HBM), ((4, T, T), BF16, pltpu.VMEM), ((256, 128), BF16, pltpu.HBM)],
+        [wide(pltpu.VMEM), wide(pltpu.VMEM), wide(pltpu.HBM), wide(pltpu.VMEM)]
+        + [((1024, 256), BF16, pltpu.VMEM), ((4, T, T), BF16, pltpu.VMEM), ((256, 128), BF16, pltpu.HBM)],
         w2, w3, wd, wh,
         scratch=[pltpu.VMEM((512, 128), F32)],
     )
@@ -397,32 +397,20 @@
     )
 
 
-def last_kernel(
-    where_ref, one_ref, g_ref, two_ref, b2_far, a_ref, vp_far, perm_far, keep_ref, came_ref, out_ref, b_ref, t_ref, d_ref,
-    down_ref, b2_ref, vp_ref, perm_ref, sems
-):
-    fetches = [
-        pltpu.make_async_copy(far, ref, sems.at[i])
-        for i, (far, ref) in enumerate(((b2_far, b2_ref), (vp_far, vp_ref), (perm_far, perm_ref)))
-    ]
-    for fetch in fetches:
-        fetch.start()
+def last_kernel(where_ref, one_ref, g_ref, two_ref, b2_ref, a_ref, vp_ref, perm_ref, down_ref, b_ref, t_ref):
     for n in range(CROPS):
         lo, hi = sorted_out(where_ref, one_ref[n], two_ref[n])
         planes = (lo, g_ref[n, 0], g_ref[n, 1], hi)
         for k, plane in enumerate(planes):
             put_three(b_ref, k * 3 * T, three_two(plane))
-        for d in range(2):
-            if n + d == 0:
-                fetches[0].wait()
-            gy = (dot(b2_ref[...], b_ref[pl.ds(d * 3 * T, 9 * T), :]) * slope(a_ref[n, d])).astype(BF16)
-            if n + d == 0:
-                fetches[1].wait()
-            t = dot_nt(gy, vp_ref[n, d])
-            if n + d == 0:
-                t_ref[...] = t
-            else:
-                t_ref[...] += t
+        gy = [
+            (dot(b2_ref[...], b_ref[pl.ds(d * 3 * T, 9 * T), :]) * slope(a_ref[n, d])).astype(BF16) for d in range(2)
+        ]
+        t = dot_nt(gy[0], vp_ref[n, 0]) + dot_nt(gy[1], vp_ref[n, 1])
+        if n == 0:
+            t_ref[...] = t
+        else:
+            t_ref[...] += t
     pairs = []
     lane = lax.broadcasted_iota(jnp.int32, (64, 128), 1)
     for tile in range(8):
@@ -433,8 +421,19 @@
         x = x + pltpu.roll(x, 126, 1)
         x = x + pltpu.roll(x, 124, 1)
         pairs.append(x.astype(BF16))
-    fetches[2].wait()
     down_ref[...] = dot(jnp.concatenate(pairs, axis=1), perm_ref[...])
+
+
+def last(*args):
+    return call(
+        last_kernel,
+        [((64, 256), F32, pltpu.VMEM)],
+        *args,
+        scratch=[pltpu.VMEM((12 * T, T), BF16), pltpu.VMEM((T, 1024), F32)],
+    )[0]
+
+
+def join_kernel(where_ref, down_ref, keep_ref, came_ref, out_ref, d_ref):
     for k, sec in enumerate((where_ref[0], 1 - where_ref[0])):
         mine = pl.ds(pl.multiple_of(sec * 32, 32), 32)
         for half in range(2):
@@ -447,22 +446,12 @@
         out_ref[at, :] = jnp.where(row >= DOWN2, d_ref[at, :], both).astype(BF16)
 
 
-def last(*args):
-    return call(
-        last_kernel,
+def joined(*args):
+    return call(
+        join_kernel,
         [((64 * ROWS, 128), BF16, pltpu.VMEM)],
         *args,
-        scratch=[
-            pltpu.VMEM((12 * T, T), BF16),
-            pltpu.VMEM((T, 1024), F32),
-            pltpu.VMEM((64 * ROWS, 128), F32),
-            pltpu.VMEM((64, 256), F32),
-            pltpu.VMEM((T, 9 * T), BF16),
-            pltpu.VMEM((CROPS, 2, 1024, T), BF16),
-            pltpu.VMEM((1024, 256), BF16),
-            pltpu.SemaphoreType.DMA((3,)),
-        ],
-        far=(4, 6, 7),
+        scratch=[pltpu.VMEM((64 * ROWS, 128), F32)],
     )[0]
 
 
@@ -522,8 +511,10 @@
     gz2_one, gz2_two = swapped(one, two)
     gw2 = weight_two(where, gz2, a2_one, a2, a2_two)
     keep, send = packed(where, gw3, gd3, gw2, gh)
+    gz2_one, gz2_two, send = lax.optimization_barrier((gz2_one, gz2_two, send))
     came = partner(send)
-    pack = last(where, gz2_one, gz2, gz2_two, b2, a2, vp, perm, keep, came)
+    down = last(where, gz2_one, gz2, gz2_two, b2, a2, vp, perm)
+    pack = joined(where, down, keep, came)
     return finish(pack.reshape(64, ROWS, 128))
 
 

time: 108 us -> 102 us (0.944)
  waiting for transfers between devices: 11 us -> 4.65 us
  Pallas kernels: 28.4 us -> 26.6 us
  blocking collectives: 37.2 us -> 38.3 us
    ppermute x4, waiting for transfers between devices: 11 us -> 4.63 us  [swapped(): return (lax.ppermute(one, 'space', near), two)]
    all_to_all x1, blocking collectives: 37.2 us -> 38.3 us  [finish(): terms = lax.all_to_all(pack, 'space', 0, 0, tiled=True)]
    pallas_call x8 -> x9, Pallas kernels: 21.7 us -> 20.8 us  [call(): pl.pallas_call(kernel, in_specs=[remote if i in far else scalar if a.dtyp...]
  transfers between devices with their start and end apart: 10 -> 10, of which waited for: 4 -> 3; matrix products, arithmetic and copies ran while one was open for 3% -> 3% of each run, Pallas kernels for 4% -> 11%
where the time goes in v5:
time: 102 us; the launch traced here: 101 us
  blocking collectives  38.3 us (38%)
  Pallas kernels  26.6 us (26%)
  starting transfers between devices  25.5 us (25%)
  waiting for transfers between devices  4.65 us (5%)
  local copies, waits for them, and re-layouts  4.47 us (4%)
    all_to_all x1, blocking collectives, finish(): terms = lax.all_to_all(pack, 'space', 0, 0, tiled=True)  38.3 us
    pallas_call x9, Pallas kernels, call(): pl.pallas_call(kernel, in_specs=[remote if i in far else scalar if a.dtyp...  20.8 us
    ppermute x4, starting transfers between devices, swapped(): return (lax.ppermute(one, 'space', near), two)  15.5 us
    ppermute x2, starting transfers between devices, partner(): return lax.ppermute(x, 'section', [(0, 1), (1, 0)])  6.51 us
    pallas_call x1, Pallas kernels, first(): pl.pallas_call(first_kernel, grid_spec=pltpu.PrefetchScalarGridSpec(num_s...  5.78 us
    ppermute x4, waiting for transfers between devices, swapped(): return (lax.ppermute(one, 'space', near), two)  4.63 us
    ppermute x4, starting transfers between devices, swapped(): two = lax.ppermute(two, 'space', far)  3.45 us
  transfers between devices with their start and end apart: 10, of which 3 were waited for; matrix products, arithmetic and copies ran while one was open for 3% of the time, Pallas kernels for 11%

profile of v5, /device:TPU:1, one launch (start us, length us, event | category | flops | bytes accessed | tf_op | source)
XLA Modules:
  0.0 101.3 jit_solution(4983930353526859685)
XLA Ops:
  0.6 0.0 copy-start
  0.7 0.1 pad_add_fusion.where_ref
  0.7 5.8 %shard_map.110 = (bf16[2,2,1024,256]{3,2,1,0:T(8,128)(2,1)S(1)}, bf16[2,2,256,256]{3,2,1,0:T(8,128)(2,1)S(1)}, bf16[2,256,256]{2,1,0:T(8,128)(2,1)S(1)}, bf16[2,256,256]{2,1,0:T(8,128)(2,1)S(1)}) custom-call(s32[2]{0:T(128)S(1)} %pad_add_fusion.where_ref, bf16[4,32,4,8,512]{4,3,2,1,0:T(8,128)(2,1)} %vol_ref.1, bf16[256,64]{1,0:T(8,128)(2,1)} %bitcast.41), custom_call_target="tpu_custom_call" | custom-call | tf_op jit(solution)/shard_map/pallas_call | solution.py:121
  6.5 0.0 copy-start.7
  6.5 2.1 %collective-permute-start = (bf16[2,256,256]{2,1,0:T(8,128)(2,1)S(1)}, bf16[2,256,256]{2,1,0:T(8,128)(2,1)S(1)}, u32[]{:S(2)}, u32[]{:S(2)}) collective-permute-start(bf16[2,256,256]{2,1,0:T(8,128)(2,1)S(1)} %get-tuple-element.32), channel_id=1, source_target_pairs={{0,1},{1,0},{2,3},{3,2},{4,5},{5,4},{6,7},{7,6},{8,9},{9,8},{10,11... | collective-permute-start | bytes 786440 | tf_op jit(solution)/shard_map/ppermute | solution.py:463
  8.7 0.7 collective-permute-start.1
  9.3 0.2 pad_maximum_fusion.w2_ref
  9.6 2.2 %shard_map.111 = (bf16[256,2304]{1,0:T(8,128)(2,1)S(1)}, bf16[256,2304]{1,0:T(8,128)(2,1)S(1)}, bf16[256,2304]{1,0:T(8,128)(2,1)}, bf16[256,2304]{1,0:T(8,128)(2...) custom-call(bf16[27,64,128]{2,1,0:T(8,128)(2,1)S(1)} %pad_maximum_fusion.w2_ref, ...), custom_call_target="tpu_custom_call" | custom-call | tf_op jit(solution)/shard_map/pallas_call | solution.py:72
  11.8 1.0 %copy-done.3 = bf16[256,2304]{1,0:T(8,128)(2,1)} copy-done((bf16[256,2304]{1,0:T(8,128)(2,1)}, bf16[256,2304]{1,0:T(8,128)(2,1)S(1)}, u32[]{:S(2)}) %copy-start.3) | copy-done | bytes 1179672
  12.8 1.3 %collective-permute-done.one_ref = bf16[2,256,256]{2,1,0:T(8,128)(2,1)S(1)} collective-permute-done((bf16[2,256,256]{2,1,0:T(8,128)(2,1)S(1)}, bf16[2,256,256]{2,1,0:T(8,128)(2,1)S(1)}, u32[]{:S(2)}, u32[]{:S(2)}) %collective-permute-start) | collective-permute-done | bytes 262176 | tf_op jit(solution)/shard_map/ppermute | solution.py:463
  14.2 0.0 collective-permute-done.1.two_ref
  14.2 3.6 %shard_map.112 = (bf16[4,256,256]{2,1,0:T(8,128)(2,1)}, bf16[256,256]{1,0:T(8,128)(2,1)S(1)}) custom-call(s32[2]{0:T(128)S(1)} %pad_add_fusion.where_ref, bf16[2,256,256]{2,1,0:T(8,128)(2,1)S(1)} %collective-permute-done.one_ref, bf16[2,2,256,256]{3,2,1,0:T(8,128)(2,1)S(1)} %get-tuple-element.33.a_ref, ...), custom_call_target="tpu_custom_call" | custom-call | tf_op jit(solution)/shard_map/pallas_call | solution.py:72
  17.8 0.0 copy-done.5
  17.8 1.3 %collective-permute-start.3 = (bf16[256,256]{1,0:T(8,128)(2,1)S(1)}, bf16[256,256]{1,0:T(8,128)(2,1)}, u32[]{:S(2)}, u32[]{:S(2)}) collective-permute-start(bf16[256,256]{1,0:T(8,128)(2,1)S(1)} %get-tuple-element.37.a_ref.a3_ref), channel_id=1, source_target_pairs={{1,2},{2,1},{3,4},{4,3},{5,6},{6,5},{7,8},{8,7},{9,10},{10,9},{11,... | collective-permute-start | bytes 393224 | tf_op jit(solution)/shard_map/ppermute | solution.py:462
  19.1 6.0 %collective-permute-start.2 = (bf16[256,256]{1,0:T(8,128)(2,1)S(1)}, bf16[256,256]{1,0:T(8,128)(2,1)}, u32[]{:S(2)}, u32[]{:S(2)}) collective-permute-start(bf16[256,256]{1,0:T(8,128)(2,1)S(1)} %get-tuple-element.37.a_ref.a3_ref), channel_id=1, source_target_pairs={{0,1},{1,0},{2,3},{3,2},{4,5},{5,4},{6,7},{7,6},{8,9},{9,8},{10,11... | collective-permute-start | bytes 393224 | tf_op jit(solution)/shard_map/ppermute | solution.py:463
  25.1 0.0 collective-permute-done.3.two_ref
  25.1 2.5 %collective-permute-done.2.one_ref = bf16[256,256]{1,0:T(8,128)(2,1)} collective-permute-done((bf16[256,256]{1,0:T(8,128)(2,1)S(1)}, bf16[256,256]{1,0:T(8,128)(2,1)}, u32[]{:S(2)}, u32[]{:S(2)}) %collective-permute-start.2) | collective-permute-done | bytes 131104 | tf_op jit(solution)/shard_map/ppermute | solution.py:463
  27.6 3.6 %shard_map.113 = (bf16[256,256]{1,0:T(8,128)(2,1)S(1)}, f32[128,128]{1,0:T(8,128)S(1)}) custom-call(s32[2]{0:T(128)S(1)} %pad_add_fusion.where_ref, bf16[256,256]{1,0:T(8,128)(2,1)} %collective-permute-done.2.one_ref, bf16[256,256]{1,0:T(8,128)(2,1)S(1)} %get-tuple-element.37.a_ref.a3_ref, bf16[256,256]{1,0:T(8,128)(2,1)} %collective-permute-done.3.two_ref, ...), custom_call_target="tpu_custom_call" | custom-call | tf_op jit(solution)/shard_map/pallas_call | solution.py:72
  31.2 0.8 collective-permute-start.5
  32.0 5.9 %collective-permute-start.4 = (bf16[256,256]{1,0:T(8,128)(2,1)S(1)}, bf16[256,256]{1,0:T(8,128)(2,1)S(1)}, u32[]{:S(2)}, u32[]{:S(2)}) collective-permute-start(bf16[256,256]{1,0:T(8,128)(2,1)S(1)} %get-tuple-element.40.g_ref), channel_id=1, source_target_pairs={{0,1},{1,0},{2,3},{3,2},{4,5},{5,4},{6,7},{7,6},{8,9},{9,8},{10,11... | collective-permute-start | bytes 393224 | tf_op jit(solution)/shard_map/ppermute | solution.py:463
  37.9 1.5 %shard_map.114.w3_ref = f32[27,128,128]{2,1,0:T(8,128)S(1)} custom-call(s32[2]{0:T(128)S(1)} %pad_add_fusion.where_ref, bf16[256,256]{1,0:T(8,128)(2,1)S(1)} %get-tuple-element.40.g_ref, bf16[256,256]{1,0:T(8,128)(2,1)} %collective-permute-done.2.one_ref, bf16[256,256]{1,0:T(8,128)(2,1)S(1)} %get-tuple-element.37.a_ref.a3_ref, ...), custom_call_target="tpu_custom_call" | custom-call | tf_op jit(solution)/shard_map/pallas_call | solution.py:72
  39.4 0.0 collective-permute-done.5.two_ref
  39.4 0.8 collective-permute-done.4.one_ref
  40.2 2.1 %shard_map.115 = (bf16[2,2,256,256]{3,2,1,0:T(8,128)(2,1)S(1)}, bf16[2,256,256]{2,1,0:T(8,128)(2,1)S(1)}, bf16[2,256,256]{2,1,0:T(8,128)(2,1)S(1)}, f32[4,128,128]{2,1,0:T(8,128)S(1)}) custom-call(s32[2]{0:T(128)S(1)} %pad_add_fusion.where_ref, bf16[256,256]{1,0:T(8,128)(2,1)S(1)} %collective-permute-done.4.one_ref, ...), custom_call_target="tpu_custom_call" | custom-call | tf_op jit(solution)/shard_map/pallas_call | solution.py:72
  42.3 1.5 %collective-permute-start.6 = (bf16[2,256,256]{2,1,0:T(8,128)(2,1)S(1)}, bf16[2,256,256]{2,1,0:T(8,128)(2,1)S(1)}, u32[]{:S(2)}, u32[]{:S(2)}) collective-permute-start(bf16[2,256,256]{2,1,0:T(8,128)(2,1)S(1)} %get-tuple-element.45), channel_id=1, source_target_pairs={{0,1},{1,0},{2,3},{3,2},{4,5},{5,4},{6,7},{7,6},{8,9},{9,8},{10,11... | collective-permute-start | bytes 786440 | tf_op jit(solution)/shard_map/ppermute | solution.py:463
  43.9 0.7 collective-permute-start.7
  44.5 2.3 %shard_map.116.w2_ref = f32[7,2,64,128]{3,2,1,0:T(8,128)S(1)} custom-call(s32[2]{0:T(128)S(1)} %pad_add_fusion.where_ref, bf16[2,2,256,256]{3,2,1,0:T(8,128)(2,1)S(1)} %get-tuple-element.49.g_ref, bf16[2,256,256]{2,1,0:T(8,128)(2,1)S(1)} %collective-permute-done.one_ref, bf16[2,2,256,256]{3,2,1,0:T(8,128)(2,1)S(1)} %get-tuple-element.33.a_ref, ...), custom_call_target="tpu_custom_call" | custom-call | tf_op jit(solution)/shard_map/pallas_call | solution.py:72
  46.9 1.5 %shard_map.117 = (f32[2560,128]{1,0:T(8,128)S(1)}, bf16[2560,128]{1,0:T(8,128)(2,1)S(1)}) custom-call(s32[2]{0:T(128)S(1)} %pad_add_fusion.where_ref, f32[27,128,128]{2,1,0:T(8,128)S(1)} %shard_map.114.w3_ref, f32[4,128,128]{2,1,0:T(8,128)S(1)} %get-tuple-element.48.d3_ref, f32[7,2,64,128]{3,2,1,0:T(8,128)S(1)} %shard_map.116.w2_ref, ...), custom_call_target="tpu_custom_call" | custom-call | tf_op jit(solution)/shard_map/pallas_call | solution.py:72
  48.4 0.0 collective-permute-done.6.one_ref
  48.4 0.0 collective-permute-done.7.two_ref
  48.4 5.0 %collective-permute-start.8 = (bf16[2560,128]{1,0:T(8,128)(2,1)S(1)}, bf16[2560,128]{1,0:T(8,128)(2,1)S(1)}, u32[]{:S(2)}, u32[]{:S(2)}) collective-permute-start(bf16[2560,128]{1,0:T(8,128)(2,1)S(1)} %get-tuple-element.58), channel_id=1, source_target_pairs={{0,64},{64,0},{1,65},{65,1},{2,66},{66,2},{3,67},{67,3},{4,68},{68... | collective-permute-start | bytes 1966088 | tf_op jit(solution)/shard_map/ppermute | solution.py:467
  53.4 3.4 %shard_map.118.down_ref = f32[64,256]{1,0:T(8,128)S(1)} custom-call(s32[2]{0:T(128)S(1)} %pad_add_fusion.where_ref, bf16[2,256,256]{2,1,0:T(8,128)(2,1)S(1)} %collective-permute-done.6.one_ref, bf16[2,2,256,256]{3,2,1,0:T(8,128)(2,1)S(1)} %get-tuple-element.49.g_ref, bf16[2,256,256]{2,1,0:T(8,128)(2,1)S(1)} %collective-permute-done.7.two_ref, ...), custom_call_target="tpu_custom_call" | custom-call | tf_op jit(solution)/shard_map/pallas_call | solution.py:72
  56.7 0.0 collective-permute-done.8.came_ref
  56.8 0.7 shard_map.119
  57.5 38.3 %all_to_all.5 = bf16[64,40,128]{2,1,0:T(8,128)(2,1)S(1)} all-to-all(bf16[64,40,128]{2,1,0:T(8,128)(2,1)S(1)} %bitcast.35), channel_id=1, replica_groups=mesh['section'=2,'space'=64] {'space'}, dimensions={0} | all-to-all | bytes 1310720 | tf_op jit(solution)/shard_map/all_to_all | solution.py:481
  95.8 0.1 convert_reduce_fusion
  95.9 0.6 slice_bitcast_fusion.1
  96.5 0.1 reshape.52
  96.6 1.5 %collective-permute-start.9 = (f32[128]{0:T(128)S(1)}, f32[128]{0:T(128)S(1)}, u32[]{:S(2)}, u32[]{:S(2)}) collective-permute-start(f32[128]{0:T(128)S(1)} %slice_bitcast_fusion.2), channel_id=1, source_target_pairs={{0,64},{64,0},{1,65},{65,1},{2,66},{66,2},{3,67},{67,3},{4,68},{68... | collective-permute-start | bytes 1544 | tf_op jit(solution)/shard_map/ppermute | solution.py:467
  98.1 0.1 reshape.50
  98.2 0.1 copy.15
  98.2 0.7 reshape.51
  98.9 0.1 copy.14
  99.1 0.8 reshape.54
  99.9 0.2 copy.13
  100.0 0.8 reshape.53
  100.8 0.0 collective-permute-done.9
  100.8 0.5 fusion
  (29 shorter events, 0.1 us)
Async XLA Ops:
  0.6 24.5 %copy-start = (s32[4,1,2,128]{3,2,1,0:T(2,128)S(1)}, s32[4,1,2,128]{3,2,1,0:T(2,128)}, u32[]{:S(2)}) copy-start(s32[4,1,2,128]{3,2,1,0:T(2,128)} %param.8) | copy-start | bytes 12292
  0.7 8.6 %copy-start.13 = (bf16[64,64,3,3,3]{1,0,4,3,2:T(8,128)(2,1)S(1)}, bf16[64,64,3,3,3]{1,0,4,3,2:T(8,128)(2,1)}, u32[]{:S(2)}) copy-start(bf16[64,64,3,3,3]{1,0,4,3,2:T(8,128)(2,1)} %param.10) | copy-start | bytes 663556
  0.7 8.9 %copy-start.11 = (bf16[128,64,2,2,2]{0,4,3,2,1:T(2,128)(2,1)S(1)}, bf16[128,64,2,2,2]{0,4,3,2,1:T(2,128)(2,1)}, u32[]{:S(2)}) copy-start(bf16[128,64,2,2,2]{0,4,3,2,1:T(2,128)(2,1)} %param.11) | copy-start | bytes 393220
  0.7 8.9 %copy-start.12 = (bf16[128,4]{0,1:T(4,128)(2,1)S(1)}, bf16[128,4]{0,1:T(4,128)(2,1)}, u32[]{:S(2)}) copy-start(bf16[128,4]{0,1:T(4,128)(2,1)} %param.13) | copy-start | bytes 3076
  6.5 3.1 %copy-start.7 = (bf16[128,128,3,3,3]{1,0,4,3,2:T(8,128)(2,1)S(1)}, bf16[128,128,3,3,3]{1,0,4,3,2:T(8,128)(2,1)}, u32[]{:S(2)}) copy-start(bf16[128,128,3,3,3]{1,0,4,3,2:T(8,128)(2,1)} %param.12) | copy-start | bytes 2654212
  6.5 7.6 %collective-permute-start = (bf16[2,256,256]{2,1,0:T(8,128)(2,1)S(1)}, bf16[2,256,256]{2,1,0:T(8,128)(2,1)S(1)}, u32[]{:S(2)}, u32[]{:S(2)}) collective-permute-start(bf16[2,256,256]{2,1,0:T(8,128)(2,1)S(1)} %get-tuple-element.32), channel_id=1, source_target_pairs={{0,1},{1,0},{2,3},{3,2},{4,5},{5,4},{6,7},{7,6},{8,9},{9,8},{10,11... | collective-permute-start | bytes 786440 | tf_op jit(solution)/shard_map/ppermute | solution.py:463
  8.7 5.5 %collective-permute-start.1 = (bf16[2,256,256]{2,1,0:T(8,128)(2,1)S(1)}, bf16[2,256,256]{2,1,0:T(8,128)(2,1)S(1)}, u32[]{:S(2)}, u32[]{:S(2)}) collective-permute-start(bf16[2,256,256]{2,1,0:T(8,128)(2,1)S(1)} %get-tuple-element.34), channel_id=1, source_target_pairs={{1,2},{2,1},{3,4},{4,3},{5,6},{6,5},{7,8},{8,7},{9,10},{10,9},{11,... | collective-permute-start | bytes 786440 | tf_op jit(solution)/shard_map/ppermute | solution.py:462
  11.8 1.0 %copy-start.3 = (bf16[256,2304]{1,0:T(8,128)(2,1)}, bf16[256,2304]{1,0:T(8,128)(2,1)S(1)}, u32[]{:S(2)}) copy-start(bf16[256,2304]{1,0:T(8,128)(2,1)S(1)} %get-tuple-element.54.b2_ref) | copy-start | bytes 3538948
  12.8 4.9 %copy-start.1 = (bf16[256,2304]{1,0:T(8,128)(2,1)}, bf16[256,2304]{1,0:T(8,128)(2,1)S(1)}, u32[]{:S(2)}) copy-start(bf16[256,2304]{1,0:T(8,128)(2,1)S(1)} %get-tuple-element.43.b3_ref) | copy-start | bytes 3538948
  12.8 4.9 %copy-start.9 = (bf16[1024,256]{1,0:T(8,128)(2,1)}, bf16[1024,256]{1,0:T(8,128)(2,1)S(1)}, u32[]{:S(2)}) copy-start(bf16[1024,256]{1,0:T(8,128)(2,1)S(1)} %get-tuple-element.56.perm_ref) | copy-start | bytes 1572868
  14.2 3.6 %copy-start.5 = (bf16[2,256,256]{2,1,0:T(8,128)(2,1)}, bf16[2,256,256]{2,1,0:T(8,128)(2,1)S(1)}, u32[]{:S(2)}) copy-start(bf16[2,256,256]{2,1,0:T(8,128)(2,1)S(1)} %collective-permute-done.1.two_ref) | copy-start | bytes 786436
  17.8 7.3 %collective-permute-start.3 = (bf16[256,256]{1,0:T(8,128)(2,1)S(1)}, bf16[256,256]{1,0:T(8,128)(2,1)}, u32[]{:S(2)}, u32[]{:S(2)}) collective-permute-start(bf16[256,256]{1,0:T(8,128)(2,1)S(1)} %get-tuple-element.37.a_ref.a3_ref), channel_id=1, source_target_pairs={{1,2},{2,1},{3,4},{4,3},{5,6},{6,5},{7,8},{8,7},{9,10},{10,9},{11,... | collective-permute-start | bytes 393224 | tf_op jit(solution)/shard_map/ppermute | solution.py:462
  19.1 8.5 %collective-permute-start.2 = (bf16[256,256]{1,0:T(8,128)(2,1)S(1)}, bf16[256,256]{1,0:T(8,128)(2,1)}, u32[]{:S(2)}, u32[]{:S(2)}) collective-permute-start(bf16[256,256]{1,0:T(8,128)(2,1)S(1)} %get-tuple-element.37.a_ref.a3_ref), channel_id=1, source_target_pairs={{0,1},{1,0},{2,3},{3,2},{4,5},{5,4},{6,7},{7,6},{8,9},{9,8},{10,11... | collective-permute-start | bytes 393224 | tf_op jit(solution)/shard_map/ppermute | solution.py:463
  31.2 9.0 %copy-start.2 = (bf16[256,2304]{1,0:T(8,128)(2,1)S(1)}, bf16[256,2304]{1,0:T(8,128)(2,1)}, u32[]{:S(2)}) copy-start(bf16[256,2304]{1,0:T(8,128)(2,1)} %copy-done.1) | copy-start | bytes 3538948
  31.2 9.0 %copy-start.8 = (bf16[4,256,256]{2,1,0:T(8,128)(2,1)S(1)}, bf16[4,256,256]{2,1,0:T(8,128)(2,1)}, u32[]{:S(2)}) copy-start(bf16[4,256,256]{2,1,0:T(8,128)(2,1)} %get-tuple-element.44.h_ref) | copy-start | bytes 1572868
  31.2 8.2 %collective-permute-start.5 = (bf16[256,256]{1,0:T(8,128)(2,1)S(1)}, bf16[256,256]{1,0:T(8,128)(2,1)S(1)}, u32[]{:S(2)}, u32[]{:S(2)}) collective-permute-start(bf16[256,256]{1,0:T(8,128)(2,1)S(1)} %get-tuple-element.40.g_ref), channel_id=1, source_target_pairs={{1,2},{2,1},{3,4},{4,3},{5,6},{6,5},{7,8},{8,7},{9,10},{10,9},{11,... | collective-permute-start | bytes 393224 | tf_op jit(solution)/shard_map/ppermute | solution.py:462
  32.0 8.2 %collective-permute-start.4 = (bf16[256,256]{1,0:T(8,128)(2,1)S(1)}, bf16[256,256]{1,0:T(8,128)(2,1)S(1)}, u32[]{:S(2)}, u32[]{:S(2)}) collective-permute-start(bf16[256,256]{1,0:T(8,128)(2,1)S(1)} %get-tuple-element.40.g_ref), channel_id=1, source_target_pairs={{0,1},{1,0},{2,3},{3,2},{4,5},{5,4},{6,7},{7,6},{8,9},{9,8},{10,11... | collective-permute-start | bytes 393224 | tf_op jit(solution)/shard_map/ppermute | solution.py:463
  40.2 4.3 %copy-start.6 = (bf16[2,256,256]{2,1,0:T(8,128)(2,1)S(1)}, bf16[2,256,256]{2,1,0:T(8,128)(2,1)}, u32[]{:S(2)}) copy-start(bf16[2,256,256]{2,1,0:T(8,128)(2,1)} %copy-done.5) | copy-start | bytes 786436
  42.3 6.0 %collective-permute-start.6 = (bf16[2,256,256]{2,1,0:T(8,128)(2,1)S(1)}, bf16[2,256,256]{2,1,0:T(8,128)(2,1)S(1)}, u32[]{:S(2)}, u32[]{:S(2)}) collective-permute-start(bf16[2,256,256]{2,1,0:T(8,128)(2,1)S(1)} %get-tuple-element.45), channel_id=1, source_target_pairs={{0,1},{1,0},{2,3},{3,2},{4,5},{5,4},{6,7},{7,6},{8,9},{9,8},{10,11... | collective-permute-start | bytes 786440 | tf_op jit(solution)/shard_map/ppermute | solution.py:463
  43.9 4.5 %collective-permute-start.7 = (bf16[2,256,256]{2,1,0:T(8,128)(2,1)S(1)}, bf16[2,256,256]{2,1,0:T(8,128)(2,1)S(1)}, u32[]{:S(2)}, u32[]{:S(2)}) collective-permute-start(bf16[2,256,256]{2,1,0:T(8,128)(2,1)S(1)} %get-tuple-element.46), channel_id=1, source_target_pairs={{1,2},{2,1},{3,4},{4,3},{5,6},{6,5},{7,8},{8,7},{9,10},{10,9},{11,... | collective-permute-start | bytes 786440 | tf_op jit(solution)/shard_map/ppermute | solution.py:462
  46.8 6.5 %copy-start.4 = (bf16[256,2304]{1,0:T(8,128)(2,1)S(1)}, bf16[256,2304]{1,0:T(8,128)(2,1)}, u32[]{:S(2)}) copy-start(bf16[256,2304]{1,0:T(8,128)(2,1)} %copy-done.3) | copy-start | bytes 3538948
  46.9 6.5 %copy-start.10 = (bf16[1024,256]{1,0:T(8,128)(2,1)S(1)}, bf16[1024,256]{1,0:T(8,128)(2,1)}, u32[]{:S(2)}) copy-start(bf16[1024,256]{1,0:T(8,128)(2,1)} %copy-done.9) | copy-start | bytes 1572868
  48.4 8.4 %collective-permute-start.8 = (bf16[2560,128]{1,0:T(8,128)(2,1)S(1)}, bf16[2560,128]{1,0:T(8,128)(2,1)S(1)}, u32[]{:S(2)}, u32[]{:S(2)}) collective-permute-start(bf16[2560,128]{1,0:T(8,128)(2,1)S(1)} %get-tuple-element.58), channel_id=1, source_target_pairs={{0,64},{64,0},{1,65},{65,1},{2,66},{66,2},{3,67},{67,3},{4,68},{68... | collective-permute-start | bytes 1966088 | tf_op jit(solution)/shard_map/ppermute | solution.py:467
  96.6 4.2 %collective-permute-start.9 = (f32[128]{0:T(128)S(1)}, f32[128]{0:T(128)S(1)}, u32[]{:S(2)}, u32[]{:S(2)}) collective-permute-start(f32[128]{0:T(128)S(1)} %slice_bitcast_fusion.2), channel_id=1, source_target_pairs={{0,64},{64,0},{1,65},{65,1},{2,66},{66,2},{3,67},{67,3},{4,68},{68... | collective-permute-start | bytes 1544 | tf_op jit(solution)/shard_map/ppermute | solution.py:467

commit v6 on v5

--- a/solution.py
+++ b/solution.py
@@ -18,7 +18,7 @@
 DOWN3, CONV2, DOWN2 = 27, 31, 38
 
 
-def params(megabytes=24):
+def params(megabytes=12):
     return pltpu.CompilerParams(vmem_limit_bytes=megabytes << 20)
 
 
@@ -84,62 +84,66 @@
     return jnp.where(even, two, one), jnp.where(even, one, two)
 
 
-def first_kernel(where_ref, vol_ref, w_ref, vp_ref, a_ref, one_ref, two_ref, sort_ref, wt_ref):
-    @pl.when(pl.program_id(0) == 0)
-    def _():
-        to = lax.broadcasted_iota(jnp.int32, (1, 512), 1)
-        source = (to % 128) * 4 + (to // 128) % 2 * 2 + to // 256
-        sort_ref[...] = jnp.where(lax.broadcasted_iota(jnp.int32, (512, 512), 0) == source, 1.0, 0.0).astype(BF16)
-        to = lax.broadcasted_iota(jnp.int32, (1, 1024), 1)
-        height = to % 8
-        source = to // 8 % 32 * 8 + to // 512 * 4 + height % 2 * 2 + to // 256 % 2
-        pick = jnp.where(lax.broadcasted_iota(jnp.int32, (256, 1024), 0) == source, 1.0, 0.0).astype(BF16)
-        w = dot_tn(w_ref[...], pick)
-        for h in range(4):
-            wt_ref[pl.ds(h * 64, 64), :] = jnp.where(height // 2 == h, w, 0.0).astype(BF16)
-
-    for d in range(2):
-        v = vol_ref[0, :, d].astype(F32).reshape(256, 512).astype(BF16)
-        s = dot(v, sort_ref[...]).astype(BF16)
-        vp_ref[0, 0, pl.ds(d * 512, 256), :] = s[:, :256]
-        vp_ref[0, 0, pl.ds(d * 512 + 256, 256), :] = s[:, 256:]
-    a = rectified(dot(wt_ref[...], vp_ref[0, 0])).astype(BF16)
-    a_ref[0, 0] = a
-    upper = pl.program_id(0) % 2
-
-    @pl.when(upper == where_ref[1])
-    def _():
-        two_ref[0] = a
-
-    @pl.when(upper != where_ref[1])
-    def _():
-        one_ref[0] = a
+def first_kernel(
+    where_ref, vol_far, w_ref, vp_far, a_ref, one_ref, two_ref, sort_ref, wt_ref, vol_ref, vp_ref, in_sems, out_sems
+):
+    steps = [(n, d) for n in range(CROPS) for d in range(2)]
+    fetches = [
+        pltpu.make_async_copy(vol_far.at[CROPS * where_ref[0] + n, :, pl.ds(2 * d, 2)], vol_ref.at[i], in_sems.at[i])
+        for i, (n, d) in enumerate(steps)
+    ]
+    stores = [
+        pltpu.make_async_copy(vp_ref.at[i], vp_far.at[n, d], out_sems.at[i]) for i, (n, d) in enumerate(steps)
+    ]
+    for fetch in fetches:
+        fetch.start()
+    to = lax.broadcasted_iota(jnp.int32, (1, 512), 1)
+    source = (to % 128) * 4 + (to // 128) % 2 * 2 + to // 256
+    sort_ref[...] = jnp.where(lax.broadcasted_iota(jnp.int32, (512, 512), 0) == source, 1.0, 0.0).astype(BF16)
+    to = lax.broadcasted_iota(jnp.int32, (1, 1024), 1)
+    height = to % 8
+    source = to // 8 % 32 * 8 + to // 512 * 4 + height % 2 * 2 + to // 256 % 2
+    pick = jnp.where(lax.broadcasted_iota(jnp.int32, (256, 1024), 0) == source, 1.0, 0.0).astype(BF16)
+    w = dot_tn(w_ref[...], pick)
+    for h in range(4):
+        wt_ref[pl.ds(h * 64, 64), :] = jnp.where(height // 2 == h, w, 0.0).astype(BF16)
+    for i, (n, d) in enumerate(steps):
+        fetches[i].wait()
+        for k in range(2):
+            v = vol_ref[i, :, k].astype(F32).reshape(256, 512).astype(BF16)
+            s = dot(v, sort_ref[...]).astype(BF16)
+            vp_ref[i, pl.ds(k * 512, 256), :] = s[:, :256]
+            vp_ref[i, pl.ds(k * 512 + 256, 256), :] = s[:, 256:]
+        stores[i].start()
+        a_ref[n, d] = rectified(dot(wt_ref[...], vp_ref[i])).astype(BF16)
+    even = where_ref[1] == 0
+    for n in range(CROPS):
+        one_ref[n] = jnp.where(even, a_ref[n, 1], a_ref[n, 0])
+        two_ref[n] = jnp.where(even, a_ref[n, 0], a_ref[n, 1])
+    for store in stores:
+        store.wait()
 
 
 def first(where, volume, w1):
-    half = pl.BlockSpec((1, T, T), lambda i, s: (i // 2, 0, 0))
+    spec = pl.BlockSpec(memory_space=pltpu.VMEM)
+    far = pl.BlockSpec(memory_space=pl.ANY)
     return pl.pallas_call(
         first_kernel,
-        grid_spec=pltpu.PrefetchScalarGridSpec(
-            num_scalar_prefetch=1,
-            grid=(4,),
-            in_specs=[
-                pl.BlockSpec((1, 32, 2, 8, 512), lambda i, s: (2 * s[0] + i // 2, 0, i % 2, 0, 0)),
-                pl.BlockSpec((256, 64), lambda i, s: (0, 0)),
-            ],
-            out_specs=[
-                pl.BlockSpec((1, 1, 1024, 256), lambda i, s: (i // 2, i % 2, 0, 0)),
-                pl.BlockSpec((1, 1, 256, 256), lambda i, s: (i // 2, i % 2, 0, 0)),
-                half,
-                half,
-            ],
-            scratch_shapes=[pltpu.VMEM((512, 512), BF16), pltpu.VMEM((256, 1024), BF16)],
-        ),
+        in_specs=[pl.BlockSpec(memory_space=pltpu.SMEM), far, spec],
+        out_specs=[far, spec, spec, spec],
         out_shape=[
-            pltpu.VMEM((CROPS, 2, 1024, 256), BF16),
+            pltpu.HBM((CROPS, 2, 1024, 256), BF16),
             pltpu.VMEM((CROPS, 2, 256, 256), BF16),
             pltpu.VMEM((CROPS, 256, 256), BF16),
             pltpu.VMEM((CROPS, 256, 256), BF16),
+        ],
+        scratch_shapes=[
+            pltpu.VMEM((512, 512), BF16),
+            pltpu.VMEM((256, 1024), BF16),
+            pltpu.VMEM((4, 32, 2, 8, 512), BF16),
+            pltpu.VMEM((4, 1024, 256), BF16),
+            pltpu.SemaphoreType.DMA((4,)),
+            pltpu.SemaphoreType.DMA((4,)),
         ],
         compiler_params=params(),
     )(where, pltpu.with_memory_space_constraint(volume, pltpu.HBM), pltpu.with_memory_space_constraint(w1, pltpu.HBM))
@@ -203,14 +207,31 @@
     )
 
 
-def second_kernel(where_ref, one_ref, a_ref, two_ref, f2_ref, wd_ref, h_ref, a3_ref, b_ref):
+def second_own_kernel(a_ref, f2_ref, out_ref, b_ref):
     for n in range(CROPS):
-        lo, hi = sorted_out(where_ref, one_ref[n], two_ref[n])
-        planes = (lo, a_ref[n, 0], a_ref[n, 1], hi)
-        for k, plane in enumerate(planes):
-            put_three(b_ref, k * 3 * T, three_two(plane))
         for d in range(2):
-            h = rectified(dot(f2_ref[...], b_ref[pl.ds(d * 3 * T, 9 * T), :])).astype(BF16)
+            put_three(b_ref, (2 * n + d) * 3 * T, three_two(a_ref[n, d]))
+        own = pl.ds(n * 6 * T, 6 * T)
+        out_ref[n, 0] = dot(f2_ref[:, 3 * T :], b_ref[own, :])
+        out_ref[n, 1] = dot(f2_ref[:, : 6 * T], b_ref[own, :])
+
+
+def second_own(a, f2):
+    return call(
+        second_own_kernel,
+        [((CROPS, 2, T, T), F32, pltpu.VMEM)],
+        a, f2,
+        scratch=[pltpu.VMEM((12 * T, T), BF16)],
+    )[0]
+
+
+def second_kernel(where_ref, one_ref, own_ref, two_ref, f2_ref, wd_ref, h_ref, a3_ref, b_ref):
+    for n in range(CROPS):
+        for d, plane in enumerate(sorted_out(where_ref, one_ref[n], two_ref[n])):
+            at = (2 * n + d) * 3 * T
+            put_three(b_ref, at, three_two(plane))
+            rest = dot(f2_ref[:, d * 6 * T : d * 6 * T + 3 * T], b_ref[pl.ds(at, 3 * T), :])
+            h = rectified(own_ref[n, d] + rest).astype(BF16)
             for p in range(2):
                 h_ref[2 * d + p, :, pl.ds(n * 128, 128)] = h[:, p * 128 : (p + 1) * 128]
     total = dot_tn(wd_ref[0], h_ref[0])
@@ -219,30 +240,36 @@
     a3_ref[...] = rectified(total).astype(BF16)
 
 
-def second(where, one, a, two, f2, wd):
+def second(where, one, own, two, f2, wd):
     return call(
         second_kernel,
         [((4, T, T), BF16, pltpu.HBM), ((T, T), BF16, pltpu.VMEM)],
-        where, one, a, two, f2, wd,
+        where, one, own, two, f2, wd,
         scratch=[pltpu.VMEM((12 * T, T), BF16)],
     )
 
 
-def head_kernel(
-    scale, where_ref, one_ref, a_ref, two_ref, f3_far, wh_far, marks_ref, gz_ref, gh_ref, b_ref, f3_ref, wh_ref, sems
-):
-    fetches = [
-        pltpu.make_async_copy(f3_far, f3_ref, sems.at[0]),
-        pltpu.make_async_copy(wh_far, wh_ref, sems.at[1]),
-    ]
-    for fetch in fetches:
-        fetch.start()
-    lo, hi = sorted_out(where_ref, one_ref[...], two_ref[...])
-    for k, plane in enumerate((lo, a_ref[...], hi)):
+def head_own_kernel(a_ref, f3_ref, wh_ref, out_ref, sides_ref, wh_out_ref, b_ref):
+    put_three(b_ref, 0, three_three(a_ref[...]))
+    out_ref[...] = dot(f3_ref[:, 3 * T : 6 * T], b_ref[...])
+    sides_ref[:, : 3 * T] = f3_ref[:, : 3 * T]
+    sides_ref[:, 3 * T :] = f3_ref[:, 6 * T :]
+    wh_out_ref[...] = wh_ref[...]
+
+
+def head_own(a, f3, wh):
+    return call(
+        head_own_kernel,
+        [((T, T), F32, pltpu.VMEM), ((T, 6 * T), BF16, pltpu.VMEM), ((256, 128), BF16, pltpu.VMEM)],
+        a, f3, wh,
+        scratch=[pltpu.VMEM((3 * T, T), BF16)],
+    )
+
+
+def head_kernel(scale, where_ref, one_ref, own_ref, two_ref, sides_ref, wh_ref, marks_ref, gz_ref, gh_ref, b_ref):
+    for k, plane in enumerate(sorted_out(where_ref, one_ref[...], two_ref[...])):
         put_three(b_ref, k * 3 * T, three_three(plane))
-    for fetch in fetches:
-        fetch.wait()
-    top = rectified(dot(f3_ref[...], b_ref[...])).astype(BF16)
+    top = rectified(own_ref[...] + dot(sides_ref[...], b_ref[...])).astype(BF16)
     row = lax.broadcasted_iota(jnp.int32, (128, T), 0)
     total = jnp.zeros((128, 128), F32)
     for h in range(2):
@@ -257,18 +284,12 @@
     gh_ref[...] = total
 
 
-def head(where, one, a, two, f3, wh, marks, scale):
+def head(where, one, own, two, sides, wh, marks, scale):
     return call(
         functools.partial(head_kernel, scale),
         [((T, T), BF16, pltpu.VMEM), ((128, 128), F32, pltpu.VMEM)],
-        where, one, a, two, f3, wh, marks,
-        scratch=[
-            pltpu.VMEM((9 * T, T), BF16),
-            pltpu.VMEM((T, 9 * T), BF16),
-            pltpu.VMEM((256, 128), BF16),
-            pltpu.SemaphoreType.DMA((2,)),
-        ],
-        far=(4, 5),
+        where, one, own, two, sides, wh, marks,
+        scratch=[pltpu.VMEM((6 * T, T), BF16)],
     )
 
 
@@ -292,13 +313,28 @@
     )[0]
 
 
+def middle_own_kernel(g_ref, b3_ref, out_ref, b_ref):
+    put_three(b_ref, 0, three_three(g_ref[...]))
+    out_ref[...] = dot(b3_ref[:, 3 * T : 6 * T], b_ref[...])
+
+
+def middle_own(g, b3):
+    return call(
+        middle_own_kernel,
+        [((T, T), F32, pltpu.VMEM)],
+        g, b3,
+        scratch=[pltpu.VMEM((3 * T, T), BF16)],
+    )[0]
+
+
 def middle_kernel(
-    where_ref, one_ref, g_ref, two_ref, b3_ref, a3_ref, h_ref, wd_ref, gz2_ref, gone_ref, gtwo_ref, gd_ref, b_ref
+    where_ref, one_ref, own_ref, two_ref, b3_ref, a3_ref, h_ref, wd_ref, gz2_ref, gone_ref, gtwo_ref, gd_ref, b_ref
 ):
-    lo, hi = sorted_out(where_ref, one_ref[...], two_ref[...])
-    for k, plane in enumerate((lo, g_ref[...], hi)):
+    rest = own_ref[...]
+    for k, plane in enumerate(sorted_out(where_ref, one_ref[...], two_ref[...])):
         put_three(b_ref, k * 3 * T, three_three(plane))
-    gy = (dot(b3_ref[...], b_ref[...]) * slope(a3_ref[...])).astype(BF16)
+        rest += dot(b3_ref[:, k * 6 * T : k * 6 * T + 3 * T], b_ref[pl.ds(k * 3 * T, 3 * T), :])
+    gy = (rest * slope(a3_ref[...])).astype(BF16)
     for d in range(2):
         for p in range(2):
             k = 2 * d + p
@@ -313,7 +349,7 @@
         gd_ref[k] = dot_nt(gy[:128], h_ref[k, :128]) + dot_nt(gy[128:], h_ref[k, 128:])
 
 
-def middle(where, one, g, two, b3, a3, h, wd):
+def middle(where, one, own, two, b3, a3, h, wd):
     return call(
         middle_kernel,
         [
@@ -322,8 +358,8 @@
             ((CROPS, T, T), BF16, pltpu.VMEM),
             ((4, 128, 128), F32, pltpu.VMEM),
         ],
-        where, one, g, two, b3, a3, h, wd,
-        scratch=[pltpu.VMEM((9 * T, T), BF16)],
+        where, one, own, two, b3, a3, h, wd,
+        scratch=[pltpu.VMEM((6 * T, T), BF16)],
     )
 
 
@@ -397,15 +433,32 @@
     )
 
 
-def last_kernel(where_ref, one_ref, g_ref, two_ref, b2_ref, a_ref, vp_ref, perm_ref, down_ref, b_ref, t_ref):
+def last_own_kernel(g_ref, b2_ref, out_ref, b_ref):
     for n in range(CROPS):
-        lo, hi = sorted_out(where_ref, one_ref[n], two_ref[n])
-        planes = (lo, g_ref[n, 0], g_ref[n, 1], hi)
-        for k, plane in enumerate(planes):
-            put_three(b_ref, k * 3 * T, three_two(plane))
-        gy = [
-            (dot(b2_ref[...], b_ref[pl.ds(d * 3 * T, 9 * T), :]) * slope(a_ref[n, d])).astype(BF16) for d in range(2)
-        ]
+        for d in range(2):
+            put_three(b_ref, (2 * n + d) * 3 * T, three_two(g_ref[n, d]))
+        own = pl.ds(n * 6 * T, 6 * T)
+        out_ref[n, 0] = dot(b2_ref[:, 3 * T :], b_ref[own, :])
+        out_ref[n, 1] = dot(b2_ref[:, : 6 * T], b_ref[own, :])
+
+
+def last_own(g, b2):
+    return call(
+        last_own_kernel,
+        [((CROPS, 2, T, T), F32, pltpu.VMEM)],
+        g, b2,
+        scratch=[pltpu.VMEM((12 * T, T), BF16)],
+    )[0]
+
+
+def last_kernel(where_ref, one_ref, own_ref, two_ref, b2_ref, a_ref, vp_ref, perm_ref, down_ref, b_ref, t_ref):
+    for n in range(CROPS):
+        gy = []
+        for d, plane in enumerate(sorted_out(where_ref, one_ref[n], two_ref[n])):
+            at = (2 * n + d) * 3 * T
+            put_three(b_ref, at, three_two(plane))
+            rest = dot(b2_ref[:, d * 6 * T : d * 6 * T + 3 * T], b_ref[pl.ds(at, 3 * T), :])
+            gy.append(((own_ref[n, d] + rest) * slope(a_ref[n, d])).astype(BF16))
         t = dot_nt(gy[0], vp_ref[n, 0]) + dot_nt(gy[1], vp_ref[n, 1])
         if n == 0:
             t_ref[...] = t
@@ -467,12 +520,59 @@
     return lax.ppermute(x, "section", [(0, 1), (1, 0)])
 
 
+def flat(x, step):
+    c = lax.broadcasted_iota(jnp.int32, (128, 128), 0) * step
+    lane = lax.broadcasted_iota(jnp.int32, (128, 128), 1)
+    x = x.T
+    pieces = []
+    for k in range(16):
+        piece = x[8 * k : 8 * k + 8]
+        for part in (step // 2, step - step // 2):
+            piece = pltpu.roll(piece, 0, 1, stride=part, stride_axis=0)
+        pieces.append(pltpu.roll(piece, 8 * k * step % 128, 1) if 8 * k * step % 128 else piece)
+    turned = jnp.concatenate(pieces, axis=0)
+    row = lax.broadcasted_iota(jnp.int32, (32, 128), 0)
+    start = lax.broadcasted_iota(jnp.int32, (32, 128), 1) * step // 128
+    exact = functools.partial(jnp.dot, precision=lax.Precision.HIGHEST, preferred_element_type=F32)
+    here = lane >= c % 128
+    same = exact(jnp.where(row == start, 1.0, 0.0), jnp.where(here, turned, 0.0))
+    return same + exact(jnp.where(row == start + 1, 1.0, 0.0), jnp.where(here, 0.0, turned))
+
+
+def unpack_kernel(sums_ref, two_ref, three_ref, conv_ref, x_ref):
+    zero = jnp.zeros((128, 128), F32)
+    x_ref[...] = zero
+    x_ref[pl.ds(0, DOWN3), :] = sums_ref[pl.ds(0, DOWN3), :]
+    conv_ref[...] = flat(x_ref[...], 27)[:27]
+    x_ref[...] = zero
+    lane = lax.broadcasted_iota(jnp.int32, (7, 128), 1)
+    rows = sums_ref[pl.ds(CONV2, 7), :]
+    for i in range(4):
+        x_ref[pl.ds(i, 7, stride=4), :] = jnp.where(lane < 32, rows if i == 0 else pltpu.roll(rows, 128 - 32 * i, 1), 0.0)
+    x_ref[pl.ds(27, 1), :] = jnp.zeros((1, 128), F32)
+    two_ref[...] = flat(x_ref[...], 27)[:7]
+    x_ref[...] = zero
+    lane = lax.broadcasted_iota(jnp.int32, (1, 128), 1)
+    for k in range(4):
+        row = sums_ref[pl.ds(DOWN3 + k, 1), :]
+        at = k // 2 * 4 + k % 2
+        x_ref[pl.ds(at, 1), :] = jnp.where(lane < 64, row, 0.0)
+        x_ref[pl.ds(at + 2, 1), :] = jnp.where(lane < 64, pltpu.roll(row, 64, 1), 0.0)
+    three_ref[...] = flat(x_ref[...], 8)[:4]
+
+
 def unpack(sums, down):
+    two, three, conv = call(
+        unpack_kernel,
+        [((7, 128), F32, pltpu.VMEM), ((4, 128), F32, pltpu.HBM), ((27, 128), F32, pltpu.HBM)],
+        sums,
+        scratch=[pltpu.VMEM((128, 128), F32)],
+    )
     return (
         down,
-        sums[CONV2:DOWN2].reshape(28, 32)[:27].T.reshape(-1),
-        sums[DOWN3:CONV2].reshape(2, 2, 2, 64).transpose(3, 0, 2, 1).reshape(-1),
-        sums[:27].T.reshape(-1),
+        two.reshape(-1)[: 27 * 32],
+        three.reshape(-1),
+        conv.reshape(-1),
         sums[DOWN2 - 1, 96:100],
     )
 
@@ -501,19 +601,25 @@
     vp, a2, one, two = first(where, volume, w1)
     a2_one, a2_two = swapped(one, two)
     f2, b2, f3, b3, perm, wd, wh = prepare(w2, w3, wd, w_head.T)
-    h2, a3 = second(where, a2_one, a2, a2_two, f2, wd)
+    own = second_own(a2, f2)
+    a2_one, a2_two, own = lax.optimization_barrier((a2_one, a2_two, own))
+    h2, a3 = second(where, a2_one, own, a2_two, f2, wd)
     a3_one, a3_two = swapped(a3, a3)
-    gz4, gh = head(where, a3_one, a3, a3_two, f3, wh, marks, scale)
+    own, sides, wh = head_own(a3, f3, wh)
+    a3_one, a3_two, own, sides, wh = lax.optimization_barrier((a3_one, a3_two, own, sides, wh))
+    gz4, gh = head(where, a3_one, own, a3_two, sides, wh, marks, scale)
     gz4_one, gz4_two = swapped(gz4, gz4)
+    own = middle_own(gz4, b3)
     gw3 = weight_three(where, gz4, a3_one, a3, a3_two)
-    gz4_one, gz4_two, gw3 = lax.optimization_barrier((gz4_one, gz4_two, gw3))
-    gz2, one, two, gd3 = middle(where, gz4_one, gz4, gz4_two, b3, a3, h2, wd)
+    gz4_one, gz4_two, gw3, own = lax.optimization_barrier((gz4_one, gz4_two, gw3, own))
+    gz2, one, two, gd3 = middle(where, gz4_one, own, gz4_two, b3, a3, h2, wd)
     gz2_one, gz2_two = swapped(one, two)
+    own = last_own(gz2, b2)
     gw2 = weight_two(where, gz2, a2_one, a2, a2_two)
     keep, send = packed(where, gw3, gd3, gw2, gh)
-    gz2_one, gz2_two, send = lax.optimization_barrier((gz2_one, gz2_two, send))
+    gz2_one, gz2_two, send, own = lax.optimization_barrier((gz2_one, gz2_two, send, own))
     came = partner(send)
-    down = last(where, gz2_one, gz2, gz2_two, b2, a2, vp, perm)
+    down = last(where, gz2_one, own, gz2_two, b2, a2, vp, perm)
     pack = joined(where, down, keep, came)
     return finish(pack.reshape(64, ROWS, 128))
 

time: 102 us -> 96.8 us (0.949)
  waiting for transfers between devices: 4.65 us -> 1.79 us
  local copies, waits for them, and re-layouts: 4.47 us -> 3.03 us
  blocking collectives: 38.3 us -> 37.2 us
    ppermute x4, waiting for transfers between devices: 4.63 us -> 1.77 us  [swapped(): return (lax.ppermute(one, 'space', near), two)]
    reshape x6 -> x0, local copies, waits for them, and re-layouts: 2.57 us -> none  [the longest x3 1 us: unpack(): sums[DOWN3:CONV2].reshape(2, 2, 2, 64).transpose(3, 0, 2, 1).reshape(-1)]
    unnamed x29 -> x32, local copies, waits for them, and re-layouts: 1.19 us -> 2.44 us
    all_to_all x1, blocking collectives: 38.3 us -> 37.2 us  [finish(): terms = lax.all_to_all(pack, 'space', 0, 0, tiled=True)]
    pallas_call x9 -> x14, Pallas kernels: 20.8 us -> 21.4 us  [call(): pl.pallas_call(kernel, in_specs=[remote if i in far else scalar if a.dtyp...]
  transfers between devices with their start and end apart: 10 -> 10, of which waited for: 3 -> 2; matrix products, arithmetic and copies ran while one was open for 3% -> 1% of each run, Pallas kernels for 11% -> 15%
where the time goes in v6:
time: 96.8 us; the launch traced here: 96.3 us
  blocking collectives  37.2 us (38%)
  Pallas kernels  27.3 us (28%)
  starting transfers between devices  25.2 us (26%)
  local copies, waits for them, and re-layouts  3.03 us (3%)
  waiting for transfers between devices  1.79 us (2%)
    all_to_all x1, blocking collectives, finish(): terms = lax.all_to_all(pack, 'space', 0, 0, tiled=True)  37.2 us
    pallas_call x14, Pallas kernels, call(): pl.pallas_call(kernel, in_specs=[remote if i in far else scalar if a.dtyp...  21.4 us
    ppermute x4, starting transfers between devices, swapped(): return (lax.ppermute(one, 'space', near), two)  15.3 us
    ppermute x2, starting transfers between devices, partner(): return lax.ppermute(x, 'section', [(0, 1), (1, 0)])  6.36 us
    pallas_call x1, Pallas kernels, first(): pl.pallas_call(first_kernel, in_specs=[pl.BlockSpec(memory_space=pltpu.SM...  5.91 us
    ppermute x4, starting transfers between devices, swapped(): two = lax.ppermute(two, 'space', far)  3.5 us
    unnamed x32, local copies, waits for them, and re-layouts  2.44 us
  transfers between devices with their start and end apart: 10, of which 2 were waited for; matrix products, arithmetic and copies ran while one was open for 1% of the time, Pallas kernels for 15%

profile of v6, /device:TPU:1, one launch (start us, length us, event | category | flops | bytes accessed | tf_op | source)
XLA Modules:
  0.0 96.3 jit_solution(17125482939936324364)
XLA Ops:
  0.6 0.0 copy-start
  0.7 0.1 pad_add_fusion.where_ref
  0.7 5.9 %shard_map.110 = (bf16[2,2,1024,256]{3,2,1,0:T(8,128)(2,1)}, bf16[2,2,256,256]{3,2,1,0:T(8,128)(2,1)S(1)}, bf16[2,256,256]{2,1,0:T(8,128)(2,1)S(1)}, bf16[2,256,256]{2,1,0:T(8,128)(2,1)S(1)}) custom-call(s32[2]{0:T(128)S(1)} %pad_add_fusion.where_ref, bf16[4,32,4,8,512]{4,3,2,1,0:T(8,128)(2,1)} %vol_far.1, bf16[256,64]{1,0:T(8,128)(2,1)} %bitcast.40), custom_call_target="tpu_custom_call" | custom-call | tf_op jit(solution)/shard_map/pallas_call | solution.py:130
  6.7 0.0 copy-start.7
  6.7 2.1 %collective-permute-start = (bf16[2,256,256]{2,1,0:T(8,128)(2,1)S(1)}, bf16[2,256,256]{2,1,0:T(8,128)(2,1)S(1)}, u32[]{:S(2)}, u32[]{:S(2)}) collective-permute-start(bf16[2,256,256]{2,1,0:T(8,128)(2,1)S(1)} %get-tuple-element.48), channel_id=1, source_target_pairs={{0,1},{1,0},{2,3},{3,2},{4,5},{5,4},{6,7},{7,6},{8,9},{9,8},{10,11... | collective-permute-start | bytes 786440 | tf_op jit(solution)/shard_map/ppermute | solution.py:516
  8.8 0.7 collective-permute-start.1
  9.5 0.2 pad_maximum_fusion.w2_ref
  9.8 2.2 %shard_map.111 = (bf16[256,2304]{1,0:T(8,128)(2,1)S(1)}, bf16[256,2304]{1,0:T(8,128)(2,1)S(1)}, bf16[256,2304]{1,0:T(8,128)(2,1)}, bf16[256,2304]{1,0:T(8,128)(2...) custom-call(bf16[27,64,128]{2,1,0:T(8,128)(2,1)S(1)} %pad_maximum_fusion.w2_ref, ...), custom_call_target="tpu_custom_call" | custom-call | tf_op jit(solution)/shard_map/pallas_call | solution.py:72
  11.9 1.1 %shard_map.112.own_ref = f32[2,2,256,256]{3,2,1,0:T(8,128)S(1)} custom-call(bf16[2,2,256,256]{3,2,1,0:T(8,128)(2,1)S(1)} %get-tuple-element.50.a_ref, bf16[256,2304]{1,0:T(8,128)(2,1)S(1)} %get-tuple-element.51.f2_ref), custom_call_target="tpu_custom_call" | custom-call | tf_op jit(solution)/shard_map/pallas_call | solution.py:72
  13.0 1.3 %collective-permute-done.one_ref = bf16[2,256,256]{2,1,0:T(8,128)(2,1)S(1)} collective-permute-done((bf16[2,256,256]{2,1,0:T(8,128)(2,1)S(1)}, bf16[2,256,256]{2,1,0:T(8,128)(2,1)S(1)}, u32[]{:S(2)}, u32[]{:S(2)}) %collective-permute-start) | collective-permute-done | bytes 262176 | tf_op jit(solution)/shard_map/ppermute | solution.py:516
  14.3 0.0 collective-permute-done.1.two_ref
  14.3 2.6 %shard_map.113 = (bf16[4,256,256]{2,1,0:T(8,128)(2,1)}, bf16[256,256]{1,0:T(8,128)(2,1)S(1)}) custom-call(s32[2]{0:T(128)S(1)} %pad_add_fusion.where_ref, bf16[2,256,256]{2,1,0:T(8,128)(2,1)S(1)} %collective-permute-done.one_ref, f32[2,2,256,256]{3,2,1,0:T(8,128)S(1)} %shard_map.112.own_ref, bf16[2,256,256]{2,1,0:T(8,128)(2,1)S(1)} %collective-permute-done.1.two_ref, ...), custom_call_target="tpu_custom_call" | custom-call | tf_op jit(solution)/shard_map/pallas_call | solution.py:72
  16.9 1.3 %collective-permute-start.3 = (bf16[256,256]{1,0:T(8,128)(2,1)S(1)}, bf16[256,256]{1,0:T(8,128)(2,1)}, u32[]{:S(2)}, u32[]{:S(2)}) collective-permute-start(bf16[256,256]{1,0:T(8,128)(2,1)S(1)} %get-tuple-element.56.a_ref.a3_ref), channel_id=1, source_target_pairs={{1,2},{2,1},{3,4},{4,3},{5,6},{6,5},{7,8},{8,7},{9,10},{10,9},{11,... | collective-permute-start | bytes 393224 | tf_op jit(solution)/shard_map/ppermute | solution.py:515
  18.2 6.0 %collective-permute-start.2 = (bf16[256,256]{1,0:T(8,128)(2,1)S(1)}, bf16[256,256]{1,0:T(8,128)(2,1)}, u32[]{:S(2)}, u32[]{:S(2)}) collective-permute-start(bf16[256,256]{1,0:T(8,128)(2,1)S(1)} %get-tuple-element.56.a_ref.a3_ref), channel_id=1, source_target_pairs={{0,1},{1,0},{2,3},{3,2},{4,5},{5,4},{6,7},{7,6},{8,9},{9,8},{10,11... | collective-permute-start | bytes 393224 | tf_op jit(solution)/shard_map/ppermute | solution.py:516
  24.2 1.3 %copy-done.2 = bf16[256,2304]{1,0:T(8,128)(2,1)S(1)} copy-done((bf16[256,2304]{1,0:T(8,128)(2,1)S(1)}, bf16[256,2304]{1,0:T(8,128)(2,1)}, u32[]{:S(2)}) %copy-start.2) | copy-done | bytes 1179672
  25.5 0.8 copy-done.12
  26.3 0.4 shard_map.114
  26.7 0.0 collective-permute-done.3.two_ref
  26.7 0.0 collective-permute-done.2.one_ref
  26.7 2.1 %shard_map.115 = (bf16[256,256]{1,0:T(8,128)(2,1)S(1)}, f32[128,128]{1,0:T(8,128)S(1)}) custom-call(s32[2]{0:T(128)S(1)} %pad_add_fusion.where_ref, bf16[256,256]{1,0:T(8,128)(2,1)} %collective-permute-done.2.one_ref, f32[256,256]{1,0:T(8,128)S(1)} %get-tuple-element.63.own_ref, bf16[256,256]{1,0:T(8,128)(2,1)} %collective-permute-done.3.two_ref, ...), custom_call_target="tpu_custom_call" | custom-call | tf_op jit(solution)/shard_map/pallas_call | solution.py:72
  28.8 0.7 collective-permute-start.5
  29.5 5.8 %collective-permute-start.4 = (bf16[256,256]{1,0:T(8,128)(2,1)S(1)}, bf16[256,256]{1,0:T(8,128)(2,1)S(1)}, u32[]{:S(2)}, u32[]{:S(2)}) collective-permute-start(bf16[256,256]{1,0:T(8,128)(2,1)S(1)} %get-tuple-element.67.g_ref), channel_id=1, source_target_pairs={{0,1},{1,0},{2,3},{3,2},{4,5},{5,4},{6,7},{7,6},{8,9},{9,8},{10,11... | collective-permute-start | bytes 393224 | tf_op jit(solution)/shard_map/ppermute | solution.py:516
  35.4 1.5 %shard_map.116.w3_ref = f32[27,128,128]{2,1,0:T(8,128)S(1)} custom-call(s32[2]{0:T(128)S(1)} %pad_add_fusion.where_ref, bf16[256,256]{1,0:T(8,128)(2,1)S(1)} %get-tuple-element.67.g_ref, bf16[256,256]{1,0:T(8,128)(2,1)} %collective-permute-done.2.one_ref, bf16[256,256]{1,0:T(8,128)(2,1)S(1)} %get-tuple-element.56.a_ref.a3_ref, ...), custom_call_target="tpu_custom_call" | custom-call | tf_op jit(solution)/shard_map/pallas_call | solution.py:72
  36.9 0.4 shard_map.117.own_ref
  37.3 0.0 collective-permute-done.5.two_ref
  37.3 0.5 collective-permute-done.4.one_ref
  37.7 0.2 copy-done.10
  37.9 1.8 %shard_map.118 = (bf16[2,2,256,256]{3,2,1,0:T(8,128)(2,1)S(1)}, bf16[2,256,256]{2,1,0:T(8,128)(2,1)S(1)}, bf16[2,256,256]{2,1,0:T(8,128)(2,1)S(1)}, f32[4,128,128]{2,1,0:T(8,128)S(1)}) custom-call(s32[2]{0:T(128)S(1)} %pad_add_fusion.where_ref, bf16[256,256]{1,0:T(8,128)(2,1)S(1)} %collective-permute-done.4.one_ref, f32[256,256]{1,0:T(8,128)S(1)} %shard_map.117.own_ref, ...), custom_call_target="tpu_custom_call" | custom-call | tf_op jit(solution)/shard_map/pallas_call | solution.py:72
  39.8 1.3 %collective-permute-start.6 = (bf16[2,256,256]{2,1,0:T(8,128)(2,1)S(1)}, bf16[2,256,256]{2,1,0:T(8,128)(2,1)S(1)}, u32[]{:S(2)}, u32[]{:S(2)}) collective-permute-start(bf16[2,256,256]{2,1,0:T(8,128)(2,1)S(1)} %get-tuple-element.73), channel_id=1, source_target_pairs={{0,1},{1,0},{2,3},{3,2},{4,5},{5,4},{6,7},{7,6},{8,9},{9,8},{10,11... | collective-permute-start | bytes 786440 | tf_op jit(solution)/shard_map/ppermute | solution.py:516
  41.1 0.8 collective-permute-start.7
  42.0 2.3 %shard_map.119.w2_ref = f32[7,2,64,128]{3,2,1,0:T(8,128)S(1)} custom-call(s32[2]{0:T(128)S(1)} %pad_add_fusion.where_ref, bf16[2,2,256,256]{3,2,1,0:T(8,128)(2,1)S(1)} %get-tuple-element.77.g_ref, bf16[2,256,256]{2,1,0:T(8,128)(2,1)S(1)} %copy-done.4, bf16[2,2,256,256]{3,2,1,0:T(8,128)(2,1)S(1)} %get-tuple-element.50.a_ref, bf16[2,256,256]{2,1,0:T(8,128)(2,1)S(1)} %copy-done.6), custom_call_target="tpu_custom_call" | custom-call | tf_op jit(solution)/shard_map/pallas_call | solution.py:72
  44.3 0.0 copy-start.9
  44.3 1.1 %shard_map.121.own_ref = f32[2,2,256,256]{3,2,1,0:T(8,128)S(1)} custom-call(bf16[2,2,256,256]{3,2,1,0:T(8,128)(2,1)S(1)} %get-tuple-element.77.g_ref, bf16[256,2304]{1,0:T(8,128)(2,1)S(1)} %get-tuple-element.80.b2_ref), custom_call_target="tpu_custom_call" | custom-call | tf_op jit(solution)/shard_map/pallas_call | solution.py:72
  45.4 1.5 %shard_map.120 = (f32[2560,128]{1,0:T(8,128)S(1)}, bf16[2560,128]{1,0:T(8,128)(2,1)S(1)}) custom-call(s32[2]{0:T(128)S(1)} %pad_add_fusion.where_ref, f32[27,128,128]{2,1,0:T(8,128)S(1)} %shard_map.116.w3_ref, f32[4,128,128]{2,1,0:T(8,128)S(1)} %get-tuple-element.76.d3_ref, f32[7,2,64,128]{3,2,1,0:T(8,128)S(1)} %shard_map.119.w2_ref, ...), custom_call_target="tpu_custom_call" | custom-call | tf_op jit(solution)/shard_map/pallas_call | solution.py:72
  46.9 0.0 collective-permute-done.6.one_ref
  46.9 0.0 collective-permute-done.7.two_ref
  46.9 4.8 %collective-permute-start.8 = (bf16[2560,128]{1,0:T(8,128)(2,1)S(1)}, bf16[2560,128]{1,0:T(8,128)(2,1)S(1)}, u32[]{:S(2)}, u32[]{:S(2)}) collective-permute-start(bf16[2560,128]{1,0:T(8,128)(2,1)S(1)} %get-tuple-element.87), channel_id=1, source_target_pairs={{0,64},{64,0},{1,65},{65,1},{2,66},{66,2},{3,67},{67,3},{4,68},{68... | collective-permute-start | bytes 1966088 | tf_op jit(solution)/shard_map/ppermute | solution.py:520
  51.7 2.4 %shard_map.122.down_ref = f32[64,256]{1,0:T(8,128)S(1)} custom-call(s32[2]{0:T(128)S(1)} %pad_add_fusion.where_ref, bf16[2,256,256]{2,1,0:T(8,128)(2,1)S(1)} %collective-permute-done.6.one_ref, f32[2,2,256,256]{3,2,1,0:T(8,128)S(1)} %shard_map.121.own_ref, bf16[2,256,256]{2,1,0:T(8,128)(2,1)S(1)} %collective-permute-done.7.two_ref, ...), custom_call_target="tpu_custom_call" | custom-call | tf_op jit(solution)/shard_map/pallas_call | solution.py:72
  54.1 0.0 collective-permute-done.8.came_ref
  54.1 0.7 shard_map.123
  54.8 37.2 %all_to_all.5 = bf16[64,40,128]{2,1,0:T(8,128)(2,1)S(1)} all-to-all(bf16[64,40,128]{2,1,0:T(8,128)(2,1)S(1)} %bitcast.34), channel_id=1, replica_groups=mesh['section'=2,'space'=64] {'space'}, dimensions={0} | all-to-all | bytes 1310720 | tf_op jit(solution)/shard_map/all_to_all | solution.py:581
  92.0 0.1 convert_reduce_fusion.sums_ref
  92.2 1.6 %collective-permute-start.9 = (f32[128]{0:T(128)S(1)}, f32[128]{0:T(128)S(1)}, u32[]{:S(2)}, u32[]{:S(2)}) collective-permute-start(f32[128]{0:T(128)S(1)} %slice_bitcast_fusion.1), channel_id=1, source_target_pairs={{0,64},{64,0},{1,65},{65,1},{2,66},{66,2},{3,67},{67,3},{4,68},{68... | collective-permute-start | bytes 1544 | tf_op jit(solution)/shard_map/ppermute | solution.py:520
  93.8 0.6 slice_bitcast_fusion
  94.3 1.4 %shard_map.124 = (f32[7,128]{1,0:T(8,128)S(1)}, f32[4,128]{1,0:T(4,128)}, f32[27,128]{1,0:T(8,128)}) custom-call(f32[40,128]{1,0:T(8,128)S(1)} %convert_reduce_fusion.sums_ref), custom_call_target="tpu_custom_call" | custom-call | tf_op jit(solution)/shard_map/pallas_call | solution.py:72
  95.7 0.0 collective-permute-done.9
  95.7 0.5 fusion
  96.3 0.1 copy-done.14
  (27 shorter events, 0.1 us)
Async XLA Ops:
  0.6 23.6 %copy-start = (s32[4,1,2,128]{3,2,1,0:T(2,128)S(1)}, s32[4,1,2,128]{3,2,1,0:T(2,128)}, u32[]{:S(2)}) copy-start(s32[4,1,2,128]{3,2,1,0:T(2,128)} %param.8) | copy-start | bytes 12292
  0.7 8.7 %copy-start.15 = (bf16[64,64,3,3,3]{1,0,4,3,2:T(8,128)(2,1)S(1)}, bf16[64,64,3,3,3]{1,0,4,3,2:T(8,128)(2,1)}, u32[]{:S(2)}) copy-start(bf16[64,64,3,3,3]{1,0,4,3,2:T(8,128)(2,1)} %param.10) | copy-start | bytes 663556
  0.7 9.0 %copy-start.11 = (bf16[128,64,2,2,2]{0,4,3,2,1:T(2,128)(2,1)S(1)}, bf16[128,64,2,2,2]{0,4,3,2,1:T(2,128)(2,1)}, u32[]{:S(2)}) copy-start(bf16[128,64,2,2,2]{0,4,3,2,1:T(2,128)(2,1)} %param.11) | copy-start | bytes 393220
  0.7 9.0 %copy-start.13 = (bf16[128,4]{0,1:T(4,128)(2,1)S(1)}, bf16[128,4]{0,1:T(4,128)(2,1)}, u32[]{:S(2)}) copy-start(bf16[128,4]{0,1:T(4,128)(2,1)} %param.13) | copy-start | bytes 3076
  6.7 3.1 %copy-start.7 = (bf16[128,128,3,3,3]{1,0,4,3,2:T(8,128)(2,1)S(1)}, bf16[128,128,3,3,3]{1,0,4,3,2:T(8,128)(2,1)}, u32[]{:S(2)}) copy-start(bf16[128,128,3,3,3]{1,0,4,3,2:T(8,128)(2,1)} %param.12) | copy-start | bytes 2654212
  6.7 7.6 %collective-permute-start = (bf16[2,256,256]{2,1,0:T(8,128)(2,1)S(1)}, bf16[2,256,256]{2,1,0:T(8,128)(2,1)S(1)}, u32[]{:S(2)}, u32[]{:S(2)}) collective-permute-start(bf16[2,256,256]{2,1,0:T(8,128)(2,1)S(1)} %get-tuple-element.48), channel_id=1, source_target_pairs={{0,1},{1,0},{2,3},{3,2},{4,5},{5,4},{6,7},{7,6},{8,9},{9,8},{10,11... | collective-permute-start | bytes 786440 | tf_op jit(solution)/shard_map/ppermute | solution.py:516
  8.8 5.5 %collective-permute-start.1 = (bf16[2,256,256]{2,1,0:T(8,128)(2,1)S(1)}, bf16[2,256,256]{2,1,0:T(8,128)(2,1)S(1)}, u32[]{:S(2)}, u32[]{:S(2)}) collective-permute-start(bf16[2,256,256]{2,1,0:T(8,128)(2,1)S(1)} %get-tuple-element.49), channel_id=1, source_target_pairs={{1,2},{2,1},{3,4},{4,3},{5,6},{6,5},{7,8},{8,7},{9,10},{10,9},{11,... | collective-permute-start | bytes 786440 | tf_op jit(solution)/shard_map/ppermute | solution.py:515
  11.9 1.1 %copy-start.8 = (bf16[1024,256]{1,0:T(8,128)(2,1)}, bf16[1024,256]{1,0:T(8,128)(2,1)S(1)}, u32[]{:S(2)}) copy-start(bf16[1024,256]{1,0:T(8,128)(2,1)S(1)} %get-tuple-element.85.perm_ref) | copy-start | bytes 1572868
  14.3 2.6 %copy-start.3 = (bf16[2,256,256]{2,1,0:T(8,128)(2,1)}, bf16[2,256,256]{2,1,0:T(8,128)(2,1)S(1)}, u32[]{:S(2)}) copy-start(bf16[2,256,256]{2,1,0:T(8,128)(2,1)S(1)} %collective-permute-done.one_ref) | copy-start | bytes 786436
  14.3 2.6 %copy-start.5 = (bf16[2,256,256]{2,1,0:T(8,128)(2,1)}, bf16[2,256,256]{2,1,0:T(8,128)(2,1)S(1)}, u32[]{:S(2)}) copy-start(bf16[2,256,256]{2,1,0:T(8,128)(2,1)S(1)} %collective-permute-done.1.two_ref) | copy-start | bytes 786436
  16.9 9.8 %collective-permute-start.3 = (bf16[256,256]{1,0:T(8,128)(2,1)S(1)}, bf16[256,256]{1,0:T(8,128)(2,1)}, u32[]{:S(2)}, u32[]{:S(2)}) collective-permute-start(bf16[256,256]{1,0:T(8,128)(2,1)S(1)} %get-tuple-element.56.a_ref.a3_ref), channel_id=1, source_target_pairs={{1,2},{2,1},{3,4},{4,3},{5,6},{6,5},{7,8},{8,7},{9,10},{10,9},{11,... | collective-permute-start | bytes 393224 | tf_op jit(solution)/shard_map/ppermute | solution.py:515
  18.2 8.5 %collective-permute-start.2 = (bf16[256,256]{1,0:T(8,128)(2,1)S(1)}, bf16[256,256]{1,0:T(8,128)(2,1)}, u32[]{:S(2)}, u32[]{:S(2)}) collective-permute-start(bf16[256,256]{1,0:T(8,128)(2,1)S(1)} %get-tuple-element.56.a_ref.a3_ref), channel_id=1, source_target_pairs={{0,1},{1,0},{2,3},{3,2},{4,5},{5,4},{6,7},{7,6},{8,9},{9,8},{10,11... | collective-permute-start | bytes 393224 | tf_op jit(solution)/shard_map/ppermute | solution.py:516
  24.2 1.3 %copy-start.2 = (bf16[256,2304]{1,0:T(8,128)(2,1)S(1)}, bf16[256,2304]{1,0:T(8,128)(2,1)}, u32[]{:S(2)}) copy-start(bf16[256,2304]{1,0:T(8,128)(2,1)} %get-tuple-element.57.f3_ref) | copy-start | bytes 3538948
  25.5 0.8 copy-start.12
  28.8 8.4 %collective-permute-start.5 = (bf16[256,256]{1,0:T(8,128)(2,1)S(1)}, bf16[256,256]{1,0:T(8,128)(2,1)S(1)}, u32[]{:S(2)}, u32[]{:S(2)}) collective-permute-start(bf16[256,256]{1,0:T(8,128)(2,1)S(1)} %get-tuple-element.67.g_ref), channel_id=1, source_target_pairs={{1,2},{2,1},{3,4},{4,3},{5,6},{6,5},{7,8},{8,7},{9,10},{10,9},{11,... | collective-permute-start | bytes 393224 | tf_op jit(solution)/shard_map/ppermute | solution.py:515
  29.5 8.2 %collective-permute-start.4 = (bf16[256,256]{1,0:T(8,128)(2,1)S(1)}, bf16[256,256]{1,0:T(8,128)(2,1)S(1)}, u32[]{:S(2)}, u32[]{:S(2)}) collective-permute-start(bf16[256,256]{1,0:T(8,128)(2,1)S(1)} %get-tuple-element.67.g_ref), channel_id=1, source_target_pairs={{0,1},{1,0},{2,3},{3,2},{4,5},{5,4},{6,7},{7,6},{8,9},{9,8},{10,11... | collective-permute-start | bytes 393224 | tf_op jit(solution)/shard_map/ppermute | solution.py:516
  36.9 1.0 %copy-start.10 = (bf16[4,256,256]{2,1,0:T(8,128)(2,1)S(1)}, bf16[4,256,256]{2,1,0:T(8,128)(2,1)}, u32[]{:S(2)}) copy-start(bf16[4,256,256]{2,1,0:T(8,128)(2,1)} %get-tuple-element.72.h_ref) | copy-start | bytes 1572868
  37.9 4.0 %copy-start.4 = (bf16[2,256,256]{2,1,0:T(8,128)(2,1)S(1)}, bf16[2,256,256]{2,1,0:T(8,128)(2,1)}, u32[]{:S(2)}) copy-start(bf16[2,256,256]{2,1,0:T(8,128)(2,1)} %copy-done.3) | copy-start | bytes 786436
  37.9 4.0 %copy-start.6 = (bf16[2,256,256]{2,1,0:T(8,128)(2,1)S(1)}, bf16[2,256,256]{2,1,0:T(8,128)(2,1)}, u32[]{:S(2)}) copy-start(bf16[2,256,256]{2,1,0:T(8,128)(2,1)} %copy-done.5) | copy-start | bytes 786436
  39.8 7.1 %collective-permute-start.6 = (bf16[2,256,256]{2,1,0:T(8,128)(2,1)S(1)}, bf16[2,256,256]{2,1,0:T(8,128)(2,1)S(1)}, u32[]{:S(2)}, u32[]{:S(2)}) collective-permute-start(bf16[2,256,256]{2,1,0:T(8,128)(2,1)S(1)} %get-tuple-element.73), channel_id=1, source_target_pairs={{0,1},{1,0},{2,3},{3,2},{4,5},{5,4},{6,7},{7,6},{8,9},{9,8},{10,11... | collective-permute-start | bytes 786440 | tf_op jit(solution)/shard_map/ppermute | solution.py:516
  41.1 5.8 %collective-permute-start.7 = (bf16[2,256,256]{2,1,0:T(8,128)(2,1)S(1)}, bf16[2,256,256]{2,1,0:T(8,128)(2,1)S(1)}, u32[]{:S(2)}, u32[]{:S(2)}) collective-permute-start(bf16[2,256,256]{2,1,0:T(8,128)(2,1)S(1)} %get-tuple-element.74), channel_id=1, source_target_pairs={{1,2},{2,1},{3,4},{4,3},{5,6},{6,5},{7,8},{8,7},{9,10},{10,9},{11,... | collective-permute-start | bytes 786440 | tf_op jit(solution)/shard_map/ppermute | solution.py:515
  44.3 7.4 %copy-start.9 = (bf16[1024,256]{1,0:T(8,128)(2,1)S(1)}, bf16[1024,256]{1,0:T(8,128)(2,1)}, u32[]{:S(2)}) copy-start(bf16[1024,256]{1,0:T(8,128)(2,1)} %copy-done.8) | copy-start | bytes 1572868
  45.4 6.3 %copy-start.1 = (bf16[2,2,1024,256]{3,2,1,0:T(8,128)(2,1)S(1)}, bf16[2,2,1024,256]{3,2,1,0:T(8,128)(2,1)}, u32[]{:S(2)}) copy-start(bf16[2,2,1024,256]{3,2,1,0:T(8,128)(2,1)} %get-tuple-element.84.vp_ref) | copy-start | bytes 6291460
  46.9 7.2 %collective-permute-start.8 = (bf16[2560,128]{1,0:T(8,128)(2,1)S(1)}, bf16[2560,128]{1,0:T(8,128)(2,1)S(1)}, u32[]{:S(2)}, u32[]{:S(2)}) collective-permute-start(bf16[2560,128]{1,0:T(8,128)(2,1)S(1)} %get-tuple-element.87), channel_id=1, source_target_pairs={{0,64},{64,0},{1,65},{65,1},{2,66},{66,2},{3,67},{67,3},{4,68},{68... | collective-permute-start | bytes 1966088 | tf_op jit(solution)/shard_map/ppermute | solution.py:520
  92.2 3.6 %collective-permute-start.9 = (f32[128]{0:T(128)S(1)}, f32[128]{0:T(128)S(1)}, u32[]{:S(2)}, u32[]{:S(2)}) collective-permute-start(f32[128]{0:T(128)S(1)} %slice_bitcast_fusion.1), channel_id=1, source_target_pairs={{0,64},{64,0},{1,65},{65,1},{2,66},{66,2},{3,67},{67,3},{4,68},{68... | collective-permute-start | bytes 1544 | tf_op jit(solution)/shard_map/ppermute | solution.py:520
  95.7 0.6 copy-start.14

commit v7 on v6

--- a/solution.py
+++ b/solution.py
@@ -150,8 +150,10 @@
 
 
 def prepare_kernel(
-    w2_ref, w3_ref, wd_ref, head_ref, f2_ref, b2_ref, f3_ref, b3_ref, perm_ref, d_ref, wh_ref, rows_ref
+    w2_ref, w3_far, wd_ref, head_ref, f2_ref, b2_ref, f3_ref, b3_ref, perm_ref, d_ref, wh_ref, rows_ref, w3_ref, sem
 ):
+    fetch = pltpu.make_async_copy(w3_far, w3_ref, sem)
+    fetch.start()
     low = lax.broadcasted_iota(jnp.int32, (64, 128), 1) < 64
     zero = jnp.zeros((64, 128), F32)
     for d in range(3):
@@ -172,11 +174,6 @@
             for (row, col), block in pairs.items():
                 f2_ref[pl.ds(row * 64, 64), pl.ds(at + col * 128, 128)] = block.astype(BF16)
             b2_ref[:, pl.ds(back, T)] = f2_ref[:, pl.ds(at, T)].astype(F32).T.astype(BF16)
-            for row in range(2):
-                for col in range(2):
-                    block = w3_ref[d * 9 + (col - row + 1) * 3 + j]
-                    f3_ref[pl.ds(row * 128, 128), pl.ds(at + col * 128, 128)] = block
-                    b3_ref[pl.ds(col * 128, 128), pl.ds(back + row * 128, 128)] = block.astype(F32).T.astype(BF16)
     rows_ref[...] = wd_ref[...].astype(F32)
     for d in range(2):
         for p in range(2):
@@ -192,6 +189,16 @@
     to = lax.broadcasted_iota(jnp.int32, (1, 256), 1)
     source = to // 4 % 2 * 512 + to % 2 * 256 + (to // 128 * 16 + to // 8 % 16) * 8 + to // 2 % 2
     perm_ref[...] = jnp.where(lax.broadcasted_iota(jnp.int32, (1024, 256), 0) == source, 1.0, 0.0).astype(BF16)
+    fetch.wait()
+    for d in range(3):
+        for j in range(3):
+            at = (d * 3 + j) * T
+            back = (8 - d * 3 - j) * T
+            for row in range(2):
+                for col in range(2):
+                    block = w3_ref[d * 9 + (col - row + 1) * 3 + j]
+                    f3_ref[pl.ds(row * 128, 128), pl.ds(at + col * 128, 128)] = block
+                    b3_ref[pl.ds(col * 128, 128), pl.ds(back + row * 128, 128)] = block.astype(F32).T.astype(BF16)
 
 
 def prepare(w2, w3, wd, wh):
@@ -200,10 +207,11 @@
 
     return call(
         prepare_kernel,
-        [wide(pltpu.VMEM), wide(pltpu.VMEM), wide(pltpu.HBM), wide(pltpu.VMEM)]
-        + [((1024, 256), BF16, pltpu.VMEM), ((4, T, T), BF16, pltpu.VMEM), ((256, 128), BF16, pltpu.HBM)],
+        [wide(pltpu.VMEM), wide(pltpu.HBM), wide(pltpu.HBM), wide(pltpu.HBM)]
+        + [((1024, 256), BF16, pltpu.HBM), ((4, T, T), BF16, pltpu.VMEM), ((256, 128), BF16, pltpu.HBM)],
         w2, w3, wd, wh,
-        scratch=[pltpu.VMEM((512, 128), F32)],
+        scratch=[pltpu.VMEM((512, 128), F32), pltpu.VMEM((27, 128, 128), BF16), pltpu.SemaphoreType.DMA],
+        far=(1,),
     )
 
 
@@ -225,10 +233,13 @@
     )[0]
 
 
-def second_kernel(where_ref, one_ref, own_ref, two_ref, f2_ref, wd_ref, h_ref, a3_ref, b_ref):
+def second_kernel(
+    where_ref, one_ref, own_ref, two_ref, f2_ref, wd_ref, marks_ref, h_ref, a3_ref, sent_ref, sides_ref, b_ref, m_ref
+):
     for n in range(CROPS):
         for d, plane in enumerate(sorted_out(where_ref, one_ref[n], two_ref[n])):
             at = (2 * n + d) * 3 * T
+            sides_ref[n, d] = plane
             put_three(b_ref, at, three_two(plane))
             rest = dot(f2_ref[:, d * 6 * T : d * 6 * T + 3 * T], b_ref[pl.ds(at, 3 * T), :])
             h = rectified(own_ref[n, d] + rest).astype(BF16)
@@ -237,65 +248,92 @@
     total = dot_tn(wd_ref[0], h_ref[0])
     for k in range(1, 4):
         total += dot_tn(wd_ref[k], h_ref[k])
-    a3_ref[...] = rectified(total).astype(BF16)
-
-
-def second(where, one, own, two, f2, wd):
+    a3 = rectified(total).astype(BF16)
+    a3_ref[...] = a3
+    m_ref[...] = jnp.zeros((16, T), F32)
+    m_ref[pl.ds(0, 2), :] = marks_ref[...].astype(F32)
+    sent_ref[pl.ds(0, T), :] = a3
+    sent_ref[pl.ds(T, 16), :] = m_ref[...].astype(BF16)
+
+
+def second(where, one, own, two, f2, wd, marks):
     return call(
         second_kernel,
-        [((4, T, T), BF16, pltpu.HBM), ((T, T), BF16, pltpu.VMEM)],
-        where, one, own, two, f2, wd,
-        scratch=[pltpu.VMEM((12 * T, T), BF16)],
-    )
-
-
-def head_own_kernel(a_ref, f3_ref, wh_ref, out_ref, sides_ref, wh_out_ref, b_ref):
+        [
+            ((4, T, T), BF16, pltpu.HBM),
+            ((T, T), BF16, pltpu.VMEM),
+            ((T + 16, T), BF16, pltpu.VMEM),
+            ((CROPS, 2, T, T), BF16, pltpu.HBM),
+        ],
+        where, one, own, two, f2, wd, marks,
+        scratch=[pltpu.VMEM((12 * T, T), BF16), pltpu.VMEM((16, T), F32)],
+    )
+
+
+def head_own_kernel(a_ref, f3_ref, wh_ref, out_ref, f3_out_ref, wh_out_ref, b_ref):
     put_three(b_ref, 0, three_three(a_ref[...]))
-    out_ref[...] = dot(f3_ref[:, 3 * T : 6 * T], b_ref[...])
-    sides_ref[:, : 3 * T] = f3_ref[:, : 3 * T]
-    sides_ref[:, 3 * T :] = f3_ref[:, 6 * T :]
+    for k in range(3):
+        out_ref[k] = dot(f3_ref[:, (2 - k) * 3 * T : (3 - k) * 3 * T], b_ref[...])
+    f3_out_ref[...] = f3_ref[...]
     wh_out_ref[...] = wh_ref[...]
 
 
 def head_own(a, f3, wh):
     return call(
         head_own_kernel,
-        [((T, T), F32, pltpu.VMEM), ((T, 6 * T), BF16, pltpu.VMEM), ((256, 128), BF16, pltpu.VMEM)],
+        [((3, T, T), F32, pltpu.VMEM), ((T, 9 * T), BF16, pltpu.VMEM), ((256, 128), BF16, pltpu.VMEM)],
         a, f3, wh,
         scratch=[pltpu.VMEM((3 * T, T), BF16)],
     )
 
 
-def head_kernel(scale, where_ref, one_ref, own_ref, two_ref, sides_ref, wh_ref, marks_ref, gz_ref, gh_ref, b_ref):
-    for k, plane in enumerate(sorted_out(where_ref, one_ref[...], two_ref[...])):
+def head_kernel(
+    scale, where_ref, one_ref, two_ref, near_ref, away_ref, own_ref, f3_ref, wh_ref, marks_ref, gz_ref, gh_ref, b_ref
+):
+    lo, hi = sorted_out(where_ref, one_ref[...], two_ref[...])
+    low_half = where_ref[2] == 0
+    lo2 = jnp.where(low_half, away_ref[...], near_ref[...])
+    hi2 = jnp.where(low_half, near_ref[...], away_ref[...])
+    for k, plane in enumerate((lo2, lo[:T], hi[:T], hi2)):
         put_three(b_ref, k * 3 * T, three_three(plane))
-    top = rectified(own_ref[...] + dot(sides_ref[...], b_ref[...])).astype(BF16)
+    sums = (
+        own_ref[0] + dot(f3_ref[:, : 6 * T], b_ref[: 6 * T, :]),
+        own_ref[1] + dot(f3_ref[:, : 3 * T], b_ref[3 * T : 6 * T, :]) + dot(f3_ref[:, 6 * T :], b_ref[6 * T : 9 * T, :]),
+        own_ref[2] + dot(f3_ref[:, 3 * T :], b_ref[6 * T :, :]),
+    )
+    marks = (lo[T:].astype(F32), marks_ref[...].astype(F32), hi[T:].astype(F32))
     row = lax.broadcasted_iota(jnp.int32, (128, T), 0)
     total = jnp.zeros((128, 128), F32)
-    for h in range(2):
-        mine = top[h * 128 : (h + 1) * 128]
-        logits = dot(wh_ref[pl.ds(128, 128), :], mine)
-        powers = jnp.where(row < 4, jnp.exp(logits), 0.0)
-        share = powers / jnp.sum(powers, axis=0, keepdims=True)
-        chosen = jnp.where(row == marks_ref[pl.ds(h, 1), :], 1.0, 0.0)
-        g = jnp.where(row < 4, (share - chosen) * scale, 0.0).astype(BF16)
-        total += dot_nt(mine, g)
-        gz_ref[pl.ds(h * 128, 128), :] = (dot(wh_ref[pl.ds(0, 128), :], g) * slope(mine)).astype(BF16)
+    for k in range(3):
+        top = rectified(sums[k]).astype(BF16)
+        for h in range(2):
+            mine = top[h * 128 : (h + 1) * 128]
+            logits = dot(wh_ref[pl.ds(128, 128), :], mine)
+            powers = jnp.where(row < 4, jnp.exp(logits), 0.0)
+            share = powers / jnp.sum(powers, axis=0, keepdims=True)
+            chosen = jnp.where(row.astype(F32) == marks[k][h : h + 1], 1.0, 0.0)
+            g = jnp.where(row < 4, (share - chosen) * scale, 0.0)
+            if k != 1:
+                g = jnp.where(where_ref[3 + k // 2] == 1, g, 0.0)
+            g = g.astype(BF16)
+            if k == 1:
+                total += dot_nt(mine, g)
+            gz_ref[k, pl.ds(h * 128, 128), :] = (dot(wh_ref[pl.ds(0, 128), :], g) * slope(mine)).astype(BF16)
     gh_ref[...] = total
 
 
-def head(where, one, own, two, sides, wh, marks, scale):
+def head(where, one, two, near, away, own, f3, wh, marks, scale):
     return call(
         functools.partial(head_kernel, scale),
-        [((T, T), BF16, pltpu.VMEM), ((128, 128), F32, pltpu.VMEM)],
-        where, one, own, two, sides, wh, marks,
-        scratch=[pltpu.VMEM((6 * T, T), BF16)],
+        [((3, T, T), BF16, pltpu.VMEM), ((128, 128), F32, pltpu.VMEM)],
+        where, one, two, near, away, own, f3, wh, marks,
+        scratch=[pltpu.VMEM((12 * T, T), BF16)],
     )
 
 
 def weight_three_kernel(where_ref, g_ref, one_ref, a_ref, two_ref, out_ref, s_ref):
-    put_three(s_ref, 0, three_three(g_ref[...]))
-    lo, hi = sorted_out(where_ref, one_ref[...], two_ref[...])
+    put_three(s_ref, 0, three_three(g_ref[1]))
+    lo, hi = sorted_out(where_ref, one_ref[:T], two_ref[:T])
     for d, a in enumerate((lo, a_ref[...], hi)):
         for j in range(3):
             t = dot_nt(s_ref[pl.ds((2 - j) * T, T), :], a)
@@ -313,27 +351,10 @@
     )[0]
 
 
-def middle_own_kernel(g_ref, b3_ref, out_ref, b_ref):
-    put_three(b_ref, 0, three_three(g_ref[...]))
-    out_ref[...] = dot(b3_ref[:, 3 * T : 6 * T], b_ref[...])
-
-
-def middle_own(g, b3):
-    return call(
-        middle_own_kernel,
-        [((T, T), F32, pltpu.VMEM)],
-        g, b3,
-        scratch=[pltpu.VMEM((3 * T, T), BF16)],
-    )[0]
-
-
-def middle_kernel(
-    where_ref, one_ref, own_ref, two_ref, b3_ref, a3_ref, h_ref, wd_ref, gz2_ref, gone_ref, gtwo_ref, gd_ref, b_ref
-):
-    rest = own_ref[...]
-    for k, plane in enumerate(sorted_out(where_ref, one_ref[...], two_ref[...])):
-        put_three(b_ref, k * 3 * T, three_three(plane))
-        rest += dot(b3_ref[:, k * 6 * T : k * 6 * T + 3 * T], b_ref[pl.ds(k * 3 * T, 3 * T), :])
+def middle_kernel(where_ref, g_ref, b3_ref, a3_ref, h_ref, wd_ref, gz2_ref, gone_ref, gtwo_ref, gd_ref, b_ref):
+    for k in range(3):
+        put_three(b_ref, k * 3 * T, three_three(g_ref[k]))
+    rest = dot(b3_ref[...], b_ref[...])
     gy = (rest * slope(a3_ref[...])).astype(BF16)
     for d in range(2):
         for p in range(2):
@@ -349,7 +370,7 @@
         gd_ref[k] = dot_nt(gy[:128], h_ref[k, :128]) + dot_nt(gy[128:], h_ref[k, 128:])
 
 
-def middle(where, one, own, two, b3, a3, h, wd):
+def middle(where, g, b3, a3, h, wd):
     return call(
         middle_kernel,
         [
@@ -358,15 +379,14 @@
             ((CROPS, T, T), BF16, pltpu.VMEM),
             ((4, 128, 128), F32, pltpu.VMEM),
         ],
-        where, one, own, two, b3, a3, h, wd,
-        scratch=[pltpu.VMEM((6 * T, T), BF16)],
-    )
-
-
-def weight_two_kernel(where_ref, g_ref, one_ref, a_ref, two_ref, out_ref, gs_ref, as_ref):
+        where, g, b3, a3, h, wd,
+        scratch=[pltpu.VMEM((9 * T, T), BF16)],
+    )
+
+
+def weight_two_kernel(g_ref, a_ref, sides_ref, out_ref, gs_ref, as_ref):
     for n in range(CROPS):
-        lo, hi = sorted_out(where_ref, one_ref[n], two_ref[n])
-        planes = (lo, a_ref[n, 0], a_ref[n, 1], hi)
+        planes = (sides_ref[n, 0], a_ref[n, 0], a_ref[n, 1], sides_ref[n, 1])
         for d in range(2):
             at = (2 * n + d) * T
             for j, (left, right) in enumerate(three_two(g_ref[n, d])):
@@ -396,11 +416,11 @@
         out_ref[g, 1] = jnp.where(low, jnp.where(block, turned[0], four[1]), jnp.where(block, turned[2], four[3]))
 
 
-def weight_two(where, g, one, a, two):
+def weight_two(g, a, sides):
     return call(
         weight_two_kernel,
         [((7, 2, 64, 128), F32, pltpu.VMEM)],
-        where, g, one, a, two,
+        g, a, sides,
         scratch=[pltpu.VMEM((3, T, 4 * T), BF16), pltpu.VMEM((3, T, 4 * T), BF16)],
     )[0]
 
@@ -516,6 +536,14 @@
     return lax.ppermute(one, "space", near), two
 
 
+def swapped_two(x):
+    count = lax.axis_size("space")
+    near = [(i, i ^ 2) for i in range(count)]
+    away = [(i, ((i + 2) ^ 2) - 2) for i in range(2, count - 2)]
+    away = lax.ppermute(x, "space", away)
+    return lax.ppermute(x, "space", near), away
+
+
 def partner(x):
     return lax.ppermute(x, "section", [(0, 1), (1, 0)])
 
@@ -588,7 +616,8 @@
     voxels = labels.shape[0] * labels.shape[1] * count * labels.shape[2] * labels.shape[3]
     scale = 1.0 / math.sqrt(voxels)
     sec = lax.axis_index("section").astype(jnp.int32)
-    where = jnp.stack([sec, lax.axis_index("space").astype(jnp.int32) % 2])
+    space = lax.axis_index("space").astype(jnp.int32)
+    where = jnp.stack([sec, space % 2, space % 4 // 2, jnp.minimum(space, 1), jnp.minimum(count - 1 - space, 1)])
 
     w1 = down_weight_two.transpose(1, 2, 3, 4, 0).reshape(256, 64)
     wd = down_weight_three.transpose(1, 2, 3, 4, 0).reshape(512, 128)
@@ -603,19 +632,19 @@
     f2, b2, f3, b3, perm, wd, wh = prepare(w2, w3, wd, w_head.T)
     own = second_own(a2, f2)
     a2_one, a2_two, own = lax.optimization_barrier((a2_one, a2_two, own))
-    h2, a3 = second(where, a2_one, own, a2_two, f2, wd)
-    a3_one, a3_two = swapped(a3, a3)
-    own, sides, wh = head_own(a3, f3, wh)
-    a3_one, a3_two, own, sides, wh = lax.optimization_barrier((a3_one, a3_two, own, sides, wh))
-    gz4, gh = head(where, a3_one, own, a3_two, sides, wh, marks, scale)
-    gz4_one, gz4_two = swapped(gz4, gz4)
-    own = middle_own(gz4, b3)
+    h2, a3, sent, sides = second(where, a2_one, own, a2_two, f2, wd, marks)
+    a3_one, a3_two = swapped(sent, sent)
+    a3_near, a3_away = swapped_two(a3)
+    own, f3, wh = head_own(a3, f3, wh)
+    a3_one, a3_two, a3_near, a3_away, own, f3, wh = lax.optimization_barrier(
+        (a3_one, a3_two, a3_near, a3_away, own, f3, wh)
+    )
+    gz4, gh = head(where, a3_one, a3_two, a3_near, a3_away, own, f3, wh, marks, scale)
+    gz2, one, two, gd3 = middle(where, gz4, b3, a3, h2, wd)
     gw3 = weight_three(where, gz4, a3_one, a3, a3_two)
-    gz4_one, gz4_two, gw3, own = lax.optimization_barrier((gz4_one, gz4_two, gw3, own))
-    gz2, one, two, gd3 = middle(where, gz4_one, own, gz4_two, b3, a3, h2, wd)
     gz2_one, gz2_two = swapped(one, two)
     own = last_own(gz2, b2)
-    gw2 = weight_two(where, gz2, a2_one, a2, a2_two)
+    gw2 = weight_two(gz2, a2, sides)
     keep, send = packed(where, gw3, gd3, gw2, gh)
     gz2_one, gz2_two, send, own = lax.optimization_barrier((gz2_one, gz2_two, send, own))
     came = partner(send)

time: 96.8 us -> 93.4 us (0.965)
  waiting for transfers between devices: 1.79 us -> 6.2 us
  blocking collectives: 37.2 us -> 33.5 us
  starting transfers between devices: 25.2 us -> 22.7 us
  local copies, waits for them, and re-layouts: 3.03 us -> 0.81 us
    ppermute x0 -> x2, starting transfers between devices: none -> 7.67 us  [the longest x1 7.02 us: swapped_two(): return (lax.ppermute(x, 'space', near), away)]
    ppermute x4 -> x3, starting transfers between devices: 15.3 us -> 8.87 us  [swapped(): return (lax.ppermute(one, 'space', near), two)]
    ppermute x0 -> x2, waiting for transfers between devices: none -> 6.14 us  [the longest x1 6.14 us: swapped_two(): return (lax.ppermute(x, 'space', near), away)]
    all_to_all x1, blocking collectives: 37.2 us -> 33.5 us  [finish(): terms = lax.all_to_all(pack, 'space', 0, 0, tiled=True)]
    ppermute x2, starting transfers between devices: 6.36 us -> 3.85 us  [partner(): return lax.ppermute(x, 'section', [(0, 1), (1, 0)])]
    unnamed x32 -> x26, local copies, waits for them, and re-layouts: 2.44 us -> 0.13 us
    ppermute x4 -> x3, waiting for transfers between devices: 1.77 us -> 0.04 us  [swapped(): return (lax.ppermute(one, 'space', near), two)]
    ppermute x4 -> x3, starting transfers between devices: 3.5 us -> 2.31 us  [swapped(): two = lax.ppermute(two, 'space', far)]
  transfers between devices with their start and end apart: 10 -> 10, of which waited for: 2 -> 1; matrix products, arithmetic and copies ran while one was open for 1% -> 1% of each run, Pallas kernels for 15% -> 15%
where the time goes in v7:
time: 93.4 us; the launch traced here: 93.1 us
  blocking collectives  33.5 us (36%)
  Pallas kernels  28.1 us (30%)
  starting transfers between devices  22.7 us (24%)
  waiting for transfers between devices  6.2 us (7%)
  between operations  0.98 us (1%)
    all_to_all x1, blocking collectives, finish(): terms = lax.all_to_all(pack, 'space', 0, 0, tiled=True)  33.5 us
    pallas_call x13, Pallas kernels, call(): pl.pallas_call(kernel, in_specs=[remote if i in far else scalar if a.dtyp...  22.2 us
    ppermute x3, starting transfers between devices, swapped(): return (lax.ppermute(one, 'space', near), two)  8.87 us
    ppermute x1, starting transfers between devices, swapped_two(): return (lax.ppermute(x, 'space', near), away)  7.02 us
    ppermute x1, waiting for transfers between devices, swapped_two(): return (lax.ppermute(x, 'space', near), away)  6.14 us
    pallas_call x1, Pallas kernels, first(): pl.pallas_call(first_kernel, in_specs=[pl.BlockSpec(memory_space=pltpu.SM...  5.9 us
    ppermute x2, starting transfers between devices, partner(): return lax.ppermute(x, 'section', [(0, 1), (1, 0)])  3.85 us
    ppermute x3, starting transfers between devices, swapped(): two = lax.ppermute(two, 'space', far)  2.31 us
  transfers between devices with their start and end apart: 10, of which 1 were waited for; matrix products, arithmetic and copies ran while one was open for 1% of the time, Pallas kernels for 15%

profile of v7, /device:TPU:1, one launch (start us, length us, event | category | flops | bytes accessed | tf_op | source)
XLA Modules:
  0.0 93.1 jit_solution(15773813920531150812)
XLA Ops:
  0.6 0.0 copy-start
  0.7 0.1 stack.23.where_ref
  0.8 5.9 %shard_map.110 = (bf16[2,2,1024,256]{3,2,1,0:T(8,128)(2,1)}, bf16[2,2,256,256]{3,2,1,0:T(8,128)(2,1)S(1)}, bf16[2,256,256]{2,1,0:T(8,128)(2,1)S(1)}, bf16[2,256,256]{2,1,0:T(8,128)(2,1)S(1)}) custom-call(s32[5]{0:T(128)S(1)} %stack.23.where_ref, bf16[4,32,4,8,512]{4,3,2,1,0:T(8,128)(2,1)} %vol_far.1, bf16[256,64]{1,0:T(8,128)(2,1)} %bitcast.43), custom_call_target="tpu_custom_call" | custom-call | tf_op jit(solution)/shard_map/pallas_call | solution.py:130
  6.7 2.1 %collective-permute-start = (bf16[2,256,256]{2,1,0:T(8,128)(2,1)S(1)}, bf16[2,256,256]{2,1,0:T(8,128)(2,1)S(1)}, u32[]{:S(2)}, u32[]{:S(2)}) collective-permute-start(bf16[2,256,256]{2,1,0:T(8,128)(2,1)S(1)} %get-tuple-element.48), channel_id=1, source_target_pairs={{0,1},{1,0},{2,3},{3,2},{4,5},{5,4},{6,7},{7,6},{8,9},{9,8},{10,11... | collective-permute-start | bytes 786440 | tf_op jit(solution)/shard_map/ppermute | solution.py:536
  8.8 0.7 collective-permute-start.1
  9.5 0.0 copy-done.12
  9.5 0.2 pad_maximum_fusion.w2_ref
  9.8 3.4 %shard_map.111 = (bf16[256,2304]{1,0:T(8,128)(2,1)S(1)}, bf16[256,2304]{1,0:T(8,128)(2,1)}, bf16[256,2304]{1,0:T(8,128)(2,1)}, bf16[256,2304]{1,0:T(8,128)(2,1)}...) custom-call(bf16[27,64,128]{2,1,0:T(8,128)(2,1)S(1)} %pad_maximum_fusion.w2_ref, ...), custom_call_target="tpu_custom_call" | custom-call | tf_op jit(solution)/shard_map/pallas_call | solution.py:72
  13.1 1.1 %shard_map.112.own_ref = f32[2,2,256,256]{3,2,1,0:T(8,128)S(1)} custom-call(bf16[2,2,256,256]{3,2,1,0:T(8,128)(2,1)S(1)} %get-tuple-element.50.a_ref, bf16[256,2304]{1,0:T(8,128)(2,1)S(1)} %get-tuple-element.51.f2_ref), custom_call_target="tpu_custom_call" | custom-call | tf_op jit(solution)/shard_map/pallas_call | solution.py:72
  14.2 0.0 copy-done
  14.3 0.0 collective-permute-done.one_ref
  14.3 0.0 collective-permute-done.1.two_ref
  14.3 2.6 %shard_map.113 = (bf16[4,256,256]{2,1,0:T(8,128)(2,1)}, bf16[256,256]{1,0:T(8,128)(2,1)S(1)}, bf16[272,256]{1,0:T(8,128)(2,1)S(1)}, bf16[2,2,256,256]{3,2,1,0:T(8,128)(2,1)}) custom-call(s32[5]{0:T(128)S(1)} %stack.23.where_ref, bf16[2,256,256]{2,1,0:T(8,128)(2,1)S(1)} %collective-permute-done.one_ref, f32[2,2,256,256]{3,2,1,0:T(8,128)S(1)} %shard_map.112.own_ref, ...), custom_call_target="tpu_custom_call" | custom-call | tf_op jit(solution)/shard_map/pallas_call | solution.py:72
  16.9 0.7 collective-permute-start.3
  17.5 6.7 %collective-permute-start.2 = (bf16[272,256]{1,0:T(8,128)(2,1)S(1)}, bf16[272,256]{1,0:T(8,128)(2,1)S(1)}, u32[]{:S(2)}, u32[]{:S(2)}) collective-permute-start(bf16[272,256]{1,0:T(8,128)(2,1)S(1)} %get-tuple-element.56), channel_id=1, source_target_pairs={{0,1},{1,0},{2,3},{3,2},{4,5},{5,4},{6,7},{7,6},{8,9},{9,8},{10,11... | collective-permute-start | bytes 417800 | tf_op jit(solution)/shard_map/ppermute | solution.py:536
  24.2 0.7 collective-permute-start.5
  24.9 7.0 %collective-permute-start.4 = (bf16[256,256]{1,0:T(8,128)(2,1)S(1)}, bf16[256,256]{1,0:T(8,128)(2,1)S(1)}, u32[]{:S(2)}, u32[]{:S(2)}) collective-permute-start(bf16[256,256]{1,0:T(8,128)(2,1)S(1)} %get-tuple-element.57.a_ref.a3_ref), channel_id=1, source_target_pairs={{0,2},{1,3},{2,0},{3,1},{4,6},{5,7},{6,4},{7,5},{8,10},{9,11},{10,... | collective-permute-start | bytes 393224 | tf_op jit(solution)/shard_map/ppermute | solution.py:544
  31.9 0.0 copy-done.9
  31.9 0.6 shard_map.114
  32.5 0.0 collective-permute-done.5.away_ref
  32.5 6.1 %collective-permute-done.4.near_ref = bf16[256,256]{1,0:T(8,128)(2,1)S(1)} collective-permute-done((bf16[256,256]{1,0:T(8,128)(2,1)S(1)}, bf16[256,256]{1,0:T(8,128)(2,1)S(1)}, u32[]{:S(2)}, u32[]{:S(2)}) %collective-permute-start.4) | collective-permute-done | bytes 131104 | tf_op jit(solution)/shard_map/ppermute | solution.py:544
  38.7 0.0 collective-permute-done.3.two_ref
  38.7 0.0 collective-permute-done.2.one_ref
  38.7 2.6 %shard_map.115 = (bf16[3,256,256]{2,1,0:T(8,128)(2,1)S(1)}, f32[128,128]{1,0:T(8,128)S(1)}) custom-call(s32[5]{0:T(128)S(1)} %stack.23.where_ref, bf16[272,256]{1,0:T(8,128)(2,1)S(1)} %collective-permute-done.2.one_ref, bf16[272,256]{1,0:T(8,128)(2,1)S(1)} %collective-permute-done.3.two_ref, bf16[256,256]{1,0:T(8,128)(2,1)S(1)} %collective-permute-done.4.near_ref, ...), custom_call_target="tpu_custom_call" | custom-call | tf_op jit(solution)/shard_map/pallas_call | solution.py:72
  41.3 2.1 %shard_map.116 = (bf16[2,2,256,256]{3,2,1,0:T(8,128)(2,1)S(1)}, bf16[2,256,256]{2,1,0:T(8,128)(2,1)S(1)}, bf16[2,256,256]{2,1,0:T(8,128)(2,1)S(1)}, f32[4,128,128]{2,1,0:T(8,128)S(1)}) custom-call(s32[5]{0:T(128)S(1)} %stack.23.where_ref, bf16[3,256,256]{2,1,0:T(8,128)(2,1)S(1)} %get-tuple-element.70.g_ref, bf16[256,2304]{1,0:T(8,128)(2,1)S(1)} %copy-done.3, ...), custom_call_target="tpu_custom_call" | custom-call | tf_op jit(solution)/shard_map/pallas_call | solution.py:72
  43.4 0.1 collective-permute-start.6
  43.5 1.0 %collective-permute-start.7 = (bf16[2,256,256]{2,1,0:T(8,128)(2,1)S(1)}, bf16[2,256,256]{2,1,0:T(8,128)(2,1)S(1)}, u32[]{:S(2)}, u32[]{:S(2)}) collective-permute-start(bf16[2,256,256]{2,1,0:T(8,128)(2,1)S(1)} %get-tuple-element.74), channel_id=1, source_target_pairs={{1,2},{2,1},{3,4},{4,3},{5,6},{6,5},{7,8},{8,7},{9,10},{10,9},{11,... | collective-permute-start | bytes 786440 | tf_op jit(solution)/shard_map/ppermute | solution.py:535
  44.5 1.1 %shard_map.117.w3_ref = f32[27,128,128]{2,1,0:T(8,128)S(1)} custom-call(s32[5]{0:T(128)S(1)} %stack.23.where_ref, bf16[3,256,256]{2,1,0:T(8,128)(2,1)S(1)} %get-tuple-element.70.g_ref, bf16[272,256]{1,0:T(8,128)(2,1)S(1)} %collective-permute-done.2.one_ref, bf16[256,256]{1,0:T(8,128)(2,1)S(1)} %get-tuple-element.57.a_ref.a3_ref, ...), custom_call_target="tpu_custom_call" | custom-call | tf_op jit(solution)/shard_map/pallas_call | solution.py:72
  45.6 0.0 copy-start.1
  45.6 0.0 copy-done.6
  45.6 1.7 %shard_map.118.w2_ref = f32[7,2,64,128]{3,2,1,0:T(8,128)S(1)} custom-call(bf16[2,2,256,256]{3,2,1,0:T(8,128)(2,1)S(1)} %get-tuple-element.76.g_ref, bf16[2,2,256,256]{3,2,1,0:T(8,128)(2,1)S(1)} %get-tuple-element.50.a_ref, bf16[2,2,256,256]{3,2,1,0:T(8,128)(2,1)S(1)} %copy-done.6), custom_call_target="tpu_custom_call" | custom-call | tf_op jit(solution)/shard_map/pallas_call | solution.py:72
  47.3 1.1 %shard_map.120.own_ref = f32[2,2,256,256]{3,2,1,0:T(8,128)S(1)} custom-call(bf16[2,2,256,256]{3,2,1,0:T(8,128)(2,1)S(1)} %get-tuple-element.76.g_ref, bf16[256,2304]{1,0:T(8,128)(2,1)S(1)} %copy-done.1), custom_call_target="tpu_custom_call" | custom-call | tf_op jit(solution)/shard_map/pallas_call | solution.py:72
  48.4 1.5 %shard_map.119 = (f32[2560,128]{1,0:T(8,128)S(1)}, bf16[2560,128]{1,0:T(8,128)(2,1)S(1)}) custom-call(s32[5]{0:T(128)S(1)} %stack.23.where_ref, f32[27,128,128]{2,1,0:T(8,128)S(1)} %shard_map.117.w3_ref, f32[4,128,128]{2,1,0:T(8,128)S(1)} %get-tuple-element.75.d3_ref, f32[7,2,64,128]{3,2,1,0:T(8,128)S(1)} %shard_map.118.w2_ref, ...), custom_call_target="tpu_custom_call" | custom-call | tf_op jit(solution)/shard_map/pallas_call | solution.py:72
  49.9 0.0 collective-permute-done.6.one_ref
  49.9 0.0 collective-permute-done.7.two_ref
  49.9 2.3 %collective-permute-start.8 = (bf16[2560,128]{1,0:T(8,128)(2,1)S(1)}, bf16[2560,128]{1,0:T(8,128)(2,1)S(1)}, u32[]{:S(2)}, u32[]{:S(2)}) collective-permute-start(bf16[2560,128]{1,0:T(8,128)(2,1)S(1)} %get-tuple-element.87), channel_id=1, source_target_pairs={{0,64},{64,0},{1,65},{65,1},{2,66},{66,2},{3,67},{67,3},{4,68},{68... | collective-permute-start | bytes 1966088 | tf_op jit(solution)/shard_map/ppermute | solution.py:548
  52.2 0.0 copy-done.5
  52.2 2.4 %shard_map.121.down_ref = f32[64,256]{1,0:T(8,128)S(1)} custom-call(s32[5]{0:T(128)S(1)} %stack.23.where_ref, bf16[2,256,256]{2,1,0:T(8,128)(2,1)S(1)} %collective-permute-done.6.one_ref, f32[2,2,256,256]{3,2,1,0:T(8,128)S(1)} %shard_map.120.own_ref, bf16[2,256,256]{2,1,0:T(8,128)(2,1)S(1)} %collective-permute-done.7.two_ref, ...), custom_call_target="tpu_custom_call" | custom-call | tf_op jit(solution)/shard_map/pallas_call | solution.py:72
  54.6 0.0 collective-permute-done.8.came_ref
  54.7 0.7 shard_map.122
  55.4 33.5 %all_to_all.5 = bf16[64,40,128]{2,1,0:T(8,128)(2,1)S(1)} all-to-all(bf16[64,40,128]{2,1,0:T(8,128)(2,1)S(1)} %bitcast.37), channel_id=1, replica_groups=mesh['section'=2,'space'=64] {'space'}, dimensions={0} | all-to-all | bytes 1310720 | tf_op jit(solution)/shard_map/all_to_all | solution.py:609
  88.8 0.1 convert_reduce_fusion.sums_ref
  88.9 1.6 %collective-permute-start.9 = (f32[128]{0:T(128)S(1)}, f32[128]{0:T(128)S(1)}, u32[]{:S(2)}, u32[]{:S(2)}) collective-permute-start(f32[128]{0:T(128)S(1)} %slice_bitcast_fusion.1), channel_id=1, source_target_pairs={{0,64},{64,0},{1,65},{65,1},{2,66},{66,2},{3,67},{67,3},{4,68},{68... | collective-permute-start | bytes 1544 | tf_op jit(solution)/shard_map/ppermute | solution.py:548
  90.5 0.6 slice_bitcast_fusion
  91.1 1.4 %shard_map.123 = (f32[7,128]{1,0:T(8,128)S(1)}, f32[4,128]{1,0:T(4,128)}, f32[27,128]{1,0:T(8,128)}) custom-call(f32[40,128]{1,0:T(8,128)S(1)} %convert_reduce_fusion.sums_ref), custom_call_target="tpu_custom_call" | custom-call | tf_op jit(solution)/shard_map/pallas_call | solution.py:72
  92.5 0.0 collective-permute-done.9
  92.5 0.5 fusion
  93.0 0.1 copy-done.11
  (20 shorter events, 0.1 us)
Async XLA Ops:
  0.6 13.6 %copy-start = (s32[4,1,2,128]{3,2,1,0:T(2,128)S(1)}, s32[4,1,2,128]{3,2,1,0:T(2,128)}, u32[]{:S(2)}) copy-start(s32[4,1,2,128]{3,2,1,0:T(2,128)} %param.8) | copy-start | bytes 12292
  0.8 8.7 %copy-start.12 = (bf16[64,64,3,3,3]{1,0,4,3,2:T(8,128)(2,1)S(1)}, bf16[64,64,3,3,3]{1,0,4,3,2:T(8,128)(2,1)}, u32[]{:S(2)}) copy-start(bf16[64,64,3,3,3]{1,0,4,3,2:T(8,128)(2,1)} %param.10) | copy-start | bytes 663556
  0.8 9.0 %copy-start.8 = (bf16[128,64,2,2,2]{0,4,3,2,1:T(2,128)(2,1)S(1)}, bf16[128,64,2,2,2]{0,4,3,2,1:T(2,128)(2,1)}, u32[]{:S(2)}) copy-start(bf16[128,64,2,2,2]{0,4,3,2,1:T(2,128)(2,1)} %param.11) | copy-start | bytes 393220
  0.8 9.0 %copy-start.10 = (bf16[128,4]{0,1:T(4,128)(2,1)S(1)}, bf16[128,4]{0,1:T(4,128)(2,1)}, u32[]{:S(2)}) copy-start(bf16[128,4]{0,1:T(4,128)(2,1)} %param.13) | copy-start | bytes 3076
  6.7 7.6 %collective-permute-start = (bf16[2,256,256]{2,1,0:T(8,128)(2,1)S(1)}, bf16[2,256,256]{2,1,0:T(8,128)(2,1)S(1)}, u32[]{:S(2)}, u32[]{:S(2)}) collective-permute-start(bf16[2,256,256]{2,1,0:T(8,128)(2,1)S(1)} %get-tuple-element.48), channel_id=1, source_target_pairs={{0,1},{1,0},{2,3},{3,2},{4,5},{5,4},{6,7},{7,6},{8,9},{9,8},{10,11... | collective-permute-start | bytes 786440 | tf_op jit(solution)/shard_map/ppermute | solution.py:536
  8.8 5.5 %collective-permute-start.1 = (bf16[2,256,256]{2,1,0:T(8,128)(2,1)S(1)}, bf16[2,256,256]{2,1,0:T(8,128)(2,1)S(1)}, u32[]{:S(2)}, u32[]{:S(2)}) collective-permute-start(bf16[2,256,256]{2,1,0:T(8,128)(2,1)S(1)} %get-tuple-element.49), channel_id=1, source_target_pairs={{1,2},{2,1},{3,4},{4,3},{5,6},{6,5},{7,8},{8,7},{9,10},{10,9},{11,... | collective-permute-start | bytes 786440 | tf_op jit(solution)/shard_map/ppermute | solution.py:535
  14.3 17.6 %copy-start.4 = (bf16[256,2304]{1,0:T(8,128)(2,1)S(1)}, bf16[256,2304]{1,0:T(8,128)(2,1)}, u32[]{:S(2)}) copy-start(bf16[256,2304]{1,0:T(8,128)(2,1)} %get-tuple-element.58.f3_ref) | copy-start | bytes 3538948
  14.3 17.6 %copy-start.9 = (bf16[256,128]{1,0:T(8,128)(2,1)S(1)}, bf16[256,128]{1,0:T(8,128)(2,1)}, u32[]{:S(2)}) copy-start(bf16[256,128]{1,0:T(8,128)(2,1)} %get-tuple-element.59.wh_ref) | copy-start | bytes 196612
  16.9 21.8 %collective-permute-start.3 = (bf16[272,256]{1,0:T(8,128)(2,1)S(1)}, bf16[272,256]{1,0:T(8,128)(2,1)S(1)}, u32[]{:S(2)}, u32[]{:S(2)}) collective-permute-start(bf16[272,256]{1,0:T(8,128)(2,1)S(1)} %get-tuple-element.56), channel_id=1, source_target_pairs={{1,2},{2,1},{3,4},{4,3},{5,6},{6,5},{7,8},{8,7},{9,10},{10,9},{11,... | collective-permute-start | bytes 417800 | tf_op jit(solution)/shard_map/ppermute | solution.py:535
  17.5 21.1 %collective-permute-start.2 = (bf16[272,256]{1,0:T(8,128)(2,1)S(1)}, bf16[272,256]{1,0:T(8,128)(2,1)S(1)}, u32[]{:S(2)}, u32[]{:S(2)}) collective-permute-start(bf16[272,256]{1,0:T(8,128)(2,1)S(1)} %get-tuple-element.56), channel_id=1, source_target_pairs={{0,1},{1,0},{2,3},{3,2},{4,5},{5,4},{6,7},{7,6},{8,9},{9,8},{10,11... | collective-permute-start | bytes 417800 | tf_op jit(solution)/shard_map/ppermute | solution.py:536
  24.2 8.3 %collective-permute-start.5 = (bf16[256,256]{1,0:T(8,128)(2,1)S(1)}, bf16[256,256]{1,0:T(8,128)(2,1)S(1)}, u32[]{:S(2)}, u32[]{:S(2)}) collective-permute-start(bf16[256,256]{1,0:T(8,128)(2,1)S(1)} %get-tuple-element.57.a_ref.a3_ref), channel_id=1, source_target_pairs={{2,4},{3,5},{4,2},{5,3},{6,8},{7,9},{8,6},{9,7},{10,12},{11,13},{1... | collective-permute-start | bytes 393224 | tf_op jit(solution)/shard_map/ppermute | solution.py:543
  24.9 13.8 %collective-permute-start.4 = (bf16[256,256]{1,0:T(8,128)(2,1)S(1)}, bf16[256,256]{1,0:T(8,128)(2,1)S(1)}, u32[]{:S(2)}, u32[]{:S(2)}) collective-permute-start(bf16[256,256]{1,0:T(8,128)(2,1)S(1)} %get-tuple-element.57.a_ref.a3_ref), channel_id=1, source_target_pairs={{0,2},{1,3},{2,0},{3,1},{4,6},{5,7},{6,4},{7,5},{8,10},{9,11},{10,... | collective-permute-start | bytes 393224 | tf_op jit(solution)/shard_map/ppermute | solution.py:544
  32.5 8.8 %copy-start.3 = (bf16[256,2304]{1,0:T(8,128)(2,1)S(1)}, bf16[256,2304]{1,0:T(8,128)(2,1)}, u32[]{:S(2)}) copy-start(bf16[256,2304]{1,0:T(8,128)(2,1)} %get-tuple-element.71.b3_ref) | copy-start | bytes 3538948
  32.5 8.8 %copy-start.7 = (bf16[4,256,256]{2,1,0:T(8,128)(2,1)S(1)}, bf16[4,256,256]{2,1,0:T(8,128)(2,1)}, u32[]{:S(2)}) copy-start(bf16[4,256,256]{2,1,0:T(8,128)(2,1)} %get-tuple-element.72.h_ref) | copy-start | bytes 1572868
  43.4 2.2 %copy-start.6 = (bf16[2,2,256,256]{3,2,1,0:T(8,128)(2,1)S(1)}, bf16[2,2,256,256]{3,2,1,0:T(8,128)(2,1)}, u32[]{:S(2)}) copy-start(bf16[2,2,256,256]{3,2,1,0:T(8,128)(2,1)} %get-tuple-element.77.sides_ref) | copy-start | bytes 1572868
  43.4 6.5 %collective-permute-start.6 = (bf16[2,256,256]{2,1,0:T(8,128)(2,1)S(1)}, bf16[2,256,256]{2,1,0:T(8,128)(2,1)S(1)}, u32[]{:S(2)}, u32[]{:S(2)}) collective-permute-start(bf16[2,256,256]{2,1,0:T(8,128)(2,1)S(1)} %get-tuple-element.73), channel_id=1, source_target_pairs={{0,1},{1,0},{2,3},{3,2},{4,5},{5,4},{6,7},{7,6},{8,9},{9,8},{10,11... | collective-permute-start | bytes 786440 | tf_op jit(solution)/shard_map/ppermute | solution.py:536
  43.5 6.4 %collective-permute-start.7 = (bf16[2,256,256]{2,1,0:T(8,128)(2,1)S(1)}, bf16[2,256,256]{2,1,0:T(8,128)(2,1)S(1)}, u32[]{:S(2)}, u32[]{:S(2)}) collective-permute-start(bf16[2,256,256]{2,1,0:T(8,128)(2,1)S(1)} %get-tuple-element.74), channel_id=1, source_target_pairs={{1,2},{2,1},{3,4},{4,3},{5,6},{6,5},{7,8},{8,7},{9,10},{10,9},{11,... | collective-permute-start | bytes 786440 | tf_op jit(solution)/shard_map/ppermute | solution.py:535
  45.6 1.8 %copy-start.1 = (bf16[256,2304]{1,0:T(8,128)(2,1)S(1)}, bf16[256,2304]{1,0:T(8,128)(2,1)}, u32[]{:S(2)}) copy-start(bf16[256,2304]{1,0:T(8,128)(2,1)} %get-tuple-element.80.b2_ref) | copy-start | bytes 3538948
  47.3 4.9 %copy-start.5 = (bf16[1024,256]{1,0:T(8,128)(2,1)S(1)}, bf16[1024,256]{1,0:T(8,128)(2,1)}, u32[]{:S(2)}) copy-start(bf16[1024,256]{1,0:T(8,128)(2,1)} %get-tuple-element.85.perm_ref) | copy-start | bytes 1572868
  48.4 3.8 %copy-start.2 = (bf16[2,2,1024,256]{3,2,1,0:T(8,128)(2,1)S(1)}, bf16[2,2,1024,256]{3,2,1,0:T(8,128)(2,1)}, u32[]{:S(2)}) copy-start(bf16[2,2,1024,256]{3,2,1,0:T(8,128)(2,1)} %get-tuple-element.84.vp_ref) | copy-start | bytes 6291460
  49.9 4.7 %collective-permute-start.8 = (bf16[2560,128]{1,0:T(8,128)(2,1)S(1)}, bf16[2560,128]{1,0:T(8,128)(2,1)S(1)}, u32[]{:S(2)}, u32[]{:S(2)}) collective-permute-start(bf16[2560,128]{1,0:T(8,128)(2,1)S(1)} %get-tuple-element.87), channel_id=1, source_target_pairs={{0,64},{64,0},{1,65},{65,1},{2,66},{66,2},{3,67},{67,3},{4,68},{68... | collective-permute-start | bytes 1966088 | tf_op jit(solution)/shard_map/ppermute | solution.py:548
  88.9 3.6 %collective-permute-start.9 = (f32[128]{0:T(128)S(1)}, f32[128]{0:T(128)S(1)}, u32[]{:S(2)}, u32[]{:S(2)}) collective-permute-start(f32[128]{0:T(128)S(1)} %slice_bitcast_fusion.1), channel_id=1, source_target_pairs={{0,64},{64,0},{1,65},{65,1},{2,66},{66,2},{3,67},{67,3},{4,68},{68... | collective-permute-start | bytes 1544 | tf_op jit(solution)/shard_map/ppermute | solution.py:548
  92.5 0.6 copy-start.11

commit v8 on v7

--- a/solution.py
+++ b/solution.py
@@ -89,8 +89,7 @@
 ):
     steps = [(n, d) for n in range(CROPS) for d in range(2)]
     fetches = [
-        pltpu.make_async_copy(vol_far.at[CROPS * where_ref[0] + n, :, pl.ds(2 * d, 2)], vol_ref.at[i], in_sems.at[i])
-        for i, (n, d) in enumerate(steps)
+        pltpu.make_async_copy(vol_far.at[CROPS * where_ref[0] + n], vol_ref.at[n], in_sems.at[n]) for n in range(CROPS)
     ]
     stores = [
         pltpu.make_async_copy(vp_ref.at[i], vp_far.at[n, d], out_sems.at[i]) for i, (n, d) in enumerate(steps)
@@ -108,9 +107,10 @@
     for h in range(4):
         wt_ref[pl.ds(h * 64, 64), :] = jnp.where(height // 2 == h, w, 0.0).astype(BF16)
     for i, (n, d) in enumerate(steps):
-        fetches[i].wait()
+        if d == 0:
+            fetches[n].wait()
         for k in range(2):
-            v = vol_ref[i, :, k].astype(F32).reshape(256, 512).astype(BF16)
+            v = vol_ref[n, :, 2 * d + k].astype(F32).reshape(256, 512).astype(BF16)
             s = dot(v, sort_ref[...]).astype(BF16)
             vp_ref[i, pl.ds(k * 512, 256), :] = s[:, :256]
             vp_ref[i, pl.ds(k * 512 + 256, 256), :] = s[:, 256:]
@@ -140,9 +140,9 @@
         scratch_shapes=[
             pltpu.VMEM((512, 512), BF16),
             pltpu.VMEM((256, 1024), BF16),
-            pltpu.VMEM((4, 32, 2, 8, 512), BF16),
+            pltpu.VMEM((CROPS, 32, 4, 8, 512), BF16),
             pltpu.VMEM((4, 1024, 256), BF16),
-            pltpu.SemaphoreType.DMA((4,)),
+            pltpu.SemaphoreType.DMA((CROPS,)),
             pltpu.SemaphoreType.DMA((4,)),
         ],
         compiler_params=params(),
@@ -567,7 +567,11 @@
     return same + exact(jnp.where(row == start + 1, 1.0, 0.0), jnp.where(here, 0.0, turned))
 
 
-def unpack_kernel(sums_ref, two_ref, three_ref, conv_ref, x_ref):
+def unpack_kernel(sums_ref, came_ref, down_ref, two_ref, three_ref, conv_ref, head_ref, x_ref):
+    down_ref[...] = sums_ref[pl.ds(DOWN2, 1), :] + came_ref[...]
+    last = sums_ref[pl.ds(DOWN2 - 1, 1), :]
+    for k in range(4):
+        head_ref[k] = jnp.sum(jnp.where(lax.broadcasted_iota(jnp.int32, (1, 128), 1) == 96 + k, last, 0.0))
     zero = jnp.zeros((128, 128), F32)
     x_ref[...] = zero
     x_ref[pl.ds(0, DOWN3), :] = sums_ref[pl.ds(0, DOWN3), :]
@@ -589,26 +593,23 @@
     three_ref[...] = flat(x_ref[...], 8)[:4]
 
 
-def unpack(sums, down):
-    two, three, conv = call(
+def unpack(sums, came):
+    spec = pl.BlockSpec(memory_space=pltpu.VMEM)
+    down, two, three, conv, head = pl.pallas_call(
         unpack_kernel,
-        [((7, 128), F32, pltpu.VMEM), ((4, 128), F32, pltpu.HBM), ((27, 128), F32, pltpu.HBM)],
-        sums,
-        scratch=[pltpu.VMEM((128, 128), F32)],
-    )
-    return (
-        down,
-        two.reshape(-1)[: 27 * 32],
-        three.reshape(-1),
-        conv.reshape(-1),
-        sums[DOWN2 - 1, 96:100],
-    )
+        in_specs=[spec] * 2,
+        out_specs=[spec] * 4 + [pl.BlockSpec(memory_space=pltpu.SMEM)],
+        out_shape=[pltpu.HBM((rows, 128), F32) for rows in (1, 7, 4, 27)] + [jax.ShapeDtypeStruct((4,), F32)],
+        scratch_shapes=[pltpu.VMEM((128, 128), F32)],
+        compiler_params=params(),
+    )(sums, came)
+    return down.reshape(-1), two.reshape(-1)[: 27 * 32], three.reshape(-1), conv.reshape(-1), head
 
 
 def finish(pack):
     terms = lax.all_to_all(pack, "space", 0, 0, tiled=True)
     sums = jnp.sum(terms.astype(F32), axis=0)
-    return unpack(sums, sums[DOWN2] + partner(sums[DOWN2 + 1]))
+    return unpack(sums, partner(sums[DOWN2 + 1 :]))
 
 
 def per_device(volume, labels, down_weight_two, w_conv_two, down_weight_three, w_conv_three, w_head):
@@ -631,7 +632,7 @@
     a2_one, a2_two = swapped(one, two)
     f2, b2, f3, b3, perm, wd, wh = prepare(w2, w3, wd, w_head.T)
     own = second_own(a2, f2)
-    a2_one, a2_two, own = lax.optimization_barrier((a2_one, a2_two, own))
+    a2_two, a2_one, own = lax.optimization_barrier((a2_two, a2_one, own))
     h2, a3, sent, sides = second(where, a2_one, own, a2_two, f2, wd, marks)
     a3_one, a3_two = swapped(sent, sent)
     a3_near, a3_away = swapped_two(a3)
@@ -646,7 +647,7 @@
     own = last_own(gz2, b2)
     gw2 = weight_two(gz2, a2, sides)
     keep, send = packed(where, gw3, gd3, gw2, gh)
-    gz2_one, gz2_two, send, own = lax.optimization_barrier((gz2_one, gz2_two, send, own))
+    gz2_two, gz2_one, send, own = lax.optimization_barrier((gz2_two, gz2_one, send, own))
     came = partner(send)
     down = last(where, gz2_one, own, gz2_two, b2, a2, vp, perm)
     pack = joined(where, down, keep, came)

time: 93.4 us -> 91.9 us (0.984)
  blocking collectives: 33.5 us -> 31.9 us
  starting transfers between devices: 22.7 us -> 23.9 us
    all_to_all x1, blocking collectives: 33.5 us -> 31.9 us  [finish(): terms = lax.all_to_all(pack, 'space', 0, 0, tiled=True)]
    pallas_call x0 -> x1, Pallas kernels: none -> 1.42 us  [unpack(): pl.pallas_call(unpack_kernel, in_specs=[spec] * 2, out_specs=[spec] * 4 +...]
    ppermute x2, starting transfers between devices: 3.85 us -> 5.27 us  [partner(): return lax.ppermute(x, 'section', [(0, 1), (1, 0)])]
    pallas_call x13 -> x12, Pallas kernels: 22.2 us -> 20.8 us  [call(): pl.pallas_call(kernel, in_specs=[remote if i in far else scalar if a.dtyp...]
    ppermute x1, waiting for transfers between devices: 6.14 us -> 4.99 us  [swapped_two(): return (lax.ppermute(x, 'space', near), away)]
  transfers between devices with their start and end apart: 10 -> 10, of which waited for: 1 -> 3; matrix products, arithmetic and copies ran while one was open for 1% -> 0% of each run, Pallas kernels for 15% -> 14%
where the time goes in v8:
time: 91.9 us; the launch traced here: 91.6 us
  blocking collectives  31.9 us (35%)
  Pallas kernels  27.5 us (30%)
  starting transfers between devices  23.9 us (26%)
  waiting for transfers between devices  6.75 us (7%)
  between operations  1.12 us (1%)
    all_to_all x1, blocking collectives, finish(): terms = lax.all_to_all(pack, 'space', 0, 0, tiled=True)  31.9 us
    pallas_call x12, Pallas kernels, call(): pl.pallas_call(kernel, in_specs=[remote if i in far else scalar if a.dtyp...  20.8 us
    ppermute x3, starting transfers between devices, swapped(): return (lax.ppermute(one, 'space', near), two)  9.19 us
    ppermute x1, starting transfers between devices, swapped_two(): return (lax.ppermute(x, 'space', near), away)  6.61 us
    pallas_call x1, Pallas kernels, first(): pl.pallas_call(first_kernel, in_specs=[pl.BlockSpec(memory_space=pltpu.SM...  5.3 us
    ppermute x2, starting transfers between devices, partner(): return lax.ppermute(x, 'section', [(0, 1), (1, 0)])  5.27 us
    ppermute x1, waiting for transfers between devices, swapped_two(): return (lax.ppermute(x, 'space', near), away)  4.99 us
    ppermute x3, starting transfers between devices, swapped(): two = lax.ppermute(two, 'space', far)  2.14 us
  transfers between devices with their start and end apart: 10, of which 3 were waited for; matrix products, arithmetic and copies ran while one was open for 0% of the time, Pallas kernels for 14%

profile of v8, /device:TPU:1, one launch (start us, length us, event | category | flops | bytes accessed | tf_op | source)
XLA Modules:
  0.0 91.6 jit_solution(3135175440212708262)
XLA Ops:
  0.6 0.0 copy-start
  0.7 0.1 stack.23.where_ref
  0.8 5.3 %shard_map.110 = (bf16[2,2,1024,256]{3,2,1,0:T(8,128)(2,1)}, bf16[2,2,256,256]{3,2,1,0:T(8,128)(2,1)S(1)}, bf16[2,256,256]{2,1,0:T(8,128)(2,1)S(1)}, bf16[2,256,256]{2,1,0:T(8,128)(2,1)S(1)}) custom-call(s32[5]{0:T(128)S(1)} %stack.23.where_ref, bf16[4,32,4,8,512]{4,3,2,1,0:T(8,128)(2,1)} %vol_far.1, bf16[256,64]{1,0:T(8,128)(2,1)} %bitcast.35), custom_call_target="tpu_custom_call" | custom-call | tf_op jit(solution)/shard_map/pallas_call | solution.py:130
  6.1 0.7 collective-permute-start
  6.8 4.6 %collective-permute-start.1 = (bf16[2,256,256]{2,1,0:T(8,128)(2,1)S(1)}, bf16[2,256,256]{2,1,0:T(8,128)(2,1)S(1)}, u32[]{:S(2)}, u32[]{:S(2)}) collective-permute-start(bf16[2,256,256]{2,1,0:T(8,128)(2,1)S(1)} %get-tuple-element.51), channel_id=1, source_target_pairs={{0,1},{1,0},{2,3},{3,2},{4,5},{5,4},{6,7},{7,6},{8,9},{9,8},{10,11... | collective-permute-start | bytes 786440 | tf_op jit(solution)/shard_map/ppermute | solution.py:536
  11.3 0.0 copy-done.11
  11.3 0.2 pad_maximum_fusion.w2_ref
  11.6 0.0 copy-done.8
  11.6 0.0 copy-done.10
  11.6 3.4 %shard_map.111 = (bf16[256,2304]{1,0:T(8,128)(2,1)S(1)}, bf16[256,2304]{1,0:T(8,128)(2,1)}, bf16[256,2304]{1,0:T(8,128)(2,1)}, bf16[256,2304]{1,0:T(8,128)(2,1)}...) custom-call(bf16[27,64,128]{2,1,0:T(8,128)(2,1)S(1)} %pad_maximum_fusion.w2_ref, ...), custom_call_target="tpu_custom_call" | custom-call | tf_op jit(solution)/shard_map/pallas_call | solution.py:72
  15.0 1.1 %shard_map.112.own_ref = f32[2,2,256,256]{3,2,1,0:T(8,128)S(1)} custom-call(bf16[2,2,256,256]{3,2,1,0:T(8,128)(2,1)S(1)} %get-tuple-element.52.a_ref, bf16[256,2304]{1,0:T(8,128)(2,1)S(1)} %get-tuple-element.53.f2_ref), custom_call_target="tpu_custom_call" | custom-call | tf_op jit(solution)/shard_map/pallas_call | solution.py:72
  16.1 0.0 copy-done
  16.1 0.0 collective-permute-done.two_ref
  16.1 0.9 %collective-permute-done.1.one_ref = bf16[2,256,256]{2,1,0:T(8,128)(2,1)S(1)} collective-permute-done((bf16[2,256,256]{2,1,0:T(8,128)(2,1)S(1)}, bf16[2,256,256]{2,1,0:T(8,128)(2,1)S(1)}, u32[]{:S(2)}, u32[]{:S(2)}) %collective-permute-start.1) | collective-permute-done | bytes 262176 | tf_op jit(solution)/shard_map/ppermute | solution.py:536
  17.1 2.6 %shard_map.113 = (bf16[4,256,256]{2,1,0:T(8,128)(2,1)}, bf16[256,256]{1,0:T(8,128)(2,1)S(1)}, bf16[272,256]{1,0:T(8,128)(2,1)S(1)}, bf16[2,2,256,256]{3,2,1,0:T(8,128)(2,1)}) custom-call(s32[5]{0:T(128)S(1)} %stack.23.where_ref, bf16[2,256,256]{2,1,0:T(8,128)(2,1)S(1)} %collective-permute-done.1.one_ref, f32[2,2,256,256]{3,2,1,0:T(8,128)S(1)} %shard_map.112.own_ref, ...), custom_call_target="tpu_custom_call" | custom-call | tf_op jit(solution)/shard_map/pallas_call | solution.py:72
  19.6 0.7 collective-permute-start.3
  20.3 3.4 %collective-permute-start.2 = (bf16[272,256]{1,0:T(8,128)(2,1)S(1)}, bf16[272,256]{1,0:T(8,128)(2,1)S(1)}, u32[]{:S(2)}, u32[]{:S(2)}) collective-permute-start(bf16[272,256]{1,0:T(8,128)(2,1)S(1)} %get-tuple-element.58), channel_id=1, source_target_pairs={{0,1},{1,0},{2,3},{3,2},{4,5},{5,4},{6,7},{7,6},{8,9},{9,8},{10,11... | collective-permute-start | bytes 417800 | tf_op jit(solution)/shard_map/ppermute | solution.py:536
  23.7 0.7 collective-permute-start.5
  24.4 6.6 %collective-permute-start.4 = (bf16[256,256]{1,0:T(8,128)(2,1)S(1)}, bf16[256,256]{1,0:T(8,128)(2,1)S(1)}, u32[]{:S(2)}, u32[]{:S(2)}) collective-permute-start(bf16[256,256]{1,0:T(8,128)(2,1)S(1)} %get-tuple-element.59.a_ref.a3_ref), channel_id=1, source_target_pairs={{0,2},{1,3},{2,0},{3,1},{4,6},{5,7},{6,4},{7,5},{8,10},{9,11},{10,... | collective-permute-start | bytes 393224 | tf_op jit(solution)/shard_map/ppermute | solution.py:544
  31.0 0.0 copy-done.4
  31.0 0.0 copy-done.9
  31.0 0.6 shard_map.114
  31.6 0.0 copy-start.3
  31.6 0.0 copy-start.7
  31.6 0.0 collective-permute-done.5.away_ref
  31.6 5.0 %collective-permute-done.4.near_ref = bf16[256,256]{1,0:T(8,128)(2,1)S(1)} collective-permute-done((bf16[256,256]{1,0:T(8,128)(2,1)S(1)}, bf16[256,256]{1,0:T(8,128)(2,1)S(1)}, u32[]{:S(2)}, u32[]{:S(2)}) %collective-permute-start.4) | collective-permute-done | bytes 131104 | tf_op jit(solution)/shard_map/ppermute | solution.py:544
  36.6 0.0 collective-permute-done.3.two_ref
  36.6 0.0 collective-permute-done.2.one_ref
  36.6 2.6 %shard_map.115 = (bf16[3,256,256]{2,1,0:T(8,128)(2,1)S(1)}, f32[128,128]{1,0:T(8,128)S(1)}) custom-call(s32[5]{0:T(128)S(1)} %stack.23.where_ref, bf16[272,256]{1,0:T(8,128)(2,1)S(1)} %collective-permute-done.2.one_ref, bf16[272,256]{1,0:T(8,128)(2,1)S(1)} %collective-permute-done.3.two_ref, bf16[256,256]{1,0:T(8,128)(2,1)S(1)} %collective-permute-done.4.near_ref, ...), custom_call_target="tpu_custom_call" | custom-call | tf_op jit(solution)/shard_map/pallas_call | solution.py:72
  39.3 2.1 %shard_map.116 = (bf16[2,2,256,256]{3,2,1,0:T(8,128)(2,1)S(1)}, bf16[2,256,256]{2,1,0:T(8,128)(2,1)S(1)}, bf16[2,256,256]{2,1,0:T(8,128)(2,1)S(1)}, f32[4,128,128]{2,1,0:T(8,128)S(1)}) custom-call(s32[5]{0:T(128)S(1)} %stack.23.where_ref, bf16[3,256,256]{2,1,0:T(8,128)(2,1)S(1)} %get-tuple-element.72.g_ref, bf16[256,2304]{1,0:T(8,128)(2,1)S(1)} %copy-done.3, ...), custom_call_target="tpu_custom_call" | custom-call | tf_op jit(solution)/shard_map/pallas_call | solution.py:72
  41.3 0.8 collective-permute-start.6
  42.2 1.2 %collective-permute-start.7 = (bf16[2,256,256]{2,1,0:T(8,128)(2,1)S(1)}, bf16[2,256,256]{2,1,0:T(8,128)(2,1)S(1)}, u32[]{:S(2)}, u32[]{:S(2)}) collective-permute-start(bf16[2,256,256]{2,1,0:T(8,128)(2,1)S(1)} %get-tuple-element.76), channel_id=1, source_target_pairs={{0,1},{1,0},{2,3},{3,2},{4,5},{5,4},{6,7},{7,6},{8,9},{9,8},{10,11... | collective-permute-start | bytes 786440 | tf_op jit(solution)/shard_map/ppermute | solution.py:536
  43.3 1.1 %shard_map.117.w3_ref = f32[27,128,128]{2,1,0:T(8,128)S(1)} custom-call(s32[5]{0:T(128)S(1)} %stack.23.where_ref, bf16[3,256,256]{2,1,0:T(8,128)(2,1)S(1)} %get-tuple-element.72.g_ref, bf16[272,256]{1,0:T(8,128)(2,1)S(1)} %collective-permute-done.2.one_ref, bf16[256,256]{1,0:T(8,128)(2,1)S(1)} %get-tuple-element.59.a_ref.a3_ref, ...), custom_call_target="tpu_custom_call" | custom-call | tf_op jit(solution)/shard_map/pallas_call | solution.py:72
  44.4 1.7 %shard_map.118.w2_ref = f32[7,2,64,128]{3,2,1,0:T(8,128)S(1)} custom-call(bf16[2,2,256,256]{3,2,1,0:T(8,128)(2,1)S(1)} %get-tuple-element.78.g_ref, bf16[2,2,256,256]{3,2,1,0:T(8,128)(2,1)S(1)} %get-tuple-element.52.a_ref, bf16[2,2,256,256]{3,2,1,0:T(8,128)(2,1)S(1)} %copy-done.6), custom_call_target="tpu_custom_call" | custom-call | tf_op jit(solution)/shard_map/pallas_call | solution.py:72
  46.2 1.1 %shard_map.120.own_ref = f32[2,2,256,256]{3,2,1,0:T(8,128)S(1)} custom-call(bf16[2,2,256,256]{3,2,1,0:T(8,128)(2,1)S(1)} %get-tuple-element.78.g_ref, bf16[256,2304]{1,0:T(8,128)(2,1)S(1)} %copy-done.1), custom_call_target="tpu_custom_call" | custom-call | tf_op jit(solution)/shard_map/pallas_call | solution.py:72
  47.3 1.5 %shard_map.119 = (f32[2560,128]{1,0:T(8,128)S(1)}, bf16[2560,128]{1,0:T(8,128)(2,1)S(1)}) custom-call(s32[5]{0:T(128)S(1)} %stack.23.where_ref, f32[27,128,128]{2,1,0:T(8,128)S(1)} %shard_map.117.w3_ref, f32[4,128,128]{2,1,0:T(8,128)S(1)} %get-tuple-element.77.d3_ref, f32[7,2,64,128]{3,2,1,0:T(8,128)S(1)} %shard_map.118.w2_ref, ...), custom_call_target="tpu_custom_call" | custom-call | tf_op jit(solution)/shard_map/pallas_call | solution.py:72
  48.8 0.0 collective-permute-done.6.two_ref
  48.8 0.0 collective-permute-done.7.one_ref
  48.8 3.7 %collective-permute-start.8 = (bf16[2560,128]{1,0:T(8,128)(2,1)S(1)}, bf16[2560,128]{1,0:T(8,128)(2,1)S(1)}, u32[]{:S(2)}, u32[]{:S(2)}) collective-permute-start(bf16[2560,128]{1,0:T(8,128)(2,1)S(1)} %get-tuple-element.89), channel_id=1, source_target_pairs={{0,64},{64,0},{1,65},{65,1},{2,66},{66,2},{3,67},{67,3},{4,68},{68... | collective-permute-start | bytes 1966088 | tf_op jit(solution)/shard_map/ppermute | solution.py:548
  52.5 0.0 copy-done.5
  52.5 2.4 %shard_map.121.down_ref = f32[64,256]{1,0:T(8,128)S(1)} custom-call(s32[5]{0:T(128)S(1)} %stack.23.where_ref, bf16[2,256,256]{2,1,0:T(8,128)(2,1)S(1)} %collective-permute-done.7.one_ref, f32[2,2,256,256]{3,2,1,0:T(8,128)S(1)} %shard_map.120.own_ref, bf16[2,256,256]{2,1,0:T(8,128)(2,1)S(1)} %collective-permute-done.6.two_ref, ...), custom_call_target="tpu_custom_call" | custom-call | tf_op jit(solution)/shard_map/pallas_call | solution.py:72
  54.9 0.0 collective-permute-done.8.came_ref
  54.9 0.7 shard_map.122
  55.6 31.9 %all_to_all.5 = bf16[64,40,128]{2,1,0:T(8,128)(2,1)S(1)} all-to-all(bf16[64,40,128]{2,1,0:T(8,128)(2,1)S(1)} %bitcast.30), channel_id=1, replica_groups=mesh['section'=2,'space'=64] {'space'}, dimensions={0} | all-to-all | bytes 1310720 | tf_op jit(solution)/shard_map/all_to_all | solution.py:610
  87.5 0.1 convert_reduce_fusion.sums_ref
  87.6 1.6 %collective-permute-start.9 = (f32[1,128]{1,0:T(1,128)S(1)}, f32[1,128]{1,0:T(1,128)S(1)}, u32[]{:S(2)}, u32[]{:S(2)}) collective-permute-start(f32[1,128]{1,0:T(1,128)S(1)} %slice.8), channel_id=1, source_target_pairs={{0,64},{64,0},{1,65},{65,1},{2,66},{66,2},{3,67},{67,3},{4,68},{68... | collective-permute-start | bytes 1544 | tf_op jit(solution)/shard_map/ppermute | solution.py:548
  89.2 0.8 collective-permute-done.9.came_ref
  90.0 1.4 %shard_map.123 = (f32[1,128]{1,0:T(1,128)}, f32[7,128]{1,0:T(8,128)}, f32[4,128]{1,0:T(4,128)}, f32[27,128]{1,0:T(8,128)}, f32[4]{0:T(128)}) custom-call(f32[40,128]{1,0:T(8,128)S(1)} %convert_reduce_fusion.sums_ref, f32[1,128]{1,0:T(1,128)S(1)} %collective-permute-done.9.came_ref), custom_call_target="tpu_custom_call" | custom-call | tf_op jit(solution)/shard_map/pallas_call | solution.py:598
  (16 shorter events, 0.0 us)
Async XLA Ops:
  0.6 15.5 %copy-start = (s32[4,1,2,128]{3,2,1,0:T(2,128)S(1)}, s32[4,1,2,128]{3,2,1,0:T(2,128)}, u32[]{:S(2)}) copy-start(s32[4,1,2,128]{3,2,1,0:T(2,128)} %param.8) | copy-start | bytes 12292
  0.8 10.6 %copy-start.11 = (bf16[64,64,3,3,3]{1,0,4,3,2:T(8,128)(2,1)S(1)}, bf16[64,64,3,3,3]{1,0,4,3,2:T(8,128)(2,1)}, u32[]{:S(2)}) copy-start(bf16[64,64,3,3,3]{1,0,4,3,2:T(8,128)(2,1)} %param.10) | copy-start | bytes 663556
  0.8 10.8 %copy-start.8 = (bf16[128,64,2,2,2]{0,4,3,2,1:T(2,128)(2,1)S(1)}, bf16[128,64,2,2,2]{0,4,3,2,1:T(2,128)(2,1)}, u32[]{:S(2)}) copy-start(bf16[128,64,2,2,2]{0,4,3,2,1:T(2,128)(2,1)} %param.11) | copy-start | bytes 393220
  0.8 10.8 %copy-start.10 = (bf16[128,4]{0,1:T(4,128)(2,1)S(1)}, bf16[128,4]{0,1:T(4,128)(2,1)}, u32[]{:S(2)}) copy-start(bf16[128,4]{0,1:T(4,128)(2,1)} %param.13) | copy-start | bytes 3076
  6.1 10.0 %collective-permute-start = (bf16[2,256,256]{2,1,0:T(8,128)(2,1)S(1)}, bf16[2,256,256]{2,1,0:T(8,128)(2,1)S(1)}, u32[]{:S(2)}, u32[]{:S(2)}) collective-permute-start(bf16[2,256,256]{2,1,0:T(8,128)(2,1)S(1)} %get-tuple-element.50), channel_id=1, source_target_pairs={{1,2},{2,1},{3,4},{4,3},{5,6},{6,5},{7,8},{8,7},{9,10},{10,9},{11,... | collective-permute-start | bytes 786440 | tf_op jit(solution)/shard_map/ppermute | solution.py:535
  6.8 10.3 %collective-permute-start.1 = (bf16[2,256,256]{2,1,0:T(8,128)(2,1)S(1)}, bf16[2,256,256]{2,1,0:T(8,128)(2,1)S(1)}, u32[]{:S(2)}, u32[]{:S(2)}) collective-permute-start(bf16[2,256,256]{2,1,0:T(8,128)(2,1)S(1)} %get-tuple-element.51), channel_id=1, source_target_pairs={{0,1},{1,0},{2,3},{3,2},{4,5},{5,4},{6,7},{7,6},{8,9},{9,8},{10,11... | collective-permute-start | bytes 786440 | tf_op jit(solution)/shard_map/ppermute | solution.py:536
  17.1 14.0 %copy-start.4 = (bf16[256,2304]{1,0:T(8,128)(2,1)S(1)}, bf16[256,2304]{1,0:T(8,128)(2,1)}, u32[]{:S(2)}) copy-start(bf16[256,2304]{1,0:T(8,128)(2,1)} %get-tuple-element.60.f3_ref) | copy-start | bytes 3538948
  17.1 14.0 %copy-start.9 = (bf16[256,128]{1,0:T(8,128)(2,1)S(1)}, bf16[256,128]{1,0:T(8,128)(2,1)}, u32[]{:S(2)}) copy-start(bf16[256,128]{1,0:T(8,128)(2,1)} %get-tuple-element.61.wh_ref) | copy-start | bytes 196612
  19.6 17.0 %collective-permute-start.3 = (bf16[272,256]{1,0:T(8,128)(2,1)S(1)}, bf16[272,256]{1,0:T(8,128)(2,1)S(1)}, u32[]{:S(2)}, u32[]{:S(2)}) collective-permute-start(bf16[272,256]{1,0:T(8,128)(2,1)S(1)} %get-tuple-element.58), channel_id=1, source_target_pairs={{1,2},{2,1},{3,4},{4,3},{5,6},{6,5},{7,8},{8,7},{9,10},{10,9},{11,... | collective-permute-start | bytes 417800 | tf_op jit(solution)/shard_map/ppermute | solution.py:535
  20.3 16.3 %collective-permute-start.2 = (bf16[272,256]{1,0:T(8,128)(2,1)S(1)}, bf16[272,256]{1,0:T(8,128)(2,1)S(1)}, u32[]{:S(2)}, u32[]{:S(2)}) collective-permute-start(bf16[272,256]{1,0:T(8,128)(2,1)S(1)} %get-tuple-element.58), channel_id=1, source_target_pairs={{0,1},{1,0},{2,3},{3,2},{4,5},{5,4},{6,7},{7,6},{8,9},{9,8},{10,11... | collective-permute-start | bytes 417800 | tf_op jit(solution)/shard_map/ppermute | solution.py:536
  23.7 7.9 %collective-permute-start.5 = (bf16[256,256]{1,0:T(8,128)(2,1)S(1)}, bf16[256,256]{1,0:T(8,128)(2,1)S(1)}, u32[]{:S(2)}, u32[]{:S(2)}) collective-permute-start(bf16[256,256]{1,0:T(8,128)(2,1)S(1)} %get-tuple-element.59.a_ref.a3_ref), channel_id=1, source_target_pairs={{2,4},{3,5},{4,2},{5,3},{6,8},{7,9},{8,6},{9,7},{10,12},{11,13},{1... | collective-permute-start | bytes 393224 | tf_op jit(solution)/shard_map/ppermute | solution.py:543
  24.4 12.2 %collective-permute-start.4 = (bf16[256,256]{1,0:T(8,128)(2,1)S(1)}, bf16[256,256]{1,0:T(8,128)(2,1)S(1)}, u32[]{:S(2)}, u32[]{:S(2)}) collective-permute-start(bf16[256,256]{1,0:T(8,128)(2,1)S(1)} %get-tuple-element.59.a_ref.a3_ref), channel_id=1, source_target_pairs={{0,2},{1,3},{2,0},{3,1},{4,6},{5,7},{6,4},{7,5},{8,10},{9,11},{10,... | collective-permute-start | bytes 393224 | tf_op jit(solution)/shard_map/ppermute | solution.py:544
  31.6 7.6 %copy-start.3 = (bf16[256,2304]{1,0:T(8,128)(2,1)S(1)}, bf16[256,2304]{1,0:T(8,128)(2,1)}, u32[]{:S(2)}) copy-start(bf16[256,2304]{1,0:T(8,128)(2,1)} %get-tuple-element.73.b3_ref) | copy-start | bytes 3538948
  31.6 7.6 %copy-start.7 = (bf16[4,256,256]{2,1,0:T(8,128)(2,1)S(1)}, bf16[4,256,256]{2,1,0:T(8,128)(2,1)}, u32[]{:S(2)}) copy-start(bf16[4,256,256]{2,1,0:T(8,128)(2,1)} %get-tuple-element.74.h_ref) | copy-start | bytes 1572868
  41.3 3.1 %copy-start.6 = (bf16[2,2,256,256]{3,2,1,0:T(8,128)(2,1)S(1)}, bf16[2,2,256,256]{3,2,1,0:T(8,128)(2,1)}, u32[]{:S(2)}) copy-start(bf16[2,2,256,256]{3,2,1,0:T(8,128)(2,1)} %get-tuple-element.79.sides_ref) | copy-start | bytes 1572868
  41.3 7.4 %collective-permute-start.6 = (bf16[2,256,256]{2,1,0:T(8,128)(2,1)S(1)}, bf16[2,256,256]{2,1,0:T(8,128)(2,1)S(1)}, u32[]{:S(2)}, u32[]{:S(2)}) collective-permute-start(bf16[2,256,256]{2,1,0:T(8,128)(2,1)S(1)} %get-tuple-element.75), channel_id=1, source_target_pairs={{1,2},{2,1},{3,4},{4,3},{5,6},{6,5},{7,8},{8,7},{9,10},{10,9},{11,... | collective-permute-start | bytes 786440 | tf_op jit(solution)/shard_map/ppermute | solution.py:535
  42.2 6.6 %collective-permute-start.7 = (bf16[2,256,256]{2,1,0:T(8,128)(2,1)S(1)}, bf16[2,256,256]{2,1,0:T(8,128)(2,1)S(1)}, u32[]{:S(2)}, u32[]{:S(2)}) collective-permute-start(bf16[2,256,256]{2,1,0:T(8,128)(2,1)S(1)} %get-tuple-element.76), channel_id=1, source_target_pairs={{0,1},{1,0},{2,3},{3,2},{4,5},{5,4},{6,7},{7,6},{8,9},{9,8},{10,11... | collective-permute-start | bytes 786440 | tf_op jit(solution)/shard_map/ppermute | solution.py:536
  44.4 1.8 %copy-start.1 = (bf16[256,2304]{1,0:T(8,128)(2,1)S(1)}, bf16[256,2304]{1,0:T(8,128)(2,1)}, u32[]{:S(2)}) copy-start(bf16[256,2304]{1,0:T(8,128)(2,1)} %get-tuple-element.82.b2_ref) | copy-start | bytes 3538948
  46.2 6.3 %copy-start.5 = (bf16[1024,256]{1,0:T(8,128)(2,1)S(1)}, bf16[1024,256]{1,0:T(8,128)(2,1)}, u32[]{:S(2)}) copy-start(bf16[1024,256]{1,0:T(8,128)(2,1)} %get-tuple-element.87.perm_ref) | copy-start | bytes 1572868
  47.3 5.2 %copy-start.2 = (bf16[2,2,1024,256]{3,2,1,0:T(8,128)(2,1)S(1)}, bf16[2,2,1024,256]{3,2,1,0:T(8,128)(2,1)}, u32[]{:S(2)}) copy-start(bf16[2,2,1024,256]{3,2,1,0:T(8,128)(2,1)} %get-tuple-element.86.vp_ref) | copy-start | bytes 6291460
  48.8 6.1 %collective-permute-start.8 = (bf16[2560,128]{1,0:T(8,128)(2,1)S(1)}, bf16[2560,128]{1,0:T(8,128)(2,1)S(1)}, u32[]{:S(2)}, u32[]{:S(2)}) collective-permute-start(bf16[2560,128]{1,0:T(8,128)(2,1)S(1)} %get-tuple-element.89), channel_id=1, source_target_pairs={{0,64},{64,0},{1,65},{65,1},{2,66},{66,2},{3,67},{67,3},{4,68},{68... | collective-permute-start | bytes 1966088 | tf_op jit(solution)/shard_map/ppermute | solution.py:548
  87.6 2.4 %collective-permute-start.9 = (f32[1,128]{1,0:T(1,128)S(1)}, f32[1,128]{1,0:T(1,128)S(1)}, u32[]{:S(2)}, u32[]{:S(2)}) collective-permute-start(f32[1,128]{1,0:T(1,128)S(1)} %slice.8), channel_id=1, source_target_pairs={{0,64},{64,0},{1,65},{65,1},{2,66},{66,2},{3,67},{67,3},{4,68},{68... | collective-permute-start | bytes 1544 | tf_op jit(solution)/shard_map/ppermute | solution.py:548

commit v9 on v8

--- a/solution.py
+++ b/solution.py
@@ -288,7 +288,8 @@
 
 
 def head_kernel(
-    scale, where_ref, one_ref, two_ref, near_ref, away_ref, own_ref, f3_ref, wh_ref, marks_ref, gz_ref, gh_ref, b_ref
+    scale, where_ref, one_ref, two_ref, near_ref, away_ref, own_ref, f3_ref, wh_ref, marks_ref, b3_ref, a3_ref, h_ref,
+    wd_ref, gz_ref, gh_ref, gz2_ref, gone_ref, gtwo_ref, gy_ref, b_ref
 ):
     lo, hi = sorted_out(where_ref, one_ref[...], two_ref[...])
     low_half = where_ref[2] == 0
@@ -320,42 +321,10 @@
                 total += dot_nt(mine, g)
             gz_ref[k, pl.ds(h * 128, 128), :] = (dot(wh_ref[pl.ds(0, 128), :], g) * slope(mine)).astype(BF16)
     gh_ref[...] = total
-
-
-def head(where, one, two, near, away, own, f3, wh, marks, scale):
-    return call(
-        functools.partial(head_kernel, scale),
-        [((3, T, T), BF16, pltpu.VMEM), ((128, 128), F32, pltpu.VMEM)],
-        where, one, two, near, away, own, f3, wh, marks,
-        scratch=[pltpu.VMEM((12 * T, T), BF16)],
-    )
-
-
-def weight_three_kernel(where_ref, g_ref, one_ref, a_ref, two_ref, out_ref, s_ref):
-    put_three(s_ref, 0, three_three(g_ref[1]))
-    lo, hi = sorted_out(where_ref, one_ref[:T], two_ref[:T])
-    for d, a in enumerate((lo, a_ref[...], hi)):
-        for j in range(3):
-            t = dot_nt(s_ref[pl.ds((2 - j) * T, T), :], a)
-            out_ref[d * 9 + j] = t[128:, :128]
-            out_ref[d * 9 + 3 + j] = t[:128, :128] + t[128:, 128:]
-            out_ref[d * 9 + 6 + j] = t[:128, 128:]
-
-
-def weight_three(where, g, one, a, two):
-    return call(
-        weight_three_kernel,
-        [((27, 128, 128), F32, pltpu.VMEM)],
-        where, g, one, a, two,
-        scratch=[pltpu.VMEM((3 * T, T), BF16)],
-    )[0]
-
-
-def middle_kernel(where_ref, g_ref, b3_ref, a3_ref, h_ref, wd_ref, gz2_ref, gone_ref, gtwo_ref, gd_ref, b_ref):
     for k in range(3):
-        put_three(b_ref, k * 3 * T, three_three(g_ref[k]))
-    rest = dot(b3_ref[...], b_ref[...])
-    gy = (rest * slope(a3_ref[...])).astype(BF16)
+        put_three(b_ref, k * 3 * T, three_three(gz_ref[k]))
+    gy = (dot(b3_ref[...], b_ref[: 9 * T, :]) * slope(a3_ref[...])).astype(BF16)
+    gy_ref[...] = gy
     for d in range(2):
         for p in range(2):
             k = 2 * d + p
@@ -366,21 +335,44 @@
     for n in range(CROPS):
         gone_ref[n] = jnp.where(even, gz2_ref[n, 1], gz2_ref[n, 0])
         gtwo_ref[n] = jnp.where(even, gz2_ref[n, 0], gz2_ref[n, 1])
-    for k in range(4):
-        gd_ref[k] = dot_nt(gy[:128], h_ref[k, :128]) + dot_nt(gy[128:], h_ref[k, 128:])
-
-
-def middle(where, g, b3, a3, h, wd):
-    return call(
-        middle_kernel,
+
+
+def head(where, one, two, near, away, own, f3, wh, marks, b3, a3, h, wd, scale):
+    return call(
+        functools.partial(head_kernel, scale),
         [
+            ((3, T, T), BF16, pltpu.VMEM),
+            ((128, 128), F32, pltpu.VMEM),
             ((CROPS, 2, T, T), BF16, pltpu.VMEM),
             ((CROPS, T, T), BF16, pltpu.VMEM),
             ((CROPS, T, T), BF16, pltpu.VMEM),
-            ((4, 128, 128), F32, pltpu.VMEM),
+            ((T, T), BF16, pltpu.VMEM),
         ],
-        where, g, b3, a3, h, wd,
-        scratch=[pltpu.VMEM((9 * T, T), BF16)],
+        where, one, two, near, away, own, f3, wh, marks, b3, a3, h, wd,
+        scratch=[pltpu.VMEM((12 * T, T), BF16)],
+    )
+
+
+def weight_three_kernel(where_ref, g_ref, one_ref, a_ref, two_ref, gy_ref, h_ref, out_ref, gd_ref, s_ref):
+    gy = gy_ref[...]
+    for k in range(4):
+        gd_ref[k] = dot_nt(gy[:128], h_ref[k, :128]) + dot_nt(gy[128:], h_ref[k, 128:])
+    put_three(s_ref, 0, three_three(g_ref[1]))
+    lo, hi = sorted_out(where_ref, one_ref[:T], two_ref[:T])
+    for d, a in enumerate((lo, a_ref[...], hi)):
+        for j in range(3):
+            t = dot_nt(s_ref[pl.ds((2 - j) * T, T), :], a)
+            out_ref[d * 9 + j] = t[128:, :128]
+            out_ref[d * 9 + 3 + j] = t[:128, :128] + t[128:, 128:]
+            out_ref[d * 9 + 6 + j] = t[:128, 128:]
+
+
+def weight_three(where, g, one, a, two, gy, h):
+    return call(
+        weight_three_kernel,
+        [((27, 128, 128), F32, pltpu.VMEM), ((4, 128, 128), F32, pltpu.VMEM)],
+        where, g, one, a, two, gy, h,
+        scratch=[pltpu.VMEM((3 * T, T), BF16)],
     )
 
 
@@ -548,7 +540,7 @@
     return lax.ppermute(x, "section", [(0, 1), (1, 0)])
 
 
-def flat(x, step):
+def flat(x, step, rows):
     c = lax.broadcasted_iota(jnp.int32, (128, 128), 0) * step
     lane = lax.broadcasted_iota(jnp.int32, (128, 128), 1)
     x = x.T
@@ -559,51 +551,48 @@
             piece = pltpu.roll(piece, 0, 1, stride=part, stride_axis=0)
         pieces.append(pltpu.roll(piece, 8 * k * step % 128, 1) if 8 * k * step % 128 else piece)
     turned = jnp.concatenate(pieces, axis=0)
-    row = lax.broadcasted_iota(jnp.int32, (32, 128), 0)
-    start = lax.broadcasted_iota(jnp.int32, (32, 128), 1) * step // 128
+    row = lax.broadcasted_iota(jnp.int32, (rows, 128), 0)
+    start = lax.broadcasted_iota(jnp.int32, (rows, 128), 1) * step // 128
     exact = functools.partial(jnp.dot, precision=lax.Precision.HIGHEST, preferred_element_type=F32)
     here = lane >= c % 128
     same = exact(jnp.where(row == start, 1.0, 0.0), jnp.where(here, turned, 0.0))
     return same + exact(jnp.where(row == start + 1, 1.0, 0.0), jnp.where(here, 0.0, turned))
 
 
-def unpack_kernel(sums_ref, came_ref, down_ref, two_ref, three_ref, conv_ref, head_ref, x_ref):
-    down_ref[...] = sums_ref[pl.ds(DOWN2, 1), :] + came_ref[...]
+def unpack_kernel(sums_ref, two_ref, three_ref, conv_ref, head_ref, x_ref, y_ref, z_ref):
     last = sums_ref[pl.ds(DOWN2 - 1, 1), :]
     for k in range(4):
         head_ref[k] = jnp.sum(jnp.where(lax.broadcasted_iota(jnp.int32, (1, 128), 1) == 96 + k, last, 0.0))
-    zero = jnp.zeros((128, 128), F32)
-    x_ref[...] = zero
+    for ref in (x_ref, y_ref, z_ref):
+        ref[...] = jnp.zeros((128, 128), F32)
     x_ref[pl.ds(0, DOWN3), :] = sums_ref[pl.ds(0, DOWN3), :]
-    conv_ref[...] = flat(x_ref[...], 27)[:27]
-    x_ref[...] = zero
     lane = lax.broadcasted_iota(jnp.int32, (7, 128), 1)
     rows = sums_ref[pl.ds(CONV2, 7), :]
     for i in range(4):
-        x_ref[pl.ds(i, 7, stride=4), :] = jnp.where(lane < 32, rows if i == 0 else pltpu.roll(rows, 128 - 32 * i, 1), 0.0)
-    x_ref[pl.ds(27, 1), :] = jnp.zeros((1, 128), F32)
-    two_ref[...] = flat(x_ref[...], 27)[:7]
-    x_ref[...] = zero
+        y_ref[pl.ds(i, 7, stride=4), :] = jnp.where(lane < 32, rows if i == 0 else pltpu.roll(rows, 128 - 32 * i, 1), 0.0)
+    y_ref[pl.ds(27, 1), :] = jnp.zeros((1, 128), F32)
     lane = lax.broadcasted_iota(jnp.int32, (1, 128), 1)
     for k in range(4):
         row = sums_ref[pl.ds(DOWN3 + k, 1), :]
         at = k // 2 * 4 + k % 2
-        x_ref[pl.ds(at, 1), :] = jnp.where(lane < 64, row, 0.0)
-        x_ref[pl.ds(at + 2, 1), :] = jnp.where(lane < 64, pltpu.roll(row, 64, 1), 0.0)
-    three_ref[...] = flat(x_ref[...], 8)[:4]
+        z_ref[pl.ds(at, 1), :] = jnp.where(lane < 64, row, 0.0)
+        z_ref[pl.ds(at + 2, 1), :] = jnp.where(lane < 64, pltpu.roll(row, 64, 1), 0.0)
+    conv_ref[...] = flat(x_ref[...], 27, 32)[:27]
+    two_ref[...] = flat(y_ref[...], 27, 8)[:7]
+    three_ref[...] = flat(z_ref[...], 8, 8)[:4]
 
 
 def unpack(sums, came):
     spec = pl.BlockSpec(memory_space=pltpu.VMEM)
-    down, two, three, conv, head = pl.pallas_call(
+    two, three, conv, head = pl.pallas_call(
         unpack_kernel,
-        in_specs=[spec] * 2,
-        out_specs=[spec] * 4 + [pl.BlockSpec(memory_space=pltpu.SMEM)],
-        out_shape=[pltpu.HBM((rows, 128), F32) for rows in (1, 7, 4, 27)] + [jax.ShapeDtypeStruct((4,), F32)],
-        scratch_shapes=[pltpu.VMEM((128, 128), F32)],
+        in_specs=[spec],
+        out_specs=[spec] * 3 + [pl.BlockSpec(memory_space=pltpu.SMEM)],
+        out_shape=[pltpu.HBM((rows, 128), F32) for rows in (7, 4, 27)] + [jax.ShapeDtypeStruct((4,), F32)],
+        scratch_shapes=[pltpu.VMEM((128, 128), F32)] * 3,
         compiler_params=params(),
-    )(sums, came)
-    return down.reshape(-1), two.reshape(-1)[: 27 * 32], three.reshape(-1), conv.reshape(-1), head
+    )(sums)
+    return sums[DOWN2] + came[0], two.reshape(-1)[: 27 * 32], three.reshape(-1), conv.reshape(-1), head
 
 
 def finish(pack):
@@ -637,12 +626,13 @@
     a3_one, a3_two = swapped(sent, sent)
     a3_near, a3_away = swapped_two(a3)
     own, f3, wh = head_own(a3, f3, wh)
-    a3_one, a3_two, a3_near, a3_away, own, f3, wh = lax.optimization_barrier(
-        (a3_one, a3_two, a3_near, a3_away, own, f3, wh)
-    )
-    gz4, gh = head(where, a3_one, a3_two, a3_near, a3_away, own, f3, wh, marks, scale)
-    gz2, one, two, gd3 = middle(where, gz4, b3, a3, h2, wd)
-    gw3 = weight_three(where, gz4, a3_one, a3, a3_two)
+    a3_two, a3_away, a3_one, a3_near, own, f3, wh = lax.optimization_barrier(
+        (a3_two, a3_away, a3_one, a3_near, own, f3, wh)
+    )
+    gz4, gh, gz2, one, two, gy3 = head(
+        where, a3_one, a3_two, a3_near, a3_away, own, f3, wh, marks, b3, a3, h2, wd, scale
+    )
+    gw3, gd3 = weight_three(where, gz4, a3_one, a3, a3_two, gy3, h2)
     gz2_one, gz2_two = swapped(one, two)
     own = last_own(gz2, b2)
     gw2 = weight_two(gz2, a2, sides)

time: 91.9 us -> 89.8 us (0.977)
  waiting for transfers between devices: 6.75 us -> 3.44 us
    ppermute x3, starting transfers between devices: 9.19 us -> 12.3 us  [swapped(): return (lax.ppermute(one, 'space', near), two)]
    ppermute x1, waiting for transfers between devices: 4.99 us -> 2.49 us  [swapped_two(): return (lax.ppermute(x, 'space', near), away)]
    ppermute x1, starting transfers between devices: 6.61 us -> 4.9 us  [swapped_two(): return (lax.ppermute(x, 'space', near), away)]
    pallas_call x12 -> x11, Pallas kernels: 20.8 us -> 19.9 us  [call(): pl.pallas_call(kernel, in_specs=[remote if i in far else scalar if a.dtyp...]
  transfers between devices with their start and end apart: 10 -> 10, of which waited for: 3 -> 2; matrix products, arithmetic and copies ran while one was open for 0% -> 0% of each run, Pallas kernels for 14% -> 16%
where the time goes in v9:
time: 89.8 us; the launch traced here: 89.4 us
  blocking collectives  32.6 us (36%)
  Pallas kernels  26.6 us (30%)
  starting transfers between devices  24.8 us (28%)
  waiting for transfers between devices  3.44 us (4%)
  between operations  0.96 us (1%)
    all_to_all x1, blocking collectives, finish(): terms = lax.all_to_all(pack, 'space', 0, 0, tiled=True)  32.6 us
    pallas_call x11, Pallas kernels, call(): pl.pallas_call(kernel, in_specs=[remote if i in far else scalar if a.dtyp...  19.9 us
    ppermute x3, starting transfers between devices, swapped(): return (lax.ppermute(one, 'space', near), two)  12.3 us
    pallas_call x1, Pallas kernels, first(): pl.pallas_call(first_kernel, in_specs=[pl.BlockSpec(memory_space=pltpu.SM...  5.3 us
    ppermute x1, starting transfers between devices, swapped_two(): return (lax.ppermute(x, 'space', near), away)  4.9 us
    ppermute x2, starting transfers between devices, partner(): return lax.ppermute(x, 'section', [(0, 1), (1, 0)])  4.87 us
    ppermute x1, waiting for transfers between devices, swapped_two(): return (lax.ppermute(x, 'space', near), away)  2.49 us
    ppermute x3, starting transfers between devices, swapped(): two = lax.ppermute(two, 'space', far)  2.14 us
  transfers between devices with their start and end apart: 10, of which 2 were waited for; matrix products, arithmetic and copies ran while one was open for 0% of the time, Pallas kernels for 16%

profile of v9, /device:TPU:1, one launch (start us, length us, event | category | flops | bytes accessed | tf_op | source)
XLA Modules:
  0.0 89.4 jit_solution(11092084099112720514)
XLA Ops:
  0.6 0.0 copy-start
  0.7 0.1 stack.23.where_ref
  0.8 5.3 %shard_map.110 = (bf16[2,2,1024,256]{3,2,1,0:T(8,128)(2,1)}, bf16[2,2,256,256]{3,2,1,0:T(8,128)(2,1)S(1)}, bf16[2,256,256]{2,1,0:T(8,128)(2,1)S(1)}, bf16[2,256,256]{2,1,0:T(8,128)(2,1)S(1)}) custom-call(s32[5]{0:T(128)S(1)} %stack.23.where_ref, bf16[4,32,4,8,512]{4,3,2,1,0:T(8,128)(2,1)} %vol_far.1, bf16[256,64]{1,0:T(8,128)(2,1)} %bitcast.36), custom_call_target="tpu_custom_call" | custom-call | tf_op jit(solution)/shard_map/pallas_call | solution.py:130
  6.1 0.7 collective-permute-start
  6.8 4.6 %collective-permute-start.1 = (bf16[2,256,256]{2,1,0:T(8,128)(2,1)S(1)}, bf16[2,256,256]{2,1,0:T(8,128)(2,1)S(1)}, u32[]{:S(2)}, u32[]{:S(2)}) collective-permute-start(bf16[2,256,256]{2,1,0:T(8,128)(2,1)S(1)} %get-tuple-element.52), channel_id=1, source_target_pairs={{0,1},{1,0},{2,3},{3,2},{4,5},{5,4},{6,7},{7,6},{8,9},{9,8},{10,11... | collective-permute-start | bytes 786440 | tf_op jit(solution)/shard_map/ppermute | solution.py:528
  11.3 0.0 copy-done.11
  11.3 0.2 pad_maximum_fusion.w2_ref
  11.6 0.0 copy-done.8
  11.6 0.0 copy-done.10
  11.6 3.4 %shard_map.111 = (bf16[256,2304]{1,0:T(8,128)(2,1)S(1)}, bf16[256,2304]{1,0:T(8,128)(2,1)}, bf16[256,2304]{1,0:T(8,128)(2,1)}, bf16[256,2304]{1,0:T(8,128)(2,1)}...) custom-call(bf16[27,64,128]{2,1,0:T(8,128)(2,1)S(1)} %pad_maximum_fusion.w2_ref, ...), custom_call_target="tpu_custom_call" | custom-call | tf_op jit(solution)/shard_map/pallas_call | solution.py:72
  15.0 1.1 %shard_map.112.own_ref = f32[2,2,256,256]{3,2,1,0:T(8,128)S(1)} custom-call(bf16[2,2,256,256]{3,2,1,0:T(8,128)(2,1)S(1)} %get-tuple-element.53.a_ref, bf16[256,2304]{1,0:T(8,128)(2,1)S(1)} %get-tuple-element.54.f2_ref), custom_call_target="tpu_custom_call" | custom-call | tf_op jit(solution)/shard_map/pallas_call | solution.py:72
  16.1 0.0 collective-permute-done.two_ref
  16.1 0.9 %collective-permute-done.1.one_ref = bf16[2,256,256]{2,1,0:T(8,128)(2,1)S(1)} collective-permute-done((bf16[2,256,256]{2,1,0:T(8,128)(2,1)S(1)}, bf16[2,256,256]{2,1,0:T(8,128)(2,1)S(1)}, u32[]{:S(2)}, u32[]{:S(2)}) %collective-permute-start.1) | collective-permute-done | bytes 262176 | tf_op jit(solution)/shard_map/ppermute | solution.py:528
  17.1 2.6 %shard_map.113 = (bf16[4,256,256]{2,1,0:T(8,128)(2,1)}, bf16[256,256]{1,0:T(8,128)(2,1)S(1)}, bf16[272,256]{1,0:T(8,128)(2,1)S(1)}, bf16[2,2,256,256]{3,2,1,0:T(8,128)(2,1)}) custom-call(s32[5]{0:T(128)S(1)} %stack.23.where_ref, bf16[2,256,256]{2,1,0:T(8,128)(2,1)S(1)} %collective-permute-done.1.one_ref, f32[2,2,256,256]{3,2,1,0:T(8,128)S(1)} %shard_map.112.own_ref, ...), custom_call_target="tpu_custom_call" | custom-call | tf_op jit(solution)/shard_map/pallas_call | solution.py:72
  19.6 1.1 %collective-permute-start.4 = (bf16[272,256]{1,0:T(8,128)(2,1)S(1)}, bf16[272,256]{1,0:T(8,128)(2,1)S(1)}, u32[]{:S(2)}, u32[]{:S(2)}) collective-permute-start(bf16[272,256]{1,0:T(8,128)(2,1)S(1)} %get-tuple-element.59), channel_id=1, source_target_pairs={{0,1},{1,0},{2,3},{3,2},{4,5},{5,4},{6,7},{7,6},{8,9},{9,8},{10,11... | collective-permute-start | bytes 417800 | tf_op jit(solution)/shard_map/ppermute | solution.py:528
  20.8 0.7 collective-permute-start.2
  21.4 4.9 %collective-permute-start.5 = (bf16[256,256]{1,0:T(8,128)(2,1)S(1)}, bf16[256,256]{1,0:T(8,128)(2,1)S(1)}, u32[]{:S(2)}, u32[]{:S(2)}) collective-permute-start(bf16[256,256]{1,0:T(8,128)(2,1)S(1)} %get-tuple-element.60.a_ref.a3_ref), channel_id=1, source_target_pairs={{0,2},{1,3},{2,0},{3,1},{4,6},{5,7},{6,4},{7,5},{8,10},{9,11},{10,... | collective-permute-start | bytes 393224 | tf_op jit(solution)/shard_map/ppermute | solution.py:536
  26.3 0.7 collective-permute-start.3
  27.0 0.6 shard_map.114
  27.6 2.5 %collective-permute-done.5.near_ref = bf16[256,256]{1,0:T(8,128)(2,1)S(1)} collective-permute-done((bf16[256,256]{1,0:T(8,128)(2,1)S(1)}, bf16[256,256]{1,0:T(8,128)(2,1)S(1)}, u32[]{:S(2)}, u32[]{:S(2)}) %collective-permute-start.5) | collective-permute-done | bytes 131104 | tf_op jit(solution)/shard_map/ppermute | solution.py:536
  30.1 0.0 collective-permute-done.3.away_ref
  30.1 0.0 collective-permute-done.4.one_ref
  30.1 0.0 collective-permute-done.2.two_ref
  30.1 0.0 copy-done.5
  30.1 0.0 copy-done.3
  30.1 0.0 copy-start.7
  30.1 3.6 %shard_map.115 = (bf16[3,256,256]{2,1,0:T(8,128)(2,1)S(1)}, f32[128,128]{1,0:T(8,128)S(1)}, bf16[2,2,256,256]{3,2,1,0:T(8,128)(2,1)S(1)}, bf16[2,256,256]{2,1,0:...) custom-call(s32[5]{0:T(128)S(1)} %stack.23.where_ref, ...), custom_call_target="tpu_custom_call" | custom-call | tf_op jit(solution)/shard_map/pallas_call | solution.py:72
  33.8 0.8 collective-permute-start.6
  34.6 6.6 %collective-permute-start.7 = (bf16[2,256,256]{2,1,0:T(8,128)(2,1)S(1)}, bf16[2,256,256]{2,1,0:T(8,128)(2,1)S(1)}, u32[]{:S(2)}, u32[]{:S(2)}) collective-permute-start(bf16[2,256,256]{2,1,0:T(8,128)(2,1)S(1)} %get-tuple-element.76), channel_id=1, source_target_pairs={{0,1},{1,0},{2,3},{3,2},{4,5},{5,4},{6,7},{7,6},{8,9},{9,8},{10,11... | collective-permute-start | bytes 786440 | tf_op jit(solution)/shard_map/ppermute | solution.py:528
  41.1 0.0 copy-done.7
  41.1 1.7 %shard_map.117.w2_ref = f32[7,2,64,128]{3,2,1,0:T(8,128)S(1)} custom-call(bf16[2,2,256,256]{3,2,1,0:T(8,128)(2,1)S(1)} %get-tuple-element.81.g_ref, bf16[2,2,256,256]{3,2,1,0:T(8,128)(2,1)S(1)} %get-tuple-element.53.a_ref, bf16[2,2,256,256]{3,2,1,0:T(8,128)(2,1)S(1)} %copy-done.7), custom_call_target="tpu_custom_call" | custom-call | tf_op jit(solution)/shard_map/pallas_call | solution.py:72
  42.9 1.1 %shard_map.119.own_ref = f32[2,2,256,256]{3,2,1,0:T(8,128)S(1)} custom-call(bf16[2,2,256,256]{3,2,1,0:T(8,128)(2,1)S(1)} %get-tuple-element.81.g_ref, bf16[256,2304]{1,0:T(8,128)(2,1)S(1)} %copy-done.1), custom_call_target="tpu_custom_call" | custom-call | tf_op jit(solution)/shard_map/pallas_call | solution.py:72
  44.0 0.0 copy-start.6
  44.0 1.2 %shard_map.116 = (f32[27,128,128]{2,1,0:T(8,128)S(1)}, f32[4,128,128]{2,1,0:T(8,128)S(1)}) custom-call(s32[5]{0:T(128)S(1)} %stack.23.where_ref, bf16[3,256,256]{2,1,0:T(8,128)(2,1)S(1)} %get-tuple-element.77.g_ref, bf16[272,256]{1,0:T(8,128)(2,1)S(1)} %collective-permute-done.4.one_ref, bf16[256,256]{1,0:T(8,128)(2,1)S(1)} %get-tuple-element.60.a_ref.a3_ref, ...), custom_call_target="tpu_custom_call" | custom-call | tf_op jit(solution)/shard_map/pallas_call | solution.py:72
  45.2 1.5 %shard_map.118 = (f32[2560,128]{1,0:T(8,128)S(1)}, bf16[2560,128]{1,0:T(8,128)(2,1)S(1)}) custom-call(s32[5]{0:T(128)S(1)} %stack.23.where_ref, f32[27,128,128]{2,1,0:T(8,128)S(1)} %get-tuple-element.79.w3_ref, f32[4,128,128]{2,1,0:T(8,128)S(1)} %get-tuple-element.80.d3_ref, f32[7,2,64,128]{3,2,1,0:T(8,128)S(1)} %shard_map.117.w2_ref, ...), custom_call_target="tpu_custom_call" | custom-call | tf_op jit(solution)/shard_map/pallas_call | solution.py:72
  46.7 0.0 collective-permute-done.6.two_ref
  46.7 0.0 collective-permute-done.7.one_ref
  46.7 3.3 %collective-permute-start.8 = (bf16[2560,128]{1,0:T(8,128)(2,1)S(1)}, bf16[2560,128]{1,0:T(8,128)(2,1)S(1)}, u32[]{:S(2)}, u32[]{:S(2)}) collective-permute-start(bf16[2560,128]{1,0:T(8,128)(2,1)S(1)} %get-tuple-element.92), channel_id=1, source_target_pairs={{0,64},{64,0},{1,65},{65,1},{2,66},{66,2},{3,67},{67,3},{4,68},{68... | collective-permute-start | bytes 1966088 | tf_op jit(solution)/shard_map/ppermute | solution.py:540
  50.0 0.0 copy-done.6
  50.0 2.5 %shard_map.120.down_ref = f32[64,256]{1,0:T(8,128)S(1)} custom-call(s32[5]{0:T(128)S(1)} %stack.23.where_ref, bf16[2,256,256]{2,1,0:T(8,128)(2,1)S(1)} %collective-permute-done.7.one_ref, f32[2,2,256,256]{3,2,1,0:T(8,128)S(1)} %shard_map.119.own_ref, bf16[2,256,256]{2,1,0:T(8,128)(2,1)S(1)} %collective-permute-done.6.two_ref, ...), custom_call_target="tpu_custom_call" | custom-call | tf_op jit(solution)/shard_map/pallas_call | solution.py:72
  52.5 0.0 collective-permute-done.8.came_ref
  52.5 0.7 shard_map.121
  53.2 32.6 %all_to_all.5 = bf16[64,40,128]{2,1,0:T(8,128)(2,1)S(1)} all-to-all(bf16[64,40,128]{2,1,0:T(8,128)(2,1)S(1)} %bitcast.31), channel_id=1, replica_groups=mesh['section'=2,'space'=64] {'space'}, dimensions={0} | all-to-all | bytes 1310720 | tf_op jit(solution)/shard_map/all_to_all | solution.py:599
  85.7 0.1 convert_reduce_fusion.sums_ref
  85.9 1.6 %collective-permute-start.9 = (f32[1,128]{1,0:T(1,128)S(1)}, f32[1,128]{1,0:T(1,128)S(1)}, u32[]{:S(2)}, u32[]{:S(2)}) collective-permute-start(f32[1,128]{1,0:T(1,128)S(1)} %slice.13), channel_id=1, source_target_pairs={{0,64},{64,0},{1,65},{65,1},{2,66},{66,2},{3,67},{67,3},{4,68},{68... | collective-permute-start | bytes 1544 | tf_op jit(solution)/shard_map/ppermute | solution.py:540
  87.5 1.4 %shard_map.122 = (f32[7,128]{1,0:T(8,128)}, f32[4,128]{1,0:T(4,128)}, f32[27,128]{1,0:T(8,128)}, f32[4]{0:T(128)}) custom-call(f32[40,128]{1,0:T(8,128)S(1)} %convert_reduce_fusion.sums_ref), custom_call_target="tpu_custom_call" | custom-call | tf_op jit(solution)/shard_map/pallas_call | solution.py:587
  88.9 0.0 collective-permute-done.9
  88.9 0.5 fusion
  (16 shorter events, 0.0 us)
Async XLA Ops:
  0.6 15.5 %copy-start = (s32[4,1,2,128]{3,2,1,0:T(2,128)S(1)}, s32[4,1,2,128]{3,2,1,0:T(2,128)}, u32[]{:S(2)}) copy-start(s32[4,1,2,128]{3,2,1,0:T(2,128)} %param.8) | copy-start | bytes 12292
  0.8 10.6 %copy-start.11 = (bf16[64,64,3,3,3]{1,0,4,3,2:T(8,128)(2,1)S(1)}, bf16[64,64,3,3,3]{1,0,4,3,2:T(8,128)(2,1)}, u32[]{:S(2)}) copy-start(bf16[64,64,3,3,3]{1,0,4,3,2:T(8,128)(2,1)} %param.10) | copy-start | bytes 663556
  0.8 10.8 %copy-start.8 = (bf16[128,64,2,2,2]{0,4,3,2,1:T(2,128)(2,1)S(1)}, bf16[128,64,2,2,2]{0,4,3,2,1:T(2,128)(2,1)}, u32[]{:S(2)}) copy-start(bf16[128,64,2,2,2]{0,4,3,2,1:T(2,128)(2,1)} %param.11) | copy-start | bytes 393220
  0.8 10.8 %copy-start.10 = (bf16[128,4]{0,1:T(4,128)(2,1)S(1)}, bf16[128,4]{0,1:T(4,128)(2,1)}, u32[]{:S(2)}) copy-start(bf16[128,4]{0,1:T(4,128)(2,1)} %param.13) | copy-start | bytes 3076
  6.1 10.0 %collective-permute-start = (bf16[2,256,256]{2,1,0:T(8,128)(2,1)S(1)}, bf16[2,256,256]{2,1,0:T(8,128)(2,1)S(1)}, u32[]{:S(2)}, u32[]{:S(2)}) collective-permute-start(bf16[2,256,256]{2,1,0:T(8,128)(2,1)S(1)} %get-tuple-element.51), channel_id=1, source_target_pairs={{1,2},{2,1},{3,4},{4,3},{5,6},{6,5},{7,8},{8,7},{9,10},{10,9},{11,... | collective-permute-start | bytes 786440 | tf_op jit(solution)/shard_map/ppermute | solution.py:527
  6.8 10.3 %collective-permute-start.1 = (bf16[2,256,256]{2,1,0:T(8,128)(2,1)S(1)}, bf16[2,256,256]{2,1,0:T(8,128)(2,1)S(1)}, u32[]{:S(2)}, u32[]{:S(2)}) collective-permute-start(bf16[2,256,256]{2,1,0:T(8,128)(2,1)S(1)} %get-tuple-element.52), channel_id=1, source_target_pairs={{0,1},{1,0},{2,3},{3,2},{4,5},{5,4},{6,7},{7,6},{8,9},{9,8},{10,11... | collective-permute-start | bytes 786440 | tf_op jit(solution)/shard_map/ppermute | solution.py:528
  17.0 10.0 %copy-start.4 = (bf16[256,2304]{1,0:T(8,128)(2,1)S(1)}, bf16[256,2304]{1,0:T(8,128)(2,1)}, u32[]{:S(2)}) copy-start(bf16[256,2304]{1,0:T(8,128)(2,1)} %get-tuple-element.61.f3_ref) | copy-start | bytes 3538948
  17.1 10.0 %copy-start.9 = (bf16[256,128]{1,0:T(8,128)(2,1)S(1)}, bf16[256,128]{1,0:T(8,128)(2,1)}, u32[]{:S(2)}) copy-start(bf16[256,128]{1,0:T(8,128)(2,1)} %get-tuple-element.62.wh_ref) | copy-start | bytes 196612
  17.1 13.1 %copy-start.5 = (bf16[256,2304]{1,0:T(8,128)(2,1)S(1)}, bf16[256,2304]{1,0:T(8,128)(2,1)}, u32[]{:S(2)}) copy-start(bf16[256,2304]{1,0:T(8,128)(2,1)} %get-tuple-element.73.b3_ref) | copy-start | bytes 3538948
  19.6 10.5 %copy-start.3 = (bf16[4,256,256]{2,1,0:T(8,128)(2,1)S(1)}, bf16[4,256,256]{2,1,0:T(8,128)(2,1)}, u32[]{:S(2)}) copy-start(bf16[4,256,256]{2,1,0:T(8,128)(2,1)} %get-tuple-element.74.h_ref) | copy-start | bytes 1572868
  19.6 10.5 %collective-permute-start.4 = (bf16[272,256]{1,0:T(8,128)(2,1)S(1)}, bf16[272,256]{1,0:T(8,128)(2,1)S(1)}, u32[]{:S(2)}, u32[]{:S(2)}) collective-permute-start(bf16[272,256]{1,0:T(8,128)(2,1)S(1)} %get-tuple-element.59), channel_id=1, source_target_pairs={{0,1},{1,0},{2,3},{3,2},{4,5},{5,4},{6,7},{7,6},{8,9},{9,8},{10,11... | collective-permute-start | bytes 417800 | tf_op jit(solution)/shard_map/ppermute | solution.py:528
  20.8 9.3 %collective-permute-start.2 = (bf16[272,256]{1,0:T(8,128)(2,1)S(1)}, bf16[272,256]{1,0:T(8,128)(2,1)S(1)}, u32[]{:S(2)}, u32[]{:S(2)}) collective-permute-start(bf16[272,256]{1,0:T(8,128)(2,1)S(1)} %get-tuple-element.59), channel_id=1, source_target_pairs={{1,2},{2,1},{3,4},{4,3},{5,6},{6,5},{7,8},{8,7},{9,10},{10,9},{11,... | collective-permute-start | bytes 417800 | tf_op jit(solution)/shard_map/ppermute | solution.py:527
  21.4 8.7 %collective-permute-start.5 = (bf16[256,256]{1,0:T(8,128)(2,1)S(1)}, bf16[256,256]{1,0:T(8,128)(2,1)S(1)}, u32[]{:S(2)}, u32[]{:S(2)}) collective-permute-start(bf16[256,256]{1,0:T(8,128)(2,1)S(1)} %get-tuple-element.60.a_ref.a3_ref), channel_id=1, source_target_pairs={{0,2},{1,3},{2,0},{3,1},{4,6},{5,7},{6,4},{7,5},{8,10},{9,11},{10,... | collective-permute-start | bytes 393224 | tf_op jit(solution)/shard_map/ppermute | solution.py:536
  26.3 3.8 %collective-permute-start.3 = (bf16[256,256]{1,0:T(8,128)(2,1)S(1)}, bf16[256,256]{1,0:T(8,128)(2,1)S(1)}, u32[]{:S(2)}, u32[]{:S(2)}) collective-permute-start(bf16[256,256]{1,0:T(8,128)(2,1)S(1)} %get-tuple-element.60.a_ref.a3_ref), channel_id=1, source_target_pairs={{2,4},{3,5},{4,2},{5,3},{6,8},{7,9},{8,6},{9,7},{10,12},{11,13},{1... | collective-permute-start | bytes 393224 | tf_op jit(solution)/shard_map/ppermute | solution.py:535
  30.1 11.0 %copy-start.7 = (bf16[2,2,256,256]{3,2,1,0:T(8,128)(2,1)S(1)}, bf16[2,2,256,256]{3,2,1,0:T(8,128)(2,1)}, u32[]{:S(2)}) copy-start(bf16[2,2,256,256]{3,2,1,0:T(8,128)(2,1)} %get-tuple-element.82.sides_ref) | copy-start | bytes 1572868
  33.8 9.1 %copy-start.1 = (bf16[256,2304]{1,0:T(8,128)(2,1)S(1)}, bf16[256,2304]{1,0:T(8,128)(2,1)}, u32[]{:S(2)}) copy-start(bf16[256,2304]{1,0:T(8,128)(2,1)} %get-tuple-element.85.b2_ref) | copy-start | bytes 3538948
  33.8 12.9 %collective-permute-start.6 = (bf16[2,256,256]{2,1,0:T(8,128)(2,1)S(1)}, bf16[2,256,256]{2,1,0:T(8,128)(2,1)S(1)}, u32[]{:S(2)}, u32[]{:S(2)}) collective-permute-start(bf16[2,256,256]{2,1,0:T(8,128)(2,1)S(1)} %get-tuple-element.75), channel_id=1, source_target_pairs={{1,2},{2,1},{3,4},{4,3},{5,6},{6,5},{7,8},{8,7},{9,10},{10,9},{11,... | collective-permute-start | bytes 786440 | tf_op jit(solution)/shard_map/ppermute | solution.py:527
  34.6 12.1 %collective-permute-start.7 = (bf16[2,256,256]{2,1,0:T(8,128)(2,1)S(1)}, bf16[2,256,256]{2,1,0:T(8,128)(2,1)S(1)}, u32[]{:S(2)}, u32[]{:S(2)}) collective-permute-start(bf16[2,256,256]{2,1,0:T(8,128)(2,1)S(1)} %get-tuple-element.76), channel_id=1, source_target_pairs={{0,1},{1,0},{2,3},{3,2},{4,5},{5,4},{6,7},{7,6},{8,9},{9,8},{10,11... | collective-permute-start | bytes 786440 | tf_op jit(solution)/shard_map/ppermute | solution.py:528
  44.0 6.0 %copy-start.6 = (bf16[1024,256]{1,0:T(8,128)(2,1)S(1)}, bf16[1024,256]{1,0:T(8,128)(2,1)}, u32[]{:S(2)}) copy-start(bf16[1024,256]{1,0:T(8,128)(2,1)} %get-tuple-element.90.perm_ref) | copy-start | bytes 1572868
  45.2 4.8 %copy-start.2 = (bf16[2,2,1024,256]{3,2,1,0:T(8,128)(2,1)S(1)}, bf16[2,2,1024,256]{3,2,1,0:T(8,128)(2,1)}, u32[]{:S(2)}) copy-start(bf16[2,2,1024,256]{3,2,1,0:T(8,128)(2,1)} %get-tuple-element.89.vp_ref) | copy-start | bytes 6291460
  46.7 5.7 %collective-permute-start.8 = (bf16[2560,128]{1,0:T(8,128)(2,1)S(1)}, bf16[2560,128]{1,0:T(8,128)(2,1)S(1)}, u32[]{:S(2)}, u32[]{:S(2)}) collective-permute-start(bf16[2560,128]{1,0:T(8,128)(2,1)S(1)} %get-tuple-element.92), channel_id=1, source_target_pairs={{0,64},{64,0},{1,65},{65,1},{2,66},{66,2},{3,67},{67,3},{4,68},{68... | collective-permute-start | bytes 1966088 | tf_op jit(solution)/shard_map/ppermute | solution.py:540
  85.9 3.0 %collective-permute-start.9 = (f32[1,128]{1,0:T(1,128)S(1)}, f32[1,128]{1,0:T(1,128)S(1)}, u32[]{:S(2)}, u32[]{:S(2)}) collective-permute-start(f32[1,128]{1,0:T(1,128)S(1)} %slice.13), channel_id=1, source_target_pairs={{0,64},{64,0},{1,65},{65,1},{2,66},{66,2},{3,67},{67,3},{4,68},{68... | collective-permute-start | bytes 1544 | tf_op jit(solution)/shard_map/ppermute | solution.py:540

commit v10 on v9

--- a/solution.py
+++ b/solution.py
@@ -174,7 +174,7 @@
             for (row, col), block in pairs.items():
                 f2_ref[pl.ds(row * 64, 64), pl.ds(at + col * 128, 128)] = block.astype(BF16)
             b2_ref[:, pl.ds(back, T)] = f2_ref[:, pl.ds(at, T)].astype(F32).T.astype(BF16)
-    rows_ref[...] = wd_ref[...].astype(F32)
+    rows_ref[pl.ds(0, 512), :] = wd_ref[...].astype(F32)
     for d in range(2):
         for p in range(2):
             for h in range(4):
@@ -210,7 +210,7 @@
         [wide(pltpu.VMEM), wide(pltpu.HBM), wide(pltpu.HBM), wide(pltpu.HBM)]
         + [((1024, 256), BF16, pltpu.HBM), ((4, T, T), BF16, pltpu.VMEM), ((256, 128), BF16, pltpu.HBM)],
         w2, w3, wd, wh,
-        scratch=[pltpu.VMEM((512, 128), F32), pltpu.VMEM((27, 128, 128), BF16), pltpu.SemaphoreType.DMA],
+        scratch=[pltpu.VMEM((520, 128), F32), pltpu.VMEM((27, 128, 128), BF16), pltpu.SemaphoreType.DMA],
         far=(1,),
     )
 
@@ -417,16 +417,17 @@
     )[0]
 
 
-def pack_kernel(where_ref, w3_ref, d3_ref, w2_ref, gh_ref, keep_ref, send_ref, pack_ref):
+def pack_kernel(where_ref, w3_ref, d3_ref, w2_ref, gh_ref, keep_ref, send_ref, pack_ref, head_ref):
     for t in range(27):
         pack_ref[pl.ds(t, 128, stride=ROWS), :] = w3_ref[t]
     for k in range(4):
         pack_ref[pl.ds(DOWN3 + k, 128, stride=ROWS), :] = d3_ref[k]
+    head_ref[pl.ds(0, 128), :] = gh_ref[...]
     lane = lax.broadcasted_iota(jnp.int32, (64, 128), 1)
     for half in range(2):
         for g in range(6):
             pack_ref[pl.ds(half * ROWS + CONV2 + g, 64, stride=2 * ROWS), :] = w2_ref[g, half]
-        heads = pltpu.roll(gh_ref[pl.ds(half, 64, stride=2), :], 96, 1)
+        heads = pltpu.roll(head_ref[pl.ds(half, 64, stride=2), :], 96, 1)
         pack_ref[pl.ds(half * ROWS + CONV2 + 6, 64, stride=2 * ROWS), :] = jnp.where(lane < 96, w2_ref[6, half], heads)
     zero = jnp.zeros((128, 128), F32)
     pack_ref[pl.ds(DOWN2, 128, stride=ROWS), :] = zero
@@ -441,7 +442,7 @@
         pack_kernel,
         [(half, F32, pltpu.VMEM), (half, BF16, pltpu.VMEM)],
         *args,
-        scratch=[pltpu.VMEM((128 * ROWS, 128), F32)],
+        scratch=[pltpu.VMEM((129 * ROWS, 128), F32), pltpu.VMEM((136, 128), F32)],
     )
 
 
@@ -516,7 +517,7 @@
         join_kernel,
         [((64 * ROWS, 128), BF16, pltpu.VMEM)],
         *args,
-        scratch=[pltpu.VMEM((64 * ROWS, 128), F32)],
+        scratch=[pltpu.VMEM((66 * ROWS, 128), F32)],
     )[0]
 
 
@@ -528,12 +529,12 @@
     return lax.ppermute(one, "space", near), two
 
 
-def swapped_two(x):
+def swapped_two(x, later):
     count = lax.axis_size("space")
     near = [(i, i ^ 2) for i in range(count)]
     away = [(i, ((i + 2) ^ 2) - 2) for i in range(2, count - 2)]
     away = lax.ppermute(x, "space", away)
-    return lax.ppermute(x, "space", near), away
+    return lax.ppermute(later, "space", near), away
 
 
 def partner(x):
@@ -624,7 +625,8 @@
     a2_two, a2_one, own = lax.optimization_barrier((a2_two, a2_one, own))
     h2, a3, sent, sides = second(where, a2_one, own, a2_two, f2, wd, marks)
     a3_one, a3_two = swapped(sent, sent)
-    a3_near, a3_away = swapped_two(a3)
+    a3_one, later = lax.optimization_barrier((a3_one, a3))
+    a3_near, a3_away = swapped_two(a3, later)
     own, f3, wh = head_own(a3, f3, wh)
     a3_two, a3_away, a3_one, a3_near, own, f3, wh = lax.optimization_barrier(
         (a3_two, a3_away, a3_one, a3_near, own, f3, wh)

time: 89.8 us -> 89.3 us (level)
  waiting for transfers between devices: 3.44 us -> 5.86 us
  blocking collectives: 32.6 us -> 30.6 us
    ppermute x3, starting transfers between devices: 12.3 us -> 8.39 us  [swapped(): return (lax.ppermute(one, 'space', near), two)]
    ppermute x1, starting transfers between devices: 4.9 us -> 7.54 us  [swapped_two(): return (lax.ppermute(later, 'space', near), away)]
    all_to_all x1, blocking collectives: 32.6 us -> 30.6 us  [finish(): terms = lax.all_to_all(pack, 'space', 0, 0, tiled=True)]
    ppermute x3, waiting for transfers between devices: 0.93 us -> 2.35 us  [swapped(): return (lax.ppermute(one, 'space', near), two)]
    ppermute x1, waiting for transfers between devices: 2.49 us -> 3.5 us  [swapped_two(): return (lax.ppermute(later, 'space', near), away)]
  transfers between devices with their start and end apart: 10 -> 10, of which waited for: 2 -> 3; matrix products, arithmetic and copies ran while one was open for 0% -> 0% of each run, Pallas kernels for 16% -> 16%
where the time goes in v10:
time: 89.3 us; the launch traced here: 89 us
  blocking collectives  30.6 us (34%)
  Pallas kernels  26.6 us (30%)
  starting transfers between devices  24 us (27%)
  waiting for transfers between devices  5.86 us (7%)
  between operations  0.94 us (1%)
    all_to_all x1, blocking collectives, finish(): terms = lax.all_to_all(pack, 'space', 0, 0, tiled=True)  30.6 us
    pallas_call x11, Pallas kernels, call(): pl.pallas_call(kernel, in_specs=[remote if i in far else scalar if a.dtyp...  19.9 us
    ppermute x3, starting transfers between devices, swapped(): return (lax.ppermute(one, 'space', near), two)  8.39 us
    ppermute x1, starting transfers between devices, swapped_two(): return (lax.ppermute(later, 'space', near), away)  7.54 us
    pallas_call x1, Pallas kernels, first(): pl.pallas_call(first_kernel, in_specs=[pl.BlockSpec(memory_space=pltpu.SM...  5.3 us
    ppermute x2, starting transfers between devices, partner(): return lax.ppermute(x, 'section', [(0, 1), (1, 0)])  5.23 us
    ppermute x1, waiting for transfers between devices, swapped_two(): return (lax.ppermute(later, 'space', near), away)  3.5 us
    ppermute x3, waiting for transfers between devices, swapped(): return (lax.ppermute(one, 'space', near), two)  2.35 us
  transfers between devices with their start and end apart: 10, of which 3 were waited for; matrix products, arithmetic and copies ran while one was open for 0% of the time, Pallas kernels for 16%

profile of v10, /device:TPU:1, one launch (start us, length us, event | category | flops | bytes accessed | tf_op | source)
XLA Modules:
  0.0 89.0 jit_solution(2952383293166110937)
XLA Ops:
  0.6 0.0 copy-start
  0.7 0.1 stack.23.where_ref
  0.8 5.3 %shard_map.110 = (bf16[2,2,1024,256]{3,2,1,0:T(8,128)(2,1)}, bf16[2,2,256,256]{3,2,1,0:T(8,128)(2,1)S(1)}, bf16[2,256,256]{2,1,0:T(8,128)(2,1)S(1)}, bf16[2,256,256]{2,1,0:T(8,128)(2,1)S(1)}) custom-call(s32[5]{0:T(128)S(1)} %stack.23.where_ref, bf16[4,32,4,8,512]{4,3,2,1,0:T(8,128)(2,1)} %vol_far.1, bf16[256,64]{1,0:T(8,128)(2,1)} %bitcast.36), custom_call_target="tpu_custom_call" | custom-call | tf_op jit(solution)/shard_map/pallas_call | solution.py:130
  6.1 0.7 collective-permute-start
  6.8 4.6 %collective-permute-start.1 = (bf16[2,256,256]{2,1,0:T(8,128)(2,1)S(1)}, bf16[2,256,256]{2,1,0:T(8,128)(2,1)S(1)}, u32[]{:S(2)}, u32[]{:S(2)}) collective-permute-start(bf16[2,256,256]{2,1,0:T(8,128)(2,1)S(1)} %get-tuple-element.54), channel_id=1, source_target_pairs={{0,1},{1,0},{2,3},{3,2},{4,5},{5,4},{6,7},{7,6},{8,9},{9,8},{10,11... | collective-permute-start | bytes 786440 | tf_op jit(solution)/shard_map/ppermute | solution.py:529
  11.3 0.0 copy-done.11
  11.3 0.2 pad_maximum_fusion.w2_ref
  11.6 0.0 copy-done.8
  11.6 0.0 copy-done.10
  11.6 3.4 %shard_map.111 = (bf16[256,2304]{1,0:T(8,128)(2,1)S(1)}, bf16[256,2304]{1,0:T(8,128)(2,1)}, bf16[256,2304]{1,0:T(8,128)(2,1)}, bf16[256,2304]{1,0:T(8,128)(2,1)}...) custom-call(bf16[27,64,128]{2,1,0:T(8,128)(2,1)S(1)} %pad_maximum_fusion.w2_ref, ...), custom_call_target="tpu_custom_call" | custom-call | tf_op jit(solution)/shard_map/pallas_call | solution.py:72
  15.0 1.1 %shard_map.112.own_ref = f32[2,2,256,256]{3,2,1,0:T(8,128)S(1)} custom-call(bf16[2,2,256,256]{3,2,1,0:T(8,128)(2,1)S(1)} %get-tuple-element.55.a_ref, bf16[256,2304]{1,0:T(8,128)(2,1)S(1)} %get-tuple-element.56.f2_ref), custom_call_target="tpu_custom_call" | custom-call | tf_op jit(solution)/shard_map/pallas_call | solution.py:72
  16.1 0.0 collective-permute-done.two_ref
  16.1 0.9 %collective-permute-done.1.one_ref = bf16[2,256,256]{2,1,0:T(8,128)(2,1)S(1)} collective-permute-done((bf16[2,256,256]{2,1,0:T(8,128)(2,1)S(1)}, bf16[2,256,256]{2,1,0:T(8,128)(2,1)S(1)}, u32[]{:S(2)}, u32[]{:S(2)}) %collective-permute-start.1) | collective-permute-done | bytes 262176 | tf_op jit(solution)/shard_map/ppermute | solution.py:529
  17.1 2.6 %shard_map.113 = (bf16[4,256,256]{2,1,0:T(8,128)(2,1)}, bf16[256,256]{1,0:T(8,128)(2,1)S(1)}, bf16[272,256]{1,0:T(8,128)(2,1)S(1)}, bf16[2,2,256,256]{3,2,1,0:T(8,128)(2,1)}) custom-call(s32[5]{0:T(128)S(1)} %stack.23.where_ref, bf16[2,256,256]{2,1,0:T(8,128)(2,1)S(1)} %collective-permute-done.1.one_ref, f32[2,2,256,256]{3,2,1,0:T(8,128)S(1)} %shard_map.112.own_ref, ...), custom_call_target="tpu_custom_call" | custom-call | tf_op jit(solution)/shard_map/pallas_call | solution.py:72
  19.6 1.1 %collective-permute-start.4 = (bf16[272,256]{1,0:T(8,128)(2,1)S(1)}, bf16[272,256]{1,0:T(8,128)(2,1)S(1)}, u32[]{:S(2)}, u32[]{:S(2)}) collective-permute-start(bf16[272,256]{1,0:T(8,128)(2,1)S(1)} %get-tuple-element.61), channel_id=1, source_target_pairs={{0,1},{1,0},{2,3},{3,2},{4,5},{5,4},{6,7},{7,6},{8,9},{9,8},{10,11... | collective-permute-start | bytes 417800 | tf_op jit(solution)/shard_map/ppermute | solution.py:529
  20.8 0.7 collective-permute-start.2
  21.4 0.7 collective-permute-start.3
  22.1 1.4 %collective-permute-done.4.one_ref = bf16[272,256]{1,0:T(8,128)(2,1)S(1)} collective-permute-done((bf16[272,256]{1,0:T(8,128)(2,1)S(1)}, bf16[272,256]{1,0:T(8,128)(2,1)S(1)}, u32[]{:S(2)}, u32[]{:S(2)}) %collective-permute-start.4) | collective-permute-done | bytes 139296 | tf_op jit(solution)/shard_map/ppermute | solution.py:529
  23.5 7.5 %collective-permute-start.5 = (bf16[256,256]{1,0:T(8,128)(2,1)S(1)}, bf16[256,256]{1,0:T(8,128)(2,1)S(1)}, u32[]{:S(2)}, u32[]{:S(2)}) collective-permute-start(bf16[256,256]{1,0:T(8,128)(2,1)S(1)} %get-tuple-element.64.a_ref.a3_ref), channel_id=1, source_target_pairs={{0,2},{1,3},{2,0},{3,1},{4,6},{5,7},{6,4},{7,5},{8,10},{9,11},{10,... | collective-permute-start | bytes 393224 | tf_op jit(solution)/shard_map/ppermute | solution.py:537
  31.1 0.6 shard_map.114
  31.7 0.0 collective-permute-done.3.away_ref
  31.7 0.0 collective-permute-done.2.two_ref
  31.7 3.5 %collective-permute-done.5.near_ref = bf16[256,256]{1,0:T(8,128)(2,1)S(1)} collective-permute-done((bf16[256,256]{1,0:T(8,128)(2,1)S(1)}, bf16[256,256]{1,0:T(8,128)(2,1)S(1)}, u32[]{:S(2)}, u32[]{:S(2)}) %collective-permute-start.5) | collective-permute-done | bytes 131104 | tf_op jit(solution)/shard_map/ppermute | solution.py:537
  35.2 0.0 copy-done.3
  35.2 3.6 %shard_map.115 = (bf16[3,256,256]{2,1,0:T(8,128)(2,1)S(1)}, f32[128,128]{1,0:T(8,128)S(1)}, bf16[2,2,256,256]{3,2,1,0:T(8,128)(2,1)S(1)}, bf16[2,256,256]{2,1,0:...) custom-call(s32[5]{0:T(128)S(1)} %stack.23.where_ref, ...), custom_call_target="tpu_custom_call" | custom-call | tf_op jit(solution)/shard_map/pallas_call | solution.py:72
  38.8 0.0 copy-start.1
  38.8 0.8 collective-permute-start.6
  39.6 2.7 %collective-permute-start.7 = (bf16[2,256,256]{2,1,0:T(8,128)(2,1)S(1)}, bf16[2,256,256]{2,1,0:T(8,128)(2,1)S(1)}, u32[]{:S(2)}, u32[]{:S(2)}) collective-permute-start(bf16[2,256,256]{2,1,0:T(8,128)(2,1)S(1)} %get-tuple-element.80), channel_id=1, source_target_pairs={{0,1},{1,0},{2,3},{3,2},{4,5},{5,4},{6,7},{7,6},{8,9},{9,8},{10,11... | collective-permute-start | bytes 786440 | tf_op jit(solution)/shard_map/ppermute | solution.py:529
  42.3 0.0 copy-done.7
  42.3 1.7 %shard_map.117.w2_ref = f32[7,2,64,128]{3,2,1,0:T(8,128)S(1)} custom-call(bf16[2,2,256,256]{3,2,1,0:T(8,128)(2,1)S(1)} %get-tuple-element.85.g_ref, bf16[2,2,256,256]{3,2,1,0:T(8,128)(2,1)S(1)} %get-tuple-element.55.a_ref, bf16[2,2,256,256]{3,2,1,0:T(8,128)(2,1)S(1)} %copy-done.7), custom_call_target="tpu_custom_call" | custom-call | tf_op jit(solution)/shard_map/pallas_call | solution.py:72
  44.1 0.0 copy-done.1
  44.1 1.1 %shard_map.119.own_ref = f32[2,2,256,256]{3,2,1,0:T(8,128)S(1)} custom-call(bf16[2,2,256,256]{3,2,1,0:T(8,128)(2,1)S(1)} %get-tuple-element.85.g_ref, bf16[256,2304]{1,0:T(8,128)(2,1)S(1)} %copy-done.1), custom_call_target="tpu_custom_call" | custom-call | tf_op jit(solution)/shard_map/pallas_call | solution.py:72
  45.2 1.2 %shard_map.116 = (f32[27,128,128]{2,1,0:T(8,128)S(1)}, f32[4,128,128]{2,1,0:T(8,128)S(1)}) custom-call(s32[5]{0:T(128)S(1)} %stack.23.where_ref, bf16[3,256,256]{2,1,0:T(8,128)(2,1)S(1)} %get-tuple-element.81.g_ref, bf16[272,256]{1,0:T(8,128)(2,1)S(1)} %collective-permute-done.4.one_ref, bf16[256,256]{1,0:T(8,128)(2,1)S(1)} %get-tuple-element.64.a_ref.a3_ref, ...), custom_call_target="tpu_custom_call" | custom-call | tf_op jit(solution)/shard_map/pallas_call | solution.py:72
  46.4 0.0 copy-start.2
  46.4 1.5 %shard_map.118 = (f32[2560,128]{1,0:T(8,128)S(1)}, bf16[2560,128]{1,0:T(8,128)(2,1)S(1)}) custom-call(s32[5]{0:T(128)S(1)} %stack.23.where_ref, f32[27,128,128]{2,1,0:T(8,128)S(1)} %get-tuple-element.83.w3_ref, f32[4,128,128]{2,1,0:T(8,128)S(1)} %get-tuple-element.84.d3_ref, f32[7,2,64,128]{3,2,1,0:T(8,128)S(1)} %shard_map.117.w2_ref, ...), custom_call_target="tpu_custom_call" | custom-call | tf_op jit(solution)/shard_map/pallas_call | solution.py:72
  47.9 0.0 collective-permute-done.6.two_ref
  47.9 0.0 collective-permute-done.7.one_ref
  47.9 3.6 %collective-permute-start.8 = (bf16[2560,128]{1,0:T(8,128)(2,1)S(1)}, bf16[2560,128]{1,0:T(8,128)(2,1)S(1)}, u32[]{:S(2)}, u32[]{:S(2)}) collective-permute-start(bf16[2560,128]{1,0:T(8,128)(2,1)S(1)} %get-tuple-element.96), channel_id=1, source_target_pairs={{0,64},{64,0},{1,65},{65,1},{2,66},{66,2},{3,67},{67,3},{4,68},{68... | collective-permute-start | bytes 1966088 | tf_op jit(solution)/shard_map/ppermute | solution.py:541
  51.5 0.0 copy-done.6
  51.5 2.5 %shard_map.120.down_ref = f32[64,256]{1,0:T(8,128)S(1)} custom-call(s32[5]{0:T(128)S(1)} %stack.23.where_ref, bf16[2,256,256]{2,1,0:T(8,128)(2,1)S(1)} %collective-permute-done.7.one_ref, f32[2,2,256,256]{3,2,1,0:T(8,128)S(1)} %shard_map.119.own_ref, bf16[2,256,256]{2,1,0:T(8,128)(2,1)S(1)} %collective-permute-done.6.two_ref, ...), custom_call_target="tpu_custom_call" | custom-call | tf_op jit(solution)/shard_map/pallas_call | solution.py:72
  54.0 0.0 collective-permute-done.8.came_ref
  54.0 0.7 shard_map.121
  54.7 30.6 %all_to_all.5 = bf16[64,40,128]{2,1,0:T(8,128)(2,1)S(1)} all-to-all(bf16[64,40,128]{2,1,0:T(8,128)(2,1)S(1)} %bitcast.31), channel_id=1, replica_groups=mesh['section'=2,'space'=64] {'space'}, dimensions={0} | all-to-all | bytes 1310720 | tf_op jit(solution)/shard_map/all_to_all | solution.py:600
  85.3 0.1 convert_reduce_fusion.sums_ref
  85.4 1.6 %collective-permute-start.9 = (f32[1,128]{1,0:T(1,128)S(1)}, f32[1,128]{1,0:T(1,128)S(1)}, u32[]{:S(2)}, u32[]{:S(2)}) collective-permute-start(f32[1,128]{1,0:T(1,128)S(1)} %slice.13), channel_id=1, source_target_pairs={{0,64},{64,0},{1,65},{65,1},{2,66},{66,2},{3,67},{67,3},{4,68},{68... | collective-permute-start | bytes 1544 | tf_op jit(solution)/shard_map/ppermute | solution.py:541
  87.0 1.4 %shard_map.122 = (f32[7,128]{1,0:T(8,128)}, f32[4,128]{1,0:T(4,128)}, f32[27,128]{1,0:T(8,128)}, f32[4]{0:T(128)}) custom-call(f32[40,128]{1,0:T(8,128)S(1)} %convert_reduce_fusion.sums_ref), custom_call_target="tpu_custom_call" | custom-call | tf_op jit(solution)/shard_map/pallas_call | solution.py:588
  88.5 0.0 collective-permute-done.9
  88.5 0.5 fusion
  (16 shorter events, 0.0 us)
Async XLA Ops:
  0.6 15.5 %copy-start = (s32[4,1,2,128]{3,2,1,0:T(2,128)S(1)}, s32[4,1,2,128]{3,2,1,0:T(2,128)}, u32[]{:S(2)}) copy-start(s32[4,1,2,128]{3,2,1,0:T(2,128)} %param.8) | copy-start | bytes 12292
  0.8 10.6 %copy-start.11 = (bf16[64,64,3,3,3]{1,0,4,3,2:T(8,128)(2,1)S(1)}, bf16[64,64,3,3,3]{1,0,4,3,2:T(8,128)(2,1)}, u32[]{:S(2)}) copy-start(bf16[64,64,3,3,3]{1,0,4,3,2:T(8,128)(2,1)} %param.10) | copy-start | bytes 663556
  0.8 10.8 %copy-start.8 = (bf16[128,64,2,2,2]{0,4,3,2,1:T(2,128)(2,1)S(1)}, bf16[128,64,2,2,2]{0,4,3,2,1:T(2,128)(2,1)}, u32[]{:S(2)}) copy-start(bf16[128,64,2,2,2]{0,4,3,2,1:T(2,128)(2,1)} %param.11) | copy-start | bytes 393220
  0.8 10.8 %copy-start.10 = (bf16[128,4]{0,1:T(4,128)(2,1)S(1)}, bf16[128,4]{0,1:T(4,128)(2,1)}, u32[]{:S(2)}) copy-start(bf16[128,4]{0,1:T(4,128)(2,1)} %param.13) | copy-start | bytes 3076
  6.1 10.0 %collective-permute-start = (bf16[2,256,256]{2,1,0:T(8,128)(2,1)S(1)}, bf16[2,256,256]{2,1,0:T(8,128)(2,1)S(1)}, u32[]{:S(2)}, u32[]{:S(2)}) collective-permute-start(bf16[2,256,256]{2,1,0:T(8,128)(2,1)S(1)} %get-tuple-element.53), channel_id=1, source_target_pairs={{1,2},{2,1},{3,4},{4,3},{5,6},{6,5},{7,8},{8,7},{9,10},{10,9},{11,... | collective-permute-start | bytes 786440 | tf_op jit(solution)/shard_map/ppermute | solution.py:528
  6.8 10.3 %collective-permute-start.1 = (bf16[2,256,256]{2,1,0:T(8,128)(2,1)S(1)}, bf16[2,256,256]{2,1,0:T(8,128)(2,1)S(1)}, u32[]{:S(2)}, u32[]{:S(2)}) collective-permute-start(bf16[2,256,256]{2,1,0:T(8,128)(2,1)S(1)} %get-tuple-element.54), channel_id=1, source_target_pairs={{0,1},{1,0},{2,3},{3,2},{4,5},{5,4},{6,7},{7,6},{8,9},{9,8},{10,11... | collective-permute-start | bytes 786440 | tf_op jit(solution)/shard_map/ppermute | solution.py:529
  17.0 14.0 %copy-start.4 = (bf16[256,2304]{1,0:T(8,128)(2,1)S(1)}, bf16[256,2304]{1,0:T(8,128)(2,1)}, u32[]{:S(2)}) copy-start(bf16[256,2304]{1,0:T(8,128)(2,1)} %get-tuple-element.65.f3_ref) | copy-start | bytes 3538948
  17.1 14.0 %copy-start.9 = (bf16[256,128]{1,0:T(8,128)(2,1)S(1)}, bf16[256,128]{1,0:T(8,128)(2,1)}, u32[]{:S(2)}) copy-start(bf16[256,128]{1,0:T(8,128)(2,1)} %get-tuple-element.66.wh_ref) | copy-start | bytes 196612
  17.1 18.1 %copy-start.5 = (bf16[256,2304]{1,0:T(8,128)(2,1)S(1)}, bf16[256,2304]{1,0:T(8,128)(2,1)}, u32[]{:S(2)}) copy-start(bf16[256,2304]{1,0:T(8,128)(2,1)} %get-tuple-element.77.b3_ref) | copy-start | bytes 3538948
  19.6 15.6 %copy-start.3 = (bf16[4,256,256]{2,1,0:T(8,128)(2,1)S(1)}, bf16[4,256,256]{2,1,0:T(8,128)(2,1)}, u32[]{:S(2)}) copy-start(bf16[4,256,256]{2,1,0:T(8,128)(2,1)} %get-tuple-element.78.h_ref) | copy-start | bytes 1572868
  19.6 3.9 %collective-permute-start.4 = (bf16[272,256]{1,0:T(8,128)(2,1)S(1)}, bf16[272,256]{1,0:T(8,128)(2,1)S(1)}, u32[]{:S(2)}, u32[]{:S(2)}) collective-permute-start(bf16[272,256]{1,0:T(8,128)(2,1)S(1)} %get-tuple-element.61), channel_id=1, source_target_pairs={{0,1},{1,0},{2,3},{3,2},{4,5},{5,4},{6,7},{7,6},{8,9},{9,8},{10,11... | collective-permute-start | bytes 417800 | tf_op jit(solution)/shard_map/ppermute | solution.py:529
  20.8 10.9 %collective-permute-start.2 = (bf16[272,256]{1,0:T(8,128)(2,1)S(1)}, bf16[272,256]{1,0:T(8,128)(2,1)S(1)}, u32[]{:S(2)}, u32[]{:S(2)}) collective-permute-start(bf16[272,256]{1,0:T(8,128)(2,1)S(1)} %get-tuple-element.61), channel_id=1, source_target_pairs={{1,2},{2,1},{3,4},{4,3},{5,6},{6,5},{7,8},{8,7},{9,10},{10,9},{11,... | collective-permute-start | bytes 417800 | tf_op jit(solution)/shard_map/ppermute | solution.py:528
  21.4 10.2 %collective-permute-start.3 = (bf16[256,256]{1,0:T(8,128)(2,1)S(1)}, bf16[256,256]{1,0:T(8,128)(2,1)S(1)}, u32[]{:S(2)}, u32[]{:S(2)}) collective-permute-start(bf16[256,256]{1,0:T(8,128)(2,1)S(1)} %get-tuple-element.64.a_ref.a3_ref), channel_id=1, source_target_pairs={{2,4},{3,5},{4,2},{5,3},{6,8},{7,9},{8,6},{9,7},{10,12},{11,13},{1... | collective-permute-start | bytes 393224 | tf_op jit(solution)/shard_map/ppermute | solution.py:536
  23.5 11.6 %collective-permute-start.5 = (bf16[256,256]{1,0:T(8,128)(2,1)S(1)}, bf16[256,256]{1,0:T(8,128)(2,1)S(1)}, u32[]{:S(2)}, u32[]{:S(2)}) collective-permute-start(bf16[256,256]{1,0:T(8,128)(2,1)S(1)} %get-tuple-element.64.a_ref.a3_ref), channel_id=1, source_target_pairs={{0,2},{1,3},{2,0},{3,1},{4,6},{5,7},{6,4},{7,5},{8,10},{9,11},{10,... | collective-permute-start | bytes 393224 | tf_op jit(solution)/shard_map/ppermute | solution.py:537
  35.2 7.1 %copy-start.7 = (bf16[2,2,256,256]{3,2,1,0:T(8,128)(2,1)S(1)}, bf16[2,2,256,256]{3,2,1,0:T(8,128)(2,1)}, u32[]{:S(2)}) copy-start(bf16[2,2,256,256]{3,2,1,0:T(8,128)(2,1)} %get-tuple-element.86.sides_ref) | copy-start | bytes 1572868
  38.8 5.3 %copy-start.1 = (bf16[256,2304]{1,0:T(8,128)(2,1)S(1)}, bf16[256,2304]{1,0:T(8,128)(2,1)}, u32[]{:S(2)}) copy-start(bf16[256,2304]{1,0:T(8,128)(2,1)} %get-tuple-element.89.b2_ref) | copy-start | bytes 3538948
  38.8 9.1 %collective-permute-start.6 = (bf16[2,256,256]{2,1,0:T(8,128)(2,1)S(1)}, bf16[2,256,256]{2,1,0:T(8,128)(2,1)S(1)}, u32[]{:S(2)}, u32[]{:S(2)}) collective-permute-start(bf16[2,256,256]{2,1,0:T(8,128)(2,1)S(1)} %get-tuple-element.79), channel_id=1, source_target_pairs={{1,2},{2,1},{3,4},{4,3},{5,6},{6,5},{7,8},{8,7},{9,10},{10,9},{11,... | collective-permute-start | bytes 786440 | tf_op jit(solution)/shard_map/ppermute | solution.py:528
  39.6 8.3 %collective-permute-start.7 = (bf16[2,256,256]{2,1,0:T(8,128)(2,1)S(1)}, bf16[2,256,256]{2,1,0:T(8,128)(2,1)S(1)}, u32[]{:S(2)}, u32[]{:S(2)}) collective-permute-start(bf16[2,256,256]{2,1,0:T(8,128)(2,1)S(1)} %get-tuple-element.80), channel_id=1, source_target_pairs={{0,1},{1,0},{2,3},{3,2},{4,5},{5,4},{6,7},{7,6},{8,9},{9,8},{10,11... | collective-permute-start | bytes 786440 | tf_op jit(solution)/shard_map/ppermute | solution.py:529
  45.2 6.4 %copy-start.6 = (bf16[1024,256]{1,0:T(8,128)(2,1)S(1)}, bf16[1024,256]{1,0:T(8,128)(2,1)}, u32[]{:S(2)}) copy-start(bf16[1024,256]{1,0:T(8,128)(2,1)} %get-tuple-element.94.perm_ref) | copy-start | bytes 1572868
  46.4 5.1 %copy-start.2 = (bf16[2,2,1024,256]{3,2,1,0:T(8,128)(2,1)S(1)}, bf16[2,2,1024,256]{3,2,1,0:T(8,128)(2,1)}, u32[]{:S(2)}) copy-start(bf16[2,2,1024,256]{3,2,1,0:T(8,128)(2,1)} %get-tuple-element.93.vp_ref) | copy-start | bytes 6291460
  47.9 6.1 %collective-permute-start.8 = (bf16[2560,128]{1,0:T(8,128)(2,1)S(1)}, bf16[2560,128]{1,0:T(8,128)(2,1)S(1)}, u32[]{:S(2)}, u32[]{:S(2)}) collective-permute-start(bf16[2560,128]{1,0:T(8,128)(2,1)S(1)} %get-tuple-element.96), channel_id=1, source_target_pairs={{0,64},{64,0},{1,65},{65,1},{2,66},{66,2},{3,67},{67,3},{4,68},{68... | collective-permute-start | bytes 1966088 | tf_op jit(solution)/shard_map/ppermute | solution.py:541
  85.4 3.1 %collective-permute-start.9 = (f32[1,128]{1,0:T(1,128)S(1)}, f32[1,128]{1,0:T(1,128)S(1)}, u32[]{:S(2)}, u32[]{:S(2)}) collective-permute-start(f32[1,128]{1,0:T(1,128)S(1)} %slice.13), channel_id=1, source_target_pairs={{0,64},{64,0},{1,65},{65,1},{2,66},{66,2},{3,67},{67,3},{4,68},{68... | collective-permute-start | bytes 1544 | tf_op jit(solution)/shard_map/ppermute | solution.py:541

commit v11 on v10

--- a/solution.py
+++ b/solution.py
@@ -446,7 +446,8 @@
     )
 
 
-def last_own_kernel(g_ref, b2_ref, out_ref, b_ref):
+def last_own_kernel(g_ref, b2_ref, a_ref, out_ref, slope_ref, b_ref):
+    slope_ref[...] = slope(a_ref[...])
     for n in range(CROPS):
         for d in range(2):
             put_three(b_ref, (2 * n + d) * 3 * T, three_two(g_ref[n, d]))
@@ -455,13 +456,13 @@
         out_ref[n, 1] = dot(b2_ref[:, : 6 * T], b_ref[own, :])
 
 
-def last_own(g, b2):
+def last_own(g, b2, a):
     return call(
         last_own_kernel,
-        [((CROPS, 2, T, T), F32, pltpu.VMEM)],
-        g, b2,
+        [((CROPS, 2, T, T), F32, pltpu.VMEM)] * 2,
+        g, b2, a,
         scratch=[pltpu.VMEM((12 * T, T), BF16)],
-    )[0]
+    )
 
 
 def last_kernel(where_ref, one_ref, own_ref, two_ref, b2_ref, a_ref, vp_ref, perm_ref, down_ref, b_ref, t_ref):
@@ -471,7 +472,7 @@
             at = (2 * n + d) * 3 * T
             put_three(b_ref, at, three_two(plane))
             rest = dot(b2_ref[:, d * 6 * T : d * 6 * T + 3 * T], b_ref[pl.ds(at, 3 * T), :])
-            gy.append(((own_ref[n, d] + rest) * slope(a_ref[n, d])).astype(BF16))
+            gy.append(((own_ref[n, d] + rest) * a_ref[n, d]).astype(BF16))
         t = dot_nt(gy[0], vp_ref[n, 0]) + dot_nt(gy[1], vp_ref[n, 1])
         if n == 0:
             t_ref[...] = t
@@ -636,12 +637,12 @@
     )
     gw3, gd3 = weight_three(where, gz4, a3_one, a3, a3_two, gy3, h2)
     gz2_one, gz2_two = swapped(one, two)
-    own = last_own(gz2, b2)
+    own, slopes = last_own(gz2, b2, a2)
     gw2 = weight_two(gz2, a2, sides)
     keep, send = packed(where, gw3, gd3, gw2, gh)
-    gz2_two, gz2_one, send, own = lax.optimization_barrier((gz2_two, gz2_one, send, own))
+    gz2_two, gz2_one, send, own, slopes = lax.optimization_barrier((gz2_two, gz2_one, send, own, slopes))
     came = partner(send)
-    down = last(where, gz2_one, own, gz2_two, b2, a2, vp, perm)
+    down = last(where, gz2_one, own, gz2_two, b2, slopes, vp, perm)
     pack = joined(where, down, keep, came)
     return finish(pack.reshape(64, ROWS, 128))
 

time: 89.3 us -> 89.5 us (level)
  no operation moved by 1% of the time
where the time goes in v11:
time: 89.5 us; the launch traced here: 89.1 us
  blocking collectives  30.6 us (34%)
  Pallas kernels  26.7 us (30%)
  starting transfers between devices  24 us (27%)
  waiting for transfers between devices  5.86 us (7%)
  between operations  0.94 us (1%)
    all_to_all x1, blocking collectives, finish(): terms = lax.all_to_all(pack, 'space', 0, 0, tiled=True)  30.6 us
    pallas_call x11, Pallas kernels, call(): pl.pallas_call(kernel, in_specs=[remote if i in far else scalar if a.dtyp...  20 us
    ppermute x3, starting transfers between devices, swapped(): return (lax.ppermute(one, 'space', near), two)  8.39 us
    ppermute x1, starting transfers between devices, swapped_two(): return (lax.ppermute(later, 'space', near), away)  7.54 us
    pallas_call x1, Pallas kernels, first(): pl.pallas_call(first_kernel, in_specs=[pl.BlockSpec(memory_space=pltpu.SM...  5.3 us
    ppermute x2, starting transfers between devices, partner(): return lax.ppermute(x, 'section', [(0, 1), (1, 0)])  5.22 us
    ppermute x1, waiting for transfers between devices, swapped_two(): return (lax.ppermute(later, 'space', near), away)  3.5 us
    ppermute x3, waiting for transfers between devices, swapped(): return (lax.ppermute(one, 'space', near), two)  2.35 us
  transfers between devices with their start and end apart: 10, of which 3 were waited for; matrix products, arithmetic and copies ran while one was open for 0% of the time, Pallas kernels for 16%

profile of v11, /device:TPU:1, one launch (start us, length us, event | category | flops | bytes accessed | tf_op | source)
XLA Modules:
  0.0 89.1 jit_solution(1643002454113266967)
XLA Ops:
  0.6 0.0 copy-start
  0.7 0.1 stack.23.where_ref
  0.8 5.3 %shard_map.110 = (bf16[2,2,1024,256]{3,2,1,0:T(8,128)(2,1)}, bf16[2,2,256,256]{3,2,1,0:T(8,128)(2,1)S(1)}, bf16[2,256,256]{2,1,0:T(8,128)(2,1)S(1)}, bf16[2,256,256]{2,1,0:T(8,128)(2,1)S(1)}) custom-call(s32[5]{0:T(128)S(1)} %stack.23.where_ref, bf16[4,32,4,8,512]{4,3,2,1,0:T(8,128)(2,1)} %vol_far.1, bf16[256,64]{1,0:T(8,128)(2,1)} %bitcast.36), custom_call_target="tpu_custom_call" | custom-call | tf_op jit(solution)/shard_map/pallas_call | solution.py:130
  6.1 0.7 collective-permute-start
  6.8 4.6 %collective-permute-start.1 = (bf16[2,256,256]{2,1,0:T(8,128)(2,1)S(1)}, bf16[2,256,256]{2,1,0:T(8,128)(2,1)S(1)}, u32[]{:S(2)}, u32[]{:S(2)}) collective-permute-start(bf16[2,256,256]{2,1,0:T(8,128)(2,1)S(1)} %get-tuple-element.57), channel_id=1, source_target_pairs={{0,1},{1,0},{2,3},{3,2},{4,5},{5,4},{6,7},{7,6},{8,9},{9,8},{10,11... | collective-permute-start | bytes 786440 | tf_op jit(solution)/shard_map/ppermute | solution.py:530
  11.3 0.0 copy-done.11
  11.3 0.2 pad_maximum_fusion.w2_ref
  11.6 0.0 copy-done.8
  11.6 0.0 copy-done.10
  11.6 3.4 %shard_map.111 = (bf16[256,2304]{1,0:T(8,128)(2,1)S(1)}, bf16[256,2304]{1,0:T(8,128)(2,1)}, bf16[256,2304]{1,0:T(8,128)(2,1)}, bf16[256,2304]{1,0:T(8,128)(2,1)}...) custom-call(bf16[27,64,128]{2,1,0:T(8,128)(2,1)S(1)} %pad_maximum_fusion.w2_ref, ...), custom_call_target="tpu_custom_call" | custom-call | tf_op jit(solution)/shard_map/pallas_call | solution.py:72
  15.0 1.1 %shard_map.112.own_ref = f32[2,2,256,256]{3,2,1,0:T(8,128)S(1)} custom-call(bf16[2,2,256,256]{3,2,1,0:T(8,128)(2,1)S(1)} %get-tuple-element.58.a_ref, bf16[256,2304]{1,0:T(8,128)(2,1)S(1)} %get-tuple-element.59.f2_ref), custom_call_target="tpu_custom_call" | custom-call | tf_op jit(solution)/shard_map/pallas_call | solution.py:72
  16.1 0.0 copy-done
  16.1 0.0 collective-permute-done.two_ref
  16.1 0.9 %collective-permute-done.1.one_ref = bf16[2,256,256]{2,1,0:T(8,128)(2,1)S(1)} collective-permute-done((bf16[2,256,256]{2,1,0:T(8,128)(2,1)S(1)}, bf16[2,256,256]{2,1,0:T(8,128)(2,1)S(1)}, u32[]{:S(2)}, u32[]{:S(2)}) %collective-permute-start.1) | collective-permute-done | bytes 262176 | tf_op jit(solution)/shard_map/ppermute | solution.py:530
  17.1 2.6 %shard_map.113 = (bf16[4,256,256]{2,1,0:T(8,128)(2,1)}, bf16[256,256]{1,0:T(8,128)(2,1)S(1)}, bf16[272,256]{1,0:T(8,128)(2,1)S(1)}, bf16[2,2,256,256]{3,2,1,0:T(8,128)(2,1)}) custom-call(s32[5]{0:T(128)S(1)} %stack.23.where_ref, bf16[2,256,256]{2,1,0:T(8,128)(2,1)S(1)} %collective-permute-done.1.one_ref, f32[2,2,256,256]{3,2,1,0:T(8,128)S(1)} %shard_map.112.own_ref, ...), custom_call_target="tpu_custom_call" | custom-call | tf_op jit(solution)/shard_map/pallas_call | solution.py:72
  19.6 1.1 %collective-permute-start.4 = (bf16[272,256]{1,0:T(8,128)(2,1)S(1)}, bf16[272,256]{1,0:T(8,128)(2,1)S(1)}, u32[]{:S(2)}, u32[]{:S(2)}) collective-permute-start(bf16[272,256]{1,0:T(8,128)(2,1)S(1)} %get-tuple-element.64), channel_id=1, source_target_pairs={{0,1},{1,0},{2,3},{3,2},{4,5},{5,4},{6,7},{7,6},{8,9},{9,8},{10,11... | collective-permute-start | bytes 417800 | tf_op jit(solution)/shard_map/ppermute | solution.py:530
  20.8 0.7 collective-permute-start.2
  21.4 0.7 collective-permute-start.3
  22.1 1.4 %collective-permute-done.4.one_ref = bf16[272,256]{1,0:T(8,128)(2,1)S(1)} collective-permute-done((bf16[272,256]{1,0:T(8,128)(2,1)S(1)}, bf16[272,256]{1,0:T(8,128)(2,1)S(1)}, u32[]{:S(2)}, u32[]{:S(2)}) %collective-permute-start.4) | collective-permute-done | bytes 139296 | tf_op jit(solution)/shard_map/ppermute | solution.py:530
  23.5 7.5 %collective-permute-start.5 = (bf16[256,256]{1,0:T(8,128)(2,1)S(1)}, bf16[256,256]{1,0:T(8,128)(2,1)S(1)}, u32[]{:S(2)}, u32[]{:S(2)}) collective-permute-start(bf16[256,256]{1,0:T(8,128)(2,1)S(1)} %get-tuple-element.67.a_ref.a3_ref), channel_id=1, source_target_pairs={{0,2},{1,3},{2,0},{3,1},{4,6},{5,7},{6,4},{7,5},{8,10},{9,11},{10,... | collective-permute-start | bytes 393224 | tf_op jit(solution)/shard_map/ppermute | solution.py:538
  31.1 0.0 copy-done.4
  31.1 0.0 copy-done.9
  31.1 0.6 shard_map.114
  31.7 0.0 collective-permute-done.3.away_ref
  31.7 0.0 collective-permute-done.2.two_ref
  31.7 3.5 %collective-permute-done.5.near_ref = bf16[256,256]{1,0:T(8,128)(2,1)S(1)} collective-permute-done((bf16[256,256]{1,0:T(8,128)(2,1)S(1)}, bf16[256,256]{1,0:T(8,128)(2,1)S(1)}, u32[]{:S(2)}, u32[]{:S(2)}) %collective-permute-start.5) | collective-permute-done | bytes 131104 | tf_op jit(solution)/shard_map/ppermute | solution.py:538
  35.2 0.0 copy-done.5
  35.2 0.0 copy-done.3
  35.2 3.6 %shard_map.115 = (bf16[3,256,256]{2,1,0:T(8,128)(2,1)S(1)}, f32[128,128]{1,0:T(8,128)S(1)}, bf16[2,2,256,256]{3,2,1,0:T(8,128)(2,1)S(1)}, bf16[2,256,256]{2,1,0:...) custom-call(s32[5]{0:T(128)S(1)} %stack.23.where_ref, ...), custom_call_target="tpu_custom_call" | custom-call | tf_op jit(solution)/shard_map/pallas_call | solution.py:72
  38.8 0.8 collective-permute-start.6
  39.6 2.7 %collective-permute-start.7 = (bf16[2,256,256]{2,1,0:T(8,128)(2,1)S(1)}, bf16[2,256,256]{2,1,0:T(8,128)(2,1)S(1)}, u32[]{:S(2)}, u32[]{:S(2)}) collective-permute-start(bf16[2,256,256]{2,1,0:T(8,128)(2,1)S(1)} %get-tuple-element.83), channel_id=1, source_target_pairs={{0,1},{1,0},{2,3},{3,2},{4,5},{5,4},{6,7},{7,6},{8,9},{9,8},{10,11... | collective-permute-start | bytes 786440 | tf_op jit(solution)/shard_map/ppermute | solution.py:530
  42.3 1.7 %shard_map.117.w2_ref = f32[7,2,64,128]{3,2,1,0:T(8,128)S(1)} custom-call(bf16[2,2,256,256]{3,2,1,0:T(8,128)(2,1)S(1)} %get-tuple-element.88.g_ref, bf16[2,2,256,256]{3,2,1,0:T(8,128)(2,1)S(1)} %get-tuple-element.58.a_ref, bf16[2,2,256,256]{3,2,1,0:T(8,128)(2,1)S(1)} %copy-done.7), custom_call_target="tpu_custom_call" | custom-call | tf_op jit(solution)/shard_map/pallas_call | solution.py:72
  44.1 1.3 %shard_map.119 = (f32[2,2,256,256]{3,2,1,0:T(8,128)S(1)}, f32[2,2,256,256]{3,2,1,0:T(8,128)S(1)}) custom-call(bf16[2,2,256,256]{3,2,1,0:T(8,128)(2,1)S(1)} %get-tuple-element.88.g_ref, bf16[256,2304]{1,0:T(8,128)(2,1)S(1)} %copy-done.1, bf16[2,2,256,256]{3,2,1,0:T(8,128)(2,1)S(1)} %get-tuple-element.58.a_ref), custom_call_target="tpu_custom_call" | custom-call | tf_op jit(solution)/shard_map/pallas_call | solution.py:72
  45.4 1.2 %shard_map.116 = (f32[27,128,128]{2,1,0:T(8,128)S(1)}, f32[4,128,128]{2,1,0:T(8,128)S(1)}) custom-call(s32[5]{0:T(128)S(1)} %stack.23.where_ref, bf16[3,256,256]{2,1,0:T(8,128)(2,1)S(1)} %get-tuple-element.84.g_ref, bf16[272,256]{1,0:T(8,128)(2,1)S(1)} %collective-permute-done.4.one_ref, bf16[256,256]{1,0:T(8,128)(2,1)S(1)} %get-tuple-element.67.a_ref.a3_ref, ...), custom_call_target="tpu_custom_call" | custom-call | tf_op jit(solution)/shard_map/pallas_call | solution.py:72
  46.6 1.5 %shard_map.118 = (f32[2560,128]{1,0:T(8,128)S(1)}, bf16[2560,128]{1,0:T(8,128)(2,1)S(1)}) custom-call(s32[5]{0:T(128)S(1)} %stack.23.where_ref, f32[27,128,128]{2,1,0:T(8,128)S(1)} %get-tuple-element.86.w3_ref, f32[4,128,128]{2,1,0:T(8,128)S(1)} %get-tuple-element.87.d3_ref, f32[7,2,64,128]{3,2,1,0:T(8,128)S(1)} %shard_map.117.w2_ref, ...), custom_call_target="tpu_custom_call" | custom-call | tf_op jit(solution)/shard_map/pallas_call | solution.py:72
  48.1 0.0 collective-permute-done.6.two_ref
  48.1 0.0 collective-permute-done.7.one_ref
  48.1 3.6 %collective-permute-start.8 = (bf16[2560,128]{1,0:T(8,128)(2,1)S(1)}, bf16[2560,128]{1,0:T(8,128)(2,1)S(1)}, u32[]{:S(2)}, u32[]{:S(2)}) collective-permute-start(bf16[2560,128]{1,0:T(8,128)(2,1)S(1)} %get-tuple-element.102), channel_id=1, source_target_pairs={{0,64},{64,0},{1,65},{65,1},{2,66},{66,2},{3,67},{67,3},{4,68},{68... | collective-permute-start | bytes 1966088 | tf_op jit(solution)/shard_map/ppermute | solution.py:542
  51.7 0.0 copy-done.2
  51.7 2.4 %shard_map.120.down_ref = f32[64,256]{1,0:T(8,128)S(1)} custom-call(s32[5]{0:T(128)S(1)} %stack.23.where_ref, bf16[2,256,256]{2,1,0:T(8,128)(2,1)S(1)} %collective-permute-done.7.one_ref, f32[2,2,256,256]{3,2,1,0:T(8,128)S(1)} %get-tuple-element.96.own_ref, bf16[2,256,256]{2,1,0:T(8,128)(2,1)S(1)} %collective-permute-done.6.two_ref, ...), custom_call_target="tpu_custom_call" | custom-call | tf_op jit(solution)/shard_map/pallas_call | solution.py:72
  54.1 0.0 collective-permute-done.8.came_ref
  54.1 0.7 shard_map.121
  54.8 30.6 %all_to_all.5 = bf16[64,40,128]{2,1,0:T(8,128)(2,1)S(1)} all-to-all(bf16[64,40,128]{2,1,0:T(8,128)(2,1)S(1)} %bitcast.31), channel_id=1, replica_groups=mesh['section'=2,'space'=64] {'space'}, dimensions={0} | all-to-all | bytes 1310720 | tf_op jit(solution)/shard_map/all_to_all | solution.py:601
  85.4 0.1 convert_reduce_fusion.sums_ref
  85.6 1.6 %collective-permute-start.9 = (f32[1,128]{1,0:T(1,128)S(1)}, f32[1,128]{1,0:T(1,128)S(1)}, u32[]{:S(2)}, u32[]{:S(2)}) collective-permute-start(f32[1,128]{1,0:T(1,128)S(1)} %slice.13), channel_id=1, source_target_pairs={{0,64},{64,0},{1,65},{65,1},{2,66},{66,2},{3,67},{67,3},{4,68},{68... | collective-permute-start | bytes 1544 | tf_op jit(solution)/shard_map/ppermute | solution.py:542
  87.2 1.4 %shard_map.122 = (f32[7,128]{1,0:T(8,128)}, f32[4,128]{1,0:T(4,128)}, f32[27,128]{1,0:T(8,128)}, f32[4]{0:T(128)}) custom-call(f32[40,128]{1,0:T(8,128)S(1)} %convert_reduce_fusion.sums_ref), custom_call_target="tpu_custom_call" | custom-call | tf_op jit(solution)/shard_map/pallas_call | solution.py:589
  88.6 0.0 collective-permute-done.9
  88.6 0.5 fusion
  (16 shorter events, 0.0 us)
Async XLA Ops:
  0.6 15.4 %copy-start = (s32[4,1,2,128]{3,2,1,0:T(2,128)S(1)}, s32[4,1,2,128]{3,2,1,0:T(2,128)}, u32[]{:S(2)}) copy-start(s32[4,1,2,128]{3,2,1,0:T(2,128)} %param.8) | copy-start | bytes 12292
  0.8 10.6 %copy-start.11 = (bf16[64,64,3,3,3]{1,0,4,3,2:T(8,128)(2,1)S(1)}, bf16[64,64,3,3,3]{1,0,4,3,2:T(8,128)(2,1)}, u32[]{:S(2)}) copy-start(bf16[64,64,3,3,3]{1,0,4,3,2:T(8,128)(2,1)} %param.10) | copy-start | bytes 663556
  0.8 10.8 %copy-start.8 = (bf16[128,64,2,2,2]{0,4,3,2,1:T(2,128)(2,1)S(1)}, bf16[128,64,2,2,2]{0,4,3,2,1:T(2,128)(2,1)}, u32[]{:S(2)}) copy-start(bf16[128,64,2,2,2]{0,4,3,2,1:T(2,128)(2,1)} %param.11) | copy-start | bytes 393220
  0.8 10.8 %copy-start.10 = (bf16[128,4]{0,1:T(4,128)(2,1)S(1)}, bf16[128,4]{0,1:T(4,128)(2,1)}, u32[]{:S(2)}) copy-start(bf16[128,4]{0,1:T(4,128)(2,1)} %param.13) | copy-start | bytes 3076
  6.1 10.0 %collective-permute-start = (bf16[2,256,256]{2,1,0:T(8,128)(2,1)S(1)}, bf16[2,256,256]{2,1,0:T(8,128)(2,1)S(1)}, u32[]{:S(2)}, u32[]{:S(2)}) collective-permute-start(bf16[2,256,256]{2,1,0:T(8,128)(2,1)S(1)} %get-tuple-element.56), channel_id=1, source_target_pairs={{1,2},{2,1},{3,4},{4,3},{5,6},{6,5},{7,8},{8,7},{9,10},{10,9},{11,... | collective-permute-start | bytes 786440 | tf_op jit(solution)/shard_map/ppermute | solution.py:529
  6.8 10.3 %collective-permute-start.1 = (bf16[2,256,256]{2,1,0:T(8,128)(2,1)S(1)}, bf16[2,256,256]{2,1,0:T(8,128)(2,1)S(1)}, u32[]{:S(2)}, u32[]{:S(2)}) collective-permute-start(bf16[2,256,256]{2,1,0:T(8,128)(2,1)S(1)} %get-tuple-element.57), channel_id=1, source_target_pairs={{0,1},{1,0},{2,3},{3,2},{4,5},{5,4},{6,7},{7,6},{8,9},{9,8},{10,11... | collective-permute-start | bytes 786440 | tf_op jit(solution)/shard_map/ppermute | solution.py:530
  17.0 14.0 %copy-start.4 = (bf16[256,2304]{1,0:T(8,128)(2,1)S(1)}, bf16[256,2304]{1,0:T(8,128)(2,1)}, u32[]{:S(2)}) copy-start(bf16[256,2304]{1,0:T(8,128)(2,1)} %get-tuple-element.68.f3_ref) | copy-start | bytes 3538948
  17.0 14.0 %copy-start.9 = (bf16[256,128]{1,0:T(8,128)(2,1)S(1)}, bf16[256,128]{1,0:T(8,128)(2,1)}, u32[]{:S(2)}) copy-start(bf16[256,128]{1,0:T(8,128)(2,1)} %get-tuple-element.69.wh_ref) | copy-start | bytes 196612
  17.1 18.1 %copy-start.5 = (bf16[256,2304]{1,0:T(8,128)(2,1)S(1)}, bf16[256,2304]{1,0:T(8,128)(2,1)}, u32[]{:S(2)}) copy-start(bf16[256,2304]{1,0:T(8,128)(2,1)} %get-tuple-element.80.b3_ref) | copy-start | bytes 3538948
  19.6 15.6 %copy-start.3 = (bf16[4,256,256]{2,1,0:T(8,128)(2,1)S(1)}, bf16[4,256,256]{2,1,0:T(8,128)(2,1)}, u32[]{:S(2)}) copy-start(bf16[4,256,256]{2,1,0:T(8,128)(2,1)} %get-tuple-element.81.h_ref) | copy-start | bytes 1572868
  19.6 3.9 %collective-permute-start.4 = (bf16[272,256]{1,0:T(8,128)(2,1)S(1)}, bf16[272,256]{1,0:T(8,128)(2,1)S(1)}, u32[]{:S(2)}, u32[]{:S(2)}) collective-permute-start(bf16[272,256]{1,0:T(8,128)(2,1)S(1)} %get-tuple-element.64), channel_id=1, source_target_pairs={{0,1},{1,0},{2,3},{3,2},{4,5},{5,4},{6,7},{7,6},{8,9},{9,8},{10,11... | collective-permute-start | bytes 417800 | tf_op jit(solution)/shard_map/ppermute | solution.py:530
  20.8 10.9 %collective-permute-start.2 = (bf16[272,256]{1,0:T(8,128)(2,1)S(1)}, bf16[272,256]{1,0:T(8,128)(2,1)S(1)}, u32[]{:S(2)}, u32[]{:S(2)}) collective-permute-start(bf16[272,256]{1,0:T(8,128)(2,1)S(1)} %get-tuple-element.64), channel_id=1, source_target_pairs={{1,2},{2,1},{3,4},{4,3},{5,6},{6,5},{7,8},{8,7},{9,10},{10,9},{11,... | collective-permute-start | bytes 417800 | tf_op jit(solution)/shard_map/ppermute | solution.py:529
  21.4 10.2 %collective-permute-start.3 = (bf16[256,256]{1,0:T(8,128)(2,1)S(1)}, bf16[256,256]{1,0:T(8,128)(2,1)S(1)}, u32[]{:S(2)}, u32[]{:S(2)}) collective-permute-start(bf16[256,256]{1,0:T(8,128)(2,1)S(1)} %get-tuple-element.67.a_ref.a3_ref), channel_id=1, source_target_pairs={{2,4},{3,5},{4,2},{5,3},{6,8},{7,9},{8,6},{9,7},{10,12},{11,13},{1... | collective-permute-start | bytes 393224 | tf_op jit(solution)/shard_map/ppermute | solution.py:537
  23.5 11.6 %collective-permute-start.5 = (bf16[256,256]{1,0:T(8,128)(2,1)S(1)}, bf16[256,256]{1,0:T(8,128)(2,1)S(1)}, u32[]{:S(2)}, u32[]{:S(2)}) collective-permute-start(bf16[256,256]{1,0:T(8,128)(2,1)S(1)} %get-tuple-element.67.a_ref.a3_ref), channel_id=1, source_target_pairs={{0,2},{1,3},{2,0},{3,1},{4,6},{5,7},{6,4},{7,5},{8,10},{9,11},{10,... | collective-permute-start | bytes 393224 | tf_op jit(solution)/shard_map/ppermute | solution.py:538
  35.2 7.1 %copy-start.7 = (bf16[2,2,256,256]{3,2,1,0:T(8,128)(2,1)S(1)}, bf16[2,2,256,256]{3,2,1,0:T(8,128)(2,1)}, u32[]{:S(2)}) copy-start(bf16[2,2,256,256]{3,2,1,0:T(8,128)(2,1)} %get-tuple-element.89.sides_ref) | copy-start | bytes 1572868
  38.8 5.3 %copy-start.1 = (bf16[256,2304]{1,0:T(8,128)(2,1)S(1)}, bf16[256,2304]{1,0:T(8,128)(2,1)}, u32[]{:S(2)}) copy-start(bf16[256,2304]{1,0:T(8,128)(2,1)} %get-tuple-element.92.b2_ref) | copy-start | bytes 3538948
  38.8 9.3 %collective-permute-start.6 = (bf16[2,256,256]{2,1,0:T(8,128)(2,1)S(1)}, bf16[2,256,256]{2,1,0:T(8,128)(2,1)S(1)}, u32[]{:S(2)}, u32[]{:S(2)}) collective-permute-start(bf16[2,256,256]{2,1,0:T(8,128)(2,1)S(1)} %get-tuple-element.82), channel_id=1, source_target_pairs={{1,2},{2,1},{3,4},{4,3},{5,6},{6,5},{7,8},{8,7},{9,10},{10,9},{11,... | collective-permute-start | bytes 786440 | tf_op jit(solution)/shard_map/ppermute | solution.py:529
  39.6 8.5 %collective-permute-start.7 = (bf16[2,256,256]{2,1,0:T(8,128)(2,1)S(1)}, bf16[2,256,256]{2,1,0:T(8,128)(2,1)S(1)}, u32[]{:S(2)}, u32[]{:S(2)}) collective-permute-start(bf16[2,256,256]{2,1,0:T(8,128)(2,1)S(1)} %get-tuple-element.83), channel_id=1, source_target_pairs={{0,1},{1,0},{2,3},{3,2},{4,5},{5,4},{6,7},{7,6},{8,9},{9,8},{10,11... | collective-permute-start | bytes 786440 | tf_op jit(solution)/shard_map/ppermute | solution.py:530
  45.4 6.3 %copy-start.6 = (bf16[1024,256]{1,0:T(8,128)(2,1)S(1)}, bf16[1024,256]{1,0:T(8,128)(2,1)}, u32[]{:S(2)}) copy-start(bf16[1024,256]{1,0:T(8,128)(2,1)} %get-tuple-element.100.perm_ref) | copy-start | bytes 1572868
  46.6 5.1 %copy-start.2 = (bf16[2,2,1024,256]{3,2,1,0:T(8,128)(2,1)S(1)}, bf16[2,2,1024,256]{3,2,1,0:T(8,128)(2,1)}, u32[]{:S(2)}) copy-start(bf16[2,2,1024,256]{3,2,1,0:T(8,128)(2,1)} %get-tuple-element.99.vp_ref) | copy-start | bytes 6291460
  48.1 6.0 %collective-permute-start.8 = (bf16[2560,128]{1,0:T(8,128)(2,1)S(1)}, bf16[2560,128]{1,0:T(8,128)(2,1)S(1)}, u32[]{:S(2)}, u32[]{:S(2)}) collective-permute-start(bf16[2560,128]{1,0:T(8,128)(2,1)S(1)} %get-tuple-element.102), channel_id=1, source_target_pairs={{0,64},{64,0},{1,65},{65,1},{2,66},{66,2},{3,67},{67,3},{4,68},{68... | collective-permute-start | bytes 1966088 | tf_op jit(solution)/shard_map/ppermute | solution.py:542
  85.6 3.1 %collective-permute-start.9 = (f32[1,128]{1,0:T(1,128)S(1)}, f32[1,128]{1,0:T(1,128)S(1)}, u32[]{:S(2)}, u32[]{:S(2)}) collective-permute-start(f32[1,128]{1,0:T(1,128)S(1)} %slice.13), channel_id=1, source_target_pairs={{0,64},{64,0},{1,65},{65,1},{2,66},{66,2},{3,67},{67,3},{4,68},{68... | collective-permute-start | bytes 1544 | tf_op jit(solution)/shard_map/ppermute | solution.py:542
